TPU v7x, 32 devices: a whole 2x2x4 slice. The times are simulated.
32 devices in a mesh: seq: 2 (over core), row: 4 (over y, x), col: 4 (over z).
Axes of the slice: x: 2, y: 2, z: 4, core: 2. Of those that a mesh axis runs over, the one named last changes fastest.
Arguments:
- tokens: bfloat16 [1024, 4096], P('seq', ('row', 'col')), may hold values from -6 to 6
- lengths: int32 [16], replicated, may hold values from 1 to 256, 1024 in all
- deal: int32 [16], replicated, may hold values from 0 to 15, each once
- pre_gain: float32 [4096], replicated, may hold values from 0.5 to 1.5
- w_inner: bfloat16 [4096, 2, 8192], P(None, None, ('row', 'col'))
- w_group: bfloat16 [4096, 2, 8, 128], P(None, None, 'row'), may hold values from -0.09375 to 0.09375
- w_step: bfloat16 [4096, 128], P(None, ('row', 'col')), may hold values from -0.09375 to 0.09375
- conv_inner: float32 [4, 8192], P(None, ('row', 'col')), may hold values from -0.5 to 0.5
- conv_group: float32 [4, 2, 8, 128], P(None, None, 'row'), may hold values from -0.5 to 0.5
- conv_bias_inner: float32 [8192], P(('row', 'col')), may hold values from -0.5 to 0.5
- conv_bias_group: float32 [2, 8, 128], P(None, 'row'), may hold values from -0.5 to 0.5
- edge_inner: bfloat16 [16, 3, 8192], P(None, None, ('row', 'col')), may hold values from -6 to 6
- edge_group: bfloat16 [16, 3, 2, 8, 128], P(None, None, None, 'row'), may hold values from -6 to 6
- init_states: float32 [16, 128, 64, 128], P(None, ('row', 'col')), may hold values from -1.25 to 1.25
- step_bias: float32 [128], P(('row', 'col')), may hold values from -5.3 to -2.3
- decay_log: float32 [128], P(('row', 'col')), may hold values from -3.9 to 0
- skip: float32 [128], P(('row', 'col')), may hold values from 0.5 to 1.5
- inner_gain: float32 [8192], P(('row', 'col')), may hold values from 0.5 to 1.5
- w_out: bfloat16 [8192, 4096], P(('row', 'col')), may hold values from -0.09375 to 0.09375
- final_gain: float32 [4096], replicated, may hold values from 0.5 to 1.5
- w_head: bfloat16 [4096, 32768], P(None, ('seq', 'row', 'col')), may hold values from -0.09375 to 0.09375
Outputs:
- hidden_out: bfloat16 [1024, 4096], P('seq', ('row', 'col'))
- final_states: float32 [16, 128, 64, 128], P('seq', ('row', 'col'))
- logits: float32 [16, 32768], P(None, ('seq', 'row', 'col'))
Inputs may be any that keep to these rules, and one draw needn't show every extreme that they name: The lengths sum to 1024 and the longest is exactly 256. `deal`: each owner slot appears once.
All inputs are finite; a program needn't handle non-finite values.
Results may differ from a plain program's by a relative error of at most 0.012.
Values may be sent and summed in bfloat16 or wider, within the bound.
No kernel may reach another device: no remote copies, remote signals or barrier semaphores. Data moves between devices by JAX's collectives and lax.ppermute only.
A program may use at most 128 MiB of HBM per device.

v0:
```python
import jax
import jax.numpy as jnp
from jax import lax
from jax.sharding import PartitionSpec as P

BLOCK = 256


EPSILON = 1e-05
HIGHEST = lax.Precision.HIGHEST


def from_behind(block, axis, distance):
    devices = range(lax.axis_size(axis))
    route = [(i - distance, i) for i in devices if i - distance in devices]
    return lax.ppermute(block, axis, route)


def from_partner(x, axis, bit):
    return lax.ppermute(x, axis, [(i, i ^ 1 << bit) for i in range(lax.axis_size(axis))])


def pick_group(table, axis, which):
    return lax.dynamic_index_in_dim(table, which, axis, keepdims=False)


def exact_pairs(spread, keys_bf, form):
    upper = spread.astype(jnp.bfloat16)
    lower_part = (spread - upper.astype(jnp.float32)).astype(jnp.bfloat16)
    first_term = jnp.einsum(form, upper, keys_bf, preferred_element_type=jnp.float32)
    return first_term + jnp.einsum(form, lower_part, keys_bf, preferred_element_type=jnp.float32)


def per_device(
    tokens,
    lengths,
    deal,
    pre_gain,
    w_inner,
    w_group,
    w_step,
    conv_inner,
    conv_group,
    conv_bias_inner,
    conv_bias_group,
    edge_inner,
    edge_group,
    init_states,
    step_bias,
    decay_log,
    skip,
    inner_gain,
    w_out,
    final_gain,
    w_head,
):
    rows = tokens.shape[0]
    model_width = pre_gain.shape[0]
    requests = lengths.shape[0]
    kernel = conv_inner.shape[0]
    inner_dev = w_inner.shape[2]
    heads_dev = w_step.shape[1]
    head_size = inner_dev // heads_dev
    state_size = w_group.shape[3]
    group_local = lax.axis_index("col") * w_group.shape[2] // lax.axis_size("col")
    w_gate_x = jnp.reshape(w_inner, (model_width, 2 * inner_dev))
    w_pair = jnp.reshape(pick_group(w_group, 2, group_local), (model_width, 2 * state_size))
    wide = lax.all_gather(tokens, ("row", "col"), axis=1, tiled=True).astype(jnp.float32)
    scaled = (wide * pre_gain).astype(jnp.bfloat16)
    gate_x = jnp.dot(scaled, w_gate_x, preferred_element_type=jnp.float32)
    pair = jnp.dot(scaled, w_pair, preferred_element_type=jnp.float32)
    steps = jnp.dot(scaled, w_step, preferred_element_type=jnp.float32)
    gate_x, pair, steps, squares = (gate_x, pair, steps, jnp.sum(wide * wide, axis=1))
    inv_rms = lax.rsqrt(squares / model_width + EPSILON)[:, None]
    gate_in = (gate_x[:, :inner_dev] * inv_rms).astype(jnp.bfloat16)
    inner_in = (gate_x[:, inner_dev:] * inv_rms).astype(jnp.bfloat16)
    pair_in = (pair * inv_rms).astype(jnp.bfloat16)
    step_raw = steps * inv_rms
    ends = jnp.cumsum(lengths)
    begins = ends - lengths
    first_row = lax.axis_index("seq") * rows
    position = first_row + jnp.arange(rows, dtype=jnp.int32)
    segment = jnp.sum((begins[None, :] <= position[:, None]).astype(jnp.int32), axis=1) - 1
    seg_before = jnp.sum((begins[None, :] < position[:, None]).astype(jnp.int32), axis=1) - 1
    member = segment[:, None] == jnp.arange(requests, dtype=jnp.int32)[None, :]
    offset = position - jnp.sum(jnp.where(member, begins[None, :], 0), axis=1)
    owner = jnp.sum(jnp.where(member, deal[None, :], 0), axis=1)
    channels = jnp.concatenate([inner_in, pair_in], axis=1)
    width_all = channels.shape[1]
    conv_taps = jnp.concatenate(
        [conv_inner, jnp.reshape(pick_group(conv_group, 2, group_local), (kernel, 2 * state_size))],
        axis=1,
    )
    conv_shift = jnp.concatenate(
        [
            conv_bias_inner,
            jnp.reshape(pick_group(conv_bias_group, 1, group_local), (2 * state_size,)),
        ]
    )
    edges = jnp.concatenate(
        [
            edge_inner,
            jnp.reshape(
                pick_group(edge_group, 3, group_local), (requests, kernel - 1, 2 * state_size)
            ),
        ],
        axis=2,
    )
    edges = jnp.reshape(edges, (requests * (kernel - 1), width_all))
    rim = from_behind(channels[rows - (kernel - 1) :], "seq", 1)
    extended = jnp.concatenate([rim, channels], axis=0)
    summed = conv_shift + conv_taps[kernel - 1] * channels.astype(jnp.float32)
    slots = jnp.arange(requests * (kernel - 1), dtype=jnp.int32)
    for back in range(1, kernel):
        earlier = extended[kernel - 1 - back : kernel - 1 - back + rows]
        slot = owner * (kernel - 1) + (kernel - 1 - back) + offset
        lookup = ((slot[:, None] == slots[None, :]) & (offset < back)[:, None]).astype(jnp.bfloat16)
        from_edge = jnp.dot(lookup, edges, preferred_element_type=jnp.float32)
        value = jnp.where((offset >= back)[:, None], earlier.astype(jnp.float32), from_edge)
        summed = summed + conv_taps[kernel - 1 - back] * value
    mixed_in = jax.nn.silu(summed).astype(jnp.bfloat16)
    blocks = rows // BLOCK
    inner_x = jnp.reshape(mixed_in[:, :inner_dev], (blocks, BLOCK, heads_dev, head_size))
    keys = jnp.reshape(mixed_in[:, inner_dev : inner_dev + state_size], (blocks, BLOCK, state_size))
    queries = jnp.reshape(mixed_in[:, inner_dev + state_size :], (blocks, BLOCK, state_size))
    step = jax.nn.softplus(step_raw + step_bias)
    log_decay = -jnp.exp(decay_log) * step
    step_blocks = jnp.reshape(step, (blocks, BLOCK, heads_dev))
    log_blocks = jnp.reshape(log_decay, (blocks, BLOCK, heads_dev))
    running = jnp.cumsum(log_blocks, axis=1)
    seg_blocks = jnp.reshape(segment, (blocks, BLOCK))
    prev_blocks = jnp.reshape(seg_before, (blocks, BLOCK))
    flag = seg_blocks == prev_blocks[:, :1]
    lower = jnp.arange(BLOCK)[:, None] >= jnp.arange(BLOCK)[None, :]
    same = (seg_blocks[:, :, None] == seg_blocks[:, None, :]) & lower[None]
    first = seg_blocks != prev_blocks
    base = jnp.einsum(
        "cts,csh->cth",
        (same & first[:, None, :]).astype(jnp.float32),
        running - log_blocks,
        precision=HIGHEST,
    )
    keep = same[..., None]
    diff = running[:, :, None, :] - running[:, None, :, :]
    decay = jnp.where(keep, jnp.exp(jnp.where(keep, diff, 0.0)), 0.0)
    scores = jnp.einsum("ctn,csn->cts", queries, keys, preferred_element_type=jnp.float32)
    weight = (scores[..., None] * decay * step_blocks[:, None, :, :]).astype(jnp.bfloat16)
    within = jnp.einsum("ctsh,cshp->cthp", weight, inner_x, preferred_element_type=jnp.float32)
    dealing = (deal[:, None] == jnp.arange(requests, dtype=jnp.int32)[None, :]).astype(jnp.float32)
    init_dealt = jnp.reshape(
        jnp.dot(dealing, jnp.reshape(init_states, (requests, -1)), precision=HIGHEST),
        init_states.shape,
    )
    member_blocks = jnp.reshape(member.astype(jnp.float32), (blocks, BLOCK, requests))
    query_wide = queries.astype(jnp.float32)
    picked = jnp.where(
        jnp.reshape(member, (blocks, BLOCK, requests))[..., None],
        queries[:, :, None, :],
        jnp.zeros((), jnp.bfloat16),
    )
    init_high = init_dealt.astype(jnp.bfloat16)
    init_rest = init_dealt - init_high.astype(jnp.float32)
    init_mid = init_rest.astype(jnp.bfloat16)
    init_low = (init_rest - init_mid.astype(jnp.float32)).astype(jnp.bfloat16)
    init_dot = jnp.einsum("ctrn,rhpn->cthp", picked, init_high, preferred_element_type=jnp.float32)
    init_dot = init_dot + jnp.einsum(
        "ctrn,rhpn->cthp", picked, init_mid, preferred_element_type=jnp.float32
    )
    init_dot = init_dot + jnp.einsum(
        "ctrn,rhpn->cthp", picked, init_low, preferred_element_type=jnp.float32
    )
    init_coef = jnp.where(flag[..., None], 0.0, jnp.exp(running - base))
    carry_coef = jnp.where(flag[..., None], jnp.exp(running), 0.0)
    local_y = within + init_coef[..., None] * init_dot
    end_local = ends - 1 - first_row
    local_pos = jnp.reshape(jnp.arange(rows, dtype=jnp.int32), (blocks, BLOCK))
    select = (local_pos[:, None, :] == end_local[None, :, None]).astype(jnp.float32)
    block_pick = jnp.sum(select, axis=2)
    sel_init = jnp.einsum("cjt,cth->cjh", select, init_coef, precision=HIGHEST)
    sel_carry = jnp.einsum("cjt,cth->cjh", select, carry_coef, precision=HIGHEST)
    sel_member = jnp.einsum("cjt,ctr->cjr", select, member_blocks, precision=HIGHEST)
    sel_inits = jnp.einsum("cjr,rhpn->cjhpn", sel_member, init_dealt, precision=HIGHEST)
    decay_req = jnp.einsum("cjt,ctsh->jsh", select, decay, precision=HIGHEST)
    step_req = jnp.einsum("cj,csh->jsh", block_pick, step_blocks, precision=HIGHEST)
    pick_bf = block_pick.astype(jnp.bfloat16)
    x_req = jnp.einsum(
        "cj,cshp->jshp", pick_bf, inner_x, preferred_element_type=jnp.float32
    ).astype(jnp.bfloat16)
    keys_req = jnp.einsum("cj,csn->jsn", pick_bf, keys, preferred_element_type=jnp.float32).astype(
        jnp.bfloat16
    )
    share_req = (decay_req * step_req).astype(jnp.bfloat16)
    share_req = lax.optimization_barrier(share_req).astype(jnp.float32)
    spread_req = share_req[..., None] * x_req.astype(jnp.float32)
    local_req = exact_pairs(spread_req, keys_req, "jshp,jsn->jhpn")
    share_last = (decay[:, BLOCK - 1] * step_blocks).astype(jnp.bfloat16)
    share_last = lax.optimization_barrier(share_last).astype(jnp.float32)
    spread_last = share_last[..., None] * inner_x.astype(jnp.float32)
    last_state = exact_pairs(spread_last, keys, "cshp,csn->chpn")
    last_init = init_coef[:, BLOCK - 1]
    last_member = member_blocks[:, BLOCK - 1]
    last_inits = jnp.einsum("cr,rhpn->chpn", last_member, init_dealt, precision=HIGHEST)
    last_state = last_state + last_init[..., None, None] * last_inits
    last_carry = carry_coef[:, BLOCK - 1]
    gain_run = jnp.ones((heads_dev,), jnp.float32)
    state_run = jnp.zeros((heads_dev, head_size, state_size), jnp.float32)
    gain_list = []
    state_list = []
    for block in range(blocks):
        gain_list.append(gain_run)
        state_list.append(state_run)
        factor = last_carry[block]
        gain_run = factor * gain_run
        state_run = factor[:, None, None] * state_run + last_state[block]

    def relay_step(turn, entering):
        leaving = gain_run[:, None, None] * entering + state_run
        return from_behind(leaving, "seq", 1)

    entry_dev = lax.fori_loop(0, lax.axis_size("seq") - 1, relay_step, jnp.zeros_like(state_run))
    entries = jnp.stack(gain_list)[:, :, None, None] * entry_dev[None] + jnp.stack(state_list)
    carry_dot = jnp.einsum("ctn,chpn->cthp", query_wide, entries, precision=HIGHEST)
    outputs = local_y + carry_coef[..., None] * carry_dot
    outputs = outputs + skip[:, None] * inner_x.astype(jnp.float32)
    finals = local_req + jnp.sum(sel_init[..., None, None] * sel_inits, axis=0)
    finals = finals + jnp.sum(sel_carry[..., None, None] * entries[:, None], axis=0)
    owned = jnp.reshape(
        jnp.dot(dealing.T, jnp.reshape(finals, (requests, -1)), precision=HIGHEST), finals.shape
    )
    final_states = lax.psum_scatter(owned, "seq", scatter_dimension=0, tiled=True)
    y_flat = jnp.reshape(outputs, (rows, inner_dev))
    gated = y_flat * jax.nn.silu(gate_in.astype(jnp.float32))
    own_squares = jnp.sum(gated * gated, axis=1)
    other_squares = from_partner(own_squares, "col", 0)
    norm_scale = lax.rsqrt((own_squares + other_squares) / (2 * inner_dev) + EPSILON)
    normed = (gated * norm_scale[:, None] * inner_gain).astype(jnp.bfloat16)
    partial_value = jnp.dot(normed, w_out, preferred_element_type=jnp.float32)
    mixed = lax.psum_scatter(partial_value, ("row", "col"), scatter_dimension=1, tiled=True)
    hidden_out = (tokens.astype(jnp.float32) + mixed).astype(jnp.bfloat16)
    chooser = (end_local[:, None] == jnp.arange(rows, dtype=jnp.int32)[None, :]).astype(
        jnp.bfloat16
    )
    ending = jnp.dot(chooser, hidden_out, preferred_element_type=jnp.float32)
    ending_rows = lax.psum(ending, "seq").astype(jnp.bfloat16)
    last_rows = lax.all_gather(ending_rows, ("row", "col"), axis=1, tiled=True)
    last_wide = last_rows.astype(jnp.float32)
    final_scale = lax.rsqrt(jnp.sum(last_wide * last_wide, axis=1) / model_width + EPSILON)
    head_in = (last_wide * final_scale[:, None] * final_gain).astype(jnp.bfloat16)
    scores_out = jnp.dot(head_in, w_head, preferred_element_type=jnp.float32)
    logits = jnp.dot(dealing.T, scores_out, precision=HIGHEST)
    return (hidden_out, final_states, logits)


def solution(mesh):
    in_specs = (
        P("seq", ("row", "col")),
        P(),
        P(),
        P(),
        P(None, None, ("row", "col")),
        P(None, None, "row", None),
        P(None, ("row", "col")),
        P(None, ("row", "col")),
        P(None, None, "row", None),
        P(("row", "col")),
        P(None, "row", None),
        P(None, None, ("row", "col")),
        P(None, None, None, "row", None),
        P(None, ("row", "col"), None, None),
        P(("row", "col")),
        P(("row", "col")),
        P(("row", "col")),
        P(("row", "col")),
        P(("row", "col"), None),
        P(),
        P(None, ("seq", "row", "col")),
    )
    out_specs = (
        P("seq", ("row", "col")),
        P("seq", ("row", "col"), None, None),
        P(None, ("seq", "row", "col")),
    )
    return jax.shard_map(
        per_device, mesh=mesh, in_specs=in_specs, out_specs=out_specs, check_vma=False
    )
```

profile of v0, /device:TPU:0, one launch (start us, length us, event | category | flops | bytes accessed | tf_op | source)
XLA Modules:
  0.0 431.8 jit_solution(6402634639965982694)
XLA Ops:
  7.2 0.7 all-gather.2.cloned.1.call-update
  8.0 8.4 %constant_dynamic-slice_fusion = bf16[4096,2,1,128]{3,2,1,0:T(2,128)(2,1)} fusion(bf16[4096,2,2,128]{3,2,1,0:T(2,128)(2,1)} %param.26, s32[]{:T(128)S(6)} %select_n.56), kind=kLoop, calls=%fused_computation.231 | loop fusion | bytes 4194308 | tf_op jit(solution)/shard_map/jit(dynamic_index_in_dim)/dynamic_slice | solution.py:24
  16.4 8.6 %copy.243 = bf16[4096,2,1,128]{0,3,1,2:T(8,128)(2,1)S(1)} copy(bf16[4096,2,1,128]{3,2,1,0:T(2,128)(2,1)} %constant_dynamic-slice_fusion) | data formatting | bytes 4194304
  25.1 9.3 %copy.245 = bf16[512,8,2,512]{3,1,2,0:T(8,128)(2,1)} copy(bf16[512,8,2,512]{3,2,1,0:T(2,128)(2,1)} %bitcast.215) | data formatting | bytes 16777216
  35.3 1.0 copy.193
  36.2 4.6 %copy.327 = f32[2,8,512,128]{3,1,2,0:T(8,128)S(1)} copy(f32[2,8,512,128]{3,2,1,0:T(8,128)} %bitcast.217) | data formatting | bytes 8388608
  40.9 2.8 copy.248
  44.6 0.6 pad_maximum_fusion.1
  45.3 0.8 convolution_bitcast_fusion
  46.1 0.6 slice_reduce_fusion.7
  46.9 0.6 broadcast_compare_fusion.5
  47.5 0.6 fusion.205
  48.0 0.6 add_add_fusion.1
  48.6 1.6 fusion.146
  50.3 1.6 fusion.149
  51.9 9.1 %subtract_convert_fusion.1 = (bf16[16,8,64,128]{3,0,2,1:T(8,128)(2,1)}, bf16[16,8,64,128]{3,0,2,1:T(8,128)(2,1)}, bf16[16,8,64,128]{3,0,2,1:T(8,128)(2,1)}, f32[16,8,64,128]{3,0,2,1:T(8,128)S(1)}) fusion(f32[8,64,128,16]{2,1,0,3:T(8,128)} %bitcast.212, s32[16]{0:T(128)S(1)} %copy-done.22), kind=kOutput, calls=%fused_computation.25 | convolution fusion | flops 208666880 | bytes 14680128 | tf_op jit(solution)/shard_map/dot_general | solution.py:151
  61.0 2.0 copy-done.2
  63.0 1.6 fusion.193
  64.6 36.0 %all-gather.2.cloned.1.call-done = bf16[512,4096]{1,0:T(8,128)(2,1)} async-done(((bf16[512,256]{1,0:T(8,128)(2,1)}), bf16[512,4096]{1,0:T(8,128)(2,1)}) %all-gather.2.cloned.1.call-update) | async-done | bytes 4194320 | tf_op jit(solution)/shard_map/all_gather | solution.py:68
  100.6 3.2 fusion.1
  104.0 1.2 broadcast_multiply_fusion
  105.3 1.2 reduce-window.18
  107.1 8.3 %fusion.20 = f32[512,1024]{1,0:T(8,128)S(1)} fusion(bf16[4096,1024]{1,0:T(8,128)(2,1)} %bitcast.216, bf16[512,4096]{1,0:T(8,128)(2,1)} %all-gather.2.cloned.1.call-done, f32[4096]{0:T(1024)S(1)} %copy-done.48), kind=kOutput, calls=%fused_computation.31 | convolution fusion | flops 4301258752 | bytes 14696448 | tf_op jit(solution)/shard_map/dot_general | solution.py:70
  115.6 1.3 fusion.92
  117.0 1.4 collective-permute-start
  118.4 0.4 fusion.106
  119.1 0.6 multiply_multiply_fusion
  119.8 9.6 %multiply_reduce_fusion.1 = f32[16,8,64,128]{3,0,2,1:T(8,128)} fusion(f32[2,16,8]{1,2,0:T(8,128)S(1)} %fusion.166, f32[2,16,16,1,1]{2,1,4,3,0:T(8,128)S(1)} %copy-done.21, f32[16,8,64,128]{3,0,2,1:T(8,128)S(1)} %copy-done.3), kind=kOutput, calls=%fused_computation.5 | convolution fusion | flops 405798912 | bytes 8391680 | tf_op jit(solution)/shard_map/cjr,rhpn->cjhpn/dot_general | solution.py:182
  129.5 0.9 copy.194
  130.4 0.6 stack.7
  131.0 1.1 maximum_maximum_fusion
  132.2 3.4 multiply_convert_fusion.1
  136.5 1.5 exponential_select_fusion
  138.1 4.5 %fusion.95 = f32[16,256,8]{1,0,2:T(8,128)} fusion(f32[2,256,256,8]{2,3,0,1:T(8,128)S(1)} %get-tuple-element.54, s32[2,256]{1,0:T(2,128)S(1)} %multiply_add_fusion, s32[16]{0:T(128)S(1)} %get-tuple-element.67), kind=kOutput, calls=%fused_computation.78 | convolution fusion | flops 201334784 | bytes 4327488 | tf_op jit(solution)/shard_map/cjt,ctsh->jsh/dot_general | solution.py:183
  142.7 1.0 copy.191
  143.7 1.2 reshape.306
  145.6 1.3 collective-permute-start.1
  146.9 0.5 fusion.65
  147.8 2.3 fusion.2
  150.1 1.6 fusion.8
  152.0 0.5 multiply_reduce_fusion
  152.5 1.4 copy-done.4
  154.0 5.7 %fusion.7 = f32[16,8,64,128]{3,2,1,0:T(8,128)S(1)} fusion(f32[16,8,64,128]{3,2,1,0:T(8,128)S(1)} %multiply_reduce_fusion, f32[16,8,64,128]{3,0,2,1:T(8,128)S(1)} %copy-done.4, f32[16,8,64,128]{3,2,1,0:T(8,128)S(1)} %fusion.8, bf16[16,256,8,64]{1,0,3,2:T(8,128)(2,1)S(1)} %get-tuple-element.47, bf16[16,256,128,1]{2,0,1,3:T(8,128)(2,1)S(1)} %fusion.65), kind=kOutput, calls=%fused_computation.16 | convolution fusion | flops 540016640 | bytes 22020096 | tf_op jit(solution)/shard_map/jshp,jsn->jhpn/dot_general | solution.py:30
  159.6 2.4 copy.326
  162.1 0.8 copy.250
  162.9 6.5 %fusion.5 = f32[16,8,64,128]{3,0,2,1:T(8,128)} fusion(f32[8,64,128,16]{2,1,0,3:T(8,128)S(1)} %bitcast.213, s32[16]{0:T(128)S(1)} %copy-done.22), kind=kOutput, calls=%fused_computation.13 | convolution fusion | flops 201326848 | bytes 8388672 | tf_op jit(solution)/shard_map/dot_general | solution.py:228
  170.1 3.2 fusion.47
  173.3 1.4 fusion.76
  174.7 0.6 copy-done.9
  175.4 1.4 fusion.83
  176.8 0.9 fusion.68
  177.7 1.7 fusion.67
  179.4 2.1 copy.237
  181.5 0.5 reshape.336
  182.0 1.8 multiply_reduce_fusion.2
  183.9 3.5 collective-permute-done.2
  187.4 7.8 %fusion.122 = f32[512,4096]{1,0:T(8,128)} fusion(bf16[512,4096]{1,0:T(8,128)(2,1)} %param.39, f32[512,512]{1,0:T(8,128)S(1)} %get-tuple-element.44, f32[512]{0:T(512)S(1)} %copy-done.20, f32[512]{0:T(512)S(1)} %add_rsqrt_fusion), kind=kOutput, calls=%fused_computation.110 | convolution fusion | flops 2148270080 | bytes 13635584 | tf_op jit(solution)/shard_map/dot_general | solution.py:237
  195.3 3.3 copy.219
  198.7 177.9 %reduce-scatter.3.cloned.1.call-done = f32[512,256]{1,0:T(8,128)} async-done(((f32[512,4096]{1,0:T(8,128)}), f32[512,256]{1,0:T(8,128)}) %reduce-scatter.3.cloned.1.call-update) | async-done | bytes 524304 | tf_op jit(solution)/shard_map/reduce_scatter | solution.py:238
  376.6 1.1 add_convert_fusion
  377.9 3.4 psum.7
  381.2 38.2 %all_gather.7 = bf16[16,4096]{1,0:T(8,128)(2,1)S(1)} all-gather(bf16[16,256]{1,0:T(8,128)(2,1)S(1)} %psum.7), channel_id=1, replica_groups=mesh['seq'=2,'row'=4,'col'=4] {'row','col'}, dimensions={1}, use_global_device_ids=true | all-gather | bytes 139264 | tf_op jit(solution)/shard_map/all_gather | solution.py:245
  419.6 4.6 %fusion.152 = f32[16,1024]{1,0:T(8,128)S(1)} fusion(bf16[4096,1024]{1,0:T(8,128)(2,1)} %param.41, bf16[16,4096]{1,0:T(8,128)(2,1)S(1)} %all_gather.7, f32[4096]{0:T(1024)S(1)} %copy-done.17, f32[16]{0:T(128)S(1)} %add_rsqrt_fusion.2), kind=kOutput, calls=%fused_computation.146 | convolution fusion | flops 134479872 | bytes 8601664 | tf_op jit(solution)/shard_map/dot_general | solution.py:249
  424.3 0.8 fusion.185
  (168 shorter events, 7.0 us)
Async XLA Ops:
  7.2 96.7 %copy-start = (bf16[4096,8]{0,1:T(8,128)(2,1)S(1)}, bf16[4096,8]{0,1:T(8,128)(2,1)}, u32[]{:S(2)}) copy-start(bf16[4096,8]{0,1:T(8,128)(2,1)} %param.27) | copy-start | bytes 196612
  7.2 93.4 %all-gather.2.cloned.1.call-start = ((), (), s32[]{:S(2)}) async-start(), calls=%async_computation.2 | async-start | bytes 4456448 | tf_op jit(solution)/shard_map/all_gather | solution.py:68
  7.9 187.4 %reduce-scatter.5.cloned.1.call-start = ((), (), s32[]{:S(2)}) async-start(), calls=%async_computation.4 | async-start | bytes 6291456 | tf_op jit(solution)/shard_map/reduce_scatter | solution.py:230
  25.0 9.4 %copy-start.18 = (bf16[16,3,512]{2,0,1:T(8,128)(2,1)S(1)}, bf16[16,3,512]{2,0,1:T(8,128)(2,1)}, u32[]{:S(2)}) copy-start(bf16[16,3,512]{2,0,1:T(8,128)(2,1)} %param.32) | copy-start | bytes 147460
  25.1 9.4 %copy-start.37 = (s32[16]{0:T(128)S(1)}, s32[16]{0:T(128)}, u32[]{:S(2)}) copy-start(s32[16]{0:T(128)} %param.22) | copy-start | bytes 196
  40.8 3.3 copy-start.38
  40.9 3.4 copy-start.19
  40.9 3.5 copy-start.42
  40.9 3.7 copy-start.36
  40.9 4.3 copy-start.25
  40.9 5.9 %copy-start.22 = (s32[16]{0:T(128)S(1)}, s32[16]{0:T(128)}, u32[]{:S(2)}) copy-start(s32[16]{0:T(128)} %param.23) | copy-start | bytes 196
  40.9 5.9 %copy-start.50 = (f32[8]{0:T(128)S(1)}, f32[8]{0:T(128)}, u32[]{:S(2)}) copy-start(f32[8]{0:T(128)} %param.36) | copy-start | bytes 100
  44.2 16.9 %copy-start.23 = (pred[2,256,16]{1,2,0:T(8,128)(4,1)}, pred[2,256,16]{1,2,0:T(8,128)(4,1)S(1)}, u32[]{:S(2)}) copy-start(pred[2,256,16]{1,2,0:T(8,128)(4,1)S(1)} %copy.198) | copy-start | bytes 24580
  48.0 58.6 %copy-start.34 = (pred[2,256]{1,0:T(4,128)(4,1)}, pred[2,256]{1,0:T(4,128)(4,1)S(1)}, u32[]{:S(2)}) copy-start(pred[2,256]{1,0:T(4,128)(4,1)S(1)} %get-tuple-element.60) | copy-start | bytes 1540
  61.0 2.0 copy-start.2
  63.0 40.8 %copy-start.48 = (f32[4096]{0:T(1024)S(1)}, f32[4096]{0:T(1024)}, u32[]{:S(2)}) copy-start(f32[4096]{0:T(1024)} %param.24) | copy-start | bytes 49156
  63.0 40.8 %copy-start.51 = (f32[8]{0:T(128)S(1)}, f32[8]{0:T(128)}, u32[]{:S(2)}) copy-start(f32[8]{0:T(128)} %param.35) | copy-start | bytes 100
  100.6 3.4 copy-start.5
  107.1 8.5 %copy-start.6 = (bf16[512,4096]{1,0:T(8,128)(2,1)S(1)}, bf16[512,4096]{1,0:T(8,128)(2,1)}, u32[]{:S(2)}) copy-start(bf16[512,4096]{1,0:T(8,128)(2,1)} %all-gather.2.cloned.1.call-done) | copy-start | bytes 12582916
  107.1 8.5 %copy-start.49 = (f32[4096]{0:T(1024)S(1)}, f32[4096]{0:T(1024)}, u32[]{:S(2)}) copy-start(f32[4096]{0:T(1024)} %param.24) | copy-start | bytes 49156
  115.4 1.5 copy-start.7
  115.6 2.8 copy-start.35
  115.6 2.8 copy-start.41
  115.6 4.1 copy-start.3
  115.6 4.0 copy-start.21
  117.0 12.4 %copy-start.11 = (bf16[512,256]{1,0:T(8,128)(2,1)}, bf16[512,256]{1,0:T(8,128)(2,1)S(1)}, u32[]{:S(2)}) copy-start(bf16[512,256]{1,0:T(8,128)(2,1)S(1)} %fusion.92) | copy-start | bytes 786436
  117.0 14.0 %collective-permute-start = (bf16[3,768]{1,0:T(4,128)(2,1)S(1)}, bf16[3,768]{1,0:T(4,128)(2,1)S(1)}, u32[]{:S(2)}, u32[]{:S(2)}) collective-permute-start(bf16[3,768]{1,0:T(4,128)(2,1)S(1)} %fusion.189), channel_id=1, source_target_pairs={{0,16},{1,17},{2,18},{3,19},{4,20},{5,21},{6,22},{7,23},{8,24},{9,... | collective-permute-start | bytes 13832 | tf_op jit(solution)/shard_map/ppermute | solution.py:16
  118.9 10.5 %copy-start.32 = (f32[2,256,8]{1,2,0:T(8,128)}, f32[2,256,8]{1,2,0:T(8,128)S(1)}, u32[]{:S(2)}) copy-start(f32[2,256,8]{1,2,0:T(8,128)S(1)} %fusion.106) | copy-start | bytes 49156
  119.7 12.4 %copy-start.27 = (f32[768]{0:T(1024)S(1)}, f32[768]{0:T(1024)}, u32[]{:S(2)}) copy-start(f32[768]{0:T(1024)} %get-tuple-element.35) | copy-start | bytes 9220
  119.7 12.4 %copy-start.28 = (f32[768]{0:T(1024)S(1)}, f32[768]{0:T(1024)}, u32[]{:S(2)}) copy-start(f32[768]{0:T(1024)} %get-tuple-element.36) | copy-start | bytes 9220
  119.7 12.4 %copy-start.29 = (f32[768]{0:T(1024)S(1)}, f32[768]{0:T(1024)}, u32[]{:S(2)}) copy-start(f32[768]{0:T(1024)} %get-tuple-element.37) | copy-start | bytes 9220
  119.7 12.4 %copy-start.30 = (f32[768]{0:T(1024)S(1)}, f32[768]{0:T(1024)}, u32[]{:S(2)}) copy-start(f32[768]{0:T(1024)} %get-tuple-element.38) | copy-start | bytes 9220
  119.7 12.4 %copy-start.31 = (f32[768]{0:T(1024)S(1)}, f32[768]{0:T(1024)}, u32[]{:S(2)}) copy-start(f32[768]{0:T(1024)} %pad_maximum_fusion.1) | copy-start | bytes 9220
  119.7 12.4 %copy-start.39 = (s32[512]{0:T(512)S(1)}, s32[512]{0:T(512)}, u32[]{:S(2)}) copy-start(s32[512]{0:T(512)} %get-tuple-element.56) | copy-start | bytes 6148
  119.7 12.4 %copy-start.43 = (pred[512]{0:T(512)(128)(4,1)S(1)}, pred[512]{0:T(512)(128)(4,1)}, u32[]{:S(2)}) copy-start(pred[512]{0:T(512)(128)(4,1)} %get-tuple-element.61) | copy-start | bytes 1540
  119.7 12.4 %copy-start.44 = (pred[512]{0:T(512)(128)(4,1)S(1)}, pred[512]{0:T(512)(128)(4,1)}, u32[]{:S(2)}) copy-start(pred[512]{0:T(512)(128)(4,1)} %get-tuple-element.62) | copy-start | bytes 1540
  119.8 12.4 %copy-start.45 = (pred[512]{0:T(512)(128)(4,1)S(1)}, pred[512]{0:T(512)(128)(4,1)}, u32[]{:S(2)}) copy-start(pred[512]{0:T(512)(128)(4,1)} %get-tuple-element.64) | copy-start | bytes 1540
  119.8 12.4 %copy-start.46 = (pred[512]{0:T(512)(128)(4,1)S(1)}, pred[512]{0:T(512)(128)(4,1)}, u32[]{:S(2)}) copy-start(pred[512]{0:T(512)(128)(4,1)} %get-tuple-element.66) | copy-start | bytes 1540
  132.2 4.3 %copy-start.12 = (pred[2,256,256]{2,0,1:T(4,128)(4,1)S(1)}, pred[2,256,256]{2,0,1:T(4,128)(4,1)}, u32[]{:S(2)}) copy-start(pred[2,256,256]{2,0,1:T(4,128)(4,1)} %copy.193) | copy-start | bytes 393220
  132.2 4.3 %copy-start.13 = (f32[2,256,8]{2,0,1:T(2,128)S(1)}, f32[2,256,8]{2,0,1:T(2,128)}, u32[]{:S(2)}) copy-start(f32[2,256,8]{2,0,1:T(2,128)} %copy.194) | copy-start | bytes 49156
  135.6 0.9 copy-start.8
  138.1 4.6 %slice-start = ((bf16[512,768]{1,0:T(8,128)(2,1)}), bf16[512,512]{1,0:T(8,128)(2,1)S(1)}, s32[]{:S(2)}) async-start(bf16[512,768]{1,0:T(8,128)(2,1)} %copy-done.8), calls=%async_computation.5 | async-start | bytes 1048576 | tf_op jit(solution)/shard_map/slice | solution.py:123
  138.1 7.4 %copy-start.40 = (f32[8]{0:T(128)S(1)}, f32[8]{0:T(128)}, u32[]{:S(2)}) copy-start(f32[8]{0:T(128)} %get-tuple-element.69) | copy-start | bytes 100
  144.9 2.6 copy-start.15
  145.6 6.3 %collective-permute-start.1 = (f32[8,64,128]{2,1,0:T(8,128)S(1)}, f32[8,64,128]{2,1,0:T(8,128)S(1)}, u32[]{:S(2)}, u32[]{:S(2)}) collective-permute-start(f32[8,64,128]{2,1,0:T(8,128)S(1)} %fusion.138), channel_id=1, source_target_pairs={{0,16},{1,17},{2,18},{3,19},{4,20},{5,21},{6,22},{7,23},{8,24},{9,... | collective-permute-start | bytes 786440 | tf_op jit(solution)/shard_map/while/body/eval_jaxpr/ppermute | solution.py:16
  150.1 1.7 copy-start.26
  151.8 2.2 copy-start.4
  169.4 0.7 copy-start.24
  169.4 207.2 %reduce-scatter.3.cloned.1.call-start = ((), (), s32[]{:S(2)}) async-start(), calls=%async_computation.3 | async-start | bytes 8912896 | tf_op jit(solution)/shard_map/reduce_scatter | solution.py:238
  170.1 3.2 copy-start.10
  173.3 2.1 copy-start.9
  173.3 2.1 copy-start.33
  176.8 0.9 copy-start.47
  179.4 8.0 %copy-start.20 = (f32[512]{0:T(512)S(1)}, f32[512]{0:T(512)}, u32[]{:S(2)}) copy-start(f32[512]{0:T(512)} %param.38) | copy-start | bytes 6148
  183.8 3.6 collective-permute-start.2
  195.2 181.3 %copy-start.14 = (bf16[512,256]{1,0:T(8,128)(2,1)S(1)}, bf16[512,256]{1,0:T(8,128)(2,1)}, u32[]{:S(2)}) copy-start(bf16[512,256]{1,0:T(8,128)(2,1)} %param.21) | copy-start | bytes 786436
  195.3 224.3 %copy-start.17 = (f32[4096]{0:T(1024)S(1)}, f32[4096]{0:T(1024)}, u32[]{:S(2)}) copy-start(f32[4096]{0:T(1024)} %param.40) | copy-start | bytes 49156
  377.7 46.6 %copy-start.16 = (bf16[512,256]{1,0:T(8,128)(2,1)}, bf16[512,256]{1,0:T(8,128)(2,1)S(1)}, u32[]{:S(2)}) copy-start(bf16[512,256]{1,0:T(8,128)(2,1)S(1)} %add_convert_fusion) | copy-start | bytes 786436
  419.6 5.5 %copy-start.1 = (bf16[4096,8]{0,1:T(8,128)(2,1)S(1)}, bf16[4096,8]{0,1:T(8,128)(2,1)}, u32[]{:S(2)}) copy-start(bf16[4096,8]{0,1:T(8,128)(2,1)} %param.27) | copy-start | bytes 196612
Sparse Core Ops, SparseCore 0:
  10.7 89.7 all-gather.1
  169.5 10.9 reduce-scatter.4
  195.4 181.1 reduce-scatter.2
where the time goes:
time: 440 us; the launch traced here: 432 us
  waiting for transfers between devices  218 us (50%)
  matrix products  83.8 us (19%)
  local copies, waits for them, and re-layouts  55 us (12%)
  blocking collectives  41.6 us (9%)
  other arithmetic  15.1 us (3%)
  between operations  15 us (3%)
    reduce_scatter x1, waiting for transfers between devices, per_device(): lax.psum_scatter(partial_value, ('row', 'col'), scatter_dimension=1, tile...  178 us
    all_gather x1, blocking collectives, per_device(): last_rows = lax.all_gather(ending_rows, ('row', 'col'), axis=1, tiled=True)  38.2 us
    unnamed x114, local copies, waits for them, and re-layouts  37 us
    all_gather x1, waiting for transfers between devices, per_device(): lax.all_gather(tokens, ('row', 'col'), axis=1, tiled=True)  36 us
    dot_general x1, matrix products, per_device(): jnp.einsum('cjr,rhpn->cjhpn', sel_member, init_dealt, precision=HIGHEST)  9.6 us
    dot_general x1, matrix products, per_device(): jnp.dot(dealing, jnp.reshape(init_states, (requests, -1)), precision=HIGH...  9.14 us
  transfers between devices with their start and end apart: 6, of which 3 were waited for; matrix products, arithmetic and copies ran while one was open for 22% of the time, Pallas kernels for 0%

commit v1 on v0

v1 whole, which is shorter than its diff:
```python
import functools

import jax
import jax.numpy as jnp
from jax import lax
from jax.experimental import pallas as pl
from jax.experimental.pallas import tpu as pltpu
from jax.sharding import PartitionSpec as P

EPSILON = 1e-05
HIGHEST = lax.Precision.HIGHEST
F32 = jnp.float32
BF16 = jnp.bfloat16
LANES = 128
RIM = 16
VMEM = 40 * 1024 * 1024
ROWS_BY_ROWS = (((1,), (1,)), ((), ()))


def from_behind(block, axis, distance):
    devices = range(lax.axis_size(axis))
    route = [(i - distance, i) for i in devices if i - distance in devices]
    return lax.ppermute(block, axis, route)


def from_partner(x, axis, bit):
    return lax.ppermute(x, axis, [(i, i ^ 1 << bit) for i in range(lax.axis_size(axis))])


def from_ahead(x, axis, distance):
    size = lax.axis_size(axis)
    return lax.ppermute(x, axis, [((i + distance) % size, i) for i in range(size)])


def call(kernel, outs, *args, prefetch=None, grid=(1,), in_specs=None, out_specs=None, cost=(0, 0)):
    params = pltpu.CompilerParams(vmem_limit_bytes=VMEM)
    shapes = [jax.ShapeDtypeStruct(shape, kind) for shape, kind in outs]

    def whole(shape):
        zeros = (0,) * len(shape)
        return pl.BlockSpec(shape, lambda *_: zeros)

    specs = [
        whole(a.shape) if spec is None else spec
        for a, spec in zip(args, in_specs or [None] * len(args))
    ]
    gives = [
        whole(shape) if spec is None else spec
        for (shape, _), spec in zip(outs, out_specs or [None] * len(outs))
    ]
    prefetch = jnp.zeros((1,), jnp.int32) if prefetch is None else prefetch
    spec = pltpu.PrefetchScalarGridSpec(
        num_scalar_prefetch=1, grid=grid, in_specs=specs, out_specs=gives
    )
    flops, moved = cost
    return pl.pallas_call(
        kernel,
        out_shape=shapes,
        grid_spec=spec,
        compiler_params=params,
        cost_estimate=pl.CostEstimate(flops=flops, bytes_accessed=moved, transcendentals=0),
    )(prefetch, *args)


def plane_gather(block):
    half = block.shape[0] // 2
    upper, lower = block[:half], block[half:]
    upper_far = from_partner(upper, "row", 1)
    lower_near = from_partner(lower, "row", 0)
    upper_rest = from_partner(jnp.concatenate([upper, upper_far], axis=1), "row", 0)
    lower_rest = from_partner(jnp.concatenate([lower, lower_near], axis=1), "row", 1)
    return upper, upper_far, upper_rest, lower, lower_near, lower_rest


def table_kernel(which, group_ref, step_ref, out_ref):
    rows, pair, _, state = group_ref.shape
    flat = group_ref[...].reshape(rows * pair * 2, state)
    depth = 256
    take = depth // 4
    row = lax.broadcasted_iota(jnp.int32, (depth // 2, depth), 0)
    column = lax.broadcasted_iota(jnp.int32, (depth // 2, depth), 1)
    source = jnp.where(row < take, 4 * row, 4 * (row - take) + 2) + which[0]
    pick = jnp.where(source == column, 1.0, 0.0).astype(BF16)
    for at in range(rows // take):
        got = jnp.dot(pick, flat[at * depth : (at + 1) * depth], preferred_element_type=F32)
        got = got.astype(BF16)
        out_ref[at * take : (at + 1) * take, :state] = got[:take]
        out_ref[at * take : (at + 1) * take, state : 2 * state] = got[take:]
    out_ref[:, 2 * state :] = jnp.zeros((rows, LANES), BF16)
    out_ref[:, 2 * state : 2 * state + step_ref.shape[1]] = step_ref[...]


def project_kernel(first, last, width, inner, model_width, blocks, *refs):
    del blocks
    pieces, refs = refs[:6], refs[6:]
    chooser_ref, refs = refs[0], refs[1:]
    gains, w_main, w_rest, refs = refs[:4], refs[4:8], refs[8:12], refs[12:]
    if not first:
        total_in, squares_in, refs = refs[0], refs[1], refs[2:]
    ends_ref, refs = refs[0], refs[1:]
    upper, upper_far, upper_rest, lower, lower_near, lower_rest = [p[...] for p in pieces]
    tops = [upper, upper_rest[:, :width], upper_far, upper_rest[:, width:]]
    bottoms = [lower, lower_near, lower_rest[:, :width], lower_rest[:, width:]]
    raw = [jnp.concatenate([top, bottom], axis=0) for top, bottom in zip(tops, bottoms)]
    ends_ref[...] = jnp.dot(
        chooser_ref[...], jnp.concatenate(raw, axis=1), preferred_element_type=F32
    )
    squares = None if first else squares_in[...]
    scaled = []
    for piece, gain in zip(raw, gains):
        wide = piece.astype(F32)
        scaled.append((wide * gain[...]).astype(BF16))
        square = wide * wide
        for at in range(0, width, LANES):
            part = square[:, at : at + LANES]
            squares = part if squares is None else squares + part
    scaled = jnp.concatenate(scaled, axis=1)
    main = jnp.dot(
        scaled, jnp.concatenate([w[...] for w in w_main], axis=0), preferred_element_type=F32
    )
    rest = jnp.dot(
        scaled, jnp.concatenate([w[...] for w in w_rest], axis=0), preferred_element_type=F32
    )
    if not first:
        main = main + total_in[:, : 2 * inner]
        rest = rest + total_in[:, 2 * inner :]
    if not last:
        total_ref, squares_ref = refs
        total_ref[:, : 2 * inner] = main
        total_ref[:, 2 * inner :] = rest
        squares_ref[...] = squares
        return
    gate_ref, channels_ref, steps_ref = refs
    inv_rms = lax.rsqrt(jnp.sum(squares, axis=1, keepdims=True) / model_width + EPSILON)
    gate_ref[...] = (main[:, :inner] * inv_rms).astype(BF16)
    channels_ref[:, :inner] = (main[:, inner:] * inv_rms).astype(BF16)
    channels_ref[:, inner:] = (rest[:, :-LANES] * inv_rms).astype(BF16)
    steps_ref[...] = rest[:, -LANES:] * inv_rms


def both_heads(table, pair, head_size):
    rows = table.shape[0]
    lane = lax.broadcasted_iota(jnp.int32, (rows, 2 * head_size), 1)
    return jnp.where(
        lane < head_size, table[:, 2 * pair : 2 * pair + 1], table[:, 2 * pair + 1 : 2 * pair + 2]
    )


def over_states(row, heads, head_size):
    return jnp.concatenate(
        [jnp.broadcast_to(row[:, h : h + 1], (head_size, LANES)) for h in range(heads)], axis=0
    )


def conv_kernel(
    heads,
    owner_last,
    channels_ref,
    rim_ref,
    edges_ref,
    taps_ref,
    bias_ref,
    steps_ref,
    step_bias_ref,
    decay_ref,
    marks_ref,
    segment_ref,
    init_ref,
    x_ref,
    keys_ref,
    queries_ref,
    run_ref,
    less_ref,
    spread_ref,
    leaving_ref,
    gain_ref,
):
    del owner_last
    rows, inner = x_ref.shape
    state = keys_ref.shape[1]
    head_size = inner // heads
    taps = taps_ref.shape[0]
    channels = channels_ref[...]
    sources = jnp.concatenate([channels, rim_ref[...], edges_ref[...]], axis=0)
    summed = bias_ref[...] + taps_ref[taps - 1 : taps] * channels.astype(F32)
    column = lax.broadcasted_iota(jnp.int32, (rows, sources.shape[0]), 1)
    for back in range(1, taps):
        pick = jnp.where(marks_ref[:, back - 1 : back] == column, 1.0, 0.0).astype(BF16)
        value = jnp.dot(pick, sources, preferred_element_type=F32)
        summed = summed + taps_ref[taps - 1 - back : taps - back] * value
    mixed = (summed / (1.0 + jnp.exp(-summed))).astype(BF16)
    x = mixed[:, :inner]
    keys = mixed[:, inner : inner + state]
    x_ref[...] = x
    keys_ref[...] = keys
    queries_ref[...] = mixed[:, inner + state :]
    raw = steps_ref[...] + step_bias_ref[...]
    step = jnp.maximum(raw, 0.0) + jnp.log1p(jnp.exp(-jnp.abs(raw)))
    log_decay = -jnp.exp(decay_ref[...]) * step
    segment = marks_ref[:, 4:5]
    same = segment == segment_ref[0:1, :]
    row = lax.broadcasted_iota(jnp.int32, (rows, rows), 0)
    other = lax.broadcasted_iota(jnp.int32, (rows, rows), 1)
    until = jnp.where(same & (other <= row), 1.0, 0.0)
    after = jnp.where(same & (other > row), 1.0, 0.0)
    run = jnp.dot(until, log_decay, precision=HIGHEST, preferred_element_type=F32)
    tail = jnp.dot(after, log_decay, precision=HIGHEST, preferred_element_type=F32)
    run_ref[...] = run
    less_ref[...] = (run - jnp.log(step)).T[:8]
    share = (jnp.exp(tail) * step).astype(BF16).astype(F32)
    spread = jnp.concatenate(
        [
            both_heads(share, p, head_size)
            * x[:, p * 2 * head_size : (p + 1) * 2 * head_size].astype(F32)
            for p in range(heads // 2)
        ],
        axis=1,
    )
    spread = spread.T.astype(BF16)
    spread_ref[...] = spread
    last = jnp.where(segment == segment[rows - 1 : rows], 1.0, 0.0)
    leaving = jnp.dot(spread, (keys.astype(F32) * last).astype(BF16), preferred_element_type=F32)
    gain = jnp.exp(run[rows - 1 : rows])
    carried = jnp.broadcast_to(marks_ref[rows - 1 : rows, 5:6], (heads * head_size, state)) > 0
    gain_wide = over_states(gain, heads, head_size)
    leaving_ref[...] = jnp.where(carried, leaving, leaving + gain_wide * init_ref[0])
    gain_ref[...] = jnp.where(carried, gain_wide, 0.0)


def scan_kernel(
    heads,
    block,
    unused,
    x_ref,
    keys_ref,
    queries_ref,
    run_ref,
    less_ref,
    marks_ref,
    segment_ref,
    table_ref,
    skip_ref,
    y_ref,
    masked_ref,
    begun_ref,
):
    del unused
    rows, inner = x_ref.shape
    head_size = inner // heads
    slots = table_ref.shape[1] // queries_ref.shape[1]
    queries = queries_ref[...].astype(F32)
    slot = marks_ref[:, 3:4]
    placed = jnp.concatenate(
        [(queries * jnp.where(slot == o, 1.0, 0.0)).astype(BF16) for o in range(slots)], axis=1
    )
    begun_ref[...] = lax.dot_general(
        placed, table_ref[...], ROWS_BY_ROWS, preferred_element_type=F32
    )
    blocks = [(t, s) for t in range(rows // block) for s in range(t + 1)]
    for at, (t, s) in enumerate(blocks):
        here, there = pl.ds(t * block, block), pl.ds(s * block, block)
        scores = lax.dot_general(
            queries_ref[here], keys_ref[there], ROWS_BY_ROWS, preferred_element_type=F32
        )
        same = marks_ref[here, 4:5] == segment_ref[0:1, there]
        if t == s:
            row = lax.broadcasted_iota(jnp.int32, (block, block), 0)
            other = lax.broadcasted_iota(jnp.int32, (block, block), 1)
            same = same & (other <= row)
        masked_ref[at] = jnp.where(same, scores, 0.0)
    grown = jnp.exp(run_ref[...])
    lane = lax.broadcasted_iota(jnp.int32, (block, 2 * head_size), 1)
    for p in range(heads // 2):
        wide = slice(p * 2 * head_size, (p + 1) * 2 * head_size)
        x = x_ref[:, wide].astype(F32)
        y = both_heads(grown, p, head_size) * begun_ref[:, wide] + skip_ref[:, wide] * x
        sums = [y[t * block : (t + 1) * block] for t in range(rows // block)]
        for at, (t, s) in enumerate(blocks):
            here, there = slice(t * block, (t + 1) * block), slice(s * block, (s + 1) * block)
            for side in range(2):
                head = 2 * p + side
                mine = (lane < head_size) if side == 0 else (lane >= head_size)
                x_own = jnp.where(mine, x[there], 0.0).astype(BF16)
                gap = run_ref[here, head : head + 1] - less_ref[head : head + 1, there]
                weight = (masked_ref[at] * jnp.exp(jnp.minimum(gap, 80.0))).astype(BF16)
                sums[t] = sums[t] + jnp.dot(weight, x_own, preferred_element_type=F32)
        for t in range(rows // block):
            y_ref[t * block : (t + 1) * block, wide] = sums[t]


def gate_kernel(
    heads, unused, y_ref, queries_ref, run_ref, marks_ref, entry_ref, gate_ref, gain_ref, out_ref, sq_ref
):
    del unused
    rows, inner = y_ref.shape
    head_size = inner // heads
    carried = jnp.where(marks_ref[:, 5:6] > 0, 1.0, 0.0)
    queries = (queries_ref[...].astype(F32) * carried).astype(BF16)
    held = lax.dot_general(
        queries, entry_ref[...].astype(BF16), ROWS_BY_ROWS, preferred_element_type=F32
    )
    grown = jnp.exp(run_ref[...])
    grown = jnp.concatenate([both_heads(grown, p, head_size) for p in range(heads // 2)], axis=1)
    gate = gate_ref[...].astype(F32)
    gated = (y_ref[...] + grown * held) * (gate / (1.0 + jnp.exp(-gate)))
    out_ref[...] = (gated * gain_ref[...]).astype(BF16)
    square = jnp.sum(gated * gated, axis=1, keepdims=True)
    sq_ref[...] = jnp.broadcast_to(square, (rows, LANES)).T[:8]


def norm_scale(own_ref, other_ref, channels):
    scale = lax.rsqrt((own_ref[0:1] + other_ref[0:1]) / channels + EPSILON)
    return jnp.broadcast_to(scale, (LANES, scale.shape[1])).T


def out_kernel(
    width, blocks, gated_ref, own_ref, other_ref, w0, w1, w2, w3, upper_out, upper_in, lower_out, lower_in
):
    del blocks
    rows, inner = gated_ref.shape
    half = rows // 2
    scale = norm_scale(own_ref, other_ref, 2 * inner)
    scale = jnp.concatenate([scale] * (width // LANES), axis=1)
    gated = gated_ref[...]
    parts = [
        jnp.dot(gated, w[...], preferred_element_type=F32) * scale for w in (w0, w1, w2, w3)
    ]
    upper_in[:, :width] = parts[0][:half]
    upper_in[:, width:] = parts[2][:half]
    upper_out[:, :width] = parts[1][:half].astype(BF16)
    upper_out[:, width:] = parts[3][:half].astype(BF16)
    lower_in[:, :width] = parts[0][half:]
    lower_in[:, width:] = parts[1][half:]
    lower_out[:, :width] = parts[2][half:].astype(BF16)
    lower_out[:, width:] = parts[3][half:].astype(BF16)


def finals_kernel(heads, added, slots, spread_ref, keys_ref, marks_ref, ends_ref, entry_ref, init_ref, *refs):
    out_ref = refs[-1]
    head_size = spread_ref.shape[0] // heads
    slot = slots[pl.program_id(0)]
    here = jnp.where(marks_ref[:, 6:7] == slot, 1.0, 0.0) * ends_ref[0][:, heads : heads + 1]
    keys = (keys_ref[...].astype(F32) * here).astype(BF16)
    state = jnp.dot(spread_ref[...], keys, preferred_element_type=F32)
    gain = over_states(ends_ref[0], heads, head_size)
    carried = jnp.broadcast_to(ends_ref[0][:, heads + 1 : heads + 2], state.shape) > 0.5
    state = state + gain * jnp.where(carried, entry_ref[...], init_ref[0])
    out_ref[0] = state + refs[0][0] if added else state


def per_device(
    tokens,
    lengths,
    deal,
    pre_gain,
    w_inner,
    w_group,
    w_step,
    conv_inner,
    conv_group,
    conv_bias_inner,
    conv_bias_group,
    edge_inner,
    edge_group,
    init_states,
    step_bias,
    decay_log,
    skip,
    inner_gain,
    w_out,
    final_gain,
    w_head,
):
    rows, width = tokens.shape
    model_width = pre_gain.shape[0]
    requests = lengths.shape[0]
    taps = conv_inner.shape[0]
    inner = w_inner.shape[2]
    heads = w_step.shape[1]
    head_size = inner // heads
    state = w_group.shape[3]
    row_at, col_at, seq_at = (lax.axis_index(name) for name in ("row", "col", "seq"))
    row_size, col_size, seq_size = (lax.axis_size(name) for name in ("row", "col", "seq"))
    group_local = col_at * w_group.shape[2] // col_size
    across = [row_at ^ i for i in range(row_size)]

    def own_group(table, axis):
        return lax.dynamic_index_in_dim(table, group_local, axis, keepdims=False)

    def in_lanes(values):
        return jnp.pad(values, (0, LANES - heads))[None, :]

    slot_ids = jnp.arange(requests, dtype=jnp.int32)
    ends = jnp.cumsum(lengths)
    begins = ends - lengths
    first_row = seq_at * rows
    local = jnp.arange(rows, dtype=jnp.int32)
    position = first_row + local
    segment = jnp.sum((begins[None, :] <= position[:, None]).astype(jnp.int32), axis=1) - 1
    member = segment[:, None] == slot_ids[None, :]
    begin_of = jnp.sum(jnp.where(member, begins[None, :], 0), axis=1)
    offset = position - begin_of
    owner = jnp.sum(jnp.where(member, deal[None, :], 0), axis=1)
    carried = (begin_of < first_row).astype(jnp.int32)
    marks = [
        jnp.where(
            offset >= back,
            jnp.where(local >= back, local - back, rows + RIM + local - back),
            rows + RIM + owner * (taps - 1) + (taps - 1 - back) + offset,
        )
        for back in range(1, taps)
    ]
    marks += [jnp.where(carried > 0, requests, owner), segment, carried, owner, owner]
    marks = jnp.stack(marks, axis=1)
    segment_row = jnp.broadcast_to(segment[None, :], (8, rows))
    dealt = deal[None, :] == slot_ids[:, None]
    slot_end = jnp.sum(jnp.where(dealt, ends[None, :], 0), axis=1) - 1 - first_row
    slot_begin = jnp.sum(jnp.where(dealt, begins[None, :], 0), axis=1) - first_row
    ends_here = (slot_end >= 0) & (slot_end < rows)
    chooser = (slot_end[:, None] == local[None, :]).astype(BF16)

    w_main = jnp.reshape(w_inner, (model_width, 2 * inner))
    w_rows = 512
    (w_rest,) = call(
        table_kernel,
        [((model_width, 2 * state + LANES), BF16)],
        w_group,
        w_step,
        prefetch=jnp.reshape(group_local, (1,)).astype(jnp.int32),
        grid=(model_width // w_rows,),
        in_specs=[
            pl.BlockSpec((w_rows,) + w_group.shape[1:], lambda i, _: (i, 0, 0, 0)),
            pl.BlockSpec((w_rows, heads), lambda i, _: (i, 0)),
        ],
        out_specs=[pl.BlockSpec((w_rows, 2 * state + LANES), lambda i, _: (i, 0))],
        cost=(model_width * state * 512, 8 * model_width * state * 2),
    )
    init_flat = jnp.reshape(init_states, (requests, inner, state))
    table = jnp.reshape(
        jnp.transpose(init_flat.astype(BF16), (1, 0, 2)), (inner, requests * state)
    )
    conv_taps = jnp.concatenate(
        [conv_inner, jnp.reshape(own_group(conv_group, 2), (taps, 2 * state))], axis=1
    )
    conv_bias = jnp.concatenate(
        [conv_bias_inner, jnp.reshape(own_group(conv_bias_group, 1), (2 * state,))]
    )[None, :]
    edges = jnp.concatenate(
        [edge_inner, jnp.reshape(own_group(edge_group, 3), (requests, taps - 1, 2 * state))],
        axis=2,
    )
    edges = jnp.reshape(edges, (requests * (taps - 1), inner + 2 * state))
    skip_row = jnp.repeat(skip, head_size)[None, :]
    gains = pre_gain[None, :]

    n_main, n_rest = 2 * inner, 2 * state + LANES
    token_ends = []
    carry = ()
    for shift in range(col_size):
        first, last = shift == 0, shift == col_size - 1
        pieces = plane_gather(tokens if first else from_ahead(tokens, "col", shift))
        blocks = jnp.stack([a * col_size + (col_at + shift) % col_size for a in across])
        in_specs = [None] * 7
        in_specs += [
            pl.BlockSpec((1, width), lambda i, b, at=at: (0, b[at])) for at in range(row_size)
        ]
        for n in (n_main, n_rest):
            in_specs += [
                pl.BlockSpec((width, n), lambda i, b, at=at: (b[at], 0)) for at in range(row_size)
            ]
        in_specs += [None] * len(carry)
        outs = [((requests, row_size * width), F32)]
        if last:
            outs += [((rows, inner), BF16), ((rows, inner + 2 * state), BF16), ((rows, LANES), F32)]
        else:
            outs += [((rows, n_main + n_rest), F32), ((rows, LANES), F32)]
        piece_ends, *carry = call(
            functools.partial(project_kernel, first, last, width, inner, model_width),
            outs,
            *pieces,
            chooser,
            *[gains] * row_size,
            *[w_main] * row_size,
            *[w_rest] * row_size,
            *carry,
            prefetch=blocks.astype(jnp.int32),
            in_specs=in_specs,
            cost=(2 * rows * row_size * width * (n_main + n_rest), 8 * 1024 * 1024),
        )
        token_ends.append(piece_ends)
    gate_in, channels, step_raw = carry

    rim = from_behind(channels[rows - RIM :], "seq", 1)
    x, keys, queries, run, less, spread, leaving, gain_carried = call(
        functools.partial(conv_kernel, heads),
        [
            ((rows, inner), BF16),
            ((rows, state), BF16),
            ((rows, state), BF16),
            ((rows, LANES), F32),
            ((8, rows), F32),
            ((inner, rows), BF16),
            ((inner, state), F32),
            ((inner, state), F32),
        ],
        channels,
        rim,
        edges,
        conv_taps,
        conv_bias,
        step_raw,
        in_lanes(step_bias),
        in_lanes(decay_log),
        marks,
        segment_row,
        init_flat,
        prefetch=owner[rows - 1 :],
        in_specs=[None] * 10 + [pl.BlockSpec((1, inner, state), lambda i, b: (b[0], 0, 0))],
        cost=(6 * rows * rows * (inner + 2 * state), 8 * 1024 * 1024),
    )
    entry = from_behind(leaving, "seq", 1)
    for _ in range(seq_size - 2):
        entry = from_behind(gain_carried * entry + leaving, "seq", 1)

    block = 256
    pairs = (rows // block) * (rows // block + 1) // 2
    y = pl.pallas_call(
        functools.partial(scan_kernel, heads, block),
        out_shape=jax.ShapeDtypeStruct((rows, inner), F32),
        grid_spec=pltpu.PrefetchScalarGridSpec(
            num_scalar_prefetch=1,
            grid=(1,),
            in_specs=[
                pl.BlockSpec(a.shape, lambda *_: (0, 0))
                for a in (x, keys, queries, run, less, marks, segment_row, table, skip_row)
            ],
            out_specs=pl.BlockSpec((rows, inner), lambda *_: (0, 0)),
            scratch_shapes=[
                pltpu.VMEM((pairs, block, block), F32),
                pltpu.VMEM((rows, inner), F32),
            ],
        ),
        compiler_params=pltpu.CompilerParams(vmem_limit_bytes=VMEM),
        cost_estimate=pl.CostEstimate(
            flops=4 * rows * rows * inner, bytes_accessed=8 * 1024 * 1024, transcendentals=0
        ),
    )(
        jnp.zeros((1,), jnp.int32),
        x,
        keys,
        queries,
        run,
        less,
        marks,
        segment_row,
        table,
        skip_row,
    )
    gated, own_squares = call(
        functools.partial(gate_kernel, heads),
        [((rows, inner), BF16), ((8, rows), F32)],
        y,
        queries,
        run,
        marks,
        entry,
        gate_in,
        inner_gain[None, :],
        cost=(2 * rows * inner * state, 4 * 1024 * 1024),
    )
    other_squares = from_partner(own_squares, "col", 0)

    mixed = 0.0
    for shift in (2, 1, 3, 0):
        blocks = jnp.stack([a * col_size + (col_at + shift) % col_size for a in across])
        half = (rows // 2, 2 * width)
        upper_out, upper_in, lower_out, lower_in = call(
            functools.partial(out_kernel, width),
            [(half, BF16), (half, F32), (half, BF16), (half, F32)],
            gated,
            own_squares,
            other_squares,
            *[w_out] * row_size,
            prefetch=blocks.astype(jnp.int32),
            in_specs=[None] * 3
            + [
                pl.BlockSpec((inner, width), lambda i, b, at=at: (0, b[at]))
                for at in range(row_size)
            ],
            cost=(2 * rows * inner * row_size * width, 4 * 1024 * 1024),
        )
        upper_got = from_partner(upper_out, "row", 0)
        lower_got = from_partner(lower_out, "row", 1)
        upper_far = (upper_in[:, width:] + upper_got[:, width:].astype(F32)).astype(BF16)
        lower_near = (lower_in[:, width:] + lower_got[:, width:].astype(F32)).astype(BF16)
        upper_far = from_partner(upper_far, "row", 1)
        lower_near = from_partner(lower_near, "row", 0)
        upper = upper_in[:, :width] + upper_got[:, :width].astype(F32) + upper_far.astype(F32)
        lower = lower_in[:, :width] + lower_got[:, :width].astype(F32) + lower_near.astype(F32)
        part = jnp.concatenate([upper, lower], axis=0)
        if shift:
            part = from_ahead(part.astype(BF16), "col", col_size - shift).astype(F32)
        mixed = mixed + part
    hidden_out = (tokens.astype(F32) + mixed).astype(BF16)

    scale = lax.rsqrt((own_squares[0] + other_squares[0]) / (2 * inner) + EPSILON)
    end_scale = jnp.sum(chooser.astype(F32) * scale[None, :], axis=1)
    normed_ends = jnp.dot(chooser, gated, preferred_element_type=F32) * end_scale[:, None]
    end_sum = jnp.dot(normed_ends.astype(BF16), w_out, preferred_element_type=F32)
    for axis, bit in (("row", 0), ("row", 1), ("col", 0), ("col", 1)):
        end_sum = end_sum + from_partner(end_sum.astype(BF16), axis, bit).astype(F32)
    ends_wide = jnp.zeros((requests, row_size, col_size, width), F32)
    for shift in range(col_size):
        for i in range(row_size):
            ends_wide = lax.dynamic_update_slice(
                ends_wide,
                jnp.reshape(
                    token_ends[shift][:, i * width : (i + 1) * width], (requests, 1, 1, width)
                ),
                (0, across[i], (col_at + shift) % col_size, 0),
            )
    ending = jnp.reshape(ends_wide, (requests, model_width)) + end_sum
    last_rows = lax.psum(ending, "seq").astype(BF16).astype(F32)
    final_scale = lax.rsqrt(jnp.sum(last_rows * last_rows, axis=1) / model_width + EPSILON)
    head_in = (last_rows * final_scale[:, None] * final_gain).astype(BF16)
    logits = jnp.dot(head_in, w_head, preferred_element_type=F32)

    end_run = jnp.dot(chooser.astype(F32), run, precision=HIGHEST)[:, :heads]
    end_gain = jnp.where(ends_here[:, None], jnp.exp(end_run), 0.0)
    end_marks = jnp.concatenate(
        [
            end_gain,
            ends_here.astype(F32)[:, None],
            (slot_begin < 0).astype(F32)[:, None],
            jnp.zeros((requests, LANES - heads - 2), F32),
        ],
        axis=1,
    )[:, None, :]

    def finals_of(slots, extra):
        count = slots.shape[0]
        by_slot = pl.BlockSpec((1, inner, state), lambda i, s: (s[i], 0, 0))
        by_step = pl.BlockSpec((1, inner, state), lambda i, s: (i, 0, 0))
        return call(
            functools.partial(finals_kernel, heads, bool(extra)),
            [((count, inner, state), F32)],
            spread,
            keys,
            marks,
            end_marks,
            entry,
            init_flat,
            *extra,
            prefetch=slots,
            grid=(count,),
            in_specs=[None] * 3
            + [pl.BlockSpec((1, 1, LANES), lambda i, s: (s[i], 0, 0)), None, by_slot]
            + [by_step] * len(extra),
            out_specs=[by_step],
            cost=(2 * count * rows * inner * state, 4 * count * inner * state * 4),
        )[0]

    if seq_size == 2:
        kept = requests // 2
        lent = finals_of((1 - seq_at) * kept + slot_ids[:kept], [])
        finals = finals_of(seq_at * kept + slot_ids[:kept], [from_partner(lent, "seq", 0)])
    else:
        finals = lax.psum_scatter(
            finals_of(slot_ids, []), "seq", scatter_dimension=0, tiled=True
        )
    final_states = jnp.reshape(finals, (finals.shape[0], heads, head_size, state))
    return (hidden_out, final_states, logits)


def solution(mesh):
    in_specs = (
        P("seq", ("row", "col")),
        P(),
        P(),
        P(),
        P(None, None, ("row", "col")),
        P(None, None, "row", None),
        P(None, ("row", "col")),
        P(None, ("row", "col")),
        P(None, None, "row", None),
        P(("row", "col")),
        P(None, "row", None),
        P(None, None, ("row", "col")),
        P(None, None, None, "row", None),
        P(None, ("row", "col"), None, None),
        P(("row", "col")),
        P(("row", "col")),
        P(("row", "col")),
        P(("row", "col")),
        P(("row", "col"), None),
        P(),
        P(None, ("seq", "row", "col")),
    )
    out_specs = (
        P("seq", ("row", "col")),
        P("seq", ("row", "col"), None, None),
        P(None, ("seq", "row", "col")),
    )
    return jax.shard_map(
        per_device, mesh=mesh, in_specs=in_specs, out_specs=out_specs, check_vma=False
    )
```

time: 440 us -> 218 us (0.50); the launches traced: 432 us -> 216 us
  waiting for transfers between devices: 218 us -> 39.5 us
  matrix products: 83.8 us -> 8.66 us
  starting transfers between devices: 3.24 us -> 54.5 us
  Pallas kernels: 0 us -> 50.1 us
  blocking collectives: 41.6 us -> 4.17 us
  between operations: 15 us -> 1.45 us
  local copies, waits for them, and re-layouts: 55 us -> 43.9 us
    reduce_scatter x2 -> x0, waiting for transfers between devices: 178 us -> none  [the longest x1 178 us: per_device(): lax.psum_scatter(partial_value, ('row', 'col'), scatter_dimension=1, tile...]
    dot_general x32 -> x3, matrix products: 83.8 us -> 8.66 us  [the longest x1 5.4 us: per_device(): logits = jnp.dot(head_in, w_head, preferred_element_type=F32)]
    pallas_call x0 -> x14, Pallas kernels: none -> 50.1 us  [the longest x13 46.8 us: call(): pl.pallas_call(kernel, out_shape=shapes, grid_spec=spec, compiler_params=...]
    ppermute x1 -> x38, starting transfers between devices: 0.19 us -> 39.6 us  [from_partner(): lax.ppermute(x, axis, [(i, i ^ 1 << bit) for i in range(lax.axis_size(axi...]
    all_gather x1 -> x0, blocking collectives: 38.2 us -> none  [per_device(): last_rows = lax.all_gather(ending_rows, ('row', 'col'), axis=1, tiled=True)]
    ppermute x1 -> x38, waiting for transfers between devices: 3.46 us -> 39.5 us  [from_partner(): lax.ppermute(x, axis, [(i, i ^ 1 << bit) for i in range(lax.axis_size(axi...]
    all_gather x1 -> x0, waiting for transfers between devices: 36 us -> none  [per_device(): lax.all_gather(tokens, ('row', 'col'), axis=1, tiled=True)]
    unnamed x114 -> x65, local copies, waits for them, and re-layouts: 37 us -> 23.5 us
  transfers between devices with their start and end apart: 6 -> 46, of which waited for: 3 -> 13; matrix products, arithmetic and copies ran while one was open for 22% -> 24% of each run, Pallas kernels for 0% -> 14%
where the time goes in v1:
time: 218 us; the launch traced here: 216 us
  starting transfers between devices  54.5 us (25%)
  Pallas kernels  50.1 us (23%)
  local copies, waits for them, and re-layouts  43.9 us (20%)
  waiting for transfers between devices  39.5 us (18%)
  other arithmetic  13.9 us (6%)
  matrix products  8.66 us (4%)
  blocking collectives  4.17 us (2%)
    pallas_call x13, Pallas kernels, call(): pl.pallas_call(kernel, out_shape=shapes, grid_spec=spec, compiler_params=...  46.8 us
    ppermute x38, starting transfers between devices, from_partner(): lax.ppermute(x, axis, [(i, i ^ 1 << bit) for i in range(lax.axis_size(axi...  39.6 us
    ppermute x38, waiting for transfers between devices, from_partner(): lax.ppermute(x, axis, [(i, i ^ 1 << bit) for i in range(lax.axis_size(axi...  39.5 us
    unnamed x65, local copies, waits for them, and re-layouts  23.5 us
    ppermute x6, starting transfers between devices, from_ahead(): lax.ppermute(x, axis, [((i + distance) % size, i) for i in range(size)])  11.3 us
    dot_general x1, matrix products, per_device(): logits = jnp.dot(head_in, w_head, preferred_element_type=F32)  5.4 us
    slice x4, local copies, waits for them, and re-layouts, plane_gather(): upper, lower = (block[:half], block[half:])  4.65 us
  transfers between devices with their start and end apart: 46, of which 13 were waited for; matrix products, arithmetic and copies ran while one was open for 24% of the time, Pallas kernels for 14%

profile of v1, /device:TPU:0, one launch (start us, length us, event | category | flops | bytes accessed | tf_op | source)
XLA Modules:
  0.0 216.3 jit_solution(10323441947122222821)
XLA Ops:
  0.6 5.1 %collective-permute-start.10 = (bf16[512,256]{1,0:T(8,128)(2,1)}, bf16[512,256]{1,0:T(8,128)(2,1)}, u32[]{:S(2)}, u32[]{:S(2)}) collective-permute-start(bf16[512,256]{1,0:T(8,128)(2,1)} %param.21), channel_id=1, source_target_pairs={{1,0},{2,1},{3,2},{0,3},{5,4},{6,5},{7,6},{4,7},{9,8},{10,9},{11,1... | collective-permute-start | bytes 786440 | tf_op jit(solution)/shard_map/ppermute | solution.py:32
  6.8 1.7 fusion.25
  8.5 1.6 collective-permute-start.15
  10.1 1.5 collective-permute-start.17
  14.0 2.2 %copy.65.step_ref = bf16[4096,8]{1,0:T(8,128)(2,1)} copy(bf16[4096,8]{0,1:T(8,128)(2,1)} %param.27) | data formatting | bytes 131072 | tf_op args[6]
  19.5 3.9 %convert_bitcast_fusion = bf16[512,16,128]{2,0,1:T(8,128)(2,1)} fusion(f32[16,8,64,128]{3,2,1,0:T(8,128)} %param.34), kind=kLoop, calls=%fused_computation | loop fusion | flops 1048576 | bytes 6291456 | tf_op jit(solution)/shard_map/transpose | solution.py:440
  24.5 1.2 copy-done.8
  25.7 2.2 %copy-done.9 = bf16[4096,2,2,128]{3,2,1,0:T(2,128)(2,1)S(1)} copy-done((bf16[4096,2,2,128]{3,2,1,0:T(2,128)(2,1)S(1)}, bf16[4096,2,2,128]{3,2,1,0:T(2,128)(2,1)}, u32[]{:S(2)}) %copy-start.9) | copy-done | bytes 4194328
  27.9 3.5 %shard_map.220.refs_15_.refs_16_.refs_17_.refs_18_ = bf16[4096,384]{1,0:T(8,128)(2,1)S(1)} custom-call(s32[1]{0:T(128)} %bitcast.10.which, bf16[4096,2,2,128]{3,2,1,0:T(2,128)(2,1)S(1)} %copy-done.9, bf16[4096,8]{1,0:T(8,128)(2,1)S(1)} %copy-done.8), custom_call_target="tpu_custom_call" | custom-call | flops 268435456 | bytes 8388608 | tf_op jit(solution)/shard_map/pallas_call | solution.py:56
  32.0 9.4 %copy.80 = bf16[512,8,2,512]{3,1,2,0:T(8,128)(2,1)} copy(bf16[512,8,2,512]{3,2,1,0:T(2,128)(2,1)} %bitcast.124) | data formatting | bytes 16777216
  41.6 3.9 %copy.68 = bf16[512,16,128]{0,2,1:T(8,128)(2,1)} copy(bf16[512,16,128]{2,0,1:T(8,128)(2,1)} %convert_bitcast_fusion) | data formatting | bytes 4194304 | tf_op jit(solution)/shard_map/transpose | solution.py:440
  45.5 3.9 %copy.70.table_ref = bf16[512,2048]{1,0:T(8,128)(2,1)} copy(bf16[512,2048]{0,1:T(8,128)(2,1)} %bitcast.125) | data formatting | bytes 4194304 | tf_op jit(solution)/shard_map/reshape | solution.py:439
  54.0 1.6 collective-permute-start.11
  55.6 1.5 collective-permute-start.13
  60.2 1.4 collective-permute-done.18.refs_5_
  61.6 1.5 collective-permute-start.3
  63.1 4.4 %shard_map.221 = (f32[16,1024]{1,0:T(8,128)S(1)}, f32[512,1408]{1,0:T(8,128)S(1)}, f32[512,128]{1,0:T(8,128)S(1)}) custom-call(s32[4]{0:T(128)S(1)} %pad_add_fusion.3.blocks, bf16[256,256]{1,0:T(8,128)(2,1)} %get-tuple-element.88.refs_0_, bf16[256,256]{1,0:T(8,128)(2,1)} %collective-permute-done.15.refs_1_, ...), custom_call_target="tpu_custom_call" | custom-call | flops 1476395008 | bytes 8388608 | tf_op jit(solution)/shard_map/pallas_call | solution.py:56
  68.9 1.6 collective-permute-start.14
  70.5 1.6 collective-permute-start.7
  72.7 1.5 collective-permute-done.1.refs_1_
  74.7 2.9 %collective-permute-done.12.refs_2_ = bf16[256,512]{1,0:T(8,128)(2,1)S(1)} collective-permute-done((bf16[256,512]{1,0:T(8,128)(2,1)S(1)}, bf16[256,512]{1,0:T(8,128)(2,1)S(1)}, u32[]{:S(2)}, u32[]{:S(2)}) %collective-permute-start.12) | collective-permute-done | bytes 262176 | tf_op jit(solution)/shard_map/ppermute | solution.py:27
  78.1 1.6 collective-permute-done.14.refs_5_
  79.7 4.2 %shard_map.222 = (f32[16,1024]{1,0:T(8,128)S(1)}, f32[512,1408]{1,0:T(8,128)S(1)}, f32[512,128]{1,0:T(8,128)S(1)}) custom-call(s32[4]{0:T(128)S(1)} %pad_add_fusion.2.blocks, bf16[256,256]{1,0:T(8,128)(2,1)S(1)} %get-tuple-element.90.refs_0_, bf16[256,256]{1,0:T(8,128)(2,1)S(1)} %collective-permute-done.11.refs_1_, ...), custom_call_target="tpu_custom_call" | custom-call | flops 1476395008 | bytes 8388608 | tf_op jit(solution)/shard_map/pallas_call | solution.py:56
  83.9 4.2 %shard_map.223 = (f32[16,1024]{1,0:T(8,128)S(1)}, f32[512,1408]{1,0:T(8,128)S(1)}, f32[512,128]{1,0:T(8,128)S(1)}) custom-call(s32[4]{0:T(128)S(1)} %pad_add_fusion.blocks, bf16[256,256]{1,0:T(8,128)(2,1)S(1)} %get-tuple-element.92.refs_0_, bf16[256,256]{1,0:T(8,128)(2,1)S(1)} %collective-permute-done.6.refs_1_, ...), custom_call_target="tpu_custom_call" | custom-call | flops 1476395008 | bytes 8388608 | tf_op jit(solution)/shard_map/pallas_call | solution.py:56
  88.2 4.4 %shard_map.224 = (f32[16,1024]{1,0:T(8,128)S(1)}, bf16[512,512]{1,0:T(8,128)(2,1)S(1)}, bf16[512,768]{1,0:T(8,128)(2,1)S(1)}, f32[512,128]{1,0:T(8,128)S(1)}) custom-call(s32[4]{0:T(128)S(1)} %pad_add_fusion.1.blocks, bf16[256,256]{1,0:T(8,128)(2,1)S(1)} %get-tuple-element.94.refs_0_, bf16[256,256]{1,0:T(8,128)(2,1)S(1)} %collective-permute-done.1.refs_1_, ...), custom_call_target="tpu_custom_call" | custom-call | flops 1476395008 | bytes 8388608 | tf_op jit(solution)/shard_map/pallas_call | solution.py:56
  92.6 1.7 collective-permute-start.19
  95.5 6.2 %shard_map.225 = (bf16[512,512]{1,0:T(8,128)(2,1)S(1)}, bf16[512,128]{1,0:T(8,128)(2,1)S(1)}, bf16[512,128]{1,0:T(8,128)(2,1)S(1)}, f32[512,128]{1,0:T(8,128)S(1...) custom-call(s32[1]{0:T(128)} %slice.189.owner_last, ...), custom_call_target="tpu_custom_call" | custom-call | flops 1207959552 | bytes 8388608 | tf_op jit(solution)/shard_map/pallas_call | solution.py:56
  103.8 1.8 collective-permute-start.20
  105.6 1.6 dynamic_update_slice.63
  107.2 1.8 reshape.373
  111.8 3.3 %shard_map.226.y_ref = f32[512,512]{1,0:T(8,128)S(1)} custom-call(s32[1]{0:T(128)} %constant.190.clone.1.unused, bf16[512,512]{1,0:T(8,128)(2,1)S(1)} %copy-done.14, bf16[512,128]{1,0:T(8,128)(2,1)S(1)} %copy-done.11, bf16[512,128]{1,0:T(8,128)(2,1)S(1)} %copy-done.16, f32[512,128]{1,0:T(8,128)S(1)} %get-tuple-element.52.run_ref, ...), custom_call_target="tpu_custom_call" | custom-call | flops 536870912 | bytes 8388608 | tf_op jit(solution)/shard_map/pallas_call | solution.py:527
  115.2 1.2 shard_map.227
  116.4 2.5 %collective-permute-start.21 = (f32[8,512]{1,0:T(8,128)S(1)}, f32[8,512]{1,0:T(8,128)S(1)}, u32[]{:S(2)}, u32[]{:S(2)}) collective-permute-start(f32[8,512]{1,0:T(8,128)S(1)} %get-tuple-element.57.own_ref), channel_id=1, source_target_pairs={{0,1},{1,0},{2,3},{3,2},{4,5},{5,4},{6,7},{7,6},{8,9},{9,8},{10,11... | collective-permute-start | bytes 49160 | tf_op jit(solution)/shard_map/ppermute | solution.py:27
  119.1 1.5 collective-permute-done.21.other_ref
  120.8 3.0 %fusion.29 = (bf16[16,4096]{1,0:T(8,128)(2,1)S(1)}, f32[16,4096]{1,0:T(8,128)S(1)}) fusion(bf16[512,4096]{1,0:T(8,128)(2,1)} %w3.7, bf16[512,512]{1,0:T(8,128)(2,1)S(1)} %get-tuple-element.56.gated_ref, f32[16]{0:T(128)S(1)} %multiply_reduce_fusion, s32[16]{0:T(128)S(1)} %get-tuple-element.84), kind=kOutput, calls=%fused_computation.129 | convolution fusion | flops 75587584 | bytes 5111936 | tf_op jit(solution)/shard_map/dot_general | solution.py:609
  124.6 2.5 %copy-done.4 = f32[16,8,64,128]{3,2,1,0:T(8,128)S(1)} copy-done((f32[16,8,64,128]{3,2,1,0:T(8,128)S(1)}, f32[16,8,64,128]{3,2,1,0:T(8,128)}, u32[]{:S(2)}) %copy-start.4) | copy-done | bytes 4194328
  127.1 5.8 %shard_map.232 = f32[8,512,128]{2,1,0:T(8,128)} custom-call(s32[8]{0:T(128)S(1)} %get-tuple-element.98.slots, bf16[512,512]{1,0:T(8,128)(2,1)S(1)} %get-tuple-element.74.spread_ref, bf16[512,128]{1,0:T(8,128)(2,1)S(1)} %copy-done.12, s32[512,8]{1,0:T(8,128)S(1)} %copy.67.marks_ref, f32[16,1,128]{2,1,0:T(1,128)S(1)} %bitcast.105, ...), custom_call_target="tpu_custom_call" | custom-call | flops 536870912 | bytes 8388608 | tf_op jit(solution)/shard_map/pallas_call | solution.py:56
  132.9 1.3 shard_map.228
  134.2 1.1 collective-permute-start.22
  136.0 1.4 collective-permute-start.43
  137.4 1.3 shard_map.229
  139.7 1.3 shard_map.230
  141.0 1.3 shard_map.231
  142.3 4.2 %collective-permute-done.43 = bf16[16,4096]{1,0:T(8,128)(2,1)S(1)} collective-permute-done((bf16[16,4096]{1,0:T(8,128)(2,1)S(1)}, bf16[16,4096]{1,0:T(8,128)(2,1)S(1)}, u32[]{:S(2)}, u32[]{:S(2)}) %collective-permute-start.43) | collective-permute-done | bytes 131104 | tf_op jit(solution)/shard_map/ppermute | solution.py:27
  147.3 1.1 collective-permute-start.32
  148.5 1.3 collective-permute-start.34
  149.8 1.1 collective-permute-start.37
  151.0 4.8 %collective-permute-done.29 = bf16[256,512]{1,0:T(8,128)(2,1)S(1)} collective-permute-done((bf16[256,512]{1,0:T(8,128)(2,1)S(1)}, bf16[256,512]{1,0:T(8,128)(2,1)S(1)}, u32[]{:S(2)}, u32[]{:S(2)}) %collective-permute-start.29) | collective-permute-done | bytes 262176 | tf_op jit(solution)/shard_map/ppermute | solution.py:27
  156.6 2.0 collective-permute-start.44
  158.7 2.8 %collective-permute-done.34 = bf16[256,512]{1,0:T(8,128)(2,1)S(1)} collective-permute-done((bf16[256,512]{1,0:T(8,128)(2,1)S(1)}, bf16[256,512]{1,0:T(8,128)(2,1)S(1)}, u32[]{:S(2)}, u32[]{:S(2)}) %collective-permute-start.34) | collective-permute-done | bytes 262176 | tf_op jit(solution)/shard_map/ppermute | solution.py:27
  162.1 1.1 collective-permute-start.25
  163.3 3.7 %collective-permute-done.39 = bf16[256,512]{1,0:T(8,128)(2,1)S(1)} collective-permute-done((bf16[256,512]{1,0:T(8,128)(2,1)S(1)}, bf16[256,512]{1,0:T(8,128)(2,1)S(1)}, u32[]{:S(2)}, u32[]{:S(2)}) %collective-permute-start.39) | collective-permute-done | bytes 262176 | tf_op jit(solution)/shard_map/ppermute | solution.py:27
  167.7 1.4 collective-permute-start.38
  169.2 4.6 %collective-permute-done.38 = bf16[256,256]{1,0:T(8,128)(2,1)S(1)} collective-permute-done((bf16[256,256]{1,0:T(8,128)(2,1)S(1)}, bf16[256,256]{1,0:T(8,128)(2,1)S(1)}, u32[]{:S(2)}, u32[]{:S(2)}) %collective-permute-start.38) | collective-permute-done | bytes 131104 | tf_op jit(solution)/shard_map/ppermute | solution.py:27
  176.9 1.1 collective-permute-start.40
  178.1 1.7 collective-permute-done.30
  179.8 1.5 collective-permute-start.45
  182.1 1.4 collective-permute-start.26
  184.3 2.0 collective-permute-start.31
  187.1 1.8 collective-permute-start.36
  189.0 8.6 %collective-permute-done.45 = bf16[16,4096]{1,0:T(8,128)(2,1)S(1)} collective-permute-done((bf16[16,4096]{1,0:T(8,128)(2,1)S(1)}, bf16[16,4096]{1,0:T(8,128)(2,1)S(1)}, u32[]{:S(2)}, u32[]{:S(2)}) %collective-permute-start.45) | collective-permute-done | bytes 131104 | tf_op jit(solution)/shard_map/ppermute | solution.py:27
  197.7 4.2 %all-reduce.3 = bf16[16,4096]{1,0:T(8,128)(2,1)S(1)} all-reduce(f32[16,4096]{1,0:T(8,128)S(1)} %add_add_fusion), channel_id=1, replica_groups=mesh['seq'=2,'row'=4,'col'=4] {'seq'}, use_global_device_ids=true, to_apply=%region_7.8 | all-reduce | flops 65536 | bytes 393216 | tf_op jit(solution)/shard_map/psum | solution.py:623
  202.1 5.4 %fusion.11 = f32[16,1024]{1,0:T(8,128)} fusion(bf16[4096,1024]{1,0:T(8,128)(2,1)} %param.41, f32[4096]{0:T(1024)S(1)} %copy-done.24, f32[16]{0:T(128)S(1)} %add_rsqrt_fusion.1, bf16[16,4096]{1,0:T(8,128)(2,1)S(1)} %all-reduce.3), kind=kOutput, calls=%fused_computation.48 | convolution fusion | flops 134479872 | bytes 8601664 | tf_op jit(solution)/shard_map/dot_general | solution.py:626
  208.4 7.9 %shard_map.233 = f32[8,512,128]{2,1,0:T(8,128)} custom-call(s32[8]{0:T(128)S(1)} %get-tuple-element.99.slots, bf16[512,512]{1,0:T(8,128)(2,1)S(1)} %get-tuple-element.74.spread_ref, bf16[512,128]{1,0:T(8,128)(2,1)S(1)} %copy-done.12, s32[512,8]{1,0:T(8,128)S(1)} %copy.67.marks_ref, f32[16,1,128]{2,1,0:T(1,128)S(1)} %bitcast.106, ...), custom_call_target="tpu_custom_call" | custom-call | flops 536870912 | bytes 8388608 | tf_op jit(solution)/shard_map/pallas_call | solution.py:56
  (216 shorter events, 37.8 us)
Async XLA Ops:
  0.6 15.5 %copy-start = (bf16[16,3,2,2,128]{4,3,2,1,0:T(2,128)(2,1)S(1)}, bf16[16,3,2,2,128]{4,3,2,1,0:T(2,128)(2,1)}, u32[]{:S(2)}) copy-start(bf16[16,3,2,2,128]{4,3,2,1,0:T(2,128)(2,1)} %param.33) | copy-start | bytes 147460
  0.6 52.3 %collective-permute-start.10 = (bf16[512,256]{1,0:T(8,128)(2,1)}, bf16[512,256]{1,0:T(8,128)(2,1)}, u32[]{:S(2)}, u32[]{:S(2)}) collective-permute-start(bf16[512,256]{1,0:T(8,128)(2,1)} %param.21), channel_id=1, source_target_pairs={{1,0},{2,1},{3,2},{0,3},{5,4},{6,5},{7,6},{4,7},{9,8},{10,9},{11,1... | collective-permute-start | bytes 786440 | tf_op jit(solution)/shard_map/ppermute | solution.py:32
  5.7 49.8 %collective-permute-start.5 = (bf16[512,256]{1,0:T(8,128)(2,1)}, bf16[512,256]{1,0:T(8,128)(2,1)}, u32[]{:S(2)}, u32[]{:S(2)}) collective-permute-start(bf16[512,256]{1,0:T(8,128)(2,1)} %param.21), channel_id=1, source_target_pairs={{2,0},{3,1},{0,2},{1,3},{6,4},{7,5},{4,6},{5,7},{10,8},{11,9},{8,1... | collective-permute-start | bytes 786440 | tf_op jit(solution)/shard_map/ppermute | solution.py:32
  5.8 52.3 %collective-permute-start = (bf16[512,256]{1,0:T(8,128)(2,1)}, bf16[512,256]{1,0:T(8,128)(2,1)}, u32[]{:S(2)}, u32[]{:S(2)}) collective-permute-start(bf16[512,256]{1,0:T(8,128)(2,1)} %param.21), channel_id=1, source_target_pairs={{3,0},{0,1},{1,2},{2,3},{7,4},{4,5},{5,6},{6,7},{11,8},{8,9},{9,10... | collective-permute-start | bytes 786440 | tf_op jit(solution)/shard_map/ppermute | solution.py:32
  8.5 15.6 %copy-start.25 = (f32[4,512]{1,0:T(4,128)S(1)}, f32[4,512]{1,0:T(4,128)}, u32[]{:S(2)}) copy-start(f32[4,512]{1,0:T(4,128)} %param.28) | copy-start | bytes 24580
  8.5 15.6 %copy-start.26 = (f32[512]{0:T(512)S(1)}, f32[512]{0:T(512)}, u32[]{:S(2)}) copy-start(f32[512]{0:T(512)} %param.30) | copy-start | bytes 6148
  8.5 15.7 %copy-start.28 = (f32[8]{0:T(128)S(1)}, f32[8]{0:T(128)}, u32[]{:S(2)}) copy-start(f32[8]{0:T(128)} %param.36) | copy-start | bytes 100
  8.5 15.7 %copy-start.29 = (f32[8]{0:T(128)S(1)}, f32[8]{0:T(128)}, u32[]{:S(2)}) copy-start(f32[8]{0:T(128)} %param.35) | copy-start | bytes 100
  8.5 41.4 %collective-permute-start.15 = (bf16[256,256]{1,0:T(8,128)(2,1)}, bf16[256,256]{1,0:T(8,128)(2,1)}, u32[]{:S(2)}, u32[]{:S(2)}) collective-permute-start(bf16[256,256]{1,0:T(8,128)(2,1)} %get-tuple-element.88.refs_0_), channel_id=1, source_target_pairs={{0,8},{4,12},{8,0},{12,4},{1,9},{5,13},{9,1},{13,5},{2,10},{6,14},... | collective-permute-start | bytes 393224 | tf_op jit(solution)/shard_map/ppermute | solution.py:27
  10.1 41.4 %collective-permute-start.17 = (bf16[256,256]{1,0:T(8,128)(2,1)}, bf16[256,256]{1,0:T(8,128)(2,1)}, u32[]{:S(2)}, u32[]{:S(2)}) collective-permute-start(bf16[256,256]{1,0:T(8,128)(2,1)} %get-tuple-element.87.refs_3_), channel_id=1, source_target_pairs={{0,4},{4,0},{8,12},{12,8},{1,5},{5,1},{9,13},{13,9},{2,6},{6,2},{1... | collective-permute-start | bytes 393224 | tf_op jit(solution)/shard_map/ppermute | solution.py:27
  41.5 7.9 %copy-start.27 = (f32[8]{0:T(128)S(1)}, f32[8]{0:T(128)}, u32[]{:S(2)}) copy-start(f32[8]{0:T(128)} %param.37) | copy-start | bytes 100
  45.5 17.6 %copy-start.7 = (f32[4096]{0:T(1024)S(1)}, f32[4096]{0:T(1024)}, u32[]{:S(2)}) copy-start(f32[4096]{0:T(1024)} %param.24) | copy-start | bytes 49156
  50.8 8.8 %collective-permute-start.16 = (bf16[256,512]{1,0:T(8,128)(2,1)S(1)}, bf16[256,512]{1,0:T(8,128)(2,1)S(1)}, u32[]{:S(2)}, u32[]{:S(2)}) collective-permute-start(bf16[256,512]{1,0:T(8,128)(2,1)S(1)} %pad_maximum_fusion.6), channel_id=1, source_target_pairs={{0,4},{4,0},{8,12},{12,8},{1,5},{5,1},{9,13},{13,9},{2,6},{6,2},{1... | collective-permute-start | bytes 786440 | tf_op jit(solution)/shard_map/ppermute | solution.py:27
  52.4 9.2 %collective-permute-start.18 = (bf16[256,512]{1,0:T(8,128)(2,1)S(1)}, bf16[256,512]{1,0:T(8,128)(2,1)S(1)}, u32[]{:S(2)}, u32[]{:S(2)}) collective-permute-start(bf16[256,512]{1,0:T(8,128)(2,1)S(1)} %pad_maximum_fusion.7), channel_id=1, source_target_pairs={{0,8},{4,12},{8,0},{12,4},{1,9},{5,13},{9,1},{13,5},{2,10},{6,14},... | collective-permute-start | bytes 786440 | tf_op jit(solution)/shard_map/ppermute | solution.py:27
  54.0 13.6 %collective-permute-start.11 = (bf16[256,256]{1,0:T(8,128)(2,1)S(1)}, bf16[256,256]{1,0:T(8,128)(2,1)S(1)}, u32[]{:S(2)}, u32[]{:S(2)}) collective-permute-start(bf16[256,256]{1,0:T(8,128)(2,1)S(1)} %get-tuple-element.90.refs_0_), channel_id=1, source_target_pairs={{0,8},{4,12},{8,0},{12,4},{1,9},{5,13},{9,1},{13,5},{2,10},{6,14},... | collective-permute-start | bytes 393224 | tf_op jit(solution)/shard_map/ppermute | solution.py:27
  55.6 12.6 %collective-permute-start.13 = (bf16[256,256]{1,0:T(8,128)(2,1)S(1)}, bf16[256,256]{1,0:T(8,128)(2,1)S(1)}, u32[]{:S(2)}, u32[]{:S(2)}) collective-permute-start(bf16[256,256]{1,0:T(8,128)(2,1)S(1)} %get-tuple-element.89.refs_3_), channel_id=1, source_target_pairs={{0,4},{4,0},{8,12},{12,8},{1,5},{5,1},{9,13},{13,9},{2,6},{6,2},{1... | collective-permute-start | bytes 393224 | tf_op jit(solution)/shard_map/ppermute | solution.py:27
  58.0 10.8 %collective-permute-start.6 = (bf16[256,256]{1,0:T(8,128)(2,1)S(1)}, bf16[256,256]{1,0:T(8,128)(2,1)S(1)}, u32[]{:S(2)}, u32[]{:S(2)}) collective-permute-start(bf16[256,256]{1,0:T(8,128)(2,1)S(1)} %get-tuple-element.92.refs_0_), channel_id=1, source_target_pairs={{0,8},{4,12},{8,0},{12,4},{1,9},{5,13},{9,1},{13,5},{2,10},{6,14},... | collective-permute-start | bytes 393224 | tf_op jit(solution)/shard_map/ppermute | solution.py:27
  59.6 10.8 %collective-permute-start.8 = (bf16[256,256]{1,0:T(8,128)(2,1)S(1)}, bf16[256,256]{1,0:T(8,128)(2,1)S(1)}, u32[]{:S(2)}, u32[]{:S(2)}) collective-permute-start(bf16[256,256]{1,0:T(8,128)(2,1)S(1)} %get-tuple-element.91.refs_3_), channel_id=1, source_target_pairs={{0,4},{4,0},{8,12},{12,8},{1,5},{5,1},{9,13},{13,9},{2,6},{6,2},{1... | collective-permute-start | bytes 393224 | tf_op jit(solution)/shard_map/ppermute | solution.py:27
  61.6 10.4 %collective-permute-start.3 = (bf16[256,256]{1,0:T(8,128)(2,1)S(1)}, bf16[256,256]{1,0:T(8,128)(2,1)S(1)}, u32[]{:S(2)}, u32[]{:S(2)}) collective-permute-start(bf16[256,256]{1,0:T(8,128)(2,1)S(1)} %get-tuple-element.93.refs_3_), channel_id=1, source_target_pairs={{0,4},{4,0},{8,12},{12,8},{1,5},{5,1},{9,13},{13,9},{2,6},{6,2},{1... | collective-permute-start | bytes 393224 | tf_op jit(solution)/shard_map/ppermute | solution.py:27
  67.6 6.5 %collective-permute-start.1 = (bf16[256,256]{1,0:T(8,128)(2,1)S(1)}, bf16[256,256]{1,0:T(8,128)(2,1)S(1)}, u32[]{:S(2)}, u32[]{:S(2)}) collective-permute-start(bf16[256,256]{1,0:T(8,128)(2,1)S(1)} %get-tuple-element.94.refs_0_), channel_id=1, source_target_pairs={{0,8},{4,12},{8,0},{12,4},{1,9},{5,13},{9,1},{13,5},{2,10},{6,14},... | collective-permute-start | bytes 393224 | tf_op jit(solution)/shard_map/ppermute | solution.py:27
  68.2 9.3 %collective-permute-start.12 = (bf16[256,512]{1,0:T(8,128)(2,1)S(1)}, bf16[256,512]{1,0:T(8,128)(2,1)S(1)}, u32[]{:S(2)}, u32[]{:S(2)}) collective-permute-start(bf16[256,512]{1,0:T(8,128)(2,1)S(1)} %pad_maximum_fusion.4), channel_id=1, source_target_pairs={{0,4},{4,0},{8,12},{12,8},{1,5},{5,1},{9,13},{13,9},{2,6},{6,2},{1... | collective-permute-start | bytes 786440 | tf_op jit(solution)/shard_map/ppermute | solution.py:27
  68.9 10.8 %collective-permute-start.14 = (bf16[256,512]{1,0:T(8,128)(2,1)S(1)}, bf16[256,512]{1,0:T(8,128)(2,1)S(1)}, u32[]{:S(2)}, u32[]{:S(2)}) collective-permute-start(bf16[256,512]{1,0:T(8,128)(2,1)S(1)} %pad_maximum_fusion.5), channel_id=1, source_target_pairs={{0,8},{4,12},{8,0},{12,4},{1,9},{5,13},{9,1},{13,5},{2,10},{6,14},... | collective-permute-start | bytes 786440 | tf_op jit(solution)/shard_map/ppermute | solution.py:27
  70.5 13.4 %collective-permute-start.7 = (bf16[256,512]{1,0:T(8,128)(2,1)S(1)}, bf16[256,512]{1,0:T(8,128)(2,1)S(1)}, u32[]{:S(2)}, u32[]{:S(2)}) collective-permute-start(bf16[256,512]{1,0:T(8,128)(2,1)S(1)} %pad_maximum_fusion.2), channel_id=1, source_target_pairs={{0,4},{4,0},{8,12},{12,8},{1,5},{5,1},{9,13},{13,9},{2,6},{6,2},{1... | collective-permute-start | bytes 786440 | tf_op jit(solution)/shard_map/ppermute | solution.py:27
  72.1 11.8 %collective-permute-start.9 = (bf16[256,512]{1,0:T(8,128)(2,1)S(1)}, bf16[256,512]{1,0:T(8,128)(2,1)S(1)}, u32[]{:S(2)}, u32[]{:S(2)}) collective-permute-start(bf16[256,512]{1,0:T(8,128)(2,1)S(1)} %pad_maximum_fusion.3), channel_id=1, source_target_pairs={{0,8},{4,12},{8,0},{12,4},{1,9},{5,13},{9,1},{13,5},{2,10},{6,14},... | collective-permute-start | bytes 786440 | tf_op jit(solution)/shard_map/ppermute | solution.py:27
  74.1 14.0 %collective-permute-start.4 = (bf16[256,512]{1,0:T(8,128)(2,1)S(1)}, bf16[256,512]{1,0:T(8,128)(2,1)S(1)}, u32[]{:S(2)}, u32[]{:S(2)}) collective-permute-start(bf16[256,512]{1,0:T(8,128)(2,1)S(1)} %pad_maximum_fusion.1), channel_id=1, source_target_pairs={{0,8},{4,12},{8,0},{12,4},{1,9},{5,13},{9,1},{13,5},{2,10},{6,14},... | collective-permute-start | bytes 786440 | tf_op jit(solution)/shard_map/ppermute | solution.py:27
  77.5 10.6 %collective-permute-start.2 = (bf16[256,512]{1,0:T(8,128)(2,1)S(1)}, bf16[256,512]{1,0:T(8,128)(2,1)S(1)}, u32[]{:S(2)}, u32[]{:S(2)}) collective-permute-start(bf16[256,512]{1,0:T(8,128)(2,1)S(1)} %pad_maximum_fusion), channel_id=1, source_target_pairs={{0,4},{4,0},{8,12},{12,8},{1,5},{5,1},{9,13},{13,9},{2,6},{6,2},{1... | collective-permute-start | bytes 786440 | tf_op jit(solution)/shard_map/ppermute | solution.py:27
  88.1 7.3 %copy-start.3 = (f32[16,8,64,128]{3,2,1,0:T(8,128)S(1)}, f32[16,8,64,128]{3,2,1,0:T(8,128)}, u32[]{:S(2)}) copy-start(f32[16,8,64,128]{3,2,1,0:T(8,128)} %param.34) | copy-start | bytes 12582916
  88.1 7.3 %copy-start.20 = (bf16[48,768]{1,0:T(8,128)(2,1)S(1)}, bf16[48,768]{1,0:T(8,128)(2,1)}, u32[]{:S(2)}) copy-start(bf16[48,768]{1,0:T(8,128)(2,1)} %pad_maximum_fusion.11.edges_ref) | copy-start | bytes 221188
  92.6 9.1 %copy-start.18 = (bf16[512,512]{1,0:T(8,128)(2,1)}, bf16[512,512]{1,0:T(8,128)(2,1)S(1)}, u32[]{:S(2)}) copy-start(bf16[512,512]{1,0:T(8,128)(2,1)S(1)} %get-tuple-element.55.gate_ref) | copy-start | bytes 1572868
  92.6 16.4 %copy-start.6 = (bf16[512,2048]{1,0:T(8,128)(2,1)S(1)}, bf16[512,2048]{1,0:T(8,128)(2,1)}, u32[]{:S(2)}) copy-start(bf16[512,2048]{1,0:T(8,128)(2,1)} %copy.70.table_ref) | copy-start | bytes 6291460
  92.6 2.8 %collective-permute-start.19 = (bf16[16,768]{1,0:T(8,128)(2,1)S(1)}, bf16[16,768]{1,0:T(8,128)(2,1)S(1)}, u32[]{:S(2)}, u32[]{:S(2)}) collective-permute-start(bf16[16,768]{1,0:T(8,128)(2,1)S(1)} %slice.198), channel_id=1, source_target_pairs={{0,16},{1,17},{2,18},{3,19},{4,20},{5,21},{6,22},{7,23},{8,24},{9,... | collective-permute-start | bytes 73736 | tf_op jit(solution)/shard_map/ppermute | solution.py:23
  95.5 19.7 %copy-start.21 = (f32[512]{0:T(512)S(1)}, f32[512]{0:T(512)}, u32[]{:S(2)}) copy-start(f32[512]{0:T(512)} %param.38) | copy-start | bytes 6148
  103.8 11.4 %collective-permute-start.20 = (f32[512,128]{1,0:T(8,128)}, f32[512,128]{1,0:T(8,128)S(1)}, u32[]{:S(2)}, u32[]{:S(2)}) collective-permute-start(f32[512,128]{1,0:T(8,128)} %get-tuple-element.54), channel_id=1, source_target_pairs={{0,16},{1,17},{2,18},{3,19},{4,20},{5,21},{6,22},{7,23},{8,24},{9,... | collective-permute-start | bytes 786440 | tf_op jit(solution)/shard_map/ppermute | solution.py:23
  115.2 9.4 %copy-start.12 = (bf16[512,128]{1,0:T(8,128)(2,1)S(1)}, bf16[512,128]{1,0:T(8,128)(2,1)}, u32[]{:S(2)}) copy-start(bf16[512,128]{1,0:T(8,128)(2,1)} %copy-done.10) | copy-start | bytes 393220
  116.4 4.2 %collective-permute-start.21 = (f32[8,512]{1,0:T(8,128)S(1)}, f32[8,512]{1,0:T(8,128)S(1)}, u32[]{:S(2)}, u32[]{:S(2)}) collective-permute-start(f32[8,512]{1,0:T(8,128)S(1)} %get-tuple-element.57.own_ref), channel_id=1, source_target_pairs={{0,1},{1,0},{2,3},{3,2},{4,5},{5,4},{6,7},{7,6},{8,9},{9,8},{10,11... | collective-permute-start | bytes 49160 | tf_op jit(solution)/shard_map/ppermute | solution.py:27
  123.9 9.0 %copy-start.2 = (bf16[512,4096]{1,0:T(8,128)(2,1)S(1)}, bf16[512,4096]{1,0:T(8,128)(2,1)}, u32[]{:S(2)}) copy-start(bf16[512,4096]{1,0:T(8,128)(2,1)} %w3.7) | copy-start | bytes 12582916
  123.9 12.1 %collective-permute-start.42 = (bf16[16,4096]{1,0:T(8,128)(2,1)S(1)}, bf16[16,4096]{1,0:T(8,128)(2,1)S(1)}, u32[]{:S(2)}, u32[]{:S(2)}) collective-permute-start(bf16[16,4096]{1,0:T(8,128)(2,1)S(1)} %get-tuple-element.100), channel_id=1, source_target_pairs={{0,4},{4,0},{8,12},{12,8},{1,5},{5,1},{9,13},{13,9},{2,6},{6,2},{1... | collective-permute-start | bytes 393224 | tf_op jit(solution)/shard_map/ppermute | solution.py:27
  132.9 75.5 %collective-permute-start.41 = (f32[8,512,128]{2,1,0:T(8,128)}, f32[8,512,128]{2,1,0:T(8,128)}, u32[]{:S(2)}, u32[]{:S(2)}) collective-permute-start(f32[8,512,128]{2,1,0:T(8,128)} %shard_map.232), channel_id=1, source_target_pairs={{0,16},{16,0},{1,17},{17,1},{2,18},{18,2},{3,19},{19,3},{4,20},{20... | collective-permute-start | bytes 6291464 | tf_op jit(solution)/shard_map/ppermute | solution.py:27
  134.2 13.1 %collective-permute-start.22 = (bf16[256,512]{1,0:T(8,128)(2,1)S(1)}, bf16[256,512]{1,0:T(8,128)(2,1)S(1)}, u32[]{:S(2)}, u32[]{:S(2)}) collective-permute-start(bf16[256,512]{1,0:T(8,128)(2,1)S(1)} %get-tuple-element.59), channel_id=1, source_target_pairs={{0,4},{4,0},{8,12},{12,8},{1,5},{5,1},{9,13},{13,9},{2,6},{6,2},{1... | collective-permute-start | bytes 786440 | tf_op jit(solution)/shard_map/ppermute | solution.py:27
  135.3 13.2 %collective-permute-start.24 = (bf16[256,512]{1,0:T(8,128)(2,1)S(1)}, bf16[256,512]{1,0:T(8,128)(2,1)S(1)}, u32[]{:S(2)}, u32[]{:S(2)}) collective-permute-start(bf16[256,512]{1,0:T(8,128)(2,1)S(1)} %get-tuple-element.61), channel_id=1, source_target_pairs={{0,8},{4,12},{8,0},{12,4},{1,9},{5,13},{9,1},{13,5},{2,10},{6,14},... | collective-permute-start | bytes 786440 | tf_op jit(solution)/shard_map/ppermute | solution.py:27
  136.0 10.5 %collective-permute-start.43 = (bf16[16,4096]{1,0:T(8,128)(2,1)S(1)}, bf16[16,4096]{1,0:T(8,128)(2,1)S(1)}, u32[]{:S(2)}, u32[]{:S(2)}) collective-permute-start(bf16[16,4096]{1,0:T(8,128)(2,1)S(1)} %fusion.9), channel_id=1, source_target_pairs={{0,8},{4,12},{8,0},{12,4},{1,9},{5,13},{9,1},{13,5},{2,10},{6,14},... | collective-permute-start | bytes 393224 | tf_op jit(solution)/shard_map/ppermute | solution.py:27
  138.7 11.1 %collective-permute-start.27 = (bf16[256,512]{1,0:T(8,128)(2,1)S(1)}, bf16[256,512]{1,0:T(8,128)(2,1)S(1)}, u32[]{:S(2)}, u32[]{:S(2)}) collective-permute-start(bf16[256,512]{1,0:T(8,128)(2,1)S(1)} %get-tuple-element.63), channel_id=1, source_target_pairs={{0,4},{4,0},{8,12},{12,8},{1,5},{5,1},{9,13},{13,9},{2,6},{6,2},{1... | collective-permute-start | bytes 786440 | tf_op jit(solution)/shard_map/ppermute | solution.py:27
  146.5 9.2 %collective-permute-start.29 = (bf16[256,512]{1,0:T(8,128)(2,1)S(1)}, bf16[256,512]{1,0:T(8,128)(2,1)S(1)}, u32[]{:S(2)}, u32[]{:S(2)}) collective-permute-start(bf16[256,512]{1,0:T(8,128)(2,1)S(1)} %get-tuple-element.65), channel_id=1, source_target_pairs={{0,8},{4,12},{8,0},{12,4},{1,9},{5,13},{9,1},{13,5},{2,10},{6,14},... | collective-permute-start | bytes 786440 | tf_op jit(solution)/shard_map/ppermute | solution.py:27
  147.3 9.3 %collective-permute-start.32 = (bf16[256,512]{1,0:T(8,128)(2,1)S(1)}, bf16[256,512]{1,0:T(8,128)(2,1)S(1)}, u32[]{:S(2)}, u32[]{:S(2)}) collective-permute-start(bf16[256,512]{1,0:T(8,128)(2,1)S(1)} %get-tuple-element.67), channel_id=1, source_target_pairs={{0,4},{4,0},{8,12},{12,8},{1,5},{5,1},{9,13},{13,9},{2,6},{6,2},{1... | collective-permute-start | bytes 786440 | tf_op jit(solution)/shard_map/ppermute | solution.py:27
  148.5 12.9 %collective-permute-start.34 = (bf16[256,512]{1,0:T(8,128)(2,1)S(1)}, bf16[256,512]{1,0:T(8,128)(2,1)S(1)}, u32[]{:S(2)}, u32[]{:S(2)}) collective-permute-start(bf16[256,512]{1,0:T(8,128)(2,1)S(1)} %get-tuple-element.69), channel_id=1, source_target_pairs={{0,8},{4,12},{8,0},{12,4},{1,9},{5,13},{9,1},{13,5},{2,10},{6,14},... | collective-permute-start | bytes 786440 | tf_op jit(solution)/shard_map/ppermute | solution.py:27
  149.8 12.3 %collective-permute-start.37 = (bf16[256,512]{1,0:T(8,128)(2,1)S(1)}, bf16[256,512]{1,0:T(8,128)(2,1)S(1)}, u32[]{:S(2)}, u32[]{:S(2)}) collective-permute-start(bf16[256,512]{1,0:T(8,128)(2,1)S(1)} %get-tuple-element.71), channel_id=1, source_target_pairs={{0,4},{4,0},{8,12},{12,8},{1,5},{5,1},{9,13},{13,9},{2,6},{6,2},{1... | collective-permute-start | bytes 786440 | tf_op jit(solution)/shard_map/ppermute | solution.py:27
  155.8 11.2 %collective-permute-start.39 = (bf16[256,512]{1,0:T(8,128)(2,1)S(1)}, bf16[256,512]{1,0:T(8,128)(2,1)S(1)}, u32[]{:S(2)}, u32[]{:S(2)}) collective-permute-start(bf16[256,512]{1,0:T(8,128)(2,1)S(1)} %get-tuple-element.73), channel_id=1, source_target_pairs={{0,8},{4,12},{8,0},{12,4},{1,9},{5,13},{9,1},{13,5},{2,10},{6,14},... | collective-permute-start | bytes 786440 | tf_op jit(solution)/shard_map/ppermute | solution.py:27
  156.6 11.1 %collective-permute-start.44 = (bf16[16,4096]{1,0:T(8,128)(2,1)S(1)}, bf16[16,4096]{1,0:T(8,128)(2,1)S(1)}, u32[]{:S(2)}, u32[]{:S(2)}) collective-permute-start(bf16[16,4096]{1,0:T(8,128)(2,1)S(1)} %fusion.24), channel_id=1, source_target_pairs={{0,1},{1,0},{2,3},{3,2},{4,5},{5,4},{6,7},{7,6},{8,9},{9,8},{10,11... | collective-permute-start | bytes 393224 | tf_op jit(solution)/shard_map/ppermute | solution.py:27
  161.4 13.5 %collective-permute-start.23 = (bf16[256,256]{1,0:T(8,128)(2,1)S(1)}, bf16[256,256]{1,0:T(8,128)(2,1)S(1)}, u32[]{:S(2)}, u32[]{:S(2)}) collective-permute-start(bf16[256,256]{1,0:T(8,128)(2,1)S(1)} %add_convert_fusion.13), channel_id=1, source_target_pairs={{0,8},{4,12},{8,0},{12,4},{1,9},{5,13},{9,1},{13,5},{2,10},{6,14},... | collective-permute-start | bytes 393224 | tf_op jit(solution)/shard_map/ppermute | solution.py:27
  162.1 13.7 %collective-permute-start.25 = (bf16[256,256]{1,0:T(8,128)(2,1)S(1)}, bf16[256,256]{1,0:T(8,128)(2,1)S(1)}, u32[]{:S(2)}, u32[]{:S(2)}) collective-permute-start(bf16[256,256]{1,0:T(8,128)(2,1)S(1)} %add_convert_fusion.11), channel_id=1, source_target_pairs={{0,4},{4,0},{8,12},{12,8},{1,5},{5,1},{9,13},{13,9},{2,6},{6,2},{1... | collective-permute-start | bytes 393224 | tf_op jit(solution)/shard_map/ppermute | solution.py:27
  167.0 9.9 %collective-permute-start.28 = (bf16[256,256]{1,0:T(8,128)(2,1)S(1)}, bf16[256,256]{1,0:T(8,128)(2,1)S(1)}, u32[]{:S(2)}, u32[]{:S(2)}) collective-permute-start(bf16[256,256]{1,0:T(8,128)(2,1)S(1)} %add_convert_fusion.9), channel_id=1, source_target_pairs={{0,8},{4,12},{8,0},{12,4},{1,9},{5,13},{9,1},{13,5},{2,10},{6,14},... | collective-permute-start | bytes 393224 | tf_op jit(solution)/shard_map/ppermute | solution.py:27
  167.7 29.9 %copy-start.23 = (f32[16,4096]{1,0:T(8,128)S(1)}, f32[16,4096]{1,0:T(8,128)}, u32[]{:S(2)}) copy-start(f32[16,4096]{1,0:T(8,128)} %reshape.373) | copy-start | bytes 786436
  167.7 6.1 %collective-permute-start.38 = (bf16[256,256]{1,0:T(8,128)(2,1)S(1)}, bf16[256,256]{1,0:T(8,128)(2,1)S(1)}, u32[]{:S(2)}, u32[]{:S(2)}) collective-permute-start(bf16[256,256]{1,0:T(8,128)(2,1)S(1)} %add_convert_fusion.1), channel_id=1, source_target_pairs={{0,8},{4,12},{8,0},{12,4},{1,9},{5,13},{9,1},{13,5},{2,10},{6,14},... | collective-permute-start | bytes 393224 | tf_op jit(solution)/shard_map/ppermute | solution.py:27
  173.8 6.0 %collective-permute-start.30 = (bf16[256,256]{1,0:T(8,128)(2,1)S(1)}, bf16[256,256]{1,0:T(8,128)(2,1)S(1)}, u32[]{:S(2)}, u32[]{:S(2)}) collective-permute-start(bf16[256,256]{1,0:T(8,128)(2,1)S(1)} %add_convert_fusion.7), channel_id=1, source_target_pairs={{0,4},{4,0},{8,12},{12,8},{1,5},{5,1},{9,13},{13,9},{2,6},{6,2},{1... | collective-permute-start | bytes 393224 | tf_op jit(solution)/shard_map/ppermute | solution.py:27
  174.9 27.2 %copy-start.24 = (f32[4096]{0:T(1024)S(1)}, f32[4096]{0:T(1024)}, u32[]{:S(2)}) copy-start(f32[4096]{0:T(1024)} %param.40) | copy-start | bytes 49156
  174.9 7.2 %collective-permute-start.33 = (bf16[256,256]{1,0:T(8,128)(2,1)S(1)}, bf16[256,256]{1,0:T(8,128)(2,1)S(1)}, u32[]{:S(2)}, u32[]{:S(2)}) collective-permute-start(bf16[256,256]{1,0:T(8,128)(2,1)S(1)} %add_convert_fusion.5), channel_id=1, source_target_pairs={{0,8},{4,12},{8,0},{12,4},{1,9},{5,13},{9,1},{13,5},{2,10},{6,14},... | collective-permute-start | bytes 393224 | tf_op jit(solution)/shard_map/ppermute | solution.py:27
  175.8 8.5 %collective-permute-start.35 = (bf16[256,256]{1,0:T(8,128)(2,1)S(1)}, bf16[256,256]{1,0:T(8,128)(2,1)S(1)}, u32[]{:S(2)}, u32[]{:S(2)}) collective-permute-start(bf16[256,256]{1,0:T(8,128)(2,1)S(1)} %add_convert_fusion.3), channel_id=1, source_target_pairs={{0,4},{4,0},{8,12},{12,8},{1,5},{5,1},{9,13},{13,9},{2,6},{6,2},{1... | collective-permute-start | bytes 393224 | tf_op jit(solution)/shard_map/ppermute | solution.py:27
  176.9 10.2 %collective-permute-start.40 = (bf16[256,256]{1,0:T(8,128)(2,1)S(1)}, bf16[256,256]{1,0:T(8,128)(2,1)S(1)}, u32[]{:S(2)}, u32[]{:S(2)}) collective-permute-start(bf16[256,256]{1,0:T(8,128)(2,1)S(1)} %add_convert_fusion), channel_id=1, source_target_pairs={{0,4},{4,0},{8,12},{12,8},{1,5},{5,1},{9,13},{13,9},{2,6},{6,2},{1... | collective-permute-start | bytes 393224 | tf_op jit(solution)/shard_map/ppermute | solution.py:27
  179.8 17.8 %collective-permute-start.45 = (bf16[16,4096]{1,0:T(8,128)(2,1)S(1)}, bf16[16,4096]{1,0:T(8,128)(2,1)S(1)}, u32[]{:S(2)}, u32[]{:S(2)}) collective-permute-start(bf16[16,4096]{1,0:T(8,128)(2,1)S(1)} %fusion.10), channel_id=1, source_target_pairs={{0,2},{1,3},{2,0},{3,1},{4,6},{5,7},{6,4},{7,5},{8,10},{9,11},{10,... | collective-permute-start | bytes 393224 | tf_op jit(solution)/shard_map/ppermute | solution.py:27
  182.1 25.4 %collective-permute-start.26 = (bf16[512,256]{1,0:T(8,128)(2,1)}, bf16[512,256]{1,0:T(8,128)(2,1)S(1)}, u32[]{:S(2)}, u32[]{:S(2)}) collective-permute-start(bf16[512,256]{1,0:T(8,128)(2,1)} %pad_maximum_fusion.8), channel_id=1, source_target_pairs={{2,0},{3,1},{0,2},{1,3},{6,4},{7,5},{4,6},{5,7},{10,8},{11,9},{8,1... | collective-permute-start | bytes 786440 | tf_op jit(solution)/shard_map/ppermute | solution.py:32
  184.3 23.2 %collective-permute-start.31 = (bf16[512,256]{1,0:T(8,128)(2,1)}, bf16[512,256]{1,0:T(8,128)(2,1)S(1)}, u32[]{:S(2)}, u32[]{:S(2)}) collective-permute-start(bf16[512,256]{1,0:T(8,128)(2,1)} %pad_maximum_fusion.9), channel_id=1, source_target_pairs={{3,0},{0,1},{1,2},{2,3},{7,4},{4,5},{5,6},{6,7},{11,8},{8,9},{9,10... | collective-permute-start | bytes 786440 | tf_op jit(solution)/shard_map/ppermute | solution.py:32
  187.1 20.4 %collective-permute-start.36 = (bf16[512,256]{1,0:T(8,128)(2,1)}, bf16[512,256]{1,0:T(8,128)(2,1)S(1)}, u32[]{:S(2)}, u32[]{:S(2)}) collective-permute-start(bf16[512,256]{1,0:T(8,128)(2,1)} %pad_maximum_fusion.10), channel_id=1, source_target_pairs={{1,0},{2,1},{3,2},{0,3},{5,4},{6,5},{7,6},{4,7},{9,8},{10,9},{11,1... | collective-permute-start | bytes 786440 | tf_op jit(solution)/shard_map/ppermute | solution.py:32
  202.1 6.3 %copy-start.5 = (f32[16,8,64,128]{3,2,1,0:T(8,128)S(1)}, f32[16,8,64,128]{3,2,1,0:T(8,128)}, u32[]{:S(2)}) copy-start(f32[16,8,64,128]{3,2,1,0:T(8,128)} %param.34) | copy-start | bytes 12582916
  208.4 7.9 %copy-start.1 = (bf16[16,3,2,2,128]{4,3,2,1,0:T(2,128)(2,1)S(1)}, bf16[16,3,2,2,128]{4,3,2,1,0:T(2,128)(2,1)}, u32[]{:S(2)}) copy-start(bf16[16,3,2,2,128]{4,3,2,1,0:T(2,128)(2,1)} %param.33) | copy-start | bytes 147460
  (12 other events, 23.1 us)

commit v2 on v1

v2 whole, which is shorter than its diff:
```python
import functools

import jax
import jax.numpy as jnp
from jax import lax
from jax.experimental import pallas as pl
from jax.experimental.pallas import tpu as pltpu
from jax.sharding import PartitionSpec as P

EPSILON = 1e-05
HIGHEST = lax.Precision.HIGHEST
F32 = jnp.float32
BF16 = jnp.bfloat16
LANES = 128
RIM = 16
MIB = 1024 * 1024
ROWS_BY_ROWS = (((1,), (1,)), ((), ()))


def from_behind(block, axis, distance):
    devices = range(lax.axis_size(axis))
    route = [(i - distance, i) for i in devices if i - distance in devices]
    return lax.ppermute(block, axis, route)


def from_partner(x, axis, bit):
    return lax.ppermute(x, axis, [(i, i ^ 1 << bit) for i in range(lax.axis_size(axis))])


def from_ahead(x, axis, distance):
    size = lax.axis_size(axis)
    return lax.ppermute(x, axis, [((i + distance) % size, i) for i in range(size)])


def after(x, *others):
    return lax.optimization_barrier((x,) + others)[0]


def call(kernel, outs, *args, prefetch=None, grid=(1,), in_specs=None, out_specs=None, scratch=(), vmem=12, work=20):
    params = pltpu.CompilerParams(vmem_limit_bytes=vmem * MIB)
    shapes = [jax.ShapeDtypeStruct(shape, kind) for shape, kind in outs]

    def whole(shape):
        zeros = (0,) * len(shape)
        return pl.BlockSpec(shape, lambda *_: zeros)

    specs = [
        whole(a.shape) if spec is None else spec
        for a, spec in zip(args, in_specs or [None] * len(args))
    ]
    gives = [
        whole(shape) if spec is None else spec
        for (shape, _), spec in zip(outs, out_specs or [None] * len(outs))
    ]
    prefetch = jnp.zeros((1,), jnp.int32) if prefetch is None else prefetch
    spec = pltpu.PrefetchScalarGridSpec(
        num_scalar_prefetch=1, grid=grid, in_specs=specs, out_specs=gives,
        scratch_shapes=[pltpu.VMEM(shape, kind) for shape, kind in scratch],
    )
    return pl.pallas_call(
        kernel,
        out_shape=shapes,
        grid_spec=spec,
        compiler_params=params,
        cost_estimate=pl.CostEstimate(flops=work * 1_000_000_000, bytes_accessed=100_000_000 if work else 1000, transcendentals=0),
    )(prefetch, *args)


def plane_gather(block):
    half = block.shape[0] // 2
    upper, lower = block[:half], block[half:]
    upper_far = from_partner(upper, "row", 1)
    lower_near = from_partner(lower, "row", 0)
    upper_rest = from_partner(jnp.concatenate([upper, upper_far], axis=1), "row", 0)
    lower_rest = from_partner(jnp.concatenate([lower, lower_near], axis=1), "row", 1)
    return upper, upper_far, upper_rest, lower, lower_near, lower_rest


def setup_kernel(taps, counts, marks_ref, segment_ref, chooser_ref, slots_ref):
    requests = chooser_ref.shape[0]
    rows = marks_ref.shape[0]
    first_row = counts[2 * requests]
    begins, owners = [], []
    total = jnp.int32(0)
    for k in range(requests):
        begins.append(total - first_row)
        owners.append(counts[requests + k])
        total = total + counts[k]
    stops = begins[1:] + [total - first_row]

    def latest(position, values):
        found = jnp.full(position.shape, values[0], jnp.int32)
        for begin, value in zip(begins[1:], values[1:]):
            found = jnp.where(position >= begin, value, found)
        return found

    position = lax.broadcasted_iota(jnp.int32, (rows, LANES), 0)
    lane = lax.broadcasted_iota(jnp.int32, (rows, LANES), 1)
    owner = latest(position, owners)
    begin = latest(position, begins)
    offset = position - begin
    marks = owner
    for back in range(1, taps):
        edge = rows + RIM + owner * (taps - 1) + (taps - 1 - back) + offset
        inside = jnp.where(position >= back, position - back, rows + RIM + position - back)
        marks = jnp.where(lane == back - 1, jnp.where(offset >= back, inside, edge), marks)
    marks = jnp.where((lane == 3) & (begin < 0), requests, marks)
    marks = jnp.where(lane == 4, begin, marks)
    marks = jnp.where(lane == 5, jnp.where(begin < 0, 1, 0), marks)
    marks_ref[...] = marks
    across = lax.broadcasted_iota(jnp.int32, (8, rows), 1)
    segment_ref[...] = latest(across, begins)
    slot = lax.broadcasted_iota(jnp.int32, (requests, rows), 0)
    column = lax.broadcasted_iota(jnp.int32, (requests, rows), 1)
    slot_lane = lax.broadcasted_iota(jnp.int32, (requests, LANES), 0)
    chooser = jnp.zeros((requests, rows), F32)
    slot_begin = jnp.zeros((requests, LANES), F32)
    slot_end = jnp.zeros((requests, LANES), F32)
    for k in range(requests):
        last = stops[k] - 1
        chooser = jnp.where((slot == owners[k]) & (column == last), 1.0, chooser)
        here = jnp.where((last >= 0) & (last < rows), 1.0, 0.0)
        slot_end = jnp.where(slot_lane == owners[k], here, slot_end)
        before = jnp.where(begins[k] < 0, 1.0, 0.0)
        slot_begin = jnp.where(slot_lane == owners[k], before, slot_begin)
    chooser_ref[...] = chooser.astype(BF16)
    slots_ref[:, :LANES] = slot_end
    slots_ref[:, LANES:] = slot_begin


def weights_kernel(parts, place, *refs):
    out_ref, gain_out = refs[4 * parts :]
    rows = refs[0].shape[0]
    for part in range(parts):
        main_ref, group_ref, step_ref, gain_ref = refs[part : 4 * parts : parts]
        weights_block(
            place[2],
            main_ref,
            group_ref,
            step_ref,
            out_ref.at[pl.ds(part * rows, rows)],
        )
        gain_out[:, part * rows : (part + 1) * rows] = gain_ref[...]


def weights_block(group, main_ref, group_ref, step_ref, out_ref):
    rows, _, inner = main_ref.shape
    state = group_ref.shape[3]
    heads = step_ref.shape[0]
    half = rows // 2
    row = lax.broadcasted_iota(jnp.int32, (rows, rows), 0)
    column = lax.broadcasted_iota(jnp.int32, (rows, rows), 1)
    source = jnp.where(row < half, 2 * row, 2 * (row - half) + 1)
    pick = jnp.where(source == column, 1.0, 0.0).astype(BF16)
    flat = main_ref[...].reshape(2 * rows, inner)
    for at in range(2):
        got = jnp.dot(pick, flat[at * rows : (at + 1) * rows], preferred_element_type=F32)
        got = got.astype(BF16)
        out_ref[at * half : (at + 1) * half, :inner] = got[:half]
        out_ref[at * half : (at + 1) * half, inner : 2 * inner] = got[half:]
    take = rows // 4
    row, column = row[:half], column[:half]
    source = jnp.where(row < take, 4 * row, 4 * (row - take) + 2) + group
    pick = jnp.where(source == column, 1.0, 0.0).astype(BF16)
    flat = group_ref[...].reshape(4 * rows, state)
    for at in range(4):
        got = jnp.dot(pick, flat[at * rows : (at + 1) * rows], preferred_element_type=F32)
        got = got.astype(BF16)
        out_ref[at * take : (at + 1) * take, 2 * inner : 2 * inner + state] = got[:take]
        out_ref[at * take : (at + 1) * take, 2 * inner + state : 2 * inner + 2 * state] = got[take:]
    steps = jnp.concatenate(
        [step_ref[...].astype(F32), jnp.zeros((LANES - heads, rows), F32)], axis=0
    )
    out_ref[:, 2 * inner + 2 * state :] = steps.T.astype(BF16)


def table_kernel(unused, init_ref, out_ref):
    del unused
    out_ref[...] = init_ref[0].astype(BF16)


def project_kernel(first, inner, model_width, unused, *refs):
    del unused
    pieces, refs = refs[:6], refs[6:]
    chooser_ref, gain_ref, weights_ref, refs = refs[0], refs[1], refs[2], refs[3:]
    if not first:
        total_in, squares_in, refs = refs[0], refs[1], refs[2:]
    if first:
        ends_ref, total_ref, squares_ref = refs
    else:
        ends_ref, gate_ref, channels_ref, steps_ref, total_ref, squares_ref = refs
    width = pieces[0].shape[1]

    def add(raw, fresh):
        ends_ref[...] = jnp.dot(chooser_ref[...], raw, preferred_element_type=F32)
        wide = raw.astype(F32)
        scaled = (wide * gain_ref[...]).astype(BF16)
        product = jnp.dot(scaled, weights_ref[...], preferred_element_type=F32)
        square = wide * wide
        parts = [square[:, at : at + LANES] for at in range(0, 2 * width, LANES)]
        if fresh:
            total_ref[...] = product if first else product + total_in[...]
            squares_ref[...] = functools.reduce(jnp.add, parts if first else parts + [squares_in[...]])
        else:
            total_ref[...] += product
            squares_ref[...] += functools.reduce(jnp.add, parts)

    upper, upper_far, upper_rest, lower, lower_near, lower_rest = pieces

    @pl.when(pl.program_id(0) == 0)
    def _():
        top = jnp.concatenate([upper[...], upper_rest[:, :width]], axis=1)
        bottom = jnp.concatenate([lower[...], lower_near[...]], axis=1)
        add(jnp.concatenate([top, bottom], axis=0), True)

    @pl.when(pl.program_id(0) == 1)
    def _():
        top = jnp.concatenate([upper_far[...], upper_rest[:, width:]], axis=1)
        add(jnp.concatenate([top, lower_rest[...]], axis=0), False)
        if first:
            return
        inv_rms = jnp.sum(squares_ref[...], axis=1, keepdims=True) / model_width
        inv_rms = lax.rsqrt(inv_rms + EPSILON)
        gate_ref[...] = (total_ref[:, :inner] * inv_rms).astype(BF16)
        channels_ref[...] = (total_ref[:, inner:-LANES] * inv_rms).astype(BF16)
        steps_ref[...] = total_ref[:, -LANES:] * inv_rms


def both_heads(table, pair, head_size):
    rows = table.shape[0]
    lane = lax.broadcasted_iota(jnp.int32, (rows, 2 * head_size), 1)
    return jnp.where(
        lane < head_size, table[:, 2 * pair : 2 * pair + 1], table[:, 2 * pair + 1 : 2 * pair + 2]
    )


def over_states(row, heads, head_size):
    return jnp.concatenate(
        [jnp.broadcast_to(row[:, h : h + 1], (head_size, LANES)) for h in range(heads)], axis=0
    )


def conv_kernel(
    heads,
    unused,
    channels_ref,
    rim_ref,
    edges_ref,
    taps_ref,
    bias_ref,
    steps_ref,
    step_bias_ref,
    decay_ref,
    marks_ref,
    segment_ref,
    init_ref,
    x_ref,
    keys_ref,
    queries_ref,
    run_ref,
    less_ref,
    spread_ref,
    leaving_ref,
    gain_ref,
):
    del unused
    rows, inner = x_ref.shape
    state = keys_ref.shape[1]
    head_size = inner // heads
    taps = taps_ref.shape[0]
    channels = channels_ref[...]
    sources = jnp.concatenate([channels, rim_ref[...], edges_ref[...]], axis=0)
    summed = bias_ref[...] + taps_ref[taps - 1 : taps] * channels.astype(F32)
    column = lax.broadcasted_iota(jnp.int32, (rows, sources.shape[0]), 1)
    for back in range(1, taps):
        pick = jnp.where(marks_ref[:, back - 1 : back] == column, 1.0, 0.0).astype(BF16)
        value = jnp.dot(pick, sources, preferred_element_type=F32)
        summed = summed + taps_ref[taps - 1 - back : taps - back] * value
    mixed = (summed / (1.0 + jnp.exp(-summed))).astype(BF16)
    x = mixed[:, :inner]
    keys = mixed[:, inner : inner + state]
    x_ref[...] = x
    keys_ref[...] = keys
    queries_ref[...] = mixed[:, inner + state :]
    raw = steps_ref[...] + step_bias_ref[...]
    step = jnp.maximum(raw, 0.0) + jnp.log1p(jnp.exp(-jnp.abs(raw)))
    log_decay = -jnp.exp(decay_ref[...]) * step
    segment = marks_ref[:, 4:5]
    same = segment == segment_ref[0:1, :]
    row = lax.broadcasted_iota(jnp.int32, (rows, rows), 0)
    other = lax.broadcasted_iota(jnp.int32, (rows, rows), 1)
    until = jnp.where(same & (other <= row), 1.0, 0.0)
    after = jnp.where(same & (other > row), 1.0, 0.0)
    run = jnp.dot(until, log_decay, precision=HIGHEST, preferred_element_type=F32)
    tail = jnp.dot(after, log_decay, precision=HIGHEST, preferred_element_type=F32)
    run_ref[...] = run
    less_ref[...] = (run - jnp.log(step)).T[:8]
    share = (jnp.exp(tail) * step).astype(BF16).astype(F32)
    spread = jnp.concatenate(
        [
            both_heads(share, p, head_size)
            * x[:, p * 2 * head_size : (p + 1) * 2 * head_size].astype(F32)
            for p in range(heads // 2)
        ],
        axis=1,
    )
    spread = spread.T.astype(BF16)
    spread_ref[...] = spread
    last = jnp.where(segment == segment[rows - 1 : rows], 1.0, 0.0)
    leaving = jnp.dot(spread, (keys.astype(F32) * last).astype(BF16), preferred_element_type=F32)
    gain = jnp.exp(run[rows - 1 : rows])
    carried = jnp.broadcast_to(marks_ref[rows - 1 : rows, 5:6], (heads * head_size, state)) > 0
    gain_wide = over_states(gain, heads, head_size)
    leaving_ref[...] = jnp.where(carried, leaving, leaving + gain_wide * init_ref[...])
    gain_ref[...] = jnp.where(carried, gain_wide, 0.0)


def scan_kernel(
    heads,
    block,
    unused,
    x_ref,
    keys_ref,
    queries_ref,
    run_ref,
    less_ref,
    marks_ref,
    segment_ref,
    table_ref,
    skip_ref,
    y_ref,
    masked_ref,
    begun_ref,
):
    del unused
    rows, inner = x_ref.shape
    head_size = inner // heads
    slots = table_ref.shape[1] // queries_ref.shape[1]
    queries = queries_ref[...].astype(F32)
    slot = marks_ref[:, 3:4]
    placed = jnp.concatenate(
        [(queries * jnp.where(slot == o, 1.0, 0.0)).astype(BF16) for o in range(slots)], axis=1
    )
    begun_ref[...] = lax.dot_general(
        placed, table_ref[...], ROWS_BY_ROWS, preferred_element_type=F32
    )
    blocks = [(t, s) for t in range(rows // block) for s in range(t + 1)]
    for at, (t, s) in enumerate(blocks):
        here, there = pl.ds(t * block, block), pl.ds(s * block, block)
        scores = lax.dot_general(
            queries_ref[here], keys_ref[there], ROWS_BY_ROWS, preferred_element_type=F32
        )
        same = marks_ref[here, 4:5] == segment_ref[0:1, there]
        if t == s:
            row = lax.broadcasted_iota(jnp.int32, (block, block), 0)
            other = lax.broadcasted_iota(jnp.int32, (block, block), 1)
            same = same & (other <= row)
        masked_ref[at] = jnp.where(same, scores, 0.0)
    grown = jnp.exp(run_ref[...])
    lane = lax.broadcasted_iota(jnp.int32, (block, 2 * head_size), 1)
    for p in range(heads // 2):
        wide = slice(p * 2 * head_size, (p + 1) * 2 * head_size)
        x = x_ref[:, wide].astype(F32)
        y = both_heads(grown, p, head_size) * begun_ref[:, wide] + both_heads(skip_ref[...], p, head_size) * x
        sums = [y[t * block : (t + 1) * block] for t in range(rows // block)]
        for at, (t, s) in enumerate(blocks):
            here, there = slice(t * block, (t + 1) * block), slice(s * block, (s + 1) * block)
            for side in range(2):
                head = 2 * p + side
                mine = (lane < head_size) if side == 0 else (lane >= head_size)
                x_own = jnp.where(mine, x[there], 0.0).astype(BF16)
                gap = run_ref[here, head : head + 1] - less_ref[head : head + 1, there]
                weight = (masked_ref[at] * jnp.exp(jnp.minimum(gap, 80.0))).astype(BF16)
                sums[t] = sums[t] + jnp.dot(weight, x_own, preferred_element_type=F32)
        for t in range(rows // block):
            y_ref[t * block : (t + 1) * block, wide] = sums[t]


def gate_kernel(
    heads, unused, y_ref, queries_ref, run_ref, marks_ref, entry_ref, gate_ref, gain_ref, out_ref, sq_ref
):
    del unused
    rows, inner = y_ref.shape
    head_size = inner // heads
    carried = jnp.where(marks_ref[:, 5:6] > 0, 1.0, 0.0)
    queries = (queries_ref[...].astype(F32) * carried).astype(BF16)
    held = lax.dot_general(
        queries, entry_ref[...].astype(BF16), ROWS_BY_ROWS, preferred_element_type=F32
    )
    grown = jnp.exp(run_ref[...])
    grown = jnp.concatenate([both_heads(grown, p, head_size) for p in range(heads // 2)], axis=1)
    gate = gate_ref[...].astype(F32)
    gated = (y_ref[...] + grown * held) * (gate / (1.0 + jnp.exp(-gate)))
    out_ref[...] = (gated * gain_ref[...]).astype(BF16)
    square = jnp.sum(gated * gated, axis=1, keepdims=True)
    sq_ref[...] = jnp.broadcast_to(square, (rows, LANES)).T[:8]


def norm_scale(own_ref, other_ref, channels):
    scale = lax.rsqrt((own_ref[0:1] + other_ref[0:1]) / channels + EPSILON)
    return jnp.broadcast_to(scale, (LANES, scale.shape[1])).T


def out_kernel(width, count, blocks, gated_ref, own_ref, other_ref, chooser_ref, *refs):
    del blocks
    weights, outs = refs[: 4 * count], refs[4 * count :]
    upper_out, upper_in, lower_out, lower_in, ends_ref = outs
    rows, inner = gated_ref.shape
    half = rows // 2
    scale = norm_scale(own_ref, other_ref, 2 * inner)
    scale = jnp.concatenate([scale] * (width // LANES), axis=1)
    gated = gated_ref[...]
    end_rows = jnp.dot(chooser_ref[...], gated, preferred_element_type=F32).astype(BF16)
    end_scale = jnp.dot(
        chooser_ref[...].astype(F32), scale, precision=HIGHEST, preferred_element_type=F32
    )
    for at, w in enumerate(weights):
        index, place = divmod(at, count)
        part = jnp.dot(gated, w[...], preferred_element_type=F32) * scale
        top, bottom = part[:half], part[half:]
        low = (index // 2) * count + place
        if index % 2:
            upper_out[:, low * width : (low + 1) * width] = top.astype(BF16)
        else:
            upper_in[:, low * width : (low + 1) * width] = top
        low = (index % 2) * count + place
        if index // 2:
            lower_out[:, low * width : (low + 1) * width] = bottom.astype(BF16)
        else:
            lower_in[:, low * width : (low + 1) * width] = bottom
        ends_ref[:, at * width : (at + 1) * width] = (
            jnp.dot(end_rows, w[...], preferred_element_type=F32) * end_scale
        )


def near_kernel(unused, upper_ref, upper_got, lower_ref, lower_got, *outs):
    del unused
    for kept, got, keep_ref, send_ref in (
        (upper_ref, upper_got, outs[0], outs[1]),
        (lower_ref, lower_got, outs[2], outs[3]),
    ):
        wide = keep_ref.shape[1]
        keep_ref[...] = kept[:, :wide] + got[:, :wide].astype(F32)
        send_ref[...] = (kept[:, wide:] + got[:, wide:].astype(F32)).astype(BF16)


def plane_kernel(unused, upper_ref, upper_got, lower_ref, lower_got, *outs):
    del unused
    half, width = upper_ref.shape[0], outs[0].shape[1]
    for at, out_ref in enumerate(outs):
        wide = slice(at * width, (at + 1) * width)
        upper = upper_ref[:, wide] + upper_got[:, wide].astype(F32)
        lower = lower_ref[:, wide] + lower_got[:, wide].astype(F32)
        out_ref[:half] = upper.astype(out_ref.dtype)
        out_ref[half:] = lower.astype(out_ref.dtype)


def hidden_kernel(unused, tokens_ref, own_ref, *refs):
    del unused
    total = own_ref[...]
    for part in refs[:-1]:
        total = total + part[...].astype(F32)
    refs[-1][...] = (tokens_ref[...].astype(F32) + total).astype(BF16)


def ends_kernel(width, block_of, place, *refs):
    sources, outs = refs[:4], refs[4:]
    half = sources[0].shape[1] // width
    for at in range(2 * half):
        which, low = divmod(at, half)
        block = block_of(which, low, place)
        to = pl.ds(pl.multiple_of(block * width, width), width)
        outs[0][:, to] = sources[which][:, low * width : (low + 1) * width]
        outs[1][:, to] = sources[2 + which][:, low * width : (low + 1) * width]


def finals_kernel(
    heads, added, first, spread_ref, keys_ref, marks_ref, ends_ref, entry_ref, init_ref, _, *refs
):
    out_ref = refs[-1]
    count, inner, state = out_ref.shape
    head_size = inner // heads
    slot = (first[0] + pl.program_id(0)) * count
    keys = keys_ref[...].astype(F32)
    owner = marks_ref[:, 6:7]
    mine = [
        (keys * jnp.where(owner == slot + i, ends_ref[i, :, heads : heads + 1], 0.0)).astype(BF16)
        for i in range(count)
    ]
    states = jnp.dot(
        spread_ref[...], jnp.concatenate(mine, axis=1), preferred_element_type=F32
    )
    for i in range(count):
        gain = over_states(ends_ref[i], heads, head_size)
        carried = jnp.broadcast_to(ends_ref[i, :, heads + 1 : heads + 2], (inner, state)) > 0.5
        value = states[:, i * state : (i + 1) * state]
        value = value + gain * jnp.where(carried, entry_ref[...], init_ref[i])
        out_ref[i] = value + refs[0][i] if added else value


def per_device(
    tokens,
    lengths,
    deal,
    pre_gain,
    w_inner,
    w_group,
    w_step,
    conv_inner,
    conv_group,
    conv_bias_inner,
    conv_bias_group,
    edge_inner,
    edge_group,
    init_states,
    step_bias,
    decay_log,
    skip,
    inner_gain,
    w_out,
    final_gain,
    w_head,
):
    rows, width = tokens.shape
    model_width = pre_gain.shape[0]
    requests = lengths.shape[0]
    taps = conv_inner.shape[0]
    inner = w_inner.shape[2]
    heads = w_step.shape[1]
    head_size = inner // heads
    state = w_group.shape[3]
    row_at, col_at, seq_at = (lax.axis_index(name) for name in ("row", "col", "seq"))
    row_size, col_size, seq_size = (lax.axis_size(name) for name in ("row", "col", "seq"))
    group_local = col_at * w_group.shape[2] // col_size

    def own_group(table, axis):
        return lax.dynamic_index_in_dim(table, group_local, axis, keepdims=False)

    def in_lanes(values):
        return jnp.pad(values, (0, LANES - heads))[None, :]

    first_row = seq_at * rows
    counts = jnp.concatenate([lengths, deal, jnp.reshape(first_row, (1,)).astype(jnp.int32)])
    marks, segment_row, chooser, slots = call(
        functools.partial(setup_kernel, taps),
        [
            ((rows, LANES), jnp.int32),
            ((8, rows), jnp.int32),
            ((requests, rows), BF16),
            ((requests, 2 * LANES), F32),
        ],
        prefetch=counts,
        vmem=4,
        work=0,
    )
    place = jnp.stack([row_at, col_at, group_local]).astype(jnp.int32)

    init_flat = jnp.reshape(init_states, (requests, inner, state))
    skip_row = in_lanes(skip)
    gains = pre_gain[None, :]

    near, far = tuple(range(col_size // 2)), tuple(range(col_size // 2, col_size))

    def block_of(shifts, at, place):
        shifts = (near, far)[shifts] if isinstance(shifts, int) else shifts
        index, shift = at // len(shifts), at % len(shifts) + shifts[0]
        return (place[0] ^ index) * col_size + (place[1] + shift) % col_size

    n_all = 2 * inner + 2 * state + LANES
    steps_across = jnp.transpose(w_step)

    def weights_of(shifts, gain_row):
        count = row_size * len(shifts)
        parts = count // 2

        def specs(shape, where):
            return [
                pl.BlockSpec(shape, lambda i, p, at=at: where(block_of(shifts, i * parts + at, p)))
                for at in range(parts)
            ]

        return call(
            functools.partial(weights_kernel, parts),
            [((count * width, n_all), BF16), ((1, count * width), F32)],
            *[w_inner] * parts,
            *[w_group] * parts,
            *[steps_across] * parts,
            *[gain_row] * parts,
            prefetch=place,
            grid=(count // parts,),
            in_specs=specs((width,) + w_inner.shape[1:], lambda b: (b, 0, 0))
            + specs((width,) + w_group.shape[1:], lambda b: (b, 0, 0, 0))
            + specs((heads, width), lambda b: (0, b))
            + specs((1, width), lambda b: (0, b)),
            out_specs=[
                pl.BlockSpec((parts * width, n_all), lambda i, p: (i, 0)),
                pl.BlockSpec((1, parts * width), lambda i, p: (0, i)),
            ],
            vmem=58,
        )

    gain_row = pre_gain[None, :]
    token_blocks = [tokens, from_ahead(tokens, "col", 1)]
    later = after(tokens, token_blocks[1])
    token_blocks += [from_ahead(later, "col", shift) for shift in range(2, col_size)]
    near_weights = weights_of(near, after(gain_row, token_blocks[1]))
    token_ends = []
    carry = ()
    for shifts in (near, far):
        first = shifts is near
        pieces = plane_gather(jnp.concatenate([token_blocks[i] for i in shifts], axis=1))
        if first:
            far_weights = weights_of(far, after(gain_row, pieces[1]))
        else:
            ready = pieces[1]
        weights, gains = near_weights if first else far_weights
        count = row_size * len(shifts)
        depth = count * width // 2
        outs = [((requests, count * width), F32)]
        totals = [((rows, n_all), F32), ((rows, LANES), F32)]
        if first:
            outs += totals
        else:
            outs += [((rows, inner), BF16), ((rows, inner + 2 * state), BF16), ((rows, LANES), F32)]
        piece_ends, *carry = call(
            functools.partial(project_kernel, first, inner, model_width),
            outs,
            *pieces,
            chooser,
            gains,
            weights,
            *carry,
            grid=(2,),
            in_specs=[None] * 7
            + [
                pl.BlockSpec((1, depth), lambda i, _: (0, i)),
                pl.BlockSpec((depth, n_all), lambda i, _: (i, 0)),
            ]
            + [None] * len(carry),
            out_specs=[pl.BlockSpec((requests, depth), lambda i, _: (0, i))]
            + [None] * (len(outs) - 1),
            scratch=[] if first else totals,
            vmem=24,
        )
        token_ends.append(piece_ends)
    gate_in, channels, step_raw = carry

    init_last = lax.dynamic_index_in_dim(init_flat, after(marks, ready)[rows - 1, 6], 0, keepdims=False)
    (table,) = call(
        table_kernel,
        [((inner, requests * state), BF16)],
        after(init_flat, ready),
        grid=(requests,),
        in_specs=[pl.BlockSpec((1, inner, state), lambda i, _: (i, 0, 0))],
        out_specs=[pl.BlockSpec((inner, state), lambda i, _: (0, i))],
        vmem=4,
        work=0,
    )
    conv_taps = jnp.concatenate(
        [conv_inner, jnp.reshape(own_group(after(conv_group, ready), 2), (taps, 2 * state))], axis=1
    )
    conv_bias = jnp.concatenate(
        [conv_bias_inner, jnp.reshape(own_group(after(conv_bias_group, ready), 1), (2 * state,))]
    )[None, :]
    edges = jnp.concatenate(
        [after(edge_inner, ready), jnp.reshape(own_group(after(edge_group, ready), 3), (requests, taps - 1, 2 * state))],
        axis=2,
    )
    edges = jnp.reshape(edges, (requests * (taps - 1), inner + 2 * state))

    rim = from_behind(channels[rows - RIM :], "seq", 1)
    x, keys, queries, run, less, spread, leaving, gain_carried = call(
        functools.partial(conv_kernel, heads),
        [
            ((rows, inner), BF16),
            ((rows, state), BF16),
            ((rows, state), BF16),
            ((rows, LANES), F32),
            ((8, rows), F32),
            ((inner, rows), BF16),
            ((inner, state), F32),
            ((inner, state), F32),
        ],
        channels,
        rim,
        edges,
        conv_taps,
        conv_bias,
        step_raw,
        in_lanes(step_bias),
        in_lanes(decay_log),
        marks,
        segment_row,
        init_last,
    )
    entry = from_behind(leaving, "seq", 1)
    for _ in range(seq_size - 2):
        entry = from_behind(gain_carried * entry + leaving, "seq", 1)

    block = 256
    pairs = (rows // block) * (rows // block + 1) // 2
    y = pl.pallas_call(
        functools.partial(scan_kernel, heads, block),
        out_shape=jax.ShapeDtypeStruct((rows, inner), F32),
        grid_spec=pltpu.PrefetchScalarGridSpec(
            num_scalar_prefetch=1,
            grid=(1,),
            in_specs=[
                pl.BlockSpec(a.shape, lambda *_: (0, 0))
                for a in (x, keys, queries, run, less, marks, segment_row, table, skip_row)
            ],
            out_specs=pl.BlockSpec((rows, inner), lambda *_: (0, 0)),
            scratch_shapes=[
                pltpu.VMEM((pairs, block, block), F32),
                pltpu.VMEM((rows, inner), F32),
            ],
        ),
        compiler_params=pltpu.CompilerParams(vmem_limit_bytes=16 * MIB),
    )(
        jnp.zeros((1,), jnp.int32),
        x,
        keys,
        queries,
        run,
        less,
        marks,
        segment_row,
        table,
        skip_row,
    )
    gated, own_squares = call(
        functools.partial(gate_kernel, heads),
        [((rows, inner), BF16), ((8, rows), F32)],
        y,
        queries,
        run,
        marks,
        entry,
        gate_in,
        inner_gain[None, :],
    )
    other_squares = from_partner(own_squares, "col", 0)

    half_out = []
    for shifts in (far, near):
        count = len(shifts)
        side = (rows // 2, 2 * count * width)
        half_out.append(
            call(
                functools.partial(out_kernel, width, count),
                [
                    (side, BF16),
                    (side, F32),
                    (side, BF16),
                    (side, F32),
                    ((requests, row_size * count * width), F32),
                ],
                gated,
                own_squares,
                other_squares,
                chooser,
                *[w_out] * (row_size * count),
                prefetch=place,
                in_specs=[None] * 4
                + [
                    pl.BlockSpec(
                        (inner, width),
                        lambda i, p, at=at, shifts=shifts: (0, block_of(shifts, at, p)),
                    )
                    for at in range(row_size * count)
                ],
                vmem=56 if shifts is far else 16,
                work=0,
            )
        )
    got = []
    for upper_out, _, lower_out, _, _ in half_out:
        got.append((from_partner(upper_out, "row", 0), from_partner(lower_out, "row", 1)))
    end_sum, end_tokens = call(
        functools.partial(ends_kernel, width, block_of),
        [((requests, model_width), F32)] * 2,
        after(half_out[1][4], got[0][0]),
        half_out[0][4],
        *token_ends,
        prefetch=place,
        vmem=4,
        work=0,
    )
    for axis, bit in (("col", 0), ("col", 1), ("row", 0), ("row", 1)):
        end_sum = end_sum + from_partner(end_sum.astype(BF16), axis, bit).astype(F32)

    def finals_after(far_ready):
        end_run = jnp.dot(chooser.astype(F32), run, precision=HIGHEST)[:, :heads]
        ends_here = slots[:, :1]
        end_marks = jnp.concatenate(
            [
                jnp.exp(end_run) * ends_here,
                ends_here,
                slots[:, LANES : LANES + 1],
                jnp.zeros((requests, LANES - heads - 2), F32),
            ],
            axis=1,
        )[:, None, :]

        kept = requests // seq_size

        def finals_of(first, steps, ready, extra):
            count = steps * kept
            by_slot = pl.BlockSpec((kept, inner, state), lambda i, s: (s[0] + i, 0, 0))
            by_step = pl.BlockSpec((kept, inner, state), lambda i, s: (i, 0, 0))
            return call(
                functools.partial(finals_kernel, heads, bool(extra)),
                [((count, inner, state), F32)],
                spread,
                keys,
                marks,
                end_marks,
                entry,
                init_flat,
                after(half_out[1][4], *ready),
                *extra,
                prefetch=jnp.reshape(first, (1,)).astype(jnp.int32),
                grid=(steps,),
                in_specs=[None] * 3
                + [pl.BlockSpec((kept, 1, LANES), lambda i, s: (s[0] + i, 0, 0)), None, by_slot]
                + [pl.BlockSpec(memory_space=pl.ANY)]
                + [by_step] * len(extra),
                out_specs=[by_step],
                vmem=20,
                work=0,
            )[0]

        if seq_size == 2:
            lent = finals_of(1 - seq_at, 1, far_ready, [])
            finals = finals_of(seq_at, 1, (), [from_partner(lent, "seq", 0)])
        else:
            finals = lax.psum_scatter(
                finals_of(jnp.int32(0), seq_size, (), []), "seq", scatter_dimension=0, tiled=True
            )
        return finals

    pieces = {}
    for shifts, outs, (upper_got, lower_got) in zip((far, near), half_out, got):
        _, upper_in, _, lower_in, _ = outs
        wide = len(shifts) * width
        upper, upper_far, lower, lower_near = call(
            near_kernel,
            [((rows // 2, wide), F32), ((rows // 2, wide), BF16)] * 2,
            upper_in,
            upper_got,
            lower_in,
            lower_got,
            vmem=8,
            work=10,
        )
        upper_far = from_partner(upper_far, "row", 1)
        lower_near = from_partner(lower_near, "row", 0)
        sums = call(
            plane_kernel,
            [((rows, width), BF16 if shift else F32) for shift in shifts],
            upper,
            upper_far,
            lower,
            lower_near,
            vmem=8,
            work=10,
        )
        if shifts is far:
            far_ready = sums
        for shift, part in zip(shifts, sums):
            pieces[shift] = from_ahead(part, "col", col_size - shift) if shift else part
    finals = finals_after(far_ready)
    if seq_size == 2:
        ending = after(end_tokens + end_sum, finals)
        ending = ending + from_partner(ending, "seq", 0)
    else:
        ending = lax.psum(end_tokens + end_sum, "seq")
    (hidden_out,) = call(
        hidden_kernel,
        [((rows, width), BF16)],
        tokens,
        *[pieces[shift] for shift in range(col_size)],
        vmem=4,
        work=30,
    )

    last_rows = ending.astype(BF16).astype(F32)
    final_scale = lax.rsqrt(jnp.sum(last_rows * last_rows, axis=1) / model_width + EPSILON)
    head_in = (last_rows * final_scale[:, None] * final_gain).astype(BF16)
    logits = jnp.dot(head_in, w_head, preferred_element_type=F32)

    final_states = jnp.reshape(finals, (finals.shape[0], heads, head_size, state))
    return (hidden_out, final_states, logits)


def solution(mesh):
    in_specs = (
        P("seq", ("row", "col")),
        P(),
        P(),
        P(),
        P(None, None, ("row", "col")),
        P(None, None, "row", None),
        P(None, ("row", "col")),
        P(None, ("row", "col")),
        P(None, None, "row", None),
        P(("row", "col")),
        P(None, "row", None),
        P(None, None, ("row", "col")),
        P(None, None, None, "row", None),
        P(None, ("row", "col"), None, None),
        P(("row", "col")),
        P(("row", "col")),
        P(("row", "col")),
        P(("row", "col")),
        P(("row", "col"), None),
        P(),
        P(None, ("seq", "row", "col")),
    )
    out_specs = (
        P("seq", ("row", "col")),
        P("seq", ("row", "col"), None, None),
        P(None, ("seq", "row", "col")),
    )
    return jax.shard_map(
        per_device, mesh=mesh, in_specs=in_specs, out_specs=out_specs, check_vma=False
    )
```

time: 218 us -> 148 us (0.68)
  local copies, waits for them, and re-layouts: 43.9 us -> 12.8 us
  starting transfers between devices: 54.5 us -> 39.3 us
  other arithmetic: 13.9 us -> 5.25 us
  waiting for transfers between devices: 39.5 us -> 32.6 us
  matrix products: 8.66 us -> 2.08 us
  blocking collectives: 4.17 us -> 0 us
    ppermute x38 -> x23, starting transfers between devices: 39.6 us -> 22.5 us  [from_partner(): lax.ppermute(x, axis, [(i, i ^ 1 << bit) for i in range(lax.axis_size(axi...]
    ppermute x38 -> x23, waiting for transfers between devices: 39.5 us -> 25 us  [from_partner(): lax.ppermute(x, axis, [(i, i ^ 1 << bit) for i in range(lax.axis_size(axi...]
    unnamed x65 -> x68, local copies, waits for them, and re-layouts: 23.5 us -> 9.98 us
    ppermute x6, waiting for transfers between devices: 0.02 us -> 6.92 us  [from_ahead(): lax.ppermute(x, axis, [((i + distance) % size, i) for i in range(size)])]
    reshape x4 -> x0, local copies, waits for them, and re-layouts: 5.75 us -> none  [the longest x1 3.92 us: per_device(): jnp.reshape(jnp.transpose(init_flat.astype(BF16), (1, 0, 2)), (inner, req...]
    slice x4 -> x2, local copies, waits for them, and re-layouts: 4.65 us -> 0.07 us  [plane_gather(): upper, lower = (block[:half], block[half:])]
    psum x1 -> x0, blocking collectives: 4.17 us -> none  [per_device(): last_rows = lax.psum(ending, 'seq').astype(BF16).astype(F32)]
    transpose x1 -> x0, local copies, waits for them, and re-layouts: 3.94 us -> none  [per_device(): jnp.transpose(init_flat.astype(BF16), (1, 0, 2))]
  transfers between devices with their start and end apart: 46 -> 31, of which waited for: 13 -> 13; matrix products, arithmetic and copies ran while one was open for 24% -> 6% of each run, Pallas kernels for 14% -> 24%
where the time goes in v2:
time: 148 us; the launch traced here: 147 us
  Pallas kernels  51.7 us (35%)
  starting transfers between devices  39.3 us (27%)
  waiting for transfers between devices  32.6 us (22%)
  local copies, waits for them, and re-layouts  12.8 us (9%)
  other arithmetic  5.25 us (4%)
  between operations  3.09 us (2%)
  matrix products  2.08 us (1%)
    pallas_call x18, Pallas kernels, call(): pl.pallas_call(kernel, out_shape=shapes, grid_spec=spec, compiler_params=...  48.5 us
    ppermute x23, waiting for transfers between devices, from_partner(): lax.ppermute(x, axis, [(i, i ^ 1 << bit) for i in range(lax.axis_size(axi...  25 us
    ppermute x23, starting transfers between devices, from_partner(): lax.ppermute(x, axis, [(i, i ^ 1 << bit) for i in range(lax.axis_size(axi...  22.5 us
    ppermute x6, starting transfers between devices, from_ahead(): lax.ppermute(x, axis, [((i + distance) % size, i) for i in range(size)])  13.1 us
    unnamed x68, local copies, waits for them, and re-layouts  9.98 us
    ppermute x6, waiting for transfers between devices, from_ahead(): lax.ppermute(x, axis, [((i + distance) % size, i) for i in range(size)])  6.92 us
    ppermute x2, starting transfers between devices, from_behind(): return lax.ppermute(block, axis, route)  3.72 us
    pallas_call x1, Pallas kernels, per_device(): pl.pallas_call(functools.partial(scan_kernel, heads, block), out_shape=ja...  3.18 us
  transfers between devices with their start and end apart: 31, of which 13 were waited for; matrix products, arithmetic and copies ran while one was open for 6% of the time, Pallas kernels for 24%

profile of v2, /device:TPU:0, one launch (start us, length us, event | category | flops | bytes accessed | tf_op | source)
XLA Modules:
  0.0 146.9 jit_solution(921666953047445306)
XLA Ops:
  0.6 5.1 %collective-permute-start = (bf16[512,256]{1,0:T(8,128)(2,1)}, bf16[512,256]{1,0:T(8,128)(2,1)S(1)}, u32[]{:S(2)}, u32[]{:S(2)}) collective-permute-start(bf16[512,256]{1,0:T(8,128)(2,1)} %tokens_ref.1), channel_id=1, source_target_pairs={{1,0},{2,1},{3,2},{0,3},{5,4},{6,5},{7,6},{4,7},{9,8},{10,9},{11,1... | collective-permute-start | bytes 786440 | tf_op jit(solution)/shard_map/ppermute | solution.py:32
  6.3 0.7 pad_add_fusion.1.counts
  7.1 1.4 shard_map.220
  8.5 0.7 pad_bitcast_fusion.1
  9.2 1.0 constant_dynamic-update-slice_fusion.3
  10.2 1.5 %collective-permute-done = bf16[512,256]{1,0:T(8,128)(2,1)S(1)} collective-permute-done((bf16[512,256]{1,0:T(8,128)(2,1)}, bf16[512,256]{1,0:T(8,128)(2,1)S(1)}, u32[]{:S(2)}, u32[]{:S(2)}) %collective-permute-start) | collective-permute-done | bytes 262176 | tf_op jit(solution)/shard_map/ppermute | solution.py:32
  11.6 1.4 collective-permute-start.1
  13.0 3.4 %collective-permute-start.2 = (bf16[512,256]{1,0:T(8,128)(2,1)}, bf16[512,256]{1,0:T(8,128)(2,1)S(1)}, u32[]{:S(2)}, u32[]{:S(2)}) collective-permute-start(bf16[512,256]{1,0:T(8,128)(2,1)} %tokens_ref.1), channel_id=1, source_target_pairs={{3,0},{0,1},{1,2},{2,3},{7,4},{4,5},{5,6},{6,7},{11,8},{8,9},{9,10... | collective-permute-start | bytes 786440 | tf_op jit(solution)/shard_map/ppermute | solution.py:32
  16.4 1.6 %collective-permute-start.7 = (bf16[256,512]{1,0:T(8,128)(2,1)S(1)}, bf16[256,512]{1,0:T(8,128)(2,1)S(1)}, u32[]{:S(2)}, u32[]{:S(2)}) collective-permute-start(bf16[256,512]{1,0:T(8,128)(2,1)S(1)} %get-tuple-element.126.refs_0_), channel_id=1, source_target_pairs={{0,8},{4,12},{8,0},{12,4},{1,9},{5,13},{9,1},{13,5},{2,10},{6,14},... | collective-permute-start | bytes 786440 | tf_op jit(solution)/shard_map/ppermute | solution.py:27
  18.0 1.5 %collective-permute-start.9 = (bf16[256,512]{1,0:T(8,128)(2,1)S(1)}, bf16[256,512]{1,0:T(8,128)(2,1)S(1)}, u32[]{:S(2)}, u32[]{:S(2)}) collective-permute-start(bf16[256,512]{1,0:T(8,128)(2,1)S(1)} %get-tuple-element.125.refs_3_), channel_id=1, source_target_pairs={{0,4},{4,0},{8,12},{12,8},{1,5},{5,1},{9,13},{13,9},{2,6},{6,2},{1... | collective-permute-start | bytes 786440 | tf_op jit(solution)/shard_map/ppermute | solution.py:27
  19.5 7.1 %shard_map.222 = (bf16[2048,1408]{1,0:T(8,128)(2,1)}, f32[1,2048]{1,0:T(1,128)}) custom-call(s32[3]{0:T(128)} %pad_add_fusion.place.blocks, bf16[4096,2,512]{2,1,0:T(2,128)(2,1)} %refs_3_.5, bf16[4096,2,512]{2,1,0:T(2,128)(2,1)} %refs_3_.5, bf16[4096,2,512]{2,1,0:T(2,128)(2,1)} %refs_3_.5, bf16[4096,2,512]{2,1,0:T(2,128)(2,1)} %refs_3_.5, ...), custom_call_target="tpu_custom_call" | custom-call | flops 20000000000 | bytes 100000000 | tf_op jit(solution)/shard_map/pallas_call | solution.py:60
  26.6 0.8 pad_maximum_fusion.2
  28.0 0.9 pad_maximum_fusion.3
  29.4 1.8 %collective-permute-done.1 = bf16[512,256]{1,0:T(8,128)(2,1)S(1)} collective-permute-done((bf16[512,256]{1,0:T(8,128)(2,1)}, bf16[512,256]{1,0:T(8,128)(2,1)S(1)}, u32[]{:S(2)}, u32[]{:S(2)}) %collective-permute-start.1) | collective-permute-done | bytes 262176 | tf_op jit(solution)/shard_map/ppermute | solution.py:32
  31.3 1.6 %collective-permute-start.3 = (bf16[256,512]{1,0:T(8,128)(2,1)S(1)}, bf16[256,512]{1,0:T(8,128)(2,1)S(1)}, u32[]{:S(2)}, u32[]{:S(2)}) collective-permute-start(bf16[256,512]{1,0:T(8,128)(2,1)S(1)} %get-tuple-element.128.refs_0_), channel_id=1, source_target_pairs={{0,8},{4,12},{8,0},{12,4},{1,9},{5,13},{9,1},{13,5},{2,10},{6,14},... | collective-permute-start | bytes 786440 | tf_op jit(solution)/shard_map/ppermute | solution.py:27
  32.9 1.6 %collective-permute-start.5 = (bf16[256,512]{1,0:T(8,128)(2,1)S(1)}, bf16[256,512]{1,0:T(8,128)(2,1)S(1)}, u32[]{:S(2)}, u32[]{:S(2)}) collective-permute-start(bf16[256,512]{1,0:T(8,128)(2,1)S(1)} %get-tuple-element.127.refs_3_), channel_id=1, source_target_pairs={{0,4},{4,0},{8,12},{12,8},{1,5},{5,1},{9,13},{13,9},{2,6},{6,2},{1... | collective-permute-start | bytes 786440 | tf_op jit(solution)/shard_map/ppermute | solution.py:27
  34.4 7.1 %shard_map.221 = (bf16[2048,1408]{1,0:T(8,128)(2,1)}, f32[1,2048]{1,0:T(1,128)}) custom-call(s32[3]{0:T(128)} %pad_add_fusion.place.blocks, bf16[4096,2,512]{2,1,0:T(2,128)(2,1)} %refs_3_.5, bf16[4096,2,512]{2,1,0:T(2,128)(2,1)} %refs_3_.5, bf16[4096,2,512]{2,1,0:T(2,128)(2,1)} %refs_3_.5, bf16[4096,2,512]{2,1,0:T(2,128)(2,1)} %refs_3_.5, ...), custom_call_target="tpu_custom_call" | custom-call | flops 20000000000 | bytes 100000000 | tf_op jit(solution)/shard_map/pallas_call | solution.py:60
  41.5 4.6 %collective-permute-done.3.refs_1_ = bf16[256,512]{1,0:T(8,128)(2,1)S(1)} collective-permute-done((bf16[256,512]{1,0:T(8,128)(2,1)S(1)}, bf16[256,512]{1,0:T(8,128)(2,1)S(1)}, u32[]{:S(2)}, u32[]{:S(2)}) %collective-permute-start.3) | collective-permute-done | bytes 262176 | tf_op jit(solution)/shard_map/ppermute | solution.py:27
  46.1 0.9 pad_maximum_fusion
  47.0 1.5 %collective-permute-start.4 = (bf16[256,1024]{1,0:T(8,128)(2,1)}, bf16[256,1024]{1,0:T(8,128)(2,1)}, u32[]{:S(2)}, u32[]{:S(2)}) collective-permute-start(bf16[256,1024]{1,0:T(8,128)(2,1)} %pad_maximum_fusion), channel_id=1, source_target_pairs={{0,4},{4,0},{8,12},{12,8},{1,5},{5,1},{9,13},{13,9},{2,6},{6,2},{1... | collective-permute-start | bytes 1572872 | tf_op jit(solution)/shard_map/ppermute | solution.py:27
  48.5 0.9 pad_maximum_fusion.1
  50.2 0.6 slice.32
  52.7 1.0 dynamic-slice_bitcast_fusion.init_ref
  53.8 2.6 %copy-done.19 = bf16[2048,1408]{1,0:T(8,128)(2,1)S(1)} copy-done((bf16[2048,1408]{1,0:T(8,128)(2,1)S(1)}, bf16[2048,1408]{1,0:T(8,128)(2,1)}, u32[]{:S(2)}) %copy-start.19) | copy-done | bytes 5767192
  56.4 5.1 %shard_map.223 = (f32[16,2048]{1,0:T(8,128)S(1)}, f32[512,1408]{1,0:T(8,128)S(1)}, f32[512,128]{1,0:T(8,128)S(1)}) custom-call(s32[1]{0:T(128)} %constant.31.clone.1.unused, bf16[256,512]{1,0:T(8,128)(2,1)S(1)} %get-tuple-element.126.refs_0_, bf16[256,512]{1,0:T(8,128)(2,1)S(1)} %collective-permute-done.7.refs_1_, ...), custom_call_target="tpu_custom_call" | custom-call | flops 20000000000 | bytes 100000000 | tf_op jit(solution)/shard_map/pallas_call | solution.py:60
  61.6 5.2 %shard_map.224 = (f32[16,2048]{1,0:T(8,128)S(1)}, bf16[512,512]{1,0:T(8,128)(2,1)S(1)}, bf16[512,768]{1,0:T(8,128)(2,1)S(1)}, f32[512,128]{1,0:T(8,128)S(1)}) custom-call(s32[1]{0:T(128)} %constant.31.clone.1.unused, bf16[256,512]{1,0:T(8,128)(2,1)S(1)} %get-tuple-element.128.refs_0_, bf16[256,512]{1,0:T(8,128)(2,1)S(1)} %collective-permute-done.3.refs_1_, ...), custom_call_target="tpu_custom_call" | custom-call | flops 20000000000 | bytes 100000000 | tf_op jit(solution)/shard_map/pallas_call | solution.py:60
  66.8 1.5 %collective-permute-start.11 = (bf16[16,768]{1,0:T(8,128)(2,1)S(1)}, bf16[16,768]{1,0:T(8,128)(2,1)S(1)}, u32[]{:S(2)}, u32[]{:S(2)}) collective-permute-start(bf16[16,768]{1,0:T(8,128)(2,1)S(1)} %slice.31), channel_id=1, source_target_pairs={{0,16},{1,17},{2,18},{3,19},{4,20},{5,21},{6,22},{7,23},{8,24},{9,... | collective-permute-start | bytes 73736 | tf_op jit(solution)/shard_map/ppermute | solution.py:23
  68.3 0.6 collective-permute-done.11.rim_ref
  68.9 5.5 %shard_map.225 = (bf16[512,512]{1,0:T(8,128)(2,1)S(1)}, bf16[512,128]{1,0:T(8,128)(2,1)S(1)}, bf16[512,128]{1,0:T(8,128)(2,1)S(1)}, f32[512,128]{1,0:T(8,128)S(1...) custom-call(s32[1]{0:T(128)} %constant.31.clone.1.unused, ...), custom_call_target="tpu_custom_call" | custom-call | flops 20000000000 | bytes 100000000 | tf_op jit(solution)/shard_map/pallas_call | solution.py:60
  74.4 2.3 %collective-permute-start.12 = (f32[512,128]{1,0:T(8,128)S(1)}, f32[512,128]{1,0:T(8,128)S(1)}, u32[]{:S(2)}, u32[]{:S(2)}) collective-permute-start(f32[512,128]{1,0:T(8,128)S(1)} %get-tuple-element.88), channel_id=1, source_target_pairs={{0,16},{1,17},{2,18},{3,19},{4,20},{5,21},{6,22},{7,23},{8,24},{9,... | collective-permute-start | bytes 786440 | tf_op jit(solution)/shard_map/ppermute | solution.py:23
  76.7 0.9 shard_map.226.table_ref
  77.6 3.2 %shard_map.227.y_ref = f32[512,512]{1,0:T(8,128)S(1)} custom-call(s32[1]{0:T(128)} %constant.31.clone.1.unused, bf16[512,512]{1,0:T(8,128)(2,1)S(1)} %get-tuple-element.82.x_ref, bf16[512,128]{1,0:T(8,128)(2,1)S(1)} %get-tuple-element.83.keys_ref, bf16[512,128]{1,0:T(8,128)(2,1)S(1)} %get-tuple-element.84.queries_ref, ...), custom_call_target="tpu_custom_call" | custom-call | tf_op jit(solution)/shard_map/pallas_call | solution.py:702
  80.8 1.2 shard_map.228
  82.0 0.8 copy-done.5
  83.0 3.5 %collective-permute-done.13.other_ref = f32[8,512]{1,0:T(8,128)S(1)} collective-permute-done((f32[8,512]{1,0:T(8,128)S(1)}, f32[8,512]{1,0:T(8,128)S(1)}, u32[]{:S(2)}, u32[]{:S(2)}) %collective-permute-start.13) | collective-permute-done | bytes 16416 | tf_op jit(solution)/shard_map/ppermute | solution.py:27
  86.5 0.6 copy-done.13
  87.1 5.4 %shard_map.232 = (bf16[256,1024]{1,0:T(8,128)(2,1)}, f32[256,1024]{1,0:T(8,128)}, bf16[256,1024]{1,0:T(8,128)(2,1)}, f32[256,1024]{1,0:T(8,128)}, f32[16,2048]{1,0:T(8,128)}) custom-call(s32[3]{0:T(128)} %pad_add_fusion.place.blocks, bf16[512,512]{1,0:T(8,128)(2,1)} %copy-done.5, f32[8,512]{1,0:T(8,128)} %copy-done.11, f32[8,512]{1,0:T(8,128)} %copy-done.13, ...), custom_call_target="tpu_custom_call" | custom-call | bytes 1000 | tf_op jit(solution)/shard_map/pallas_call | solution.py:60
  93.0 1.5 %collective-permute-start.20 = (bf16[256,1024]{1,0:T(8,128)(2,1)}, bf16[256,1024]{1,0:T(8,128)(2,1)}, u32[]{:S(2)}, u32[]{:S(2)}) collective-permute-start(bf16[256,1024]{1,0:T(8,128)(2,1)} %get-tuple-element.105), channel_id=1, source_target_pairs={{0,8},{4,12},{8,0},{12,4},{1,9},{5,13},{9,1},{13,5},{2,10},{6,14},... | collective-permute-start | bytes 1572872 | tf_op jit(solution)/shard_map/ppermute | solution.py:27
  95.0 2.2 %copy-done.2 = bf16[512,4096]{1,0:T(8,128)(2,1)S(1)} copy-done((bf16[512,4096]{1,0:T(8,128)(2,1)S(1)}, bf16[512,4096]{1,0:T(8,128)(2,1)}, u32[]{:S(2)}) %copy-start.2) | copy-done | bytes 4194328
  97.2 0.7 copy-done.12
  98.0 0.7 copy-done.14
  98.7 2.4 %shard_map.229 = (bf16[256,1024]{1,0:T(8,128)(2,1)S(1)}, f32[256,1024]{1,0:T(8,128)S(1)}, bf16[256,1024]{1,0:T(8,128)(2,1)S(1)}, f32[256,1024]{1,0:T(8,128)S(1)}, f32[16,2048]{1,0:T(8,128)S(1)}) custom-call(s32[3]{0:T(128)S(1)} %copy-done.15, bf16[512,512]{1,0:T(8,128)(2,1)S(1)} %copy-done.6, f32[8,512]{1,0:T(8,128)S(1)} %copy-done.12, ...), custom_call_target="tpu_custom_call" | custom-call | bytes 1000 | tf_op jit(solution)/shard_map/pallas_call | solution.py:60
  101.1 1.5 %collective-permute-start.14 = (bf16[256,1024]{1,0:T(8,128)(2,1)S(1)}, bf16[256,1024]{1,0:T(8,128)(2,1)S(1)}, u32[]{:S(2)}, u32[]{:S(2)}) collective-permute-start(bf16[256,1024]{1,0:T(8,128)(2,1)S(1)} %get-tuple-element.93), channel_id=1, source_target_pairs={{0,4},{4,0},{8,12},{12,8},{1,5},{5,1},{9,13},{13,9},{2,6},{6,2},{1... | collective-permute-start | bytes 1572872 | tf_op jit(solution)/shard_map/ppermute | solution.py:27
  103.2 4.4 %collective-permute-done.19.upper_got = bf16[256,1024]{1,0:T(8,128)(2,1)S(1)} collective-permute-done((bf16[256,1024]{1,0:T(8,128)(2,1)}, bf16[256,1024]{1,0:T(8,128)(2,1)S(1)}, u32[]{:S(2)}, u32[]{:S(2)}) %collective-permute-start.19) | collective-permute-done | bytes 524320 | tf_op jit(solution)/shard_map/ppermute | solution.py:27
  107.6 0.6 shard_map.238
  108.5 1.2 shard_map.233
  109.7 1.6 %collective-permute-start.21 = (bf16[256,512]{1,0:T(8,128)(2,1)S(1)}, bf16[256,512]{1,0:T(8,128)(2,1)S(1)}, u32[]{:S(2)}, u32[]{:S(2)}) collective-permute-start(bf16[256,512]{1,0:T(8,128)(2,1)S(1)} %get-tuple-element.107), channel_id=1, source_target_pairs={{0,8},{4,12},{8,0},{12,4},{1,9},{5,13},{9,1},{13,5},{2,10},{6,14},... | collective-permute-start | bytes 786440 | tf_op jit(solution)/shard_map/ppermute | solution.py:27
  111.3 1.2 collective-permute-start.22
  112.5 2.0 %collective-permute-done.26 = bf16[16,4096]{1,0:T(8,128)(2,1)S(1)} collective-permute-done((bf16[16,4096]{1,0:T(8,128)(2,1)S(1)}, bf16[16,4096]{1,0:T(8,128)(2,1)S(1)}, u32[]{:S(2)}, u32[]{:S(2)}) %collective-permute-start.26) | collective-permute-done | bytes 131104 | tf_op jit(solution)/shard_map/ppermute | solution.py:27
  114.6 4.2 %collective-permute-done.14.upper_got = bf16[256,1024]{1,0:T(8,128)(2,1)S(1)} collective-permute-done((bf16[256,1024]{1,0:T(8,128)(2,1)S(1)}, bf16[256,1024]{1,0:T(8,128)(2,1)S(1)}, u32[]{:S(2)}, u32[]{:S(2)}) %collective-permute-start.14) | collective-permute-done | bytes 524320 | tf_op jit(solution)/shard_map/ppermute | solution.py:27
  119.0 2.1 %collective-permute-start.16 = (bf16[256,512]{1,0:T(8,128)(2,1)S(1)}, bf16[256,512]{1,0:T(8,128)(2,1)S(1)}, u32[]{:S(2)}, u32[]{:S(2)}) collective-permute-start(bf16[256,512]{1,0:T(8,128)(2,1)S(1)} %get-tuple-element.97), channel_id=1, source_target_pairs={{0,8},{4,12},{8,0},{12,4},{1,9},{5,13},{9,1},{13,5},{2,10},{6,14},... | collective-permute-start | bytes 786440 | tf_op jit(solution)/shard_map/ppermute | solution.py:27
  121.1 1.5 %collective-permute-start.17 = (bf16[256,512]{1,0:T(8,128)(2,1)S(1)}, bf16[256,512]{1,0:T(8,128)(2,1)S(1)}, u32[]{:S(2)}, u32[]{:S(2)}) collective-permute-start(bf16[256,512]{1,0:T(8,128)(2,1)S(1)} %get-tuple-element.99), channel_id=1, source_target_pairs={{0,4},{4,0},{8,12},{12,8},{1,5},{5,1},{9,13},{13,9},{2,6},{6,2},{1... | collective-permute-start | bytes 786440 | tf_op jit(solution)/shard_map/ppermute | solution.py:27
  122.7 0.6 collective-permute-start.28
  123.2 0.9 collective-permute-done.21.upper_got
  124.8 2.4 %collective-permute-start.24 = (bf16[512,256]{1,0:T(8,128)(2,1)S(1)}, bf16[512,256]{1,0:T(8,128)(2,1)S(1)}, u32[]{:S(2)}, u32[]{:S(2)}) collective-permute-start(bf16[512,256]{1,0:T(8,128)(2,1)S(1)} %get-tuple-element.111), channel_id=1, source_target_pairs={{1,0},{2,1},{3,2},{0,3},{5,4},{6,5},{7,6},{4,7},{9,8},{10,9},{11,1... | collective-permute-start | bytes 786440 | tf_op jit(solution)/shard_map/ppermute | solution.py:32
  127.2 1.4 shard_map.236
  128.7 1.4 collective-permute-done.28
  130.1 1.6 %collective-permute-start.29 = (bf16[16,4096]{1,0:T(8,128)(2,1)S(1)}, bf16[16,4096]{1,0:T(8,128)(2,1)S(1)}, u32[]{:S(2)}, u32[]{:S(2)}) collective-permute-start(bf16[16,4096]{1,0:T(8,128)(2,1)S(1)} %fusion.6), channel_id=1, source_target_pairs={{0,8},{4,12},{8,0},{12,4},{1,9},{5,13},{9,1},{13,5},{2,10},{6,14},... | collective-permute-start | bytes 393224 | tf_op jit(solution)/shard_map/ppermute | solution.py:27
  132.4 3.7 %collective-permute-done.29 = bf16[16,4096]{1,0:T(8,128)(2,1)S(1)} collective-permute-done((bf16[16,4096]{1,0:T(8,128)(2,1)S(1)}, bf16[16,4096]{1,0:T(8,128)(2,1)S(1)}, u32[]{:S(2)}, u32[]{:S(2)}) %collective-permute-start.29) | collective-permute-done | bytes 131104 | tf_op jit(solution)/shard_map/ppermute | solution.py:27
  136.2 2.8 %shard_map.237 = f32[8,512,128]{2,1,0:T(8,128)} custom-call(s32[1]{0:T(128)} %bitcast.14.first, bf16[512,512]{1,0:T(8,128)(2,1)S(1)} %get-tuple-element.112.spread_ref, bf16[512,128]{1,0:T(8,128)(2,1)S(1)} %get-tuple-element.83.keys_ref, s32[512,128]{1,0:T(8,128)S(1)} %get-tuple-element.81.marks_ref, f32[16,1,128]{2,1,0:T(1,128)S(1)} %bitcast.38, ...), custom_call_target="tpu_custom_call" | custom-call | bytes 1000 | tf_op jit(solution)/shard_map/pallas_call | solution.py:60
  139.0 3.7 %collective-permute-done.23.refs_1_ = bf16[512,256]{1,0:T(8,128)(2,1)S(1)} collective-permute-done((bf16[512,256]{1,0:T(8,128)(2,1)S(1)}, bf16[512,256]{1,0:T(8,128)(2,1)S(1)}, u32[]{:S(2)}, u32[]{:S(2)}) %collective-permute-start.23) | collective-permute-done | bytes 262176 | tf_op jit(solution)/shard_map/ppermute | solution.py:32
  142.7 0.9 shard_map.235
  143.8 1.2 slice-done.1
  145.0 1.9 %fusion.7 = f32[16,1024]{1,0:T(8,128)} fusion(bf16[4096,1024]{1,0:T(8,128)(2,1)S(1)} %bitcast.41, bf16[16,4096]{1,0:T(8,128)(2,1)S(1)} %get-tuple-element.124, f32[4096]{0:T(1024)S(1)} %copy-done.23, f32[16]{0:T(128)S(1)} %add_rsqrt_fusion), kind=kOutput, calls=%fused_computation.20 | convolution fusion | flops 134479872 | bytes 8601664 | tf_op jit(solution)/shard_map/dot_general | solution.py:890
  (123 shorter events, 6.8 us)
Async XLA Ops:
  0.6 49.2 %copy-start = (bf16[16,3,2,2,128]{4,3,2,1,0:T(2,128)(2,1)S(1)}, bf16[16,3,2,2,128]{4,3,2,1,0:T(2,128)(2,1)}, u32[]{:S(2)}) copy-start(bf16[16,3,2,2,128]{4,3,2,1,0:T(2,128)(2,1)} %param.33) | copy-start | bytes 147460
  0.6 11.0 %collective-permute-start = (bf16[512,256]{1,0:T(8,128)(2,1)}, bf16[512,256]{1,0:T(8,128)(2,1)S(1)}, u32[]{:S(2)}, u32[]{:S(2)}) collective-permute-start(bf16[512,256]{1,0:T(8,128)(2,1)} %tokens_ref.1), channel_id=1, source_target_pairs={{1,0},{2,1},{3,2},{0,3},{5,4},{6,5},{7,6},{4,7},{9,8},{10,9},{11,1... | collective-permute-start | bytes 786440 | tf_op jit(solution)/shard_map/ppermute | solution.py:32
  8.5 53.1 %copy-start.8 = (bf16[16,512]{1,0:T(8,128)(2,1)}, bf16[16,512]{1,0:T(8,128)(2,1)S(1)}, u32[]{:S(2)}) copy-start(bf16[16,512]{1,0:T(8,128)(2,1)S(1)} %get-tuple-element.64.refs_6_.chooser_ref) | copy-start | bytes 49156
  11.6 19.5 %collective-permute-start.1 = (bf16[512,256]{1,0:T(8,128)(2,1)}, bf16[512,256]{1,0:T(8,128)(2,1)S(1)}, u32[]{:S(2)}, u32[]{:S(2)}) collective-permute-start(bf16[512,256]{1,0:T(8,128)(2,1)} %tokens_ref.1), channel_id=1, source_target_pairs={{2,0},{3,1},{0,2},{1,3},{6,4},{7,5},{4,6},{5,7},{10,8},{11,9},{8,1... | collective-permute-start | bytes 786440 | tf_op jit(solution)/shard_map/ppermute | solution.py:32
  13.0 18.2 %collective-permute-start.2 = (bf16[512,256]{1,0:T(8,128)(2,1)}, bf16[512,256]{1,0:T(8,128)(2,1)S(1)}, u32[]{:S(2)}, u32[]{:S(2)}) collective-permute-start(bf16[512,256]{1,0:T(8,128)(2,1)} %tokens_ref.1), channel_id=1, source_target_pairs={{3,0},{0,1},{1,2},{2,3},{7,4},{4,5},{5,6},{6,7},{11,8},{8,9},{9,10... | collective-permute-start | bytes 786440 | tf_op jit(solution)/shard_map/ppermute | solution.py:32
  16.4 10.2 %collective-permute-start.7 = (bf16[256,512]{1,0:T(8,128)(2,1)S(1)}, bf16[256,512]{1,0:T(8,128)(2,1)S(1)}, u32[]{:S(2)}, u32[]{:S(2)}) collective-permute-start(bf16[256,512]{1,0:T(8,128)(2,1)S(1)} %get-tuple-element.126.refs_0_), channel_id=1, source_target_pairs={{0,8},{4,12},{8,0},{12,4},{1,9},{5,13},{9,1},{13,5},{2,10},{6,14},... | collective-permute-start | bytes 786440 | tf_op jit(solution)/shard_map/ppermute | solution.py:27
  18.0 10.0 %collective-permute-start.9 = (bf16[256,512]{1,0:T(8,128)(2,1)S(1)}, bf16[256,512]{1,0:T(8,128)(2,1)S(1)}, u32[]{:S(2)}, u32[]{:S(2)}) collective-permute-start(bf16[256,512]{1,0:T(8,128)(2,1)S(1)} %get-tuple-element.125.refs_3_), channel_id=1, source_target_pairs={{0,4},{4,0},{8,12},{12,8},{1,5},{5,1},{9,13},{13,9},{2,6},{6,2},{1... | collective-permute-start | bytes 786440 | tf_op jit(solution)/shard_map/ppermute | solution.py:27
  27.5 26.2 %collective-permute-start.8 = (bf16[256,1024]{1,0:T(8,128)(2,1)}, bf16[256,1024]{1,0:T(8,128)(2,1)S(1)}, u32[]{:S(2)}, u32[]{:S(2)}) collective-permute-start(bf16[256,1024]{1,0:T(8,128)(2,1)} %pad_maximum_fusion.2), channel_id=1, source_target_pairs={{0,4},{4,0},{8,12},{12,8},{1,5},{5,1},{9,13},{13,9},{2,6},{6,2},{1... | collective-permute-start | bytes 1572872 | tf_op jit(solution)/shard_map/ppermute | solution.py:27
  28.9 24.8 %collective-permute-start.10 = (bf16[256,1024]{1,0:T(8,128)(2,1)}, bf16[256,1024]{1,0:T(8,128)(2,1)}, u32[]{:S(2)}, u32[]{:S(2)}) collective-permute-start(bf16[256,1024]{1,0:T(8,128)(2,1)} %pad_maximum_fusion.3), channel_id=1, source_target_pairs={{0,8},{4,12},{8,0},{12,4},{1,9},{5,13},{9,1},{13,5},{2,10},{6,14},... | collective-permute-start | bytes 1572872 | tf_op jit(solution)/shard_map/ppermute | solution.py:27
  31.3 14.9 %collective-permute-start.3 = (bf16[256,512]{1,0:T(8,128)(2,1)S(1)}, bf16[256,512]{1,0:T(8,128)(2,1)S(1)}, u32[]{:S(2)}, u32[]{:S(2)}) collective-permute-start(bf16[256,512]{1,0:T(8,128)(2,1)S(1)} %get-tuple-element.128.refs_0_), channel_id=1, source_target_pairs={{0,8},{4,12},{8,0},{12,4},{1,9},{5,13},{9,1},{13,5},{2,10},{6,14},... | collective-permute-start | bytes 786440 | tf_op jit(solution)/shard_map/ppermute | solution.py:27
  32.8 17.2 %copy-start.24 = (bf16[16,3,512]{2,0,1:T(8,128)(2,1)S(1)}, bf16[16,3,512]{2,0,1:T(8,128)(2,1)}, u32[]{:S(2)}) copy-start(bf16[16,3,512]{2,0,1:T(8,128)(2,1)} %param.32) | copy-start | bytes 147460
  32.8 17.3 %copy-start.27 = (f32[4,2,2,128]{3,2,1,0:T(2,128)S(1)}, f32[4,2,2,128]{3,2,1,0:T(2,128)}, u32[]{:S(2)}) copy-start(f32[4,2,2,128]{3,2,1,0:T(2,128)} %param.29) | copy-start | bytes 24580
  32.8 19.8 %copy-start.28 = (f32[2,2,128]{2,1,0:T(2,128)S(1)}, f32[2,2,128]{2,1,0:T(2,128)}, u32[]{:S(2)}) copy-start(f32[2,2,128]{2,1,0:T(2,128)} %param.31) | copy-start | bytes 6148
  32.8 19.9 %copy-start.25 = (f32[4,512]{1,0:T(4,128)S(1)}, f32[4,512]{1,0:T(4,128)}, u32[]{:S(2)}) copy-start(f32[4,512]{1,0:T(4,128)} %param.28) | copy-start | bytes 24580
  32.8 20.9 %copy-start.21 = (f32[1,2048]{1,0:T(1,128)S(1)}, f32[1,2048]{1,0:T(1,128)}, u32[]{:S(2)}) copy-start(f32[1,2048]{1,0:T(1,128)} %get-tuple-element.69.refs_7_) | copy-start | bytes 24580
  32.9 15.6 %collective-permute-start.5 = (bf16[256,512]{1,0:T(8,128)(2,1)S(1)}, bf16[256,512]{1,0:T(8,128)(2,1)S(1)}, u32[]{:S(2)}, u32[]{:S(2)}) collective-permute-start(bf16[256,512]{1,0:T(8,128)(2,1)S(1)} %get-tuple-element.127.refs_3_), channel_id=1, source_target_pairs={{0,4},{4,0},{8,12},{12,8},{1,5},{5,1},{9,13},{13,9},{2,6},{6,2},{1... | collective-permute-start | bytes 786440 | tf_op jit(solution)/shard_map/ppermute | solution.py:27
  47.0 14.6 %collective-permute-start.4 = (bf16[256,1024]{1,0:T(8,128)(2,1)}, bf16[256,1024]{1,0:T(8,128)(2,1)}, u32[]{:S(2)}, u32[]{:S(2)}) collective-permute-start(bf16[256,1024]{1,0:T(8,128)(2,1)} %pad_maximum_fusion), channel_id=1, source_target_pairs={{0,4},{4,0},{8,12},{12,8},{1,5},{5,1},{9,13},{13,9},{2,6},{6,2},{1... | collective-permute-start | bytes 1572872 | tf_op jit(solution)/shard_map/ppermute | solution.py:27
  49.4 12.2 %collective-permute-start.6 = (bf16[256,1024]{1,0:T(8,128)(2,1)}, bf16[256,1024]{1,0:T(8,128)(2,1)}, u32[]{:S(2)}, u32[]{:S(2)}) collective-permute-start(bf16[256,1024]{1,0:T(8,128)(2,1)} %pad_maximum_fusion.1), channel_id=1, source_target_pairs={{0,8},{4,12},{8,0},{12,4},{1,9},{5,13},{9,1},{13,5},{2,10},{6,14},... | collective-permute-start | bytes 1572872 | tf_op jit(solution)/shard_map/ppermute | solution.py:27
  53.7 2.6 %copy-start.19 = (bf16[2048,1408]{1,0:T(8,128)(2,1)S(1)}, bf16[2048,1408]{1,0:T(8,128)(2,1)}, u32[]{:S(2)}) copy-start(bf16[2048,1408]{1,0:T(8,128)(2,1)} %get-tuple-element.70.refs_8_) | copy-start | bytes 17301508
  56.4 5.2 %copy-start.20 = (bf16[2048,1408]{1,0:T(8,128)(2,1)S(1)}, bf16[2048,1408]{1,0:T(8,128)(2,1)}, u32[]{:S(2)}) copy-start(bf16[2048,1408]{1,0:T(8,128)(2,1)} %get-tuple-element.67.refs_8_) | copy-start | bytes 17301508
  56.4 5.2 %copy-start.22 = (f32[1,2048]{1,0:T(1,128)S(1)}, f32[1,2048]{1,0:T(1,128)}, u32[]{:S(2)}) copy-start(f32[1,2048]{1,0:T(1,128)} %get-tuple-element.66.refs_7_) | copy-start | bytes 24580
  61.6 6.7 %copy-start.26 = (f32[512]{0:T(512)S(1)}, f32[512]{0:T(512)}, u32[]{:S(2)}) copy-start(f32[512]{0:T(512)} %param.30) | copy-start | bytes 6148
  66.8 2.1 %collective-permute-start.11 = (bf16[16,768]{1,0:T(8,128)(2,1)S(1)}, bf16[16,768]{1,0:T(8,128)(2,1)S(1)}, u32[]{:S(2)}, u32[]{:S(2)}) collective-permute-start(bf16[16,768]{1,0:T(8,128)(2,1)S(1)} %slice.31), channel_id=1, source_target_pairs={{0,16},{1,17},{2,18},{3,19},{4,20},{5,21},{6,22},{7,23},{8,24},{9,... | collective-permute-start | bytes 73736 | tf_op jit(solution)/shard_map/ppermute | solution.py:23
  68.9 7.7 %copy-start.29 = (f32[8]{0:T(128)S(1)}, f32[8]{0:T(128)}, u32[]{:S(2)}) copy-start(f32[8]{0:T(128)} %param.37) | copy-start | bytes 100
  68.9 7.7 %copy-start.3 = (f32[16,8,64,128]{3,2,1,0:T(8,128)S(1)}, f32[16,8,64,128]{3,2,1,0:T(8,128)}, u32[]{:S(2)}) copy-start(f32[16,8,64,128]{3,2,1,0:T(8,128)} %param.34) | copy-start | bytes 12582916
  74.4 6.4 %collective-permute-start.12 = (f32[512,128]{1,0:T(8,128)S(1)}, f32[512,128]{1,0:T(8,128)S(1)}, u32[]{:S(2)}, u32[]{:S(2)}) collective-permute-start(f32[512,128]{1,0:T(8,128)S(1)} %get-tuple-element.88), channel_id=1, source_target_pairs={{0,16},{1,17},{2,18},{3,19},{4,20},{5,21},{6,22},{7,23},{8,24},{9,... | collective-permute-start | bytes 786440 | tf_op jit(solution)/shard_map/ppermute | solution.py:23
  76.7 4.1 %copy-start.18 = (f32[512]{0:T(512)S(1)}, f32[512]{0:T(512)}, u32[]{:S(2)}) copy-start(f32[512]{0:T(512)} %param.38) | copy-start | bytes 6148
  82.0 0.8 copy-start.5
  82.8 3.7 %copy-start.11 = (f32[8,512]{1,0:T(8,128)}, f32[8,512]{1,0:T(8,128)S(1)}, u32[]{:S(2)}) copy-start(f32[8,512]{1,0:T(8,128)S(1)} %get-tuple-element.91.own_ref) | copy-start | bytes 49156
  82.8 3.7 %collective-permute-start.13 = (f32[8,512]{1,0:T(8,128)S(1)}, f32[8,512]{1,0:T(8,128)S(1)}, u32[]{:S(2)}, u32[]{:S(2)}) collective-permute-start(f32[8,512]{1,0:T(8,128)S(1)} %get-tuple-element.91.own_ref), channel_id=1, source_target_pairs={{0,1},{1,0},{2,3},{3,2},{4,5},{5,4},{6,7},{7,6},{8,9},{9,8},{10,11... | collective-permute-start | bytes 49160 | tf_op jit(solution)/shard_map/ppermute | solution.py:27
  86.5 0.6 copy-start.13
  87.1 7.6 %copy-start.9 = (bf16[16,512]{1,0:T(8,128)(2,1)S(1)}, bf16[16,512]{1,0:T(8,128)(2,1)}, u32[]{:S(2)}) copy-start(bf16[16,512]{1,0:T(8,128)(2,1)} %copy-done.8) | copy-start | bytes 49156
  87.1 7.9 %copy-start.6 = (bf16[512,512]{1,0:T(8,128)(2,1)S(1)}, bf16[512,512]{1,0:T(8,128)(2,1)}, u32[]{:S(2)}) copy-start(bf16[512,512]{1,0:T(8,128)(2,1)} %copy-done.5) | copy-start | bytes 1572868
  87.1 7.9 %copy-start.15 = (s32[3]{0:T(128)S(1)}, s32[3]{0:T(128)}, u32[]{:S(2)}) copy-start(s32[3]{0:T(128)} %pad_add_fusion.place.blocks) | copy-start | bytes 40
  92.5 15.1 %collective-permute-start.19 = (bf16[256,1024]{1,0:T(8,128)(2,1)}, bf16[256,1024]{1,0:T(8,128)(2,1)S(1)}, u32[]{:S(2)}, u32[]{:S(2)}) collective-permute-start(bf16[256,1024]{1,0:T(8,128)(2,1)} %get-tuple-element.103), channel_id=1, source_target_pairs={{0,4},{4,0},{8,12},{12,8},{1,5},{5,1},{9,13},{13,9},{2,6},{6,2},{1... | collective-permute-start | bytes 1572872 | tf_op jit(solution)/shard_map/ppermute | solution.py:27
  93.0 15.5 %collective-permute-start.20 = (bf16[256,1024]{1,0:T(8,128)(2,1)}, bf16[256,1024]{1,0:T(8,128)(2,1)}, u32[]{:S(2)}, u32[]{:S(2)}) collective-permute-start(bf16[256,1024]{1,0:T(8,128)(2,1)} %get-tuple-element.105), channel_id=1, source_target_pairs={{0,8},{4,12},{8,0},{12,4},{1,9},{5,13},{9,1},{13,5},{2,10},{6,14},... | collective-permute-start | bytes 1572872 | tf_op jit(solution)/shard_map/ppermute | solution.py:27
  95.0 2.2 %copy-start.2 = (bf16[512,4096]{1,0:T(8,128)(2,1)S(1)}, bf16[512,4096]{1,0:T(8,128)(2,1)}, u32[]{:S(2)}) copy-start(bf16[512,4096]{1,0:T(8,128)(2,1)} %refs_7_.7) | copy-start | bytes 12582916
  97.2 0.7 copy-start.12
  97.9 0.7 copy-start.14
  98.7 8.9 %copy-start.10 = (f32[16,2048]{1,0:T(8,128)S(1)}, f32[16,2048]{1,0:T(8,128)}, u32[]{:S(2)}) copy-start(f32[16,2048]{1,0:T(8,128)} %get-tuple-element.117.refs_1_) | copy-start | bytes 393220
  98.7 9.9 %copy-start.16 = (f32[256,1024]{1,0:T(8,128)S(1)}, f32[256,1024]{1,0:T(8,128)}, u32[]{:S(2)}) copy-start(f32[256,1024]{1,0:T(8,128)} %get-tuple-element.102.upper_ref) | copy-start | bytes 3145732
  98.7 9.9 %copy-start.17 = (f32[256,1024]{1,0:T(8,128)S(1)}, f32[256,1024]{1,0:T(8,128)}, u32[]{:S(2)}) copy-start(f32[256,1024]{1,0:T(8,128)} %get-tuple-element.104.lower_ref) | copy-start | bytes 3145732
  101.1 17.7 %collective-permute-start.14 = (bf16[256,1024]{1,0:T(8,128)(2,1)S(1)}, bf16[256,1024]{1,0:T(8,128)(2,1)S(1)}, u32[]{:S(2)}, u32[]{:S(2)}) collective-permute-start(bf16[256,1024]{1,0:T(8,128)(2,1)S(1)} %get-tuple-element.93), channel_id=1, source_target_pairs={{0,4},{4,0},{8,12},{12,8},{1,5},{5,1},{9,13},{13,9},{2,6},{6,2},{1... | collective-permute-start | bytes 1572872 | tf_op jit(solution)/shard_map/ppermute | solution.py:27
  102.6 16.2 %collective-permute-start.15 = (bf16[256,1024]{1,0:T(8,128)(2,1)S(1)}, bf16[256,1024]{1,0:T(8,128)(2,1)S(1)}, u32[]{:S(2)}, u32[]{:S(2)}) collective-permute-start(bf16[256,1024]{1,0:T(8,128)(2,1)S(1)} %get-tuple-element.95), channel_id=1, source_target_pairs={{0,8},{4,12},{8,0},{12,4},{1,9},{5,13},{9,1},{13,5},{2,10},{6,14},... | collective-permute-start | bytes 1572872 | tf_op jit(solution)/shard_map/ppermute | solution.py:27
  108.2 6.3 %collective-permute-start.26 = (bf16[16,4096]{1,0:T(8,128)(2,1)S(1)}, bf16[16,4096]{1,0:T(8,128)(2,1)S(1)}, u32[]{:S(2)}, u32[]{:S(2)}) collective-permute-start(bf16[16,4096]{1,0:T(8,128)(2,1)S(1)} %convert_element_type.38), channel_id=1, source_target_pairs={{0,1},{1,0},{2,3},{3,2},{4,5},{5,4},{6,7},{7,6},{8,9},{9,8},{10,11... | collective-permute-start | bytes 393224 | tf_op jit(solution)/shard_map/ppermute | solution.py:27
  109.7 14.4 %collective-permute-start.21 = (bf16[256,512]{1,0:T(8,128)(2,1)S(1)}, bf16[256,512]{1,0:T(8,128)(2,1)S(1)}, u32[]{:S(2)}, u32[]{:S(2)}) collective-permute-start(bf16[256,512]{1,0:T(8,128)(2,1)S(1)} %get-tuple-element.107), channel_id=1, source_target_pairs={{0,8},{4,12},{8,0},{12,4},{1,9},{5,13},{9,1},{13,5},{2,10},{6,14},... | collective-permute-start | bytes 786440 | tf_op jit(solution)/shard_map/ppermute | solution.py:27
  111.3 13.1 %collective-permute-start.22 = (bf16[256,512]{1,0:T(8,128)(2,1)S(1)}, bf16[256,512]{1,0:T(8,128)(2,1)S(1)}, u32[]{:S(2)}, u32[]{:S(2)}) collective-permute-start(bf16[256,512]{1,0:T(8,128)(2,1)S(1)} %get-tuple-element.109), channel_id=1, source_target_pairs={{0,4},{4,0},{8,12},{12,8},{1,5},{5,1},{9,13},{13,9},{2,6},{6,2},{1... | collective-permute-start | bytes 786440 | tf_op jit(solution)/shard_map/ppermute | solution.py:27
  114.5 8.1 %collective-permute-start.27 = (bf16[16,4096]{1,0:T(8,128)(2,1)S(1)}, bf16[16,4096]{1,0:T(8,128)(2,1)S(1)}, u32[]{:S(2)}, u32[]{:S(2)}) collective-permute-start(bf16[16,4096]{1,0:T(8,128)(2,1)S(1)} %fusion.5), channel_id=1, source_target_pairs={{0,2},{1,3},{2,0},{3,1},{4,6},{5,7},{6,4},{7,5},{8,10},{9,11},{10,... | collective-permute-start | bytes 393224 | tf_op jit(solution)/shard_map/ppermute | solution.py:27
  119.0 11.1 %collective-permute-start.16 = (bf16[256,512]{1,0:T(8,128)(2,1)S(1)}, bf16[256,512]{1,0:T(8,128)(2,1)S(1)}, u32[]{:S(2)}, u32[]{:S(2)}) collective-permute-start(bf16[256,512]{1,0:T(8,128)(2,1)S(1)} %get-tuple-element.97), channel_id=1, source_target_pairs={{0,8},{4,12},{8,0},{12,4},{1,9},{5,13},{9,1},{13,5},{2,10},{6,14},... | collective-permute-start | bytes 786440 | tf_op jit(solution)/shard_map/ppermute | solution.py:27
  121.1 10.6 %collective-permute-start.17 = (bf16[256,512]{1,0:T(8,128)(2,1)S(1)}, bf16[256,512]{1,0:T(8,128)(2,1)S(1)}, u32[]{:S(2)}, u32[]{:S(2)}) collective-permute-start(bf16[256,512]{1,0:T(8,128)(2,1)S(1)} %get-tuple-element.99), channel_id=1, source_target_pairs={{0,4},{4,0},{8,12},{12,8},{1,5},{5,1},{9,13},{13,9},{2,6},{6,2},{1... | collective-permute-start | bytes 786440 | tf_op jit(solution)/shard_map/ppermute | solution.py:27
  122.7 7.4 %collective-permute-start.28 = (bf16[16,4096]{1,0:T(8,128)(2,1)S(1)}, bf16[16,4096]{1,0:T(8,128)(2,1)S(1)}, u32[]{:S(2)}, u32[]{:S(2)}) collective-permute-start(bf16[16,4096]{1,0:T(8,128)(2,1)S(1)} %fusion.11), channel_id=1, source_target_pairs={{0,4},{4,0},{8,12},{12,8},{1,5},{5,1},{9,13},{13,9},{2,6},{6,2},{1... | collective-permute-start | bytes 393224 | tf_op jit(solution)/shard_map/ppermute | solution.py:27
  124.4 2.8 %copy-start.4 = (f32[16,8,64,128]{3,2,1,0:T(8,128)S(1)}, f32[16,8,64,128]{3,2,1,0:T(8,128)}, u32[]{:S(2)}) copy-start(f32[16,8,64,128]{3,2,1,0:T(8,128)} %param.34) | copy-start | bytes 12582916
  124.5 18.2 %collective-permute-start.23 = (bf16[512,256]{1,0:T(8,128)(2,1)S(1)}, bf16[512,256]{1,0:T(8,128)(2,1)S(1)}, u32[]{:S(2)}, u32[]{:S(2)}) collective-permute-start(bf16[512,256]{1,0:T(8,128)(2,1)S(1)} %get-tuple-element.110), channel_id=1, source_target_pairs={{2,0},{3,1},{0,2},{1,3},{6,4},{7,5},{4,6},{5,7},{10,8},{11,9},{8,1... | collective-permute-start | bytes 786440 | tf_op jit(solution)/shard_map/ppermute | solution.py:32
  124.8 17.9 %collective-permute-start.24 = (bf16[512,256]{1,0:T(8,128)(2,1)S(1)}, bf16[512,256]{1,0:T(8,128)(2,1)S(1)}, u32[]{:S(2)}, u32[]{:S(2)}) collective-permute-start(bf16[512,256]{1,0:T(8,128)(2,1)S(1)} %get-tuple-element.111), channel_id=1, source_target_pairs={{1,0},{2,1},{3,2},{0,3},{5,4},{6,5},{7,6},{4,7},{9,8},{10,9},{11,1... | collective-permute-start | bytes 786440 | tf_op jit(solution)/shard_map/ppermute | solution.py:32
  130.0 6.1 %collective-permute-start.25 = (f32[8,512,128]{2,1,0:T(8,128)S(1)}, f32[8,512,128]{2,1,0:T(8,128)S(1)}, u32[]{:S(2)}, u32[]{:S(2)}) collective-permute-start(f32[8,512,128]{2,1,0:T(8,128)S(1)} %shard_map.236), channel_id=1, source_target_pairs={{0,16},{16,0},{1,17},{17,1},{2,18},{18,2},{3,19},{19,3},{4,20},{20... | collective-permute-start | bytes 6291464 | tf_op jit(solution)/shard_map/ppermute | solution.py:27
  130.1 6.0 %collective-permute-start.29 = (bf16[16,4096]{1,0:T(8,128)(2,1)S(1)}, bf16[16,4096]{1,0:T(8,128)(2,1)S(1)}, u32[]{:S(2)}, u32[]{:S(2)}) collective-permute-start(bf16[16,4096]{1,0:T(8,128)(2,1)S(1)} %fusion.6), channel_id=1, source_target_pairs={{0,8},{4,12},{8,0},{12,4},{1,9},{5,13},{9,1},{13,5},{2,10},{6,14},... | collective-permute-start | bytes 393224 | tf_op jit(solution)/shard_map/ppermute | solution.py:27
  131.8 10.9 %collective-permute-start.18 = (bf16[512,256]{1,0:T(8,128)(2,1)S(1)}, bf16[512,256]{1,0:T(8,128)(2,1)S(1)}, u32[]{:S(2)}, u32[]{:S(2)}) collective-permute-start(bf16[512,256]{1,0:T(8,128)(2,1)S(1)} %get-tuple-element.101), channel_id=1, source_target_pairs={{3,0},{0,1},{1,2},{2,3},{7,4},{4,5},{5,6},{6,7},{11,8},{8,9},{9,10... | collective-permute-start | bytes 786440 | tf_op jit(solution)/shard_map/ppermute | solution.py:32
  136.2 6.5 %copy-start.7 = (bf16[512,256]{1,0:T(8,128)(2,1)S(1)}, bf16[512,256]{1,0:T(8,128)(2,1)}, u32[]{:S(2)}) copy-start(bf16[512,256]{1,0:T(8,128)(2,1)} %tokens_ref.1) | copy-start | bytes 786436
  136.2 7.6 %slice-start = ((s8[8388608]{0:T(1024)(128)(4,1)}), s8[4194304]{0:T(1024)(128)(4,1)S(1)}, s32[]{:S(2)}) async-start(s8[8388608]{0:T(1024)(128)(4,1)} %bitcast.40), calls=%async_computation | async-start | bytes 8388608
  139.0 4.6 %collective-permute-start.30 = (f32[16,4096]{1,0:T(8,128)S(1)}, f32[16,4096]{1,0:T(8,128)S(1)}, u32[]{:S(2)}, u32[]{:S(2)}) collective-permute-start(f32[16,4096]{1,0:T(8,128)S(1)} %add_add_fusion), channel_id=1, source_target_pairs={{0,16},{16,0},{1,17},{17,1},{2,18},{18,2},{3,19},{19,3},{4,20},{20... | collective-permute-start | bytes 786440 | tf_op jit(solution)/shard_map/ppermute | solution.py:27
  142.7 2.3 %slice-start.1 = ((s8[8388608]{0:T(1024)(128)(4,1)}), s8[4194304]{0:T(1024)(128)(4,1)S(1)}, s32[]{:S(2)}) async-start(s8[8388608]{0:T(1024)(128)(4,1)} %bitcast.40), calls=%async_computation.1 | async-start | bytes 8388608
  142.7 2.3 %copy-start.23 = (f32[4096]{0:T(1024)S(1)}, f32[4096]{0:T(1024)}, u32[]{:S(2)}) copy-start(f32[4096]{0:T(1024)} %param.40) | copy-start | bytes 49156
  143.8 3.1 %copy-start.1 = (bf16[16,3,2,2,128]{4,3,2,1,0:T(2,128)(2,1)S(1)}, bf16[16,3,2,2,128]{4,3,2,1,0:T(2,128)(2,1)}, u32[]{:S(2)}) copy-start(bf16[16,3,2,2,128]{4,3,2,1,0:T(2,128)(2,1)} %param.33) | copy-start | bytes 147460

commit v3 on v2

--- a/solution.py
+++ b/solution.py
@@ -74,6 +74,12 @@
     upper_rest = from_partner(jnp.concatenate([upper, upper_far], axis=1), "row", 0)
     lower_rest = from_partner(jnp.concatenate([lower, lower_near], axis=1), "row", 1)
     return upper, upper_far, upper_rest, lower, lower_near, lower_rest
+
+
+def block_of(shifts, at, place, col_size):
+    gap = shifts[-1] - shifts[0] if len(shifts) > 1 else 0
+    shift = shifts[0] + (at % len(shifts)) * gap
+    return (place[0] ^ (at // len(shifts))) * col_size + (place[1] + shift) % col_size
 
 
 def setup_kernel(taps, counts, marks_ref, segment_ref, chooser_ref, slots_ref):
@@ -179,13 +185,13 @@
     out_ref[...] = init_ref[0].astype(BF16)
 
 
-def project_kernel(first, inner, model_width, unused, *refs):
+def project_kernel(first, last, inner, model_width, unused, *refs):
     del unused
     pieces, refs = refs[:6], refs[6:]
     chooser_ref, gain_ref, weights_ref, refs = refs[0], refs[1], refs[2], refs[3:]
     if not first:
         total_in, squares_in, refs = refs[0], refs[1], refs[2:]
-    if first:
+    if not last:
         ends_ref, total_ref, squares_ref = refs
     else:
         ends_ref, gate_ref, channels_ref, steps_ref, total_ref, squares_ref = refs
@@ -217,7 +223,7 @@
     def _():
         top = jnp.concatenate([upper_far[...], upper_rest[:, width:]], axis=1)
         add(jnp.concatenate([top, lower_rest[...]], axis=0), False)
-        if first:
+        if not last:
             return
         inv_rms = jnp.sum(squares_ref[...], axis=1, keepdims=True) / model_width
         inv_rms = lax.rsqrt(inv_rms + EPSILON)
@@ -401,14 +407,17 @@
     return jnp.broadcast_to(scale, (LANES, scale.shape[1])).T
 
 
-def out_kernel(width, count, blocks, gated_ref, own_ref, other_ref, chooser_ref, *refs):
+def out_kernel(width, count, scaled, blocks, gated_ref, own_ref, other_ref, chooser_ref, *refs):
     del blocks
     weights, outs = refs[: 4 * count], refs[4 * count :]
     upper_out, upper_in, lower_out, lower_in, ends_ref = outs
     rows, inner = gated_ref.shape
     half = rows // 2
-    scale = norm_scale(own_ref, other_ref, 2 * inner)
-    scale = jnp.concatenate([scale] * (width // LANES), axis=1)
+    if scaled:
+        scale = norm_scale(own_ref, other_ref, 2 * inner)
+        scale = jnp.concatenate([scale] * (width // LANES), axis=1)
+    else:
+        scale = jnp.ones((rows, width), F32)
     gated = gated_ref[...]
     end_rows = jnp.dot(chooser_ref[...], gated, preferred_element_type=F32).astype(BF16)
     end_scale = jnp.dot(
@@ -419,15 +428,11 @@
         part = jnp.dot(gated, w[...], preferred_element_type=F32) * scale
         top, bottom = part[:half], part[half:]
         low = (index // 2) * count + place
-        if index % 2:
-            upper_out[:, low * width : (low + 1) * width] = top.astype(BF16)
-        else:
-            upper_in[:, low * width : (low + 1) * width] = top
+        target = upper_out if index % 2 else upper_in
+        target[:, low * width : (low + 1) * width] = top.astype(target.dtype)
         low = (index % 2) * count + place
-        if index // 2:
-            lower_out[:, low * width : (low + 1) * width] = bottom.astype(BF16)
-        else:
-            lower_in[:, low * width : (low + 1) * width] = bottom
+        target = lower_out if index // 2 else lower_in
+        target[:, low * width : (low + 1) * width] = bottom.astype(target.dtype)
         ends_ref[:, at * width : (at + 1) * width] = (
             jnp.dot(end_rows, w[...], preferred_element_type=F32) * end_scale
         )
@@ -440,8 +445,8 @@
         (lower_ref, lower_got, outs[2], outs[3]),
     ):
         wide = keep_ref.shape[1]
-        keep_ref[...] = kept[:, :wide] + got[:, :wide].astype(F32)
-        send_ref[...] = (kept[:, wide:] + got[:, wide:].astype(F32)).astype(BF16)
+        keep_ref[...] = kept[:, :wide].astype(F32) + got[:, :wide].astype(F32)
+        send_ref[...] = (kept[:, wide:].astype(F32) + got[:, wide:].astype(F32)).astype(BF16)
 
 
 def plane_kernel(unused, upper_ref, upper_got, lower_ref, lower_got, *outs):
@@ -463,15 +468,30 @@
     refs[-1][...] = (tokens_ref[...].astype(F32) + total).astype(BF16)
 
 
-def ends_kernel(width, block_of, place, *refs):
-    sources, outs = refs[:4], refs[4:]
-    half = sources[0].shape[1] // width
-    for at in range(2 * half):
-        which, low = divmod(at, half)
-        block = block_of(which, low, place)
-        to = pl.ds(pl.multiple_of(block * width, width), width)
-        outs[0][:, to] = sources[which][:, low * width : (low + 1) * width]
-        outs[1][:, to] = sources[2 + which][:, low * width : (low + 1) * width]
+def scale_kernel(unused, own_ref, other_ref, chooser_ref, channels_ref, *refs):
+    del unused
+    raw, outs = refs[:5], refs[5:]
+    half = raw[0].shape[0]
+    scale = norm_scale(own_ref, other_ref, 2 * channels_ref.shape[1])
+    end_scale = jnp.dot(
+        chooser_ref[...].astype(F32), scale, precision=HIGHEST, preferred_element_type=F32
+    )
+    for at, (source, out_ref) in enumerate(zip(raw, outs)):
+        factor = end_scale if at == 4 else scale[:half] if at < 2 else scale[half:]
+        for lane in range(0, source.shape[1], LANES):
+            value = source[:, lane : lane + LANES] * factor
+            out_ref[:, lane : lane + LANES] = value.astype(out_ref.dtype)
+
+
+def ends_kernel(width, col_size, sum_groups, gather_groups, place, *refs):
+    sources, outs = refs[:-2], refs[-2:]
+    groups = [(shifts, outs[0]) for shifts in sum_groups]
+    groups += [(shifts, outs[1]) for shifts in gather_groups]
+    for source, (shifts, out_ref) in zip(sources, groups):
+        for at in range(source.shape[1] // width):
+            block = block_of(shifts, at, place, col_size)
+            to = pl.ds(pl.multiple_of(block * width, width), width)
+            out_ref[:, to] = source[:, at * width : (at + 1) * width]
 
 
 def finals_kernel(
@@ -559,12 +579,8 @@
     skip_row = in_lanes(skip)
     gains = pre_gain[None, :]
 
-    near, far = tuple(range(col_size // 2)), tuple(range(col_size // 2, col_size))
-
-    def block_of(shifts, at, place):
-        shifts = (near, far)[shifts] if isinstance(shifts, int) else shifts
-        index, shift = at // len(shifts), at % len(shifts) + shifts[0]
-        return (place[0] ^ index) * col_size + (place[1] + shift) % col_size
+    gather_groups = ((0,1),(2,3))
+    sum_groups = ((2,3),(0,1))
 
     n_all = 2 * inner + 2 * state + LANES
     steps_across = jnp.transpose(w_step)
@@ -575,7 +591,9 @@
 
         def specs(shape, where):
             return [
-                pl.BlockSpec(shape, lambda i, p, at=at: where(block_of(shifts, i * parts + at, p)))
+                pl.BlockSpec(shape, lambda i, p, at=at: where(
+                    block_of(shifts, i * parts + at, p, col_size)
+                ))
                 for at in range(parts)
             ]
 
@@ -600,30 +618,31 @@
         )
 
     gain_row = pre_gain[None, :]
-    token_blocks = [tokens, from_ahead(tokens, "col", 1)]
-    later = after(tokens, token_blocks[1])
-    token_blocks += [from_ahead(later, "col", shift) for shift in range(2, col_size)]
-    near_weights = weights_of(near, after(gain_row, token_blocks[1]))
+    token_blocks = {0: tokens}
+    token_blocks[1] = from_ahead(tokens, "col", 1)
+    later, token_blocks[1] = lax.optimization_barrier((tokens, token_blocks[1]))
+    for shift in range(2, col_size):
+        source = token_blocks[1] if shift == 2 else later
+        token_blocks[shift] = from_ahead(source, "col", 1 if shift == 2 else shift)
+    gain_row = after(gain_row, token_blocks[1])
     token_ends = []
     carry = ()
-    for shifts in (near, far):
-        first = shifts is near
+    ready = ()
+    for shifts in gather_groups:
+        first, last = shifts == gather_groups[0], shifts == gather_groups[-1]
         pieces = plane_gather(jnp.concatenate([token_blocks[i] for i in shifts], axis=1))
-        if first:
-            far_weights = weights_of(far, after(gain_row, pieces[1]))
-        else:
-            ready = pieces[1]
-        weights, gains = near_weights if first else far_weights
+        weights, gains = weights_of(shifts, after(gain_row, *ready) if ready else gain_row)
+        ready = (pieces[1],)
         count = row_size * len(shifts)
         depth = count * width // 2
         outs = [((requests, count * width), F32)]
         totals = [((rows, n_all), F32), ((rows, LANES), F32)]
-        if first:
+        if not last:
             outs += totals
         else:
             outs += [((rows, inner), BF16), ((rows, inner + 2 * state), BF16), ((rows, LANES), F32)]
         piece_ends, *carry = call(
-            functools.partial(project_kernel, first, inner, model_width),
+            functools.partial(project_kernel, first, last, inner, model_width),
             outs,
             *pieces,
             chooser,
@@ -639,11 +658,12 @@
             + [None] * len(carry),
             out_specs=[pl.BlockSpec((requests, depth), lambda i, _: (0, i))]
             + [None] * (len(outs) - 1),
-            scratch=[] if first else totals,
+            scratch=totals if last else [],
             vmem=24,
         )
         token_ends.append(piece_ends)
     gate_in, channels, step_raw = carry
+    ready = gains
 
     init_last = lax.dynamic_index_in_dim(init_flat, after(marks, ready)[rows - 1, 6], 0, keepdims=False)
     (table,) = call(
@@ -689,7 +709,7 @@
         step_raw,
         in_lanes(step_bias),
         in_lanes(decay_log),
-        marks,
+        after(marks, table),
         segment_row,
         init_last,
     )
@@ -741,46 +761,53 @@
     )
     other_squares = from_partner(own_squares, "col", 0)
 
-    half_out = []
-    for shifts in (far, near):
+    half_out, got = [], []
+    for shifts in sum_groups:
         count = len(shifts)
+        first = shifts == sum_groups[0]
         side = (rows // 2, 2 * count * width)
-        half_out.append(
-            call(
-                functools.partial(out_kernel, width, count),
-                [
-                    (side, BF16),
-                    (side, F32),
-                    (side, BF16),
-                    (side, F32),
-                    ((requests, row_size * count * width), F32),
-                ],
-                gated,
+        kinds = [BF16] * 4
+        ends_out = ((requests, row_size * count * width), F32)
+        outs = call(
+            functools.partial(out_kernel, width, count, not first),
+            [(side, F32 if first else kind) for kind in kinds] + [ends_out],
+            gated,
+            own_squares,
+            own_squares if first else other_squares,
+            chooser,
+            *[w_out] * (row_size * count),
+            prefetch=place,
+            in_specs=[None] * 4
+            + [
+                pl.BlockSpec(
+                    (inner, width),
+                    lambda i, p, at=at, shifts=shifts: (0, block_of(shifts, at, p, col_size)),
+                )
+                for at in range(row_size * count)
+            ],
+            vmem=16,
+            work=10 if first else 0,
+        )
+        if first:
+            other_squares = after(other_squares, outs[0])
+            outs = call(
+                scale_kernel,
+                [(side, kind) for kind in kinds] + [ends_out],
                 own_squares,
                 other_squares,
                 chooser,
-                *[w_out] * (row_size * count),
-                prefetch=place,
-                in_specs=[None] * 4
-                + [
-                    pl.BlockSpec(
-                        (inner, width),
-                        lambda i, p, at=at, shifts=shifts: (0, block_of(shifts, at, p)),
-                    )
-                    for at in range(row_size * count)
-                ],
-                vmem=56 if shifts is far else 16,
+                gated,
+                *outs,
+                vmem=12,
                 work=0,
             )
-        )
-    got = []
-    for upper_out, _, lower_out, _, _ in half_out:
-        got.append((from_partner(upper_out, "row", 0), from_partner(lower_out, "row", 1)))
+        half_out.append(outs)
+        got.append((from_partner(outs[0], "row", 0), from_partner(outs[2], "row", 1)))
     end_sum, end_tokens = call(
-        functools.partial(ends_kernel, width, block_of),
+        functools.partial(ends_kernel, width, col_size, sum_groups, gather_groups),
         [((requests, model_width), F32)] * 2,
-        after(half_out[1][4], got[0][0]),
-        half_out[0][4],
+        after(half_out[0][4], *got[0]),
+        *[outs[4] for outs in half_out[1:]],
         *token_ends,
         prefetch=place,
         vmem=4,
@@ -840,7 +867,7 @@
         return finals
 
     pieces = {}
-    for shifts, outs, (upper_got, lower_got) in zip((far, near), half_out, got):
+    for shifts, outs, (upper_got, lower_got) in zip(sum_groups, half_out, got):
         _, upper_in, _, lower_in, _ = outs
         wide = len(shifts) * width
         upper, upper_far, lower, lower_near = call(
@@ -865,7 +892,7 @@
             vmem=8,
             work=10,
         )
-        if shifts is far:
+        if shifts == sum_groups[-2]:
             far_ready = sums
         for shift, part in zip(shifts, sums):
             pieces[shift] = from_ahead(part, "col", col_size - shift) if shift else part

time: 148 us -> 142 us (0.959)
  waiting for transfers between devices: 32.6 us -> 28.7 us
  Pallas kernels: 51.7 us -> 48.9 us
  local copies, waits for them, and re-layouts: 12.8 us -> 14.3 us
  other arithmetic: 5.25 us -> 3.76 us
    pallas_call x18 -> x19, Pallas kernels: 48.5 us -> 45.8 us  [call(): pl.pallas_call(kernel, out_shape=shapes, grid_spec=spec, compiler_params=...]
    ppermute x23, waiting for transfers between devices: 25 us -> 22.8 us  [from_partner(): lax.ppermute(x, axis, [(i, i ^ 1 << bit) for i in range(lax.axis_size(axi...]
    unnamed x68 -> x52, local copies, waits for them, and re-layouts: 9.98 us -> 11.5 us
  transfers between devices with their start and end apart: 31 -> 31, of which waited for: 13 -> 15; matrix products, arithmetic and copies ran while one was open for 6% -> 5% of each run, Pallas kernels for 24% -> 26%
where the time goes in v3:
time: 142 us; the launch traced here: 141 us
  Pallas kernels  48.9 us (34%)
  starting transfers between devices  39.9 us (28%)
  waiting for transfers between devices  28.7 us (20%)
  local copies, waits for them, and re-layouts  14.3 us (10%)
  other arithmetic  3.76 us (3%)
  between operations  2.84 us (2%)
  matrix products  2.08 us (1%)
    pallas_call x19, Pallas kernels, call(): pl.pallas_call(kernel, out_shape=shapes, grid_spec=spec, compiler_params=...  45.8 us
    ppermute x23, waiting for transfers between devices, from_partner(): lax.ppermute(x, axis, [(i, i ^ 1 << bit) for i in range(lax.axis_size(axi...  22.8 us
    ppermute x23, starting transfers between devices, from_partner(): lax.ppermute(x, axis, [(i, i ^ 1 << bit) for i in range(lax.axis_size(axi...  22.1 us
    ppermute x6, starting transfers between devices, from_ahead(): lax.ppermute(x, axis, [((i + distance) % size, i) for i in range(size)])  14.3 us
    unnamed x52, local copies, waits for them, and re-layouts  11.5 us
    ppermute x6, waiting for transfers between devices, from_ahead(): lax.ppermute(x, axis, [((i + distance) % size, i) for i in range(size)])  5.88 us
    ppermute x2, starting transfers between devices, from_behind(): return lax.ppermute(block, axis, route)  3.53 us
    pallas_call x1, Pallas kernels, per_device(): pl.pallas_call(functools.partial(scan_kernel, heads, block), out_shape=ja...  3.18 us
  transfers between devices with their start and end apart: 31, of which 15 were waited for; matrix products, arithmetic and copies ran while one was open for 5% of the time, Pallas kernels for 26%

profile of v3, /device:TPU:0, one launch (start us, length us, event | category | flops | bytes accessed | tf_op | source)
XLA Modules:
  0.0 140.5 jit_solution(12890049857980179688)
XLA Ops:
  0.6 5.1 %collective-permute-start = (bf16[512,256]{1,0:T(8,128)(2,1)}, bf16[512,256]{1,0:T(8,128)(2,1)S(1)}, u32[]{:S(2)}, u32[]{:S(2)}) collective-permute-start(bf16[512,256]{1,0:T(8,128)(2,1)} %tokens_ref.1), channel_id=1, source_target_pairs={{1,0},{2,1},{3,2},{0,3},{5,4},{6,5},{7,6},{4,7},{9,8},{10,9},{11,1... | collective-permute-start | bytes 786440 | tf_op jit(solution)/shard_map/ppermute | solution.py:32
  6.4 0.7 pad_add_fusion.1.counts
  7.1 1.4 %shard_map.220 = (s32[512,128]{1,0:T(8,128)S(1)}, s32[8,512]{1,0:T(8,128)S(1)}, bf16[16,512]{1,0:T(8,128)(2,1)S(1)}, f32[16,256]{1,0:T(8,128)S(1)}) custom-call(s32[33]{0:T(128)S(1)} %pad_add_fusion.1.counts), custom_call_target="tpu_custom_call" | custom-call | bytes 1000 | tf_op jit(solution)/shard_map/pallas_call | solution.py:60
  8.5 0.7 pad_bitcast_fusion.1
  9.2 1.0 constant_dynamic-update-slice_fusion.3
  10.2 1.4 %collective-permute-done = bf16[512,256]{1,0:T(8,128)(2,1)S(1)} collective-permute-done((bf16[512,256]{1,0:T(8,128)(2,1)}, bf16[512,256]{1,0:T(8,128)(2,1)S(1)}, u32[]{:S(2)}, u32[]{:S(2)}) %collective-permute-start) | collective-permute-done | bytes 262176 | tf_op jit(solution)/shard_map/ppermute | solution.py:32
  11.6 4.2 %collective-permute-start.1 = (bf16[512,256]{1,0:T(8,128)(2,1)S(1)}, bf16[512,256]{1,0:T(8,128)(2,1)S(1)}, u32[]{:S(2)}, u32[]{:S(2)}) collective-permute-start(bf16[512,256]{1,0:T(8,128)(2,1)S(1)} %collective-permute-done), channel_id=1, source_target_pairs={{1,0},{2,1},{3,2},{0,3},{5,4},{6,5},{7,6},{4,7},{9,8},{10,9},{11,1... | collective-permute-start | bytes 786440 | tf_op jit(solution)/shard_map/ppermute | solution.py:32
  15.9 1.6 %collective-permute-start.7 = (bf16[256,512]{1,0:T(8,128)(2,1)S(1)}, bf16[256,512]{1,0:T(8,128)(2,1)S(1)}, u32[]{:S(2)}, u32[]{:S(2)}) collective-permute-start(bf16[256,512]{1,0:T(8,128)(2,1)S(1)} %get-tuple-element.142.refs_0_), channel_id=1, source_target_pairs={{0,8},{4,12},{8,0},{12,4},{1,9},{5,13},{9,1},{13,5},{2,10},{6,14},... | collective-permute-start | bytes 786440 | tf_op jit(solution)/shard_map/ppermute | solution.py:27
  17.5 1.5 %collective-permute-start.9 = (bf16[256,512]{1,0:T(8,128)(2,1)S(1)}, bf16[256,512]{1,0:T(8,128)(2,1)S(1)}, u32[]{:S(2)}, u32[]{:S(2)}) collective-permute-start(bf16[256,512]{1,0:T(8,128)(2,1)S(1)} %get-tuple-element.141.refs_3_), channel_id=1, source_target_pairs={{0,4},{4,0},{8,12},{12,8},{1,5},{5,1},{9,13},{13,9},{2,6},{6,2},{1... | collective-permute-start | bytes 786440 | tf_op jit(solution)/shard_map/ppermute | solution.py:27
  18.9 7.1 %shard_map.222 = (bf16[2048,1408]{1,0:T(8,128)(2,1)}, f32[1,2048]{1,0:T(1,128)}) custom-call(s32[3]{0:T(128)} %pad_add_fusion.place.blocks, bf16[4096,2,512]{2,1,0:T(2,128)(2,1)} %refs_3_.5, bf16[4096,2,512]{2,1,0:T(2,128)(2,1)} %refs_3_.5, bf16[4096,2,512]{2,1,0:T(2,128)(2,1)} %refs_3_.5, bf16[4096,2,512]{2,1,0:T(2,128)(2,1)} %refs_3_.5, ...), custom_call_target="tpu_custom_call" | custom-call | flops 20000000000 | bytes 100000000 | tf_op jit(solution)/shard_map/pallas_call | solution.py:60
  26.1 0.9 pad_maximum_fusion.2
  27.5 0.9 pad_maximum_fusion.3
  29.0 7.1 %shard_map.221 = (bf16[2048,1408]{1,0:T(8,128)(2,1)}, f32[1,2048]{1,0:T(1,128)}) custom-call(s32[3]{0:T(128)} %pad_add_fusion.place.blocks, bf16[4096,2,512]{2,1,0:T(2,128)(2,1)} %refs_3_.5, bf16[4096,2,512]{2,1,0:T(2,128)(2,1)} %refs_3_.5, bf16[4096,2,512]{2,1,0:T(2,128)(2,1)} %refs_3_.5, bf16[4096,2,512]{2,1,0:T(2,128)(2,1)} %refs_3_.5, ...), custom_call_target="tpu_custom_call" | custom-call | flops 20000000000 | bytes 100000000 | tf_op jit(solution)/shard_map/pallas_call | solution.py:60
  36.2 1.5 %collective-permute-start.5 = (bf16[256,512]{1,0:T(8,128)(2,1)S(1)}, bf16[256,512]{1,0:T(8,128)(2,1)S(1)}, u32[]{:S(2)}, u32[]{:S(2)}) collective-permute-start(bf16[256,512]{1,0:T(8,128)(2,1)S(1)} %get-tuple-element.143.refs_3_), channel_id=1, source_target_pairs={{0,4},{4,0},{8,12},{12,8},{1,5},{5,1},{9,13},{13,9},{2,6},{6,2},{1... | collective-permute-start | bytes 786440 | tf_op jit(solution)/shard_map/ppermute | solution.py:27
  37.7 1.5 %collective-permute-start.3 = (bf16[256,512]{1,0:T(8,128)(2,1)S(1)}, bf16[256,512]{1,0:T(8,128)(2,1)S(1)}, u32[]{:S(2)}, u32[]{:S(2)}) collective-permute-start(bf16[256,512]{1,0:T(8,128)(2,1)S(1)} %get-tuple-element.144.refs_0_), channel_id=1, source_target_pairs={{0,8},{4,12},{8,0},{12,4},{1,9},{5,13},{9,1},{13,5},{2,10},{6,14},... | collective-permute-start | bytes 786440 | tf_op jit(solution)/shard_map/ppermute | solution.py:27
  41.8 1.0 dynamic-slice_bitcast_fusion.init_ref
  42.8 1.9 %collective-permute-done.5.refs_4_ = bf16[256,512]{1,0:T(8,128)(2,1)S(1)} collective-permute-done((bf16[256,512]{1,0:T(8,128)(2,1)S(1)}, bf16[256,512]{1,0:T(8,128)(2,1)S(1)}, u32[]{:S(2)}, u32[]{:S(2)}) %collective-permute-start.5) | collective-permute-done | bytes 262176 | tf_op jit(solution)/shard_map/ppermute | solution.py:27
  45.4 1.5 %collective-permute-done.3.refs_1_ = bf16[256,512]{1,0:T(8,128)(2,1)S(1)} collective-permute-done((bf16[256,512]{1,0:T(8,128)(2,1)S(1)}, bf16[256,512]{1,0:T(8,128)(2,1)S(1)}, u32[]{:S(2)}, u32[]{:S(2)}) %collective-permute-start.3) | collective-permute-done | bytes 262176 | tf_op jit(solution)/shard_map/ppermute | solution.py:27
  46.9 1.6 %collective-permute-start.4 = (bf16[256,1024]{1,0:T(8,128)(2,1)S(1)}, bf16[256,1024]{1,0:T(8,128)(2,1)S(1)}, u32[]{:S(2)}, u32[]{:S(2)}) collective-permute-start(bf16[256,1024]{1,0:T(8,128)(2,1)S(1)} %pad_maximum_fusion), channel_id=1, source_target_pairs={{0,4},{4,0},{8,12},{12,8},{1,5},{5,1},{9,13},{13,9},{2,6},{6,2},{1... | collective-permute-start | bytes 1572872 | tf_op jit(solution)/shard_map/ppermute | solution.py:27
  48.5 2.6 %copy-done.11 = bf16[2048,1408]{1,0:T(8,128)(2,1)S(1)} copy-done((bf16[2048,1408]{1,0:T(8,128)(2,1)S(1)}, bf16[2048,1408]{1,0:T(8,128)(2,1)}, u32[]{:S(2)}) %copy-start.11) | copy-done | bytes 5767192
  51.1 5.0 %shard_map.223 = (f32[16,2048]{1,0:T(8,128)S(1)}, f32[512,1408]{1,0:T(8,128)S(1)}, f32[512,128]{1,0:T(8,128)S(1)}) custom-call(s32[1]{0:T(128)} %constant.31.clone.1.unused, bf16[256,512]{1,0:T(8,128)(2,1)S(1)} %get-tuple-element.142.refs_0_, bf16[256,512]{1,0:T(8,128)(2,1)S(1)} %collective-permute-done.7.refs_1_, ...), custom_call_target="tpu_custom_call" | custom-call | flops 20000000000 | bytes 100000000 | tf_op jit(solution)/shard_map/pallas_call | solution.py:60
  56.1 1.1 collective-permute-done.6.refs_5_
  57.4 2.6 %copy-done.12 = bf16[2048,1408]{1,0:T(8,128)(2,1)S(1)} copy-done((bf16[2048,1408]{1,0:T(8,128)(2,1)S(1)}, bf16[2048,1408]{1,0:T(8,128)(2,1)}, u32[]{:S(2)}) %copy-start.12) | copy-done | bytes 5767192
  60.0 3.9 %shard_map.224 = (f32[16,2048]{1,0:T(8,128)S(1)}, bf16[512,512]{1,0:T(8,128)(2,1)S(1)}, bf16[512,768]{1,0:T(8,128)(2,1)S(1)}, f32[512,128]{1,0:T(8,128)S(1)}) custom-call(s32[1]{0:T(128)} %constant.31.clone.1.unused, bf16[256,512]{1,0:T(8,128)(2,1)S(1)} %get-tuple-element.144.refs_0_, bf16[256,512]{1,0:T(8,128)(2,1)S(1)} %collective-permute-done.3.refs_1_, ...), custom_call_target="tpu_custom_call" | custom-call | flops 20000000000 | bytes 100000000 | tf_op jit(solution)/shard_map/pallas_call | solution.py:60
  64.0 1.5 %collective-permute-start.11 = (bf16[16,768]{1,0:T(8,128)(2,1)S(1)}, bf16[16,768]{1,0:T(8,128)(2,1)S(1)}, u32[]{:S(2)}, u32[]{:S(2)}) collective-permute-start(bf16[16,768]{1,0:T(8,128)(2,1)S(1)} %slice.31), channel_id=1, source_target_pairs={{0,16},{1,17},{2,18},{3,19},{4,20},{5,21},{6,22},{7,23},{8,24},{9,... | collective-permute-start | bytes 73736 | tf_op jit(solution)/shard_map/ppermute | solution.py:23
  65.5 0.9 shard_map.225.table_ref
  66.4 5.5 %shard_map.226 = (bf16[512,512]{1,0:T(8,128)(2,1)S(1)}, bf16[512,128]{1,0:T(8,128)(2,1)S(1)}, bf16[512,128]{1,0:T(8,128)(2,1)S(1)}, f32[512,128]{1,0:T(8,128)S(1...) custom-call(s32[1]{0:T(128)} %constant.31.clone.1.unused, ...), custom_call_target="tpu_custom_call" | custom-call | flops 20000000000 | bytes 100000000 | tf_op jit(solution)/shard_map/pallas_call | solution.py:60
  71.9 2.1 %collective-permute-start.12 = (f32[512,128]{1,0:T(8,128)S(1)}, f32[512,128]{1,0:T(8,128)S(1)}, u32[]{:S(2)}, u32[]{:S(2)}) collective-permute-start(f32[512,128]{1,0:T(8,128)S(1)} %get-tuple-element.98), channel_id=1, source_target_pairs={{0,16},{1,17},{2,18},{3,19},{4,20},{5,21},{6,22},{7,23},{8,24},{9,... | collective-permute-start | bytes 786440 | tf_op jit(solution)/shard_map/ppermute | solution.py:23
  74.0 3.2 %shard_map.227.y_ref = f32[512,512]{1,0:T(8,128)S(1)} custom-call(s32[1]{0:T(128)} %constant.31.clone.1.unused, bf16[512,512]{1,0:T(8,128)(2,1)S(1)} %get-tuple-element.93.x_ref, bf16[512,128]{1,0:T(8,128)(2,1)S(1)} %get-tuple-element.94.keys_ref, bf16[512,128]{1,0:T(8,128)(2,1)S(1)} %get-tuple-element.95.queries_ref, ...), custom_call_target="tpu_custom_call" | custom-call | tf_op jit(solution)/shard_map/pallas_call | solution.py:722
  77.2 1.2 shard_map.228
  78.4 0.9 copy-done.2
  79.4 2.3 %shard_map.229 = (f32[256,1024]{1,0:T(8,128)S(1)}, f32[256,1024]{1,0:T(8,128)S(1)}, f32[256,1024]{1,0:T(8,128)S(1)}, f32[256,1024]{1,0:T(8,128)S(1)}, f32[16,2048]{1,0:T(8,128)S(1)}) custom-call(s32[3]{0:T(128)S(1)} %copy-done.7, bf16[512,512]{1,0:T(8,128)(2,1)S(1)} %get-tuple-element.100.gated_ref.channels_ref, ...), custom_call_target="tpu_custom_call" | custom-call | flops 10000000000 | bytes 100000000 | tf_op jit(solution)/shard_map/pallas_call | solution.py:60
  82.2 1.4 %shard_map.233 = (bf16[256,1024]{1,0:T(8,128)(2,1)}, bf16[256,1024]{1,0:T(8,128)(2,1)S(1)}, bf16[256,1024]{1,0:T(8,128)(2,1)}, bf16[256,1024]{1,0:T(8,128)(2,1)S(1)}, f32[16,2048]{1,0:T(8,128)S(1)}) custom-call(s32[1]{0:T(128)} %constant.31.clone.1.unused, f32[8,512]{1,0:T(8,128)S(1)} %get-tuple-element.101.own_ref.other_ref, ...), custom_call_target="tpu_custom_call" | custom-call | bytes 1000 | tf_op jit(solution)/shard_map/pallas_call | solution.py:60
  83.6 0.8 copy-done.8
  84.4 1.3 collective-permute-start.19
  85.7 0.9 collective-permute-start.20
  87.1 2.2 %copy-done.3 = bf16[512,4096]{1,0:T(8,128)(2,1)S(1)} copy-done((bf16[512,4096]{1,0:T(8,128)(2,1)S(1)}, bf16[512,4096]{1,0:T(8,128)(2,1)}, u32[]{:S(2)}) %copy-start.3) | copy-done | bytes 4194328
  89.3 2.4 %shard_map.230 = (bf16[256,1024]{1,0:T(8,128)(2,1)S(1)}, bf16[256,1024]{1,0:T(8,128)(2,1)S(1)}, bf16[256,1024]{1,0:T(8,128)(2,1)S(1)}, bf16[256,1024]{1,0:T(8,128)(2,1)S(1)}, f32[16,2048]{1,0:T(8,128)S(1)}) custom-call(s32[3]{0:T(128)S(1)} %copy-done.7, bf16[512,512]{1,0:T(8,128)(2,1)S(1)} %get-tuple-element.100.gated_ref.channels_ref, ...), custom_call_target="tpu_custom_call" | custom-call | bytes 1000 | tf_op jit(solution)/shard_map/pallas_call | solution.py:60
  91.7 1.0 collective-permute-start.14
  92.7 0.9 collective-permute-start.15
  93.6 6.0 %collective-permute-done.19.upper_got = bf16[256,1024]{1,0:T(8,128)(2,1)} collective-permute-done((bf16[256,1024]{1,0:T(8,128)(2,1)}, bf16[256,1024]{1,0:T(8,128)(2,1)}, u32[]{:S(2)}, u32[]{:S(2)}) %collective-permute-start.19) | collective-permute-done | bytes 524320 | tf_op jit(solution)/shard_map/ppermute | solution.py:27
  99.6 1.3 collective-permute-done.20.lower_got
  102.2 1.4 %shard_map.234 = (f32[256,512]{1,0:T(8,128)S(1)}, bf16[256,512]{1,0:T(8,128)(2,1)S(1)}, f32[256,512]{1,0:T(8,128)S(1)}, bf16[256,512]{1,0:T(8,128)(2,1)S(1)}) custom-call(s32[1]{0:T(128)} %constant.31.clone.1.unused, bf16[256,1024]{1,0:T(8,128)(2,1)S(1)} %get-tuple-element.118.upper_ref, bf16[256,1024]{1,0:T(8,128)(2,1)} %collective-permute-done.19.upper_got, ...), custom_call_target="tpu_custom_call" | custom-call | flops 10000000000 | bytes 100000000 | tf_op jit(solution)/shard_map/pallas_call | solution.py:60
  103.6 1.0 collective-permute-start.21
  104.6 0.9 collective-permute-start.22
  105.5 1.5 %collective-permute-done.26 = bf16[16,4096]{1,0:T(8,128)(2,1)S(1)} collective-permute-done((bf16[16,4096]{1,0:T(8,128)(2,1)S(1)}, bf16[16,4096]{1,0:T(8,128)(2,1)S(1)}, u32[]{:S(2)}, u32[]{:S(2)}) %collective-permute-start.26) | collective-permute-done | bytes 131104 | tf_op jit(solution)/shard_map/ppermute | solution.py:27
  107.0 2.3 %collective-permute-start.27 = (bf16[16,4096]{1,0:T(8,128)(2,1)S(1)}, bf16[16,4096]{1,0:T(8,128)(2,1)S(1)}, u32[]{:S(2)}, u32[]{:S(2)}) collective-permute-start(bf16[16,4096]{1,0:T(8,128)(2,1)S(1)} %fusion.5), channel_id=1, source_target_pairs={{0,2},{1,3},{2,0},{3,1},{4,6},{5,7},{6,4},{7,5},{8,10},{9,11},{10,... | collective-permute-start | bytes 393224 | tf_op jit(solution)/shard_map/ppermute | solution.py:27
  109.3 1.4 collective-permute-done.14.upper_got
  110.7 1.3 collective-permute-done.15.lower_got
  112.2 1.0 collective-permute-start.16
  113.2 0.9 collective-permute-start.17
  114.4 0.9 collective-permute-start.28
  115.4 2.3 %collective-permute-done.21.upper_got = bf16[256,512]{1,0:T(8,128)(2,1)S(1)} collective-permute-done((bf16[256,512]{1,0:T(8,128)(2,1)S(1)}, bf16[256,512]{1,0:T(8,128)(2,1)S(1)}, u32[]{:S(2)}, u32[]{:S(2)}) %collective-permute-start.21) | collective-permute-done | bytes 262176 | tf_op jit(solution)/shard_map/ppermute | solution.py:27
  117.7 2.7 %collective-permute-start.23 = (bf16[512,256]{1,0:T(8,128)(2,1)S(1)}, bf16[512,256]{1,0:T(8,128)(2,1)S(1)}, u32[]{:S(2)}, u32[]{:S(2)}) collective-permute-start(bf16[512,256]{1,0:T(8,128)(2,1)S(1)} %get-tuple-element.126), channel_id=1, source_target_pairs={{2,0},{3,1},{0,2},{1,3},{6,4},{7,5},{4,6},{5,7},{10,8},{11,9},{8,1... | collective-permute-start | bytes 786440 | tf_op jit(solution)/shard_map/ppermute | solution.py:32
  120.5 0.9 collective-permute-start.24
  121.4 1.4 %shard_map.237 = f32[8,512,128]{2,1,0:T(8,128)S(1)} custom-call(s32[1]{0:T(128)} %bitcast.16.first, bf16[512,512]{1,0:T(8,128)(2,1)S(1)} %get-tuple-element.128.spread_ref, bf16[512,128]{1,0:T(8,128)(2,1)S(1)} %get-tuple-element.94.keys_ref, s32[512,128]{1,0:T(8,128)S(1)} %get-tuple-element.92.marks_ref, f32[16,1,128]{2,1,0:T(1,128)S(1)} %bitcast.37, ...), custom_call_target="tpu_custom_call" | custom-call | bytes 1000 | tf_op jit(solution)/shard_map/pallas_call | solution.py:60
  123.0 0.8 collective-permute-start.29
  124.0 1.3 collective-permute-start.18
  125.3 3.7 %collective-permute-done.29 = bf16[16,4096]{1,0:T(8,128)(2,1)S(1)} collective-permute-done((bf16[16,4096]{1,0:T(8,128)(2,1)S(1)}, bf16[16,4096]{1,0:T(8,128)(2,1)S(1)}, u32[]{:S(2)}, u32[]{:S(2)}) %collective-permute-start.29) | collective-permute-done | bytes 131104 | tf_op jit(solution)/shard_map/ppermute | solution.py:27
  129.1 2.8 %shard_map.238 = f32[8,512,128]{2,1,0:T(8,128)} custom-call(s32[1]{0:T(128)} %bitcast.14.first, bf16[512,512]{1,0:T(8,128)(2,1)S(1)} %get-tuple-element.128.spread_ref, bf16[512,128]{1,0:T(8,128)(2,1)S(1)} %get-tuple-element.94.keys_ref, s32[512,128]{1,0:T(8,128)S(1)} %get-tuple-element.92.marks_ref, f32[16,1,128]{2,1,0:T(1,128)S(1)} %bitcast.38, ...), custom_call_target="tpu_custom_call" | custom-call | bytes 1000 | tf_op jit(solution)/shard_map/pallas_call | solution.py:60
  131.9 4.4 %collective-permute-done.23.refs_1_ = bf16[512,256]{1,0:T(8,128)(2,1)S(1)} collective-permute-done((bf16[512,256]{1,0:T(8,128)(2,1)S(1)}, bf16[512,256]{1,0:T(8,128)(2,1)S(1)}, u32[]{:S(2)}, u32[]{:S(2)}) %collective-permute-start.23) | collective-permute-done | bytes 262176 | tf_op jit(solution)/shard_map/ppermute | solution.py:32
  136.4 0.9 shard_map.236
  137.5 1.2 slice-done.1
  138.7 1.9 %fusion.7 = f32[16,1024]{1,0:T(8,128)} fusion(bf16[4096,1024]{1,0:T(8,128)(2,1)S(1)} %bitcast.41, bf16[16,4096]{1,0:T(8,128)(2,1)S(1)} %get-tuple-element.140, f32[4096]{0:T(1024)S(1)} %copy-done.15, f32[16]{0:T(128)S(1)} %add_rsqrt_fusion), kind=kOutput, calls=%fused_computation.20 | convolution fusion | flops 134479872 | bytes 8601664 | tf_op jit(solution)/shard_map/dot_general | solution.py:917
  (108 shorter events, 7.2 us)
Async XLA Ops:
  0.6 38.6 %copy-start = (bf16[16,3,2,2,128]{4,3,2,1,0:T(2,128)(2,1)S(1)}, bf16[16,3,2,2,128]{4,3,2,1,0:T(2,128)(2,1)}, u32[]{:S(2)}) copy-start(bf16[16,3,2,2,128]{4,3,2,1,0:T(2,128)(2,1)} %param.33) | copy-start | bytes 147460
  0.6 11.0 %collective-permute-start = (bf16[512,256]{1,0:T(8,128)(2,1)}, bf16[512,256]{1,0:T(8,128)(2,1)S(1)}, u32[]{:S(2)}, u32[]{:S(2)}) collective-permute-start(bf16[512,256]{1,0:T(8,128)(2,1)} %tokens_ref.1), channel_id=1, source_target_pairs={{1,0},{2,1},{3,2},{0,3},{5,4},{6,5},{7,6},{4,7},{9,8},{10,9},{11,1... | collective-permute-start | bytes 786440 | tf_op jit(solution)/shard_map/ppermute | solution.py:32
  11.6 24.4 %collective-permute-start.1 = (bf16[512,256]{1,0:T(8,128)(2,1)S(1)}, bf16[512,256]{1,0:T(8,128)(2,1)S(1)}, u32[]{:S(2)}, u32[]{:S(2)}) collective-permute-start(bf16[512,256]{1,0:T(8,128)(2,1)S(1)} %collective-permute-done), channel_id=1, source_target_pairs={{1,0},{2,1},{3,2},{0,3},{5,4},{6,5},{7,6},{4,7},{9,8},{10,9},{11,1... | collective-permute-start | bytes 786440 | tf_op jit(solution)/shard_map/ppermute | solution.py:32
  15.9 10.2 %collective-permute-start.7 = (bf16[256,512]{1,0:T(8,128)(2,1)S(1)}, bf16[256,512]{1,0:T(8,128)(2,1)S(1)}, u32[]{:S(2)}, u32[]{:S(2)}) collective-permute-start(bf16[256,512]{1,0:T(8,128)(2,1)S(1)} %get-tuple-element.142.refs_0_), channel_id=1, source_target_pairs={{0,8},{4,12},{8,0},{12,4},{1,9},{5,13},{9,1},{13,5},{2,10},{6,14},... | collective-permute-start | bytes 786440 | tf_op jit(solution)/shard_map/ppermute | solution.py:27
  17.5 10.0 %collective-permute-start.9 = (bf16[256,512]{1,0:T(8,128)(2,1)S(1)}, bf16[256,512]{1,0:T(8,128)(2,1)S(1)}, u32[]{:S(2)}, u32[]{:S(2)}) collective-permute-start(bf16[256,512]{1,0:T(8,128)(2,1)S(1)} %get-tuple-element.141.refs_3_), channel_id=1, source_target_pairs={{0,4},{4,0},{8,12},{12,8},{1,5},{5,1},{9,13},{13,9},{2,6},{6,2},{1... | collective-permute-start | bytes 786440 | tf_op jit(solution)/shard_map/ppermute | solution.py:27
  18.9 17.1 %collective-permute-start.2 = (bf16[512,256]{1,0:T(8,128)(2,1)}, bf16[512,256]{1,0:T(8,128)(2,1)S(1)}, u32[]{:S(2)}, u32[]{:S(2)}) collective-permute-start(bf16[512,256]{1,0:T(8,128)(2,1)} %tokens_ref.1), channel_id=1, source_target_pairs={{3,0},{0,1},{1,2},{2,3},{7,4},{4,5},{5,6},{6,7},{11,8},{8,9},{9,10... | collective-permute-start | bytes 786440 | tf_op jit(solution)/shard_map/ppermute | solution.py:32
  26.9 21.5 %collective-permute-start.8 = (bf16[256,1024]{1,0:T(8,128)(2,1)}, bf16[256,1024]{1,0:T(8,128)(2,1)S(1)}, u32[]{:S(2)}, u32[]{:S(2)}) collective-permute-start(bf16[256,1024]{1,0:T(8,128)(2,1)} %pad_maximum_fusion.2), channel_id=1, source_target_pairs={{0,4},{4,0},{8,12},{12,8},{1,5},{5,1},{9,13},{13,9},{2,6},{6,2},{1... | collective-permute-start | bytes 1572872 | tf_op jit(solution)/shard_map/ppermute | solution.py:27
  28.4 11.0 %copy-start.16 = (bf16[16,3,512]{2,0,1:T(8,128)(2,1)S(1)}, bf16[16,3,512]{2,0,1:T(8,128)(2,1)}, u32[]{:S(2)}) copy-start(bf16[16,3,512]{2,0,1:T(8,128)(2,1)} %param.32) | copy-start | bytes 147460
  28.4 11.1 %copy-start.19 = (f32[4,2,2,128]{3,2,1,0:T(2,128)S(1)}, f32[4,2,2,128]{3,2,1,0:T(2,128)}, u32[]{:S(2)}) copy-start(f32[4,2,2,128]{3,2,1,0:T(2,128)} %param.29) | copy-start | bytes 24580
  28.4 11.2 %copy-start.17 = (f32[4,512]{1,0:T(4,128)S(1)}, f32[4,512]{1,0:T(4,128)}, u32[]{:S(2)}) copy-start(f32[4,512]{1,0:T(4,128)} %param.28) | copy-start | bytes 24580
  28.4 11.2 %copy-start.20 = (f32[2,2,128]{2,1,0:T(2,128)S(1)}, f32[2,2,128]{2,1,0:T(2,128)}, u32[]{:S(2)}) copy-start(f32[2,2,128]{2,1,0:T(2,128)} %param.31) | copy-start | bytes 6148
  28.4 20.1 %collective-permute-start.10 = (bf16[256,1024]{1,0:T(8,128)(2,1)}, bf16[256,1024]{1,0:T(8,128)(2,1)}, u32[]{:S(2)}, u32[]{:S(2)}) collective-permute-start(bf16[256,1024]{1,0:T(8,128)(2,1)} %pad_maximum_fusion.3), channel_id=1, source_target_pairs={{0,8},{4,12},{8,0},{12,4},{1,9},{5,13},{9,1},{13,5},{2,10},{6,14},... | collective-permute-start | bytes 1572872 | tf_op jit(solution)/shard_map/ppermute | solution.py:27
  36.0 12.4 %copy-start.13 = (f32[1,2048]{1,0:T(1,128)S(1)}, f32[1,2048]{1,0:T(1,128)}, u32[]{:S(2)}) copy-start(f32[1,2048]{1,0:T(1,128)} %get-tuple-element.78.refs_7_) | copy-start | bytes 24580
  36.2 8.5 %collective-permute-start.5 = (bf16[256,512]{1,0:T(8,128)(2,1)S(1)}, bf16[256,512]{1,0:T(8,128)(2,1)S(1)}, u32[]{:S(2)}, u32[]{:S(2)}) collective-permute-start(bf16[256,512]{1,0:T(8,128)(2,1)S(1)} %get-tuple-element.143.refs_3_), channel_id=1, source_target_pairs={{0,4},{4,0},{8,12},{12,8},{1,5},{5,1},{9,13},{13,9},{2,6},{6,2},{1... | collective-permute-start | bytes 786440 | tf_op jit(solution)/shard_map/ppermute | solution.py:27
  37.7 9.1 %collective-permute-start.3 = (bf16[256,512]{1,0:T(8,128)(2,1)S(1)}, bf16[256,512]{1,0:T(8,128)(2,1)S(1)}, u32[]{:S(2)}, u32[]{:S(2)}) collective-permute-start(bf16[256,512]{1,0:T(8,128)(2,1)S(1)} %get-tuple-element.144.refs_0_), channel_id=1, source_target_pairs={{0,8},{4,12},{8,0},{12,4},{1,9},{5,13},{9,1},{13,5},{2,10},{6,14},... | collective-permute-start | bytes 786440 | tf_op jit(solution)/shard_map/ppermute | solution.py:27
  44.8 12.4 %collective-permute-start.6 = (bf16[256,1024]{1,0:T(8,128)(2,1)S(1)}, bf16[256,1024]{1,0:T(8,128)(2,1)S(1)}, u32[]{:S(2)}, u32[]{:S(2)}) collective-permute-start(bf16[256,1024]{1,0:T(8,128)(2,1)S(1)} %pad_maximum_fusion.1), channel_id=1, source_target_pairs={{0,8},{4,12},{8,0},{12,4},{1,9},{5,13},{9,1},{13,5},{2,10},{6,14},... | collective-permute-start | bytes 1572872 | tf_op jit(solution)/shard_map/ppermute | solution.py:27
  46.9 10.5 %collective-permute-start.4 = (bf16[256,1024]{1,0:T(8,128)(2,1)S(1)}, bf16[256,1024]{1,0:T(8,128)(2,1)S(1)}, u32[]{:S(2)}, u32[]{:S(2)}) collective-permute-start(bf16[256,1024]{1,0:T(8,128)(2,1)S(1)} %pad_maximum_fusion), channel_id=1, source_target_pairs={{0,4},{4,0},{8,12},{12,8},{1,5},{5,1},{9,13},{13,9},{2,6},{6,2},{1... | collective-permute-start | bytes 1572872 | tf_op jit(solution)/shard_map/ppermute | solution.py:27
  48.5 2.6 %copy-start.11 = (bf16[2048,1408]{1,0:T(8,128)(2,1)S(1)}, bf16[2048,1408]{1,0:T(8,128)(2,1)}, u32[]{:S(2)}) copy-start(bf16[2048,1408]{1,0:T(8,128)(2,1)} %get-tuple-element.79.refs_8_) | copy-start | bytes 17301508
  51.1 6.3 %copy-start.14 = (f32[1,2048]{1,0:T(1,128)S(1)}, f32[1,2048]{1,0:T(1,128)}, u32[]{:S(2)}) copy-start(f32[1,2048]{1,0:T(1,128)} %get-tuple-element.76.refs_7_) | copy-start | bytes 24580
  57.4 2.6 %copy-start.12 = (bf16[2048,1408]{1,0:T(8,128)(2,1)S(1)}, bf16[2048,1408]{1,0:T(8,128)(2,1)}, u32[]{:S(2)}) copy-start(bf16[2048,1408]{1,0:T(8,128)(2,1)} %get-tuple-element.77.refs_8_) | copy-start | bytes 17301508
  60.0 5.5 %copy-start.18 = (f32[512]{0:T(512)S(1)}, f32[512]{0:T(512)}, u32[]{:S(2)}) copy-start(f32[512]{0:T(512)} %param.30) | copy-start | bytes 6148
  60.0 5.5 %copy-start.4 = (f32[16,8,64,128]{3,2,1,0:T(8,128)S(1)}, f32[16,8,64,128]{3,2,1,0:T(8,128)}, u32[]{:S(2)}) copy-start(f32[16,8,64,128]{3,2,1,0:T(8,128)} %param.34) | copy-start | bytes 12582916
  64.0 2.4 %collective-permute-start.11 = (bf16[16,768]{1,0:T(8,128)(2,1)S(1)}, bf16[16,768]{1,0:T(8,128)(2,1)S(1)}, u32[]{:S(2)}, u32[]{:S(2)}) collective-permute-start(bf16[16,768]{1,0:T(8,128)(2,1)S(1)} %slice.31), channel_id=1, source_target_pairs={{0,16},{1,17},{2,18},{3,19},{4,20},{5,21},{6,22},{7,23},{8,24},{9,... | collective-permute-start | bytes 73736 | tf_op jit(solution)/shard_map/ppermute | solution.py:23
  66.4 7.5 %copy-start.21 = (f32[8]{0:T(128)S(1)}, f32[8]{0:T(128)}, u32[]{:S(2)}) copy-start(f32[8]{0:T(128)} %param.37) | copy-start | bytes 100
  71.9 5.3 %copy-start.10 = (f32[512]{0:T(512)S(1)}, f32[512]{0:T(512)}, u32[]{:S(2)}) copy-start(f32[512]{0:T(512)} %param.38) | copy-start | bytes 6148
  71.9 5.3 %collective-permute-start.12 = (f32[512,128]{1,0:T(8,128)S(1)}, f32[512,128]{1,0:T(8,128)S(1)}, u32[]{:S(2)}, u32[]{:S(2)}) collective-permute-start(f32[512,128]{1,0:T(8,128)S(1)} %get-tuple-element.98), channel_id=1, source_target_pairs={{0,16},{1,17},{2,18},{3,19},{4,20},{5,21},{6,22},{7,23},{8,24},{9,... | collective-permute-start | bytes 786440 | tf_op jit(solution)/shard_map/ppermute | solution.py:23
  77.2 2.2 %copy-start.2 = (bf16[512,4096]{1,0:T(8,128)(2,1)S(1)}, bf16[512,4096]{1,0:T(8,128)(2,1)}, u32[]{:S(2)}) copy-start(bf16[512,4096]{1,0:T(8,128)(2,1)} %refs_7_.7) | copy-start | bytes 12582916
  77.2 2.2 %copy-start.7 = (s32[3]{0:T(128)S(1)}, s32[3]{0:T(128)}, u32[]{:S(2)}) copy-start(s32[3]{0:T(128)} %pad_add_fusion.place.blocks) | copy-start | bytes 40
  78.4 3.8 %collective-permute-start.13 = (f32[8,512]{1,0:T(8,128)S(1)}, f32[8,512]{1,0:T(8,128)S(1)}, u32[]{:S(2)}, u32[]{:S(2)}) collective-permute-start(f32[8,512]{1,0:T(8,128)S(1)} %get-tuple-element.101.own_ref.other_ref), channel_id=1, source_target_pairs={{0,1},{1,0},{2,3},{3,2},{4,5},{5,4},{6,7},{7,6},{8,9},{9,8},{10,11... | collective-permute-start | bytes 49160 | tf_op jit(solution)/shard_map/ppermute | solution.py:27
  83.6 0.8 copy-start.8
  84.4 15.2 %collective-permute-start.19 = (bf16[256,1024]{1,0:T(8,128)(2,1)}, bf16[256,1024]{1,0:T(8,128)(2,1)}, u32[]{:S(2)}, u32[]{:S(2)}) collective-permute-start(bf16[256,1024]{1,0:T(8,128)(2,1)} %get-tuple-element.119), channel_id=1, source_target_pairs={{0,4},{4,0},{8,12},{12,8},{1,5},{5,1},{9,13},{13,9},{2,6},{6,2},{1... | collective-permute-start | bytes 1572872 | tf_op jit(solution)/shard_map/ppermute | solution.py:27
  85.7 15.2 %collective-permute-start.20 = (bf16[256,1024]{1,0:T(8,128)(2,1)}, bf16[256,1024]{1,0:T(8,128)(2,1)}, u32[]{:S(2)}, u32[]{:S(2)}) collective-permute-start(bf16[256,1024]{1,0:T(8,128)(2,1)} %get-tuple-element.121), channel_id=1, source_target_pairs={{0,8},{4,12},{8,0},{12,4},{1,9},{5,13},{9,1},{13,5},{2,10},{6,14},... | collective-permute-start | bytes 1572872 | tf_op jit(solution)/shard_map/ppermute | solution.py:27
  87.1 2.2 %copy-start.3 = (bf16[512,4096]{1,0:T(8,128)(2,1)S(1)}, bf16[512,4096]{1,0:T(8,128)(2,1)}, u32[]{:S(2)}) copy-start(bf16[512,4096]{1,0:T(8,128)(2,1)} %refs_7_.7) | copy-start | bytes 12582916
  89.3 12.9 %copy-start.9 = (bf16[256,1024]{1,0:T(8,128)(2,1)S(1)}, bf16[256,1024]{1,0:T(8,128)(2,1)}, u32[]{:S(2)}) copy-start(bf16[256,1024]{1,0:T(8,128)(2,1)} %copy-done.8) | copy-start | bytes 1572868
  91.7 19.0 %collective-permute-start.14 = (bf16[256,1024]{1,0:T(8,128)(2,1)S(1)}, bf16[256,1024]{1,0:T(8,128)(2,1)S(1)}, u32[]{:S(2)}, u32[]{:S(2)}) collective-permute-start(bf16[256,1024]{1,0:T(8,128)(2,1)S(1)} %get-tuple-element.105), channel_id=1, source_target_pairs={{0,4},{4,0},{8,12},{12,8},{1,5},{5,1},{9,13},{13,9},{2,6},{6,2},{1... | collective-permute-start | bytes 1572872 | tf_op jit(solution)/shard_map/ppermute | solution.py:27
  92.7 19.3 %collective-permute-start.15 = (bf16[256,1024]{1,0:T(8,128)(2,1)S(1)}, bf16[256,1024]{1,0:T(8,128)(2,1)S(1)}, u32[]{:S(2)}, u32[]{:S(2)}) collective-permute-start(bf16[256,1024]{1,0:T(8,128)(2,1)S(1)} %get-tuple-element.107), channel_id=1, source_target_pairs={{0,8},{4,12},{8,0},{12,4},{1,9},{5,13},{9,1},{13,5},{2,10},{6,14},... | collective-permute-start | bytes 1572872 | tf_op jit(solution)/shard_map/ppermute | solution.py:27
  101.5 5.5 %collective-permute-start.26 = (bf16[16,4096]{1,0:T(8,128)(2,1)S(1)}, bf16[16,4096]{1,0:T(8,128)(2,1)S(1)}, u32[]{:S(2)}, u32[]{:S(2)}) collective-permute-start(bf16[16,4096]{1,0:T(8,128)(2,1)S(1)} %convert_element_type.38), channel_id=1, source_target_pairs={{0,1},{1,0},{2,3},{3,2},{4,5},{5,4},{6,7},{7,6},{8,9},{9,8},{10,11... | collective-permute-start | bytes 393224 | tf_op jit(solution)/shard_map/ppermute | solution.py:27
  103.6 14.0 %collective-permute-start.21 = (bf16[256,512]{1,0:T(8,128)(2,1)S(1)}, bf16[256,512]{1,0:T(8,128)(2,1)S(1)}, u32[]{:S(2)}, u32[]{:S(2)}) collective-permute-start(bf16[256,512]{1,0:T(8,128)(2,1)S(1)} %get-tuple-element.123), channel_id=1, source_target_pairs={{0,8},{4,12},{8,0},{12,4},{1,9},{5,13},{9,1},{13,5},{2,10},{6,14},... | collective-permute-start | bytes 786440 | tf_op jit(solution)/shard_map/ppermute | solution.py:27
  104.6 13.0 %collective-permute-start.22 = (bf16[256,512]{1,0:T(8,128)(2,1)S(1)}, bf16[256,512]{1,0:T(8,128)(2,1)S(1)}, u32[]{:S(2)}, u32[]{:S(2)}) collective-permute-start(bf16[256,512]{1,0:T(8,128)(2,1)S(1)} %get-tuple-element.125), channel_id=1, source_target_pairs={{0,4},{4,0},{8,12},{12,8},{1,5},{5,1},{9,13},{13,9},{2,6},{6,2},{1... | collective-permute-start | bytes 786440 | tf_op jit(solution)/shard_map/ppermute | solution.py:27
  107.0 7.3 %collective-permute-start.27 = (bf16[16,4096]{1,0:T(8,128)(2,1)S(1)}, bf16[16,4096]{1,0:T(8,128)(2,1)S(1)}, u32[]{:S(2)}, u32[]{:S(2)}) collective-permute-start(bf16[16,4096]{1,0:T(8,128)(2,1)S(1)} %fusion.5), channel_id=1, source_target_pairs={{0,2},{1,3},{2,0},{3,1},{4,6},{5,7},{6,4},{7,5},{8,10},{9,11},{10,... | collective-permute-start | bytes 393224 | tf_op jit(solution)/shard_map/ppermute | solution.py:27
  112.2 10.8 %collective-permute-start.16 = (bf16[256,512]{1,0:T(8,128)(2,1)S(1)}, bf16[256,512]{1,0:T(8,128)(2,1)S(1)}, u32[]{:S(2)}, u32[]{:S(2)}) collective-permute-start(bf16[256,512]{1,0:T(8,128)(2,1)S(1)} %get-tuple-element.109), channel_id=1, source_target_pairs={{0,8},{4,12},{8,0},{12,4},{1,9},{5,13},{9,1},{13,5},{2,10},{6,14},... | collective-permute-start | bytes 786440 | tf_op jit(solution)/shard_map/ppermute | solution.py:27
  113.2 10.7 %collective-permute-start.17 = (bf16[256,512]{1,0:T(8,128)(2,1)S(1)}, bf16[256,512]{1,0:T(8,128)(2,1)S(1)}, u32[]{:S(2)}, u32[]{:S(2)}) collective-permute-start(bf16[256,512]{1,0:T(8,128)(2,1)S(1)} %get-tuple-element.111), channel_id=1, source_target_pairs={{0,4},{4,0},{8,12},{12,8},{1,5},{5,1},{9,13},{13,9},{2,6},{6,2},{1... | collective-permute-start | bytes 786440 | tf_op jit(solution)/shard_map/ppermute | solution.py:27
  114.4 8.5 %collective-permute-start.28 = (bf16[16,4096]{1,0:T(8,128)(2,1)S(1)}, bf16[16,4096]{1,0:T(8,128)(2,1)S(1)}, u32[]{:S(2)}, u32[]{:S(2)}) collective-permute-start(bf16[16,4096]{1,0:T(8,128)(2,1)S(1)} %fusion.11), channel_id=1, source_target_pairs={{0,4},{4,0},{8,12},{12,8},{1,5},{5,1},{9,13},{13,9},{2,6},{6,2},{1... | collective-permute-start | bytes 393224 | tf_op jit(solution)/shard_map/ppermute | solution.py:27
  117.6 3.8 %copy-start.5 = (f32[16,8,64,128]{3,2,1,0:T(8,128)S(1)}, f32[16,8,64,128]{3,2,1,0:T(8,128)}, u32[]{:S(2)}) copy-start(f32[16,8,64,128]{3,2,1,0:T(8,128)} %param.34) | copy-start | bytes 12582916
  117.7 18.6 %collective-permute-start.23 = (bf16[512,256]{1,0:T(8,128)(2,1)S(1)}, bf16[512,256]{1,0:T(8,128)(2,1)S(1)}, u32[]{:S(2)}, u32[]{:S(2)}) collective-permute-start(bf16[512,256]{1,0:T(8,128)(2,1)S(1)} %get-tuple-element.126), channel_id=1, source_target_pairs={{2,0},{3,1},{0,2},{1,3},{6,4},{7,5},{4,6},{5,7},{10,8},{11,9},{8,1... | collective-permute-start | bytes 786440 | tf_op jit(solution)/shard_map/ppermute | solution.py:32
  120.5 15.9 %collective-permute-start.24 = (bf16[512,256]{1,0:T(8,128)(2,1)S(1)}, bf16[512,256]{1,0:T(8,128)(2,1)S(1)}, u32[]{:S(2)}, u32[]{:S(2)}) collective-permute-start(bf16[512,256]{1,0:T(8,128)(2,1)S(1)} %get-tuple-element.127), channel_id=1, source_target_pairs={{1,0},{2,1},{3,2},{0,3},{5,4},{6,5},{7,6},{4,7},{9,8},{10,9},{11,1... | collective-permute-start | bytes 786440 | tf_op jit(solution)/shard_map/ppermute | solution.py:32
  122.9 6.2 %collective-permute-start.25 = (f32[8,512,128]{2,1,0:T(8,128)S(1)}, f32[8,512,128]{2,1,0:T(8,128)S(1)}, u32[]{:S(2)}, u32[]{:S(2)}) collective-permute-start(f32[8,512,128]{2,1,0:T(8,128)S(1)} %shard_map.237), channel_id=1, source_target_pairs={{0,16},{16,0},{1,17},{17,1},{2,18},{18,2},{3,19},{19,3},{4,20},{20... | collective-permute-start | bytes 6291464 | tf_op jit(solution)/shard_map/ppermute | solution.py:27
  123.0 6.0 %collective-permute-start.29 = (bf16[16,4096]{1,0:T(8,128)(2,1)S(1)}, bf16[16,4096]{1,0:T(8,128)(2,1)S(1)}, u32[]{:S(2)}, u32[]{:S(2)}) collective-permute-start(bf16[16,4096]{1,0:T(8,128)(2,1)S(1)} %fusion.6), channel_id=1, source_target_pairs={{0,8},{4,12},{8,0},{12,4},{1,9},{5,13},{9,1},{13,5},{2,10},{6,14},... | collective-permute-start | bytes 393224 | tf_op jit(solution)/shard_map/ppermute | solution.py:27
  124.0 12.4 %collective-permute-start.18 = (bf16[512,256]{1,0:T(8,128)(2,1)S(1)}, bf16[512,256]{1,0:T(8,128)(2,1)S(1)}, u32[]{:S(2)}, u32[]{:S(2)}) collective-permute-start(bf16[512,256]{1,0:T(8,128)(2,1)S(1)} %get-tuple-element.113), channel_id=1, source_target_pairs={{3,0},{0,1},{1,2},{2,3},{7,4},{4,5},{5,6},{6,7},{11,8},{8,9},{9,10... | collective-permute-start | bytes 786440 | tf_op jit(solution)/shard_map/ppermute | solution.py:32
  129.1 7.3 %copy-start.6 = (bf16[512,256]{1,0:T(8,128)(2,1)S(1)}, bf16[512,256]{1,0:T(8,128)(2,1)}, u32[]{:S(2)}) copy-start(bf16[512,256]{1,0:T(8,128)(2,1)} %tokens_ref.1) | copy-start | bytes 786436
  129.1 8.3 %slice-start = ((s8[8388608]{0:T(1024)(128)(4,1)}), s8[4194304]{0:T(1024)(128)(4,1)S(1)}, s32[]{:S(2)}) async-start(s8[8388608]{0:T(1024)(128)(4,1)} %bitcast.40), calls=%async_computation | async-start | bytes 8388608
  131.9 5.3 %collective-permute-start.30 = (f32[16,4096]{1,0:T(8,128)S(1)}, f32[16,4096]{1,0:T(8,128)S(1)}, u32[]{:S(2)}, u32[]{:S(2)}) collective-permute-start(f32[16,4096]{1,0:T(8,128)S(1)} %add_add_fusion), channel_id=1, source_target_pairs={{0,16},{16,0},{1,17},{17,1},{2,18},{18,2},{3,19},{19,3},{4,20},{20... | collective-permute-start | bytes 786440 | tf_op jit(solution)/shard_map/ppermute | solution.py:27
  136.4 2.3 %slice-start.1 = ((s8[8388608]{0:T(1024)(128)(4,1)}), s8[4194304]{0:T(1024)(128)(4,1)S(1)}, s32[]{:S(2)}) async-start(s8[8388608]{0:T(1024)(128)(4,1)} %bitcast.40), calls=%async_computation.1 | async-start | bytes 8388608
  136.4 2.3 %copy-start.15 = (f32[4096]{0:T(1024)S(1)}, f32[4096]{0:T(1024)}, u32[]{:S(2)}) copy-start(f32[4096]{0:T(1024)} %param.40) | copy-start | bytes 49156
  137.4 3.1 %copy-start.1 = (bf16[16,3,2,2,128]{4,3,2,1,0:T(2,128)(2,1)S(1)}, bf16[16,3,2,2,128]{4,3,2,1,0:T(2,128)(2,1)}, u32[]{:S(2)}) copy-start(bf16[16,3,2,2,128]{4,3,2,1,0:T(2,128)(2,1)} %param.33) | copy-start | bytes 147460

commit v4 on v3

--- a/solution.py
+++ b/solution.py
@@ -275,12 +275,15 @@
     head_size = inner // heads
     taps = taps_ref.shape[0]
     channels = channels_ref[...]
-    sources = jnp.concatenate([channels, rim_ref[...], edges_ref[...]], axis=0)
-    summed = bias_ref[...] + taps_ref[taps - 1 : taps] * channels.astype(F32)
+    sources = jnp.concatenate([rim_ref[...], edges_ref[...]], axis=0)
+    wide = channels.astype(F32)
+    summed = bias_ref[...] + taps_ref[taps - 1 : taps] * wide
     column = lax.broadcasted_iota(jnp.int32, (rows, sources.shape[0]), 1)
     for back in range(1, taps):
-        pick = jnp.where(marks_ref[:, back - 1 : back] == column, 1.0, 0.0).astype(BF16)
+        mark = marks_ref[:, back - 1 : back]
+        pick = jnp.where(mark - rows == column, 1.0, 0.0).astype(BF16)
         value = jnp.dot(pick, sources, preferred_element_type=F32)
+        value = value + jnp.where(mark < rows, 1.0, 0.0) * pltpu.roll(wide, back, 0)
         summed = summed + taps_ref[taps - 1 - back : taps - back] * value
     mixed = (summed / (1.0 + jnp.exp(-summed))).astype(BF16)
     x = mixed[:, :inner]
@@ -295,10 +298,26 @@
     same = segment == segment_ref[0:1, :]
     row = lax.broadcasted_iota(jnp.int32, (rows, rows), 0)
     other = lax.broadcasted_iota(jnp.int32, (rows, rows), 1)
-    until = jnp.where(same & (other <= row), 1.0, 0.0)
-    after = jnp.where(same & (other > row), 1.0, 0.0)
-    run = jnp.dot(until, log_decay, precision=HIGHEST, preferred_element_type=F32)
-    tail = jnp.dot(after, log_decay, precision=HIGHEST, preferred_element_type=F32)
+    until = jnp.where(same & (other <= row), 1.0, 0.0).astype(BF16)
+    after = jnp.where(same & (other > row), 1.0, 0.0).astype(BF16)
+    lane = lax.broadcasted_iota(jnp.int32, log_decay.shape, 1)
+    own = jnp.where(lane < heads, log_decay, 0.0)
+    high = own.astype(BF16).astype(F32)
+    middle = (own - high).astype(BF16).astype(F32)
+    low = own - high - middle
+    parts = high + pltpu.roll(middle, heads, 1) + pltpu.roll(low, 2 * heads, 1)
+    parts = parts.astype(BF16)
+
+    def summed_over(mask):
+        sums = jnp.dot(mask, parts, preferred_element_type=F32)
+        return (
+            sums
+            + pltpu.roll(sums, LANES - heads, 1)
+            + pltpu.roll(sums, LANES - 2 * heads, 1)
+        )
+
+    run = summed_over(until)
+    tail = summed_over(after)
     run_ref[...] = run
     less_ref[...] = (run - jnp.log(step)).T[:8]
     share = (jnp.exp(tail) * step).astype(BF16).astype(F32)
@@ -620,7 +639,7 @@
     gain_row = pre_gain[None, :]
     token_blocks = {0: tokens}
     token_blocks[1] = from_ahead(tokens, "col", 1)
-    later, token_blocks[1] = lax.optimization_barrier((tokens, token_blocks[1]))
+    later = after(tokens, token_blocks[1])
     for shift in range(2, col_size):
         source = token_blocks[1] if shift == 2 else later
         token_blocks[shift] = from_ahead(source, "col", 1 if shift == 2 else shift)

time: 142 us -> 140 us (0.986)
  waiting for transfers between devices: 28.7 us -> 30.7 us
  starting transfers between devices: 39.9 us -> 38.1 us
    ppermute x23, waiting for transfers between devices: 22.8 us -> 24.5 us  [from_partner(): lax.ppermute(x, axis, [(i, i ^ 1 << bit) for i in range(lax.axis_size(axi...]
  transfers between devices with their start and end apart: 31 -> 31, of which waited for: 15 -> 16; matrix products, arithmetic and copies ran while one was open for 5% -> 5% of each run, Pallas kernels for 26% -> 27%
where the time goes in v4:
time: 140 us; the launch traced here: 139 us
  Pallas kernels  47.5 us (34%)
  starting transfers between devices  38.1 us (27%)
  waiting for transfers between devices  30.7 us (22%)
  local copies, waits for them, and re-layouts  14.3 us (10%)
  other arithmetic  3.75 us (3%)
  between operations  2.82 us (2%)
  matrix products  2.08 us (1%)
    pallas_call x19, Pallas kernels, call(): pl.pallas_call(kernel, out_shape=shapes, grid_spec=spec, compiler_params=...  44.4 us
    ppermute x23, waiting for transfers between devices, from_partner(): lax.ppermute(x, axis, [(i, i ^ 1 << bit) for i in range(lax.axis_size(axi...  24.5 us
    ppermute x23, starting transfers between devices, from_partner(): lax.ppermute(x, axis, [(i, i ^ 1 << bit) for i in range(lax.axis_size(axi...  20.9 us
    ppermute x6, starting transfers between devices, from_ahead(): lax.ppermute(x, axis, [((i + distance) % size, i) for i in range(size)])  13.6 us
    unnamed x52, local copies, waits for them, and re-layouts  11.5 us
    ppermute x6, waiting for transfers between devices, from_ahead(): lax.ppermute(x, axis, [((i + distance) % size, i) for i in range(size)])  6.13 us
    ppermute x2, starting transfers between devices, from_behind(): return lax.ppermute(block, axis, route)  3.53 us
    pallas_call x1, Pallas kernels, per_device(): pl.pallas_call(functools.partial(scan_kernel, heads, block), out_shape=ja...  3.18 us
  transfers between devices with their start and end apart: 31, of which 16 were waited for; matrix products, arithmetic and copies ran while one was open for 5% of the time, Pallas kernels for 27%

profile of v4, /device:TPU:0, one launch (start us, length us, event | category | flops | bytes accessed | tf_op | source)
XLA Modules:
  0.0 139.3 jit_solution(8526836098668447042)
XLA Ops:
  0.6 5.1 %collective-permute-start = (bf16[512,256]{1,0:T(8,128)(2,1)}, bf16[512,256]{1,0:T(8,128)(2,1)S(1)}, u32[]{:S(2)}, u32[]{:S(2)}) collective-permute-start(bf16[512,256]{1,0:T(8,128)(2,1)} %tokens_ref.1), channel_id=1, source_target_pairs={{1,0},{2,1},{3,2},{0,3},{5,4},{6,5},{7,6},{4,7},{9,8},{10,9},{11,1... | collective-permute-start | bytes 786440 | tf_op jit(solution)/shard_map/ppermute | solution.py:32
  6.4 0.7 pad_add_fusion.1.counts
  7.1 1.4 %shard_map.220 = (s32[512,128]{1,0:T(8,128)S(1)}, s32[8,512]{1,0:T(8,128)S(1)}, bf16[16,512]{1,0:T(8,128)(2,1)S(1)}, f32[16,256]{1,0:T(8,128)S(1)}) custom-call(s32[33]{0:T(128)S(1)} %pad_add_fusion.1.counts), custom_call_target="tpu_custom_call" | custom-call | bytes 1000 | tf_op jit(solution)/shard_map/pallas_call | solution.py:60
  8.5 0.7 pad_bitcast_fusion.1
  9.2 1.0 constant_dynamic-update-slice_fusion.3
  10.2 1.4 %collective-permute-done = bf16[512,256]{1,0:T(8,128)(2,1)S(1)} collective-permute-done((bf16[512,256]{1,0:T(8,128)(2,1)}, bf16[512,256]{1,0:T(8,128)(2,1)S(1)}, u32[]{:S(2)}, u32[]{:S(2)}) %collective-permute-start) | collective-permute-done | bytes 262176 | tf_op jit(solution)/shard_map/ppermute | solution.py:32
  11.7 1.6 %collective-permute-start.7 = (bf16[256,512]{1,0:T(8,128)(2,1)S(1)}, bf16[256,512]{1,0:T(8,128)(2,1)S(1)}, u32[]{:S(2)}, u32[]{:S(2)}) collective-permute-start(bf16[256,512]{1,0:T(8,128)(2,1)S(1)} %get-tuple-element.140.refs_0_), channel_id=1, source_target_pairs={{0,8},{4,12},{8,0},{12,4},{1,9},{5,13},{9,1},{13,5},{2,10},{6,14},... | collective-permute-start | bytes 786440 | tf_op jit(solution)/shard_map/ppermute | solution.py:27
  13.3 1.5 %collective-permute-start.9 = (bf16[256,512]{1,0:T(8,128)(2,1)S(1)}, bf16[256,512]{1,0:T(8,128)(2,1)S(1)}, u32[]{:S(2)}, u32[]{:S(2)}) collective-permute-start(bf16[256,512]{1,0:T(8,128)(2,1)S(1)} %get-tuple-element.139.refs_3_), channel_id=1, source_target_pairs={{0,4},{4,0},{8,12},{12,8},{1,5},{5,1},{9,13},{13,9},{2,6},{6,2},{1... | collective-permute-start | bytes 786440 | tf_op jit(solution)/shard_map/ppermute | solution.py:27
  15.1 7.1 %shard_map.222 = (bf16[2048,1408]{1,0:T(8,128)(2,1)}, f32[1,2048]{1,0:T(1,128)}) custom-call(s32[3]{0:T(128)} %pad_add_fusion.place.blocks, bf16[4096,2,512]{2,1,0:T(2,128)(2,1)} %refs_3_.5, bf16[4096,2,512]{2,1,0:T(2,128)(2,1)} %refs_3_.5, bf16[4096,2,512]{2,1,0:T(2,128)(2,1)} %refs_3_.5, bf16[4096,2,512]{2,1,0:T(2,128)(2,1)} %refs_3_.5, ...), custom_call_target="tpu_custom_call" | custom-call | flops 20000000000 | bytes 100000000 | tf_op jit(solution)/shard_map/pallas_call | solution.py:60
  22.2 4.1 %collective-permute-start.1 = (bf16[512,256]{1,0:T(8,128)(2,1)S(1)}, bf16[512,256]{1,0:T(8,128)(2,1)S(1)}, u32[]{:S(2)}, u32[]{:S(2)}) collective-permute-start(bf16[512,256]{1,0:T(8,128)(2,1)S(1)} %collective-permute-done), channel_id=1, source_target_pairs={{1,0},{2,1},{3,2},{0,3},{5,4},{6,5},{7,6},{4,7},{9,8},{10,9},{11,1... | collective-permute-start | bytes 786440 | tf_op jit(solution)/shard_map/ppermute | solution.py:32
  26.3 0.9 pad_maximum_fusion.2
  27.7 0.9 pad_maximum_fusion.3
  29.2 7.1 %shard_map.221 = (bf16[2048,1408]{1,0:T(8,128)(2,1)}, f32[1,2048]{1,0:T(1,128)}) custom-call(s32[3]{0:T(128)} %pad_add_fusion.place.blocks, bf16[4096,2,512]{2,1,0:T(2,128)(2,1)} %refs_3_.5, bf16[4096,2,512]{2,1,0:T(2,128)(2,1)} %refs_3_.5, bf16[4096,2,512]{2,1,0:T(2,128)(2,1)} %refs_3_.5, bf16[4096,2,512]{2,1,0:T(2,128)(2,1)} %refs_3_.5, ...), custom_call_target="tpu_custom_call" | custom-call | flops 20000000000 | bytes 100000000 | tf_op jit(solution)/shard_map/pallas_call | solution.py:60
  36.4 1.6 %collective-permute-start.5 = (bf16[256,512]{1,0:T(8,128)(2,1)S(1)}, bf16[256,512]{1,0:T(8,128)(2,1)S(1)}, u32[]{:S(2)}, u32[]{:S(2)}) collective-permute-start(bf16[256,512]{1,0:T(8,128)(2,1)S(1)} %get-tuple-element.141.refs_3_), channel_id=1, source_target_pairs={{0,4},{4,0},{8,12},{12,8},{1,5},{5,1},{9,13},{13,9},{2,6},{6,2},{1... | collective-permute-start | bytes 786440 | tf_op jit(solution)/shard_map/ppermute | solution.py:27
  37.9 1.5 %collective-permute-start.3 = (bf16[256,512]{1,0:T(8,128)(2,1)S(1)}, bf16[256,512]{1,0:T(8,128)(2,1)S(1)}, u32[]{:S(2)}, u32[]{:S(2)}) collective-permute-start(bf16[256,512]{1,0:T(8,128)(2,1)S(1)} %get-tuple-element.142.refs_0_), channel_id=1, source_target_pairs={{0,8},{4,12},{8,0},{12,4},{1,9},{5,13},{9,1},{13,5},{2,10},{6,14},... | collective-permute-start | bytes 786440 | tf_op jit(solution)/shard_map/ppermute | solution.py:27
  42.1 1.0 dynamic-slice_bitcast_fusion.init_ref
  43.0 1.9 %collective-permute-done.5.refs_4_ = bf16[256,512]{1,0:T(8,128)(2,1)S(1)} collective-permute-done((bf16[256,512]{1,0:T(8,128)(2,1)S(1)}, bf16[256,512]{1,0:T(8,128)(2,1)S(1)}, u32[]{:S(2)}, u32[]{:S(2)}) %collective-permute-start.5) | collective-permute-done | bytes 262176 | tf_op jit(solution)/shard_map/ppermute | solution.py:27
  45.6 1.5 %collective-permute-done.3.refs_1_ = bf16[256,512]{1,0:T(8,128)(2,1)S(1)} collective-permute-done((bf16[256,512]{1,0:T(8,128)(2,1)S(1)}, bf16[256,512]{1,0:T(8,128)(2,1)S(1)}, u32[]{:S(2)}, u32[]{:S(2)}) %collective-permute-start.3) | collective-permute-done | bytes 262176 | tf_op jit(solution)/shard_map/ppermute | solution.py:27
  47.1 1.6 %collective-permute-start.4 = (bf16[256,1024]{1,0:T(8,128)(2,1)S(1)}, bf16[256,1024]{1,0:T(8,128)(2,1)S(1)}, u32[]{:S(2)}, u32[]{:S(2)}) collective-permute-start(bf16[256,1024]{1,0:T(8,128)(2,1)S(1)} %pad_maximum_fusion), channel_id=1, source_target_pairs={{0,4},{4,0},{8,12},{12,8},{1,5},{5,1},{9,13},{13,9},{2,6},{6,2},{1... | collective-permute-start | bytes 1572872 | tf_op jit(solution)/shard_map/ppermute | solution.py:27
  48.7 2.6 %copy-done.11 = bf16[2048,1408]{1,0:T(8,128)(2,1)S(1)} copy-done((bf16[2048,1408]{1,0:T(8,128)(2,1)S(1)}, bf16[2048,1408]{1,0:T(8,128)(2,1)}, u32[]{:S(2)}) %copy-start.11) | copy-done | bytes 5767192
  51.3 5.0 %shard_map.223 = (f32[16,2048]{1,0:T(8,128)S(1)}, f32[512,1408]{1,0:T(8,128)S(1)}, f32[512,128]{1,0:T(8,128)S(1)}) custom-call(s32[1]{0:T(128)} %constant.31.clone.1.unused, bf16[256,512]{1,0:T(8,128)(2,1)S(1)} %get-tuple-element.140.refs_0_, bf16[256,512]{1,0:T(8,128)(2,1)S(1)} %collective-permute-done.7.refs_1_, ...), custom_call_target="tpu_custom_call" | custom-call | flops 20000000000 | bytes 100000000 | tf_op jit(solution)/shard_map/pallas_call | solution.py:60
  56.4 1.1 collective-permute-done.6.refs_5_
  57.6 2.6 %copy-done.12 = bf16[2048,1408]{1,0:T(8,128)(2,1)S(1)} copy-done((bf16[2048,1408]{1,0:T(8,128)(2,1)S(1)}, bf16[2048,1408]{1,0:T(8,128)(2,1)}, u32[]{:S(2)}) %copy-start.12) | copy-done | bytes 5767192
  60.2 3.9 %shard_map.224 = (f32[16,2048]{1,0:T(8,128)S(1)}, bf16[512,512]{1,0:T(8,128)(2,1)S(1)}, bf16[512,768]{1,0:T(8,128)(2,1)S(1)}, f32[512,128]{1,0:T(8,128)S(1)}) custom-call(s32[1]{0:T(128)} %constant.31.clone.1.unused, bf16[256,512]{1,0:T(8,128)(2,1)S(1)} %get-tuple-element.142.refs_0_, bf16[256,512]{1,0:T(8,128)(2,1)S(1)} %collective-permute-done.3.refs_1_, ...), custom_call_target="tpu_custom_call" | custom-call | flops 20000000000 | bytes 100000000 | tf_op jit(solution)/shard_map/pallas_call | solution.py:60
  64.2 1.5 %collective-permute-start.11 = (bf16[16,768]{1,0:T(8,128)(2,1)S(1)}, bf16[16,768]{1,0:T(8,128)(2,1)S(1)}, u32[]{:S(2)}, u32[]{:S(2)}) collective-permute-start(bf16[16,768]{1,0:T(8,128)(2,1)S(1)} %slice.31), channel_id=1, source_target_pairs={{0,16},{1,17},{2,18},{3,19},{4,20},{5,21},{6,22},{7,23},{8,24},{9,... | collective-permute-start | bytes 73736 | tf_op jit(solution)/shard_map/ppermute | solution.py:23
  65.8 0.9 shard_map.225.table_ref
  66.7 4.1 %shard_map.226 = (bf16[512,512]{1,0:T(8,128)(2,1)S(1)}, bf16[512,128]{1,0:T(8,128)(2,1)S(1)}, bf16[512,128]{1,0:T(8,128)(2,1)S(1)}, f32[512,128]{1,0:T(8,128)S(1...) custom-call(s32[1]{0:T(128)} %constant.31.clone.1.unused, ...), custom_call_target="tpu_custom_call" | custom-call | flops 20000000000 | bytes 100000000 | tf_op jit(solution)/shard_map/pallas_call | solution.py:60
  70.8 2.0 %collective-permute-start.12 = (f32[512,128]{1,0:T(8,128)S(1)}, f32[512,128]{1,0:T(8,128)S(1)}, u32[]{:S(2)}, u32[]{:S(2)}) collective-permute-start(f32[512,128]{1,0:T(8,128)S(1)} %get-tuple-element.96), channel_id=1, source_target_pairs={{0,16},{1,17},{2,18},{3,19},{4,20},{5,21},{6,22},{7,23},{8,24},{9,... | collective-permute-start | bytes 786440 | tf_op jit(solution)/shard_map/ppermute | solution.py:23
  72.8 3.2 %shard_map.227.y_ref = f32[512,512]{1,0:T(8,128)S(1)} custom-call(s32[1]{0:T(128)} %constant.31.clone.1.unused, bf16[512,512]{1,0:T(8,128)(2,1)S(1)} %get-tuple-element.91.x_ref, bf16[512,128]{1,0:T(8,128)(2,1)S(1)} %get-tuple-element.92.keys_ref, bf16[512,128]{1,0:T(8,128)(2,1)S(1)} %get-tuple-element.93.queries_ref, ...), custom_call_target="tpu_custom_call" | custom-call | tf_op jit(solution)/shard_map/pallas_call | solution.py:741
  76.1 1.2 shard_map.228
  77.3 0.9 copy-done.2
  78.2 2.3 %shard_map.229 = (f32[256,1024]{1,0:T(8,128)S(1)}, f32[256,1024]{1,0:T(8,128)S(1)}, f32[256,1024]{1,0:T(8,128)S(1)}, f32[256,1024]{1,0:T(8,128)S(1)}, f32[16,2048]{1,0:T(8,128)S(1)}) custom-call(s32[3]{0:T(128)S(1)} %copy-done.7, bf16[512,512]{1,0:T(8,128)(2,1)S(1)} %get-tuple-element.98.gated_ref.channels_ref, ...), custom_call_target="tpu_custom_call" | custom-call | flops 10000000000 | bytes 100000000 | tf_op jit(solution)/shard_map/pallas_call | solution.py:60
  81.0 1.4 %shard_map.233 = (bf16[256,1024]{1,0:T(8,128)(2,1)}, bf16[256,1024]{1,0:T(8,128)(2,1)S(1)}, bf16[256,1024]{1,0:T(8,128)(2,1)}, bf16[256,1024]{1,0:T(8,128)(2,1)S(1)}, f32[16,2048]{1,0:T(8,128)S(1)}) custom-call(s32[1]{0:T(128)} %constant.31.clone.1.unused, f32[8,512]{1,0:T(8,128)S(1)} %get-tuple-element.99.own_ref.other_ref, ...), custom_call_target="tpu_custom_call" | custom-call | bytes 1000 | tf_op jit(solution)/shard_map/pallas_call | solution.py:60
  82.4 0.8 copy-done.8
  83.2 1.3 collective-permute-start.19
  84.5 0.9 collective-permute-start.20
  85.9 2.2 %copy-done.3 = bf16[512,4096]{1,0:T(8,128)(2,1)S(1)} copy-done((bf16[512,4096]{1,0:T(8,128)(2,1)S(1)}, bf16[512,4096]{1,0:T(8,128)(2,1)}, u32[]{:S(2)}) %copy-start.3) | copy-done | bytes 4194328
  88.1 2.4 %shard_map.230 = (bf16[256,1024]{1,0:T(8,128)(2,1)S(1)}, bf16[256,1024]{1,0:T(8,128)(2,1)S(1)}, bf16[256,1024]{1,0:T(8,128)(2,1)S(1)}, bf16[256,1024]{1,0:T(8,128)(2,1)S(1)}, f32[16,2048]{1,0:T(8,128)S(1)}) custom-call(s32[3]{0:T(128)S(1)} %copy-done.7, bf16[512,512]{1,0:T(8,128)(2,1)S(1)} %get-tuple-element.98.gated_ref.channels_ref, ...), custom_call_target="tpu_custom_call" | custom-call | bytes 1000 | tf_op jit(solution)/shard_map/pallas_call | solution.py:60
  90.6 1.0 collective-permute-start.14
  91.5 0.9 collective-permute-start.15
  92.4 6.0 %collective-permute-done.19.upper_got = bf16[256,1024]{1,0:T(8,128)(2,1)} collective-permute-done((bf16[256,1024]{1,0:T(8,128)(2,1)}, bf16[256,1024]{1,0:T(8,128)(2,1)}, u32[]{:S(2)}, u32[]{:S(2)}) %collective-permute-start.19) | collective-permute-done | bytes 524320 | tf_op jit(solution)/shard_map/ppermute | solution.py:27
  98.4 1.3 collective-permute-done.20.lower_got
  101.0 1.4 %shard_map.234 = (f32[256,512]{1,0:T(8,128)S(1)}, bf16[256,512]{1,0:T(8,128)(2,1)S(1)}, f32[256,512]{1,0:T(8,128)S(1)}, bf16[256,512]{1,0:T(8,128)(2,1)S(1)}) custom-call(s32[1]{0:T(128)} %constant.31.clone.1.unused, bf16[256,1024]{1,0:T(8,128)(2,1)S(1)} %get-tuple-element.116.upper_ref, bf16[256,1024]{1,0:T(8,128)(2,1)} %collective-permute-done.19.upper_got, ...), custom_call_target="tpu_custom_call" | custom-call | flops 10000000000 | bytes 100000000 | tf_op jit(solution)/shard_map/pallas_call | solution.py:60
  102.4 1.0 collective-permute-start.21
  103.4 0.9 collective-permute-start.22
  104.3 2.0 %collective-permute-done.26 = bf16[16,4096]{1,0:T(8,128)(2,1)S(1)} collective-permute-done((bf16[16,4096]{1,0:T(8,128)(2,1)S(1)}, bf16[16,4096]{1,0:T(8,128)(2,1)S(1)}, u32[]{:S(2)}, u32[]{:S(2)}) %collective-permute-start.26) | collective-permute-done | bytes 131104 | tf_op jit(solution)/shard_map/ppermute | solution.py:27
  106.3 1.0 collective-permute-start.27
  107.3 2.2 %collective-permute-done.14.upper_got = bf16[256,1024]{1,0:T(8,128)(2,1)S(1)} collective-permute-done((bf16[256,1024]{1,0:T(8,128)(2,1)S(1)}, bf16[256,1024]{1,0:T(8,128)(2,1)S(1)}, u32[]{:S(2)}, u32[]{:S(2)}) %collective-permute-start.14) | collective-permute-done | bytes 524320 | tf_op jit(solution)/shard_map/ppermute | solution.py:27
  109.5 1.3 collective-permute-done.15.lower_got
  111.1 1.0 collective-permute-start.16
  112.1 0.9 collective-permute-start.17
  113.5 0.8 collective-permute-start.28
  114.2 2.3 %collective-permute-done.21.upper_got = bf16[256,512]{1,0:T(8,128)(2,1)S(1)} collective-permute-done((bf16[256,512]{1,0:T(8,128)(2,1)S(1)}, bf16[256,512]{1,0:T(8,128)(2,1)S(1)}, u32[]{:S(2)}, u32[]{:S(2)}) %collective-permute-start.21) | collective-permute-done | bytes 262176 | tf_op jit(solution)/shard_map/ppermute | solution.py:27
  116.6 0.9 collective-permute-start.23
  117.5 2.1 %collective-permute-start.24 = (bf16[512,256]{1,0:T(8,128)(2,1)S(1)}, bf16[512,256]{1,0:T(8,128)(2,1)S(1)}, u32[]{:S(2)}, u32[]{:S(2)}) collective-permute-start(bf16[512,256]{1,0:T(8,128)(2,1)S(1)} %get-tuple-element.125), channel_id=1, source_target_pairs={{1,0},{2,1},{3,2},{0,3},{5,4},{6,5},{7,6},{4,7},{9,8},{10,9},{11,1... | collective-permute-start | bytes 786440 | tf_op jit(solution)/shard_map/ppermute | solution.py:32
  119.6 1.4 %shard_map.237 = f32[8,512,128]{2,1,0:T(8,128)S(1)} custom-call(s32[1]{0:T(128)} %bitcast.16.first, bf16[512,512]{1,0:T(8,128)(2,1)S(1)} %get-tuple-element.126.spread_ref, bf16[512,128]{1,0:T(8,128)(2,1)S(1)} %get-tuple-element.92.keys_ref, s32[512,128]{1,0:T(8,128)S(1)} %get-tuple-element.90.marks_ref, f32[16,1,128]{2,1,0:T(1,128)S(1)} %bitcast.37, ...), custom_call_target="tpu_custom_call" | custom-call | bytes 1000 | tf_op jit(solution)/shard_map/pallas_call | solution.py:60
  121.5 1.2 collective-permute-start.29
  122.8 1.1 collective-permute-start.18
  123.9 3.6 %collective-permute-done.29 = bf16[16,4096]{1,0:T(8,128)(2,1)S(1)} collective-permute-done((bf16[16,4096]{1,0:T(8,128)(2,1)S(1)}, bf16[16,4096]{1,0:T(8,128)(2,1)S(1)}, u32[]{:S(2)}, u32[]{:S(2)}) %collective-permute-start.29) | collective-permute-done | bytes 131104 | tf_op jit(solution)/shard_map/ppermute | solution.py:27
  127.6 2.8 %shard_map.238 = f32[8,512,128]{2,1,0:T(8,128)} custom-call(s32[1]{0:T(128)} %bitcast.14.first, bf16[512,512]{1,0:T(8,128)(2,1)S(1)} %get-tuple-element.126.spread_ref, bf16[512,128]{1,0:T(8,128)(2,1)S(1)} %get-tuple-element.92.keys_ref, s32[512,128]{1,0:T(8,128)S(1)} %get-tuple-element.90.marks_ref, f32[16,1,128]{2,1,0:T(1,128)S(1)} %bitcast.38, ...), custom_call_target="tpu_custom_call" | custom-call | bytes 1000 | tf_op jit(solution)/shard_map/pallas_call | solution.py:60
  130.4 4.7 %collective-permute-done.23.refs_1_ = bf16[512,256]{1,0:T(8,128)(2,1)S(1)} collective-permute-done((bf16[512,256]{1,0:T(8,128)(2,1)S(1)}, bf16[512,256]{1,0:T(8,128)(2,1)S(1)}, u32[]{:S(2)}, u32[]{:S(2)}) %collective-permute-start.23) | collective-permute-done | bytes 262176 | tf_op jit(solution)/shard_map/ppermute | solution.py:32
  135.1 0.9 shard_map.236
  136.2 1.2 slice-done.1
  137.4 1.9 %fusion.7 = f32[16,1024]{1,0:T(8,128)} fusion(bf16[4096,1024]{1,0:T(8,128)(2,1)S(1)} %bitcast.41, bf16[16,4096]{1,0:T(8,128)(2,1)S(1)} %get-tuple-element.138, f32[4096]{0:T(1024)S(1)} %copy-done.15, f32[16]{0:T(128)S(1)} %add_rsqrt_fusion), kind=kOutput, calls=%fused_computation.20 | convolution fusion | flops 134479872 | bytes 8601664 | tf_op jit(solution)/shard_map/dot_general | solution.py:936
  (108 shorter events, 8.0 us)
Async XLA Ops:
  0.6 38.8 %copy-start = (bf16[16,3,2,2,128]{4,3,2,1,0:T(2,128)(2,1)S(1)}, bf16[16,3,2,2,128]{4,3,2,1,0:T(2,128)(2,1)}, u32[]{:S(2)}) copy-start(bf16[16,3,2,2,128]{4,3,2,1,0:T(2,128)(2,1)} %param.33) | copy-start | bytes 147460
  0.6 11.0 %collective-permute-start = (bf16[512,256]{1,0:T(8,128)(2,1)}, bf16[512,256]{1,0:T(8,128)(2,1)S(1)}, u32[]{:S(2)}, u32[]{:S(2)}) collective-permute-start(bf16[512,256]{1,0:T(8,128)(2,1)} %tokens_ref.1), channel_id=1, source_target_pairs={{1,0},{2,1},{3,2},{0,3},{5,4},{6,5},{7,6},{4,7},{9,8},{10,9},{11,1... | collective-permute-start | bytes 786440 | tf_op jit(solution)/shard_map/ppermute | solution.py:32
  11.7 14.6 %collective-permute-start.7 = (bf16[256,512]{1,0:T(8,128)(2,1)S(1)}, bf16[256,512]{1,0:T(8,128)(2,1)S(1)}, u32[]{:S(2)}, u32[]{:S(2)}) collective-permute-start(bf16[256,512]{1,0:T(8,128)(2,1)S(1)} %get-tuple-element.140.refs_0_), channel_id=1, source_target_pairs={{0,8},{4,12},{8,0},{12,4},{1,9},{5,13},{9,1},{13,5},{2,10},{6,14},... | collective-permute-start | bytes 786440 | tf_op jit(solution)/shard_map/ppermute | solution.py:27
  13.3 14.4 %collective-permute-start.9 = (bf16[256,512]{1,0:T(8,128)(2,1)S(1)}, bf16[256,512]{1,0:T(8,128)(2,1)S(1)}, u32[]{:S(2)}, u32[]{:S(2)}) collective-permute-start(bf16[256,512]{1,0:T(8,128)(2,1)S(1)} %get-tuple-element.139.refs_3_), channel_id=1, source_target_pairs={{0,4},{4,0},{8,12},{12,8},{1,5},{5,1},{9,13},{13,9},{2,6},{6,2},{1... | collective-permute-start | bytes 786440 | tf_op jit(solution)/shard_map/ppermute | solution.py:27
  14.8 21.5 %collective-permute-start.2 = (bf16[512,256]{1,0:T(8,128)(2,1)}, bf16[512,256]{1,0:T(8,128)(2,1)S(1)}, u32[]{:S(2)}, u32[]{:S(2)}) collective-permute-start(bf16[512,256]{1,0:T(8,128)(2,1)} %tokens_ref.1), channel_id=1, source_target_pairs={{3,0},{0,1},{1,2},{2,3},{7,4},{4,5},{5,6},{6,7},{11,8},{8,9},{9,10... | collective-permute-start | bytes 786440 | tf_op jit(solution)/shard_map/ppermute | solution.py:32
  22.2 14.0 %collective-permute-start.1 = (bf16[512,256]{1,0:T(8,128)(2,1)S(1)}, bf16[512,256]{1,0:T(8,128)(2,1)S(1)}, u32[]{:S(2)}, u32[]{:S(2)}) collective-permute-start(bf16[512,256]{1,0:T(8,128)(2,1)S(1)} %collective-permute-done), channel_id=1, source_target_pairs={{1,0},{2,1},{3,2},{0,3},{5,4},{6,5},{7,6},{4,7},{9,8},{10,9},{11,1... | collective-permute-start | bytes 786440 | tf_op jit(solution)/shard_map/ppermute | solution.py:32
  27.2 21.5 %collective-permute-start.8 = (bf16[256,1024]{1,0:T(8,128)(2,1)}, bf16[256,1024]{1,0:T(8,128)(2,1)S(1)}, u32[]{:S(2)}, u32[]{:S(2)}) collective-permute-start(bf16[256,1024]{1,0:T(8,128)(2,1)} %pad_maximum_fusion.2), channel_id=1, source_target_pairs={{0,4},{4,0},{8,12},{12,8},{1,5},{5,1},{9,13},{13,9},{2,6},{6,2},{1... | collective-permute-start | bytes 1572872 | tf_op jit(solution)/shard_map/ppermute | solution.py:27
  28.6 11.1 %copy-start.16 = (bf16[16,3,512]{2,0,1:T(8,128)(2,1)S(1)}, bf16[16,3,512]{2,0,1:T(8,128)(2,1)}, u32[]{:S(2)}) copy-start(bf16[16,3,512]{2,0,1:T(8,128)(2,1)} %param.32) | copy-start | bytes 147460
  28.6 11.2 %copy-start.19 = (f32[4,2,2,128]{3,2,1,0:T(2,128)S(1)}, f32[4,2,2,128]{3,2,1,0:T(2,128)}, u32[]{:S(2)}) copy-start(f32[4,2,2,128]{3,2,1,0:T(2,128)} %param.29) | copy-start | bytes 24580
  28.6 11.2 %copy-start.17 = (f32[4,512]{1,0:T(4,128)S(1)}, f32[4,512]{1,0:T(4,128)}, u32[]{:S(2)}) copy-start(f32[4,512]{1,0:T(4,128)} %param.28) | copy-start | bytes 24580
  28.6 11.2 %copy-start.20 = (f32[2,2,128]{2,1,0:T(2,128)S(1)}, f32[2,2,128]{2,1,0:T(2,128)}, u32[]{:S(2)}) copy-start(f32[2,2,128]{2,1,0:T(2,128)} %param.31) | copy-start | bytes 6148
  28.6 20.1 %collective-permute-start.10 = (bf16[256,1024]{1,0:T(8,128)(2,1)}, bf16[256,1024]{1,0:T(8,128)(2,1)}, u32[]{:S(2)}, u32[]{:S(2)}) collective-permute-start(bf16[256,1024]{1,0:T(8,128)(2,1)} %pad_maximum_fusion.3), channel_id=1, source_target_pairs={{0,8},{4,12},{8,0},{12,4},{1,9},{5,13},{9,1},{13,5},{2,10},{6,14},... | collective-permute-start | bytes 1572872 | tf_op jit(solution)/shard_map/ppermute | solution.py:27
  36.3 12.5 %copy-start.13 = (f32[1,2048]{1,0:T(1,128)S(1)}, f32[1,2048]{1,0:T(1,128)}, u32[]{:S(2)}) copy-start(f32[1,2048]{1,0:T(1,128)} %get-tuple-element.76.refs_7_) | copy-start | bytes 24580
  36.4 8.6 %collective-permute-start.5 = (bf16[256,512]{1,0:T(8,128)(2,1)S(1)}, bf16[256,512]{1,0:T(8,128)(2,1)S(1)}, u32[]{:S(2)}, u32[]{:S(2)}) collective-permute-start(bf16[256,512]{1,0:T(8,128)(2,1)S(1)} %get-tuple-element.141.refs_3_), channel_id=1, source_target_pairs={{0,4},{4,0},{8,12},{12,8},{1,5},{5,1},{9,13},{13,9},{2,6},{6,2},{1... | collective-permute-start | bytes 786440 | tf_op jit(solution)/shard_map/ppermute | solution.py:27
  37.9 9.1 %collective-permute-start.3 = (bf16[256,512]{1,0:T(8,128)(2,1)S(1)}, bf16[256,512]{1,0:T(8,128)(2,1)S(1)}, u32[]{:S(2)}, u32[]{:S(2)}) collective-permute-start(bf16[256,512]{1,0:T(8,128)(2,1)S(1)} %get-tuple-element.142.refs_0_), channel_id=1, source_target_pairs={{0,8},{4,12},{8,0},{12,4},{1,9},{5,13},{9,1},{13,5},{2,10},{6,14},... | collective-permute-start | bytes 786440 | tf_op jit(solution)/shard_map/ppermute | solution.py:27
  45.0 12.4 %collective-permute-start.6 = (bf16[256,1024]{1,0:T(8,128)(2,1)S(1)}, bf16[256,1024]{1,0:T(8,128)(2,1)S(1)}, u32[]{:S(2)}, u32[]{:S(2)}) collective-permute-start(bf16[256,1024]{1,0:T(8,128)(2,1)S(1)} %pad_maximum_fusion.1), channel_id=1, source_target_pairs={{0,8},{4,12},{8,0},{12,4},{1,9},{5,13},{9,1},{13,5},{2,10},{6,14},... | collective-permute-start | bytes 1572872 | tf_op jit(solution)/shard_map/ppermute | solution.py:27
  47.1 10.5 %collective-permute-start.4 = (bf16[256,1024]{1,0:T(8,128)(2,1)S(1)}, bf16[256,1024]{1,0:T(8,128)(2,1)S(1)}, u32[]{:S(2)}, u32[]{:S(2)}) collective-permute-start(bf16[256,1024]{1,0:T(8,128)(2,1)S(1)} %pad_maximum_fusion), channel_id=1, source_target_pairs={{0,4},{4,0},{8,12},{12,8},{1,5},{5,1},{9,13},{13,9},{2,6},{6,2},{1... | collective-permute-start | bytes 1572872 | tf_op jit(solution)/shard_map/ppermute | solution.py:27
  48.7 2.6 %copy-start.11 = (bf16[2048,1408]{1,0:T(8,128)(2,1)S(1)}, bf16[2048,1408]{1,0:T(8,128)(2,1)}, u32[]{:S(2)}) copy-start(bf16[2048,1408]{1,0:T(8,128)(2,1)} %get-tuple-element.77.refs_8_) | copy-start | bytes 17301508
  51.3 6.3 %copy-start.14 = (f32[1,2048]{1,0:T(1,128)S(1)}, f32[1,2048]{1,0:T(1,128)}, u32[]{:S(2)}) copy-start(f32[1,2048]{1,0:T(1,128)} %get-tuple-element.74.refs_7_) | copy-start | bytes 24580
  57.6 2.6 %copy-start.12 = (bf16[2048,1408]{1,0:T(8,128)(2,1)S(1)}, bf16[2048,1408]{1,0:T(8,128)(2,1)}, u32[]{:S(2)}) copy-start(bf16[2048,1408]{1,0:T(8,128)(2,1)} %get-tuple-element.75.refs_8_) | copy-start | bytes 17301508
  60.2 5.5 %copy-start.18 = (f32[512]{0:T(512)S(1)}, f32[512]{0:T(512)}, u32[]{:S(2)}) copy-start(f32[512]{0:T(512)} %param.30) | copy-start | bytes 6148
  60.2 5.5 %copy-start.4 = (f32[16,8,64,128]{3,2,1,0:T(8,128)S(1)}, f32[16,8,64,128]{3,2,1,0:T(8,128)}, u32[]{:S(2)}) copy-start(f32[16,8,64,128]{3,2,1,0:T(8,128)} %param.34) | copy-start | bytes 12582916
  64.2 2.5 %collective-permute-start.11 = (bf16[16,768]{1,0:T(8,128)(2,1)S(1)}, bf16[16,768]{1,0:T(8,128)(2,1)S(1)}, u32[]{:S(2)}, u32[]{:S(2)}) collective-permute-start(bf16[16,768]{1,0:T(8,128)(2,1)S(1)} %slice.31), channel_id=1, source_target_pairs={{0,16},{1,17},{2,18},{3,19},{4,20},{5,21},{6,22},{7,23},{8,24},{9,... | collective-permute-start | bytes 73736 | tf_op jit(solution)/shard_map/ppermute | solution.py:23
  66.7 6.1 %copy-start.21 = (f32[8]{0:T(128)S(1)}, f32[8]{0:T(128)}, u32[]{:S(2)}) copy-start(f32[8]{0:T(128)} %param.37) | copy-start | bytes 100
  70.8 5.3 %copy-start.10 = (f32[512]{0:T(512)S(1)}, f32[512]{0:T(512)}, u32[]{:S(2)}) copy-start(f32[512]{0:T(512)} %param.38) | copy-start | bytes 6148
  70.8 5.2 %collective-permute-start.12 = (f32[512,128]{1,0:T(8,128)S(1)}, f32[512,128]{1,0:T(8,128)S(1)}, u32[]{:S(2)}, u32[]{:S(2)}) collective-permute-start(f32[512,128]{1,0:T(8,128)S(1)} %get-tuple-element.96), channel_id=1, source_target_pairs={{0,16},{1,17},{2,18},{3,19},{4,20},{5,21},{6,22},{7,23},{8,24},{9,... | collective-permute-start | bytes 786440 | tf_op jit(solution)/shard_map/ppermute | solution.py:23
  76.0 2.2 %copy-start.2 = (bf16[512,4096]{1,0:T(8,128)(2,1)S(1)}, bf16[512,4096]{1,0:T(8,128)(2,1)}, u32[]{:S(2)}) copy-start(bf16[512,4096]{1,0:T(8,128)(2,1)} %refs_7_.7) | copy-start | bytes 12582916
  76.0 2.2 %copy-start.7 = (s32[3]{0:T(128)S(1)}, s32[3]{0:T(128)}, u32[]{:S(2)}) copy-start(s32[3]{0:T(128)} %pad_add_fusion.place.blocks) | copy-start | bytes 40
  77.2 3.8 %collective-permute-start.13 = (f32[8,512]{1,0:T(8,128)S(1)}, f32[8,512]{1,0:T(8,128)S(1)}, u32[]{:S(2)}, u32[]{:S(2)}) collective-permute-start(f32[8,512]{1,0:T(8,128)S(1)} %get-tuple-element.99.own_ref.other_ref), channel_id=1, source_target_pairs={{0,1},{1,0},{2,3},{3,2},{4,5},{5,4},{6,7},{7,6},{8,9},{9,8},{10,11... | collective-permute-start | bytes 49160 | tf_op jit(solution)/shard_map/ppermute | solution.py:27
  82.4 0.8 copy-start.8
  83.2 15.2 %collective-permute-start.19 = (bf16[256,1024]{1,0:T(8,128)(2,1)}, bf16[256,1024]{1,0:T(8,128)(2,1)}, u32[]{:S(2)}, u32[]{:S(2)}) collective-permute-start(bf16[256,1024]{1,0:T(8,128)(2,1)} %get-tuple-element.117), channel_id=1, source_target_pairs={{0,4},{4,0},{8,12},{12,8},{1,5},{5,1},{9,13},{13,9},{2,6},{6,2},{1... | collective-permute-start | bytes 1572872 | tf_op jit(solution)/shard_map/ppermute | solution.py:27
  84.5 15.2 %collective-permute-start.20 = (bf16[256,1024]{1,0:T(8,128)(2,1)}, bf16[256,1024]{1,0:T(8,128)(2,1)}, u32[]{:S(2)}, u32[]{:S(2)}) collective-permute-start(bf16[256,1024]{1,0:T(8,128)(2,1)} %get-tuple-element.119), channel_id=1, source_target_pairs={{0,8},{4,12},{8,0},{12,4},{1,9},{5,13},{9,1},{13,5},{2,10},{6,14},... | collective-permute-start | bytes 1572872 | tf_op jit(solution)/shard_map/ppermute | solution.py:27
  85.9 2.2 %copy-start.3 = (bf16[512,4096]{1,0:T(8,128)(2,1)S(1)}, bf16[512,4096]{1,0:T(8,128)(2,1)}, u32[]{:S(2)}) copy-start(bf16[512,4096]{1,0:T(8,128)(2,1)} %refs_7_.7) | copy-start | bytes 12582916
  88.1 12.9 %copy-start.9 = (bf16[256,1024]{1,0:T(8,128)(2,1)S(1)}, bf16[256,1024]{1,0:T(8,128)(2,1)}, u32[]{:S(2)}) copy-start(bf16[256,1024]{1,0:T(8,128)(2,1)} %copy-done.8) | copy-start | bytes 1572868
  90.6 19.0 %collective-permute-start.14 = (bf16[256,1024]{1,0:T(8,128)(2,1)S(1)}, bf16[256,1024]{1,0:T(8,128)(2,1)S(1)}, u32[]{:S(2)}, u32[]{:S(2)}) collective-permute-start(bf16[256,1024]{1,0:T(8,128)(2,1)S(1)} %get-tuple-element.103), channel_id=1, source_target_pairs={{0,4},{4,0},{8,12},{12,8},{1,5},{5,1},{9,13},{13,9},{2,6},{6,2},{1... | collective-permute-start | bytes 1572872 | tf_op jit(solution)/shard_map/ppermute | solution.py:27
  91.5 19.3 %collective-permute-start.15 = (bf16[256,1024]{1,0:T(8,128)(2,1)S(1)}, bf16[256,1024]{1,0:T(8,128)(2,1)S(1)}, u32[]{:S(2)}, u32[]{:S(2)}) collective-permute-start(bf16[256,1024]{1,0:T(8,128)(2,1)S(1)} %get-tuple-element.105), channel_id=1, source_target_pairs={{0,8},{4,12},{8,0},{12,4},{1,9},{5,13},{9,1},{13,5},{2,10},{6,14},... | collective-permute-start | bytes 1572872 | tf_op jit(solution)/shard_map/ppermute | solution.py:27
  100.4 5.9 %collective-permute-start.26 = (bf16[16,4096]{1,0:T(8,128)(2,1)S(1)}, bf16[16,4096]{1,0:T(8,128)(2,1)S(1)}, u32[]{:S(2)}, u32[]{:S(2)}) collective-permute-start(bf16[16,4096]{1,0:T(8,128)(2,1)S(1)} %convert_element_type.38), channel_id=1, source_target_pairs={{0,1},{1,0},{2,3},{3,2},{4,5},{5,4},{6,7},{7,6},{8,9},{9,8},{10,11... | collective-permute-start | bytes 393224 | tf_op jit(solution)/shard_map/ppermute | solution.py:27
  102.4 14.0 %collective-permute-start.21 = (bf16[256,512]{1,0:T(8,128)(2,1)S(1)}, bf16[256,512]{1,0:T(8,128)(2,1)S(1)}, u32[]{:S(2)}, u32[]{:S(2)}) collective-permute-start(bf16[256,512]{1,0:T(8,128)(2,1)S(1)} %get-tuple-element.121), channel_id=1, source_target_pairs={{0,8},{4,12},{8,0},{12,4},{1,9},{5,13},{9,1},{13,5},{2,10},{6,14},... | collective-permute-start | bytes 786440 | tf_op jit(solution)/shard_map/ppermute | solution.py:27
  103.4 13.0 %collective-permute-start.22 = (bf16[256,512]{1,0:T(8,128)(2,1)S(1)}, bf16[256,512]{1,0:T(8,128)(2,1)S(1)}, u32[]{:S(2)}, u32[]{:S(2)}) collective-permute-start(bf16[256,512]{1,0:T(8,128)(2,1)S(1)} %get-tuple-element.123), channel_id=1, source_target_pairs={{0,4},{4,0},{8,12},{12,8},{1,5},{5,1},{9,13},{13,9},{2,6},{6,2},{1... | collective-permute-start | bytes 786440 | tf_op jit(solution)/shard_map/ppermute | solution.py:27
  106.3 7.1 %collective-permute-start.27 = (bf16[16,4096]{1,0:T(8,128)(2,1)S(1)}, bf16[16,4096]{1,0:T(8,128)(2,1)S(1)}, u32[]{:S(2)}, u32[]{:S(2)}) collective-permute-start(bf16[16,4096]{1,0:T(8,128)(2,1)S(1)} %fusion.5), channel_id=1, source_target_pairs={{0,2},{1,3},{2,0},{3,1},{4,6},{5,7},{6,4},{7,5},{8,10},{9,11},{10,... | collective-permute-start | bytes 393224 | tf_op jit(solution)/shard_map/ppermute | solution.py:27
  111.1 10.4 %collective-permute-start.16 = (bf16[256,512]{1,0:T(8,128)(2,1)S(1)}, bf16[256,512]{1,0:T(8,128)(2,1)S(1)}, u32[]{:S(2)}, u32[]{:S(2)}) collective-permute-start(bf16[256,512]{1,0:T(8,128)(2,1)S(1)} %get-tuple-element.107), channel_id=1, source_target_pairs={{0,8},{4,12},{8,0},{12,4},{1,9},{5,13},{9,1},{13,5},{2,10},{6,14},... | collective-permute-start | bytes 786440 | tf_op jit(solution)/shard_map/ppermute | solution.py:27
  112.1 10.6 %collective-permute-start.17 = (bf16[256,512]{1,0:T(8,128)(2,1)S(1)}, bf16[256,512]{1,0:T(8,128)(2,1)S(1)}, u32[]{:S(2)}, u32[]{:S(2)}) collective-permute-start(bf16[256,512]{1,0:T(8,128)(2,1)S(1)} %get-tuple-element.109), channel_id=1, source_target_pairs={{0,4},{4,0},{8,12},{12,8},{1,5},{5,1},{9,13},{13,9},{2,6},{6,2},{1... | collective-permute-start | bytes 786440 | tf_op jit(solution)/shard_map/ppermute | solution.py:27
  113.5 8.0 %collective-permute-start.28 = (bf16[16,4096]{1,0:T(8,128)(2,1)S(1)}, bf16[16,4096]{1,0:T(8,128)(2,1)S(1)}, u32[]{:S(2)}, u32[]{:S(2)}) collective-permute-start(bf16[16,4096]{1,0:T(8,128)(2,1)S(1)} %fusion.11), channel_id=1, source_target_pairs={{0,4},{4,0},{8,12},{12,8},{1,5},{5,1},{9,13},{13,9},{2,6},{6,2},{1... | collective-permute-start | bytes 393224 | tf_op jit(solution)/shard_map/ppermute | solution.py:27
  116.5 3.1 %copy-start.5 = (f32[16,8,64,128]{3,2,1,0:T(8,128)S(1)}, f32[16,8,64,128]{3,2,1,0:T(8,128)}, u32[]{:S(2)}) copy-start(f32[16,8,64,128]{3,2,1,0:T(8,128)} %param.34) | copy-start | bytes 12582916
  116.6 18.5 %collective-permute-start.23 = (bf16[512,256]{1,0:T(8,128)(2,1)S(1)}, bf16[512,256]{1,0:T(8,128)(2,1)S(1)}, u32[]{:S(2)}, u32[]{:S(2)}) collective-permute-start(bf16[512,256]{1,0:T(8,128)(2,1)S(1)} %get-tuple-element.124), channel_id=1, source_target_pairs={{2,0},{3,1},{0,2},{1,3},{6,4},{7,5},{4,6},{5,7},{10,8},{11,9},{8,1... | collective-permute-start | bytes 786440 | tf_op jit(solution)/shard_map/ppermute | solution.py:32
  117.5 17.6 %collective-permute-start.24 = (bf16[512,256]{1,0:T(8,128)(2,1)S(1)}, bf16[512,256]{1,0:T(8,128)(2,1)S(1)}, u32[]{:S(2)}, u32[]{:S(2)}) collective-permute-start(bf16[512,256]{1,0:T(8,128)(2,1)S(1)} %get-tuple-element.125), channel_id=1, source_target_pairs={{1,0},{2,1},{3,2},{0,3},{5,4},{6,5},{7,6},{4,7},{9,8},{10,9},{11,1... | collective-permute-start | bytes 786440 | tf_op jit(solution)/shard_map/ppermute | solution.py:32
  121.4 6.1 %collective-permute-start.25 = (f32[8,512,128]{2,1,0:T(8,128)S(1)}, f32[8,512,128]{2,1,0:T(8,128)S(1)}, u32[]{:S(2)}, u32[]{:S(2)}) collective-permute-start(f32[8,512,128]{2,1,0:T(8,128)S(1)} %shard_map.237), channel_id=1, source_target_pairs={{0,16},{16,0},{1,17},{17,1},{2,18},{18,2},{3,19},{19,3},{4,20},{20... | collective-permute-start | bytes 6291464 | tf_op jit(solution)/shard_map/ppermute | solution.py:27
  121.5 6.0 %collective-permute-start.29 = (bf16[16,4096]{1,0:T(8,128)(2,1)S(1)}, bf16[16,4096]{1,0:T(8,128)(2,1)S(1)}, u32[]{:S(2)}, u32[]{:S(2)}) collective-permute-start(bf16[16,4096]{1,0:T(8,128)(2,1)S(1)} %fusion.6), channel_id=1, source_target_pairs={{0,8},{4,12},{8,0},{12,4},{1,9},{5,13},{9,1},{13,5},{2,10},{6,14},... | collective-permute-start | bytes 393224 | tf_op jit(solution)/shard_map/ppermute | solution.py:27
  122.8 12.3 %collective-permute-start.18 = (bf16[512,256]{1,0:T(8,128)(2,1)S(1)}, bf16[512,256]{1,0:T(8,128)(2,1)S(1)}, u32[]{:S(2)}, u32[]{:S(2)}) collective-permute-start(bf16[512,256]{1,0:T(8,128)(2,1)S(1)} %get-tuple-element.111), channel_id=1, source_target_pairs={{3,0},{0,1},{1,2},{2,3},{7,4},{4,5},{5,6},{6,7},{11,8},{8,9},{9,10... | collective-permute-start | bytes 786440 | tf_op jit(solution)/shard_map/ppermute | solution.py:32
  127.6 7.5 %copy-start.6 = (bf16[512,256]{1,0:T(8,128)(2,1)S(1)}, bf16[512,256]{1,0:T(8,128)(2,1)}, u32[]{:S(2)}) copy-start(bf16[512,256]{1,0:T(8,128)(2,1)} %tokens_ref.1) | copy-start | bytes 786436
  127.6 8.6 %slice-start = ((s8[8388608]{0:T(1024)(128)(4,1)}), s8[4194304]{0:T(1024)(128)(4,1)S(1)}, s32[]{:S(2)}) async-start(s8[8388608]{0:T(1024)(128)(4,1)} %bitcast.40), calls=%async_computation | async-start | bytes 8388608
  130.4 5.6 %collective-permute-start.30 = (f32[16,4096]{1,0:T(8,128)S(1)}, f32[16,4096]{1,0:T(8,128)S(1)}, u32[]{:S(2)}, u32[]{:S(2)}) collective-permute-start(f32[16,4096]{1,0:T(8,128)S(1)} %add_add_fusion), channel_id=1, source_target_pairs={{0,16},{16,0},{1,17},{17,1},{2,18},{18,2},{3,19},{19,3},{4,20},{20... | collective-permute-start | bytes 786440 | tf_op jit(solution)/shard_map/ppermute | solution.py:27
  135.1 2.3 %slice-start.1 = ((s8[8388608]{0:T(1024)(128)(4,1)}), s8[4194304]{0:T(1024)(128)(4,1)S(1)}, s32[]{:S(2)}) async-start(s8[8388608]{0:T(1024)(128)(4,1)} %bitcast.40), calls=%async_computation.1 | async-start | bytes 8388608
  135.1 2.3 %copy-start.15 = (f32[4096]{0:T(1024)S(1)}, f32[4096]{0:T(1024)}, u32[]{:S(2)}) copy-start(f32[4096]{0:T(1024)} %param.40) | copy-start | bytes 49156
  136.2 3.1 %copy-start.1 = (bf16[16,3,2,2,128]{4,3,2,1,0:T(2,128)(2,1)S(1)}, bf16[16,3,2,2,128]{4,3,2,1,0:T(2,128)(2,1)}, u32[]{:S(2)}) copy-start(bf16[16,3,2,2,128]{4,3,2,1,0:T(2,128)(2,1)} %param.33) | copy-start | bytes 147460

commit v5 on v4

--- a/solution.py
+++ b/solution.py
@@ -731,6 +731,7 @@
         after(marks, table),
         segment_row,
         init_last,
+        work=4,
     )
     entry = from_behind(leaving, "seq", 1)
     for _ in range(seq_size - 2):
@@ -777,6 +778,7 @@
         entry,
         gate_in,
         inner_gain[None, :],
+        work=1,
     )
     other_squares = from_partner(own_squares, "col", 0)
 
@@ -805,7 +807,7 @@
                 for at in range(row_size * count)
             ],
             vmem=16,
-            work=10 if first else 0,
+            work=2 if first else 0,
         )
         if first:
             other_squares = after(other_squares, outs[0])

time: 140 us -> 139 us (level)
  waiting for transfers between devices: 30.7 us -> 28.5 us
  starting transfers between devices: 38.1 us -> 39.9 us
  transfers between devices with their start and end apart: 31 -> 31, of which waited for: 16 -> 14; matrix products, arithmetic and copies ran while one was open for 5% -> 5% of each run, Pallas kernels for 27% -> 27%
where the time goes in v5:
time: 139 us; the launch traced here: 138 us
  Pallas kernels  47.5 us (34%)
  starting transfers between devices  39.9 us (29%)
  waiting for transfers between devices  28.5 us (21%)
  local copies, waits for them, and re-layouts  13.4 us (10%)
  other arithmetic  3.72 us (3%)
  between operations  2.84 us (2%)
  matrix products  2.08 us (1%)
    pallas_call x19, Pallas kernels, call(): pl.pallas_call(kernel, out_shape=shapes, grid_spec=spec, compiler_params=...  44.3 us
    ppermute x23, waiting for transfers between devices, from_partner(): lax.ppermute(x, axis, [(i, i ^ 1 << bit) for i in range(lax.axis_size(axi...  23.5 us
    ppermute x23, starting transfers between devices, from_partner(): lax.ppermute(x, axis, [(i, i ^ 1 << bit) for i in range(lax.axis_size(axi...  21.8 us
    ppermute x6, starting transfers between devices, from_ahead(): lax.ppermute(x, axis, [((i + distance) % size, i) for i in range(size)])  14.4 us
    unnamed x52, local copies, waits for them, and re-layouts  10.6 us
    ppermute x6, waiting for transfers between devices, from_ahead(): lax.ppermute(x, axis, [((i + distance) % size, i) for i in range(size)])  5.07 us
    ppermute x2, starting transfers between devices, from_behind(): return lax.ppermute(block, axis, route)  3.66 us
    pallas_call x1, Pallas kernels, per_device(): pl.pallas_call(functools.partial(scan_kernel, heads, block), out_shape=ja...  3.18 us
  transfers between devices with their start and end apart: 31, of which 14 were waited for; matrix products, arithmetic and copies ran while one was open for 5% of the time, Pallas kernels for 27%

profile of v5, /device:TPU:0, one launch (start us, length us, event | category | flops | bytes accessed | tf_op | source)
XLA Modules:
  0.0 138.0 jit_solution(7206373680545379667)
XLA Ops:
  0.6 5.1 %collective-permute-start = (bf16[512,256]{1,0:T(8,128)(2,1)}, bf16[512,256]{1,0:T(8,128)(2,1)S(1)}, u32[]{:S(2)}, u32[]{:S(2)}) collective-permute-start(bf16[512,256]{1,0:T(8,128)(2,1)} %tokens_ref.1), channel_id=1, source_target_pairs={{1,0},{2,1},{3,2},{0,3},{5,4},{6,5},{7,6},{4,7},{9,8},{10,9},{11,1... | collective-permute-start | bytes 786440 | tf_op jit(solution)/shard_map/ppermute | solution.py:32
  6.4 0.7 pad_add_fusion.1.counts
  7.1 1.4 %shard_map.220 = (s32[512,128]{1,0:T(8,128)S(1)}, s32[8,512]{1,0:T(8,128)S(1)}, bf16[16,512]{1,0:T(8,128)(2,1)S(1)}, f32[16,256]{1,0:T(8,128)S(1)}) custom-call(s32[33]{0:T(128)S(1)} %pad_add_fusion.1.counts), custom_call_target="tpu_custom_call" | custom-call | bytes 1000 | tf_op jit(solution)/shard_map/pallas_call | solution.py:60
  8.5 0.7 pad_bitcast_fusion.1
  9.2 1.0 constant_dynamic-update-slice_fusion.3
  10.2 1.4 %collective-permute-done = bf16[512,256]{1,0:T(8,128)(2,1)S(1)} collective-permute-done((bf16[512,256]{1,0:T(8,128)(2,1)}, bf16[512,256]{1,0:T(8,128)(2,1)S(1)}, u32[]{:S(2)}, u32[]{:S(2)}) %collective-permute-start) | collective-permute-done | bytes 262176 | tf_op jit(solution)/shard_map/ppermute | solution.py:32
  11.7 1.6 %collective-permute-start.7 = (bf16[256,512]{1,0:T(8,128)(2,1)S(1)}, bf16[256,512]{1,0:T(8,128)(2,1)S(1)}, u32[]{:S(2)}, u32[]{:S(2)}) collective-permute-start(bf16[256,512]{1,0:T(8,128)(2,1)S(1)} %get-tuple-element.140.refs_0_), channel_id=1, source_target_pairs={{0,8},{4,12},{8,0},{12,4},{1,9},{5,13},{9,1},{13,5},{2,10},{6,14},... | collective-permute-start | bytes 786440 | tf_op jit(solution)/shard_map/ppermute | solution.py:27
  13.3 1.5 %collective-permute-start.9 = (bf16[256,512]{1,0:T(8,128)(2,1)S(1)}, bf16[256,512]{1,0:T(8,128)(2,1)S(1)}, u32[]{:S(2)}, u32[]{:S(2)}) collective-permute-start(bf16[256,512]{1,0:T(8,128)(2,1)S(1)} %get-tuple-element.139.refs_3_), channel_id=1, source_target_pairs={{0,4},{4,0},{8,12},{12,8},{1,5},{5,1},{9,13},{13,9},{2,6},{6,2},{1... | collective-permute-start | bytes 786440 | tf_op jit(solution)/shard_map/ppermute | solution.py:27
  15.1 7.1 %shard_map.222 = (bf16[2048,1408]{1,0:T(8,128)(2,1)}, f32[1,2048]{1,0:T(1,128)}) custom-call(s32[3]{0:T(128)} %pad_add_fusion.place.blocks, bf16[4096,2,512]{2,1,0:T(2,128)(2,1)} %refs_3_.5, bf16[4096,2,512]{2,1,0:T(2,128)(2,1)} %refs_3_.5, bf16[4096,2,512]{2,1,0:T(2,128)(2,1)} %refs_3_.5, bf16[4096,2,512]{2,1,0:T(2,128)(2,1)} %refs_3_.5, ...), custom_call_target="tpu_custom_call" | custom-call | flops 20000000000 | bytes 100000000 | tf_op jit(solution)/shard_map/pallas_call | solution.py:60
  22.2 4.1 %collective-permute-start.1 = (bf16[512,256]{1,0:T(8,128)(2,1)S(1)}, bf16[512,256]{1,0:T(8,128)(2,1)S(1)}, u32[]{:S(2)}, u32[]{:S(2)}) collective-permute-start(bf16[512,256]{1,0:T(8,128)(2,1)S(1)} %collective-permute-done), channel_id=1, source_target_pairs={{1,0},{2,1},{3,2},{0,3},{5,4},{6,5},{7,6},{4,7},{9,8},{10,9},{11,1... | collective-permute-start | bytes 786440 | tf_op jit(solution)/shard_map/ppermute | solution.py:32
  26.3 0.9 pad_maximum_fusion.2
  27.7 0.9 pad_maximum_fusion.3
  29.2 7.1 %shard_map.221 = (bf16[2048,1408]{1,0:T(8,128)(2,1)}, f32[1,2048]{1,0:T(1,128)}) custom-call(s32[3]{0:T(128)} %pad_add_fusion.place.blocks, bf16[4096,2,512]{2,1,0:T(2,128)(2,1)} %refs_3_.5, bf16[4096,2,512]{2,1,0:T(2,128)(2,1)} %refs_3_.5, bf16[4096,2,512]{2,1,0:T(2,128)(2,1)} %refs_3_.5, bf16[4096,2,512]{2,1,0:T(2,128)(2,1)} %refs_3_.5, ...), custom_call_target="tpu_custom_call" | custom-call | flops 20000000000 | bytes 100000000 | tf_op jit(solution)/shard_map/pallas_call | solution.py:60
  36.4 1.6 %collective-permute-start.5 = (bf16[256,512]{1,0:T(8,128)(2,1)S(1)}, bf16[256,512]{1,0:T(8,128)(2,1)S(1)}, u32[]{:S(2)}, u32[]{:S(2)}) collective-permute-start(bf16[256,512]{1,0:T(8,128)(2,1)S(1)} %get-tuple-element.141.refs_3_), channel_id=1, source_target_pairs={{0,4},{4,0},{8,12},{12,8},{1,5},{5,1},{9,13},{13,9},{2,6},{6,2},{1... | collective-permute-start | bytes 786440 | tf_op jit(solution)/shard_map/ppermute | solution.py:27
  37.9 1.5 %collective-permute-start.3 = (bf16[256,512]{1,0:T(8,128)(2,1)S(1)}, bf16[256,512]{1,0:T(8,128)(2,1)S(1)}, u32[]{:S(2)}, u32[]{:S(2)}) collective-permute-start(bf16[256,512]{1,0:T(8,128)(2,1)S(1)} %get-tuple-element.142.refs_0_), channel_id=1, source_target_pairs={{0,8},{4,12},{8,0},{12,4},{1,9},{5,13},{9,1},{13,5},{2,10},{6,14},... | collective-permute-start | bytes 786440 | tf_op jit(solution)/shard_map/ppermute | solution.py:27
  42.1 1.0 dynamic-slice_bitcast_fusion.init_ref
  43.0 1.9 %collective-permute-done.5.refs_4_ = bf16[256,512]{1,0:T(8,128)(2,1)S(1)} collective-permute-done((bf16[256,512]{1,0:T(8,128)(2,1)S(1)}, bf16[256,512]{1,0:T(8,128)(2,1)S(1)}, u32[]{:S(2)}, u32[]{:S(2)}) %collective-permute-start.5) | collective-permute-done | bytes 262176 | tf_op jit(solution)/shard_map/ppermute | solution.py:27
  45.6 1.5 %collective-permute-done.3.refs_1_ = bf16[256,512]{1,0:T(8,128)(2,1)S(1)} collective-permute-done((bf16[256,512]{1,0:T(8,128)(2,1)S(1)}, bf16[256,512]{1,0:T(8,128)(2,1)S(1)}, u32[]{:S(2)}, u32[]{:S(2)}) %collective-permute-start.3) | collective-permute-done | bytes 262176 | tf_op jit(solution)/shard_map/ppermute | solution.py:27
  47.1 1.6 %collective-permute-start.4 = (bf16[256,1024]{1,0:T(8,128)(2,1)S(1)}, bf16[256,1024]{1,0:T(8,128)(2,1)S(1)}, u32[]{:S(2)}, u32[]{:S(2)}) collective-permute-start(bf16[256,1024]{1,0:T(8,128)(2,1)S(1)} %pad_maximum_fusion), channel_id=1, source_target_pairs={{0,4},{4,0},{8,12},{12,8},{1,5},{5,1},{9,13},{13,9},{2,6},{6,2},{1... | collective-permute-start | bytes 1572872 | tf_op jit(solution)/shard_map/ppermute | solution.py:27
  48.7 2.6 %copy-done.11 = bf16[2048,1408]{1,0:T(8,128)(2,1)S(1)} copy-done((bf16[2048,1408]{1,0:T(8,128)(2,1)S(1)}, bf16[2048,1408]{1,0:T(8,128)(2,1)}, u32[]{:S(2)}) %copy-start.11) | copy-done | bytes 5767192
  51.3 5.0 %shard_map.223 = (f32[16,2048]{1,0:T(8,128)S(1)}, f32[512,1408]{1,0:T(8,128)S(1)}, f32[512,128]{1,0:T(8,128)S(1)}) custom-call(s32[1]{0:T(128)} %constant.31.clone.1.unused, bf16[256,512]{1,0:T(8,128)(2,1)S(1)} %get-tuple-element.140.refs_0_, bf16[256,512]{1,0:T(8,128)(2,1)S(1)} %collective-permute-done.7.refs_1_, ...), custom_call_target="tpu_custom_call" | custom-call | flops 20000000000 | bytes 100000000 | tf_op jit(solution)/shard_map/pallas_call | solution.py:60
  56.4 1.1 collective-permute-done.6.refs_5_
  57.6 2.6 %copy-done.12 = bf16[2048,1408]{1,0:T(8,128)(2,1)S(1)} copy-done((bf16[2048,1408]{1,0:T(8,128)(2,1)S(1)}, bf16[2048,1408]{1,0:T(8,128)(2,1)}, u32[]{:S(2)}) %copy-start.12) | copy-done | bytes 5767192
  60.2 3.9 %shard_map.224 = (f32[16,2048]{1,0:T(8,128)S(1)}, bf16[512,512]{1,0:T(8,128)(2,1)S(1)}, bf16[512,768]{1,0:T(8,128)(2,1)S(1)}, f32[512,128]{1,0:T(8,128)S(1)}) custom-call(s32[1]{0:T(128)} %constant.31.clone.1.unused, bf16[256,512]{1,0:T(8,128)(2,1)S(1)} %get-tuple-element.142.refs_0_, bf16[256,512]{1,0:T(8,128)(2,1)S(1)} %collective-permute-done.3.refs_1_, ...), custom_call_target="tpu_custom_call" | custom-call | flops 20000000000 | bytes 100000000 | tf_op jit(solution)/shard_map/pallas_call | solution.py:60
  64.2 1.5 %collective-permute-start.11 = (bf16[16,768]{1,0:T(8,128)(2,1)S(1)}, bf16[16,768]{1,0:T(8,128)(2,1)S(1)}, u32[]{:S(2)}, u32[]{:S(2)}) collective-permute-start(bf16[16,768]{1,0:T(8,128)(2,1)S(1)} %slice.31), channel_id=1, source_target_pairs={{0,16},{1,17},{2,18},{3,19},{4,20},{5,21},{6,22},{7,23},{8,24},{9,... | collective-permute-start | bytes 73736 | tf_op jit(solution)/shard_map/ppermute | solution.py:23
  65.8 0.9 shard_map.225.table_ref
  66.7 4.1 %shard_map.226 = (bf16[512,512]{1,0:T(8,128)(2,1)S(1)}, bf16[512,128]{1,0:T(8,128)(2,1)S(1)}, bf16[512,128]{1,0:T(8,128)(2,1)S(1)}, f32[512,128]{1,0:T(8,128)S(1...) custom-call(s32[1]{0:T(128)} %constant.31.clone.1.unused, ...), custom_call_target="tpu_custom_call" | custom-call | flops 4000000000 | bytes 100000000 | tf_op jit(solution)/shard_map/pallas_call | solution.py:60
  70.8 2.2 %collective-permute-start.12 = (f32[512,128]{1,0:T(8,128)S(1)}, f32[512,128]{1,0:T(8,128)S(1)}, u32[]{:S(2)}, u32[]{:S(2)}) collective-permute-start(f32[512,128]{1,0:T(8,128)S(1)} %get-tuple-element.96), channel_id=1, source_target_pairs={{0,16},{1,17},{2,18},{3,19},{4,20},{5,21},{6,22},{7,23},{8,24},{9,... | collective-permute-start | bytes 786440 | tf_op jit(solution)/shard_map/ppermute | solution.py:23
  73.0 3.2 %shard_map.227.y_ref = f32[512,512]{1,0:T(8,128)S(1)} custom-call(s32[1]{0:T(128)} %constant.31.clone.1.unused, bf16[512,512]{1,0:T(8,128)(2,1)S(1)} %get-tuple-element.91.x_ref, bf16[512,128]{1,0:T(8,128)(2,1)S(1)} %get-tuple-element.92.keys_ref, bf16[512,128]{1,0:T(8,128)(2,1)S(1)} %get-tuple-element.93.queries_ref, ...), custom_call_target="tpu_custom_call" | custom-call | tf_op jit(solution)/shard_map/pallas_call | solution.py:742
  76.2 1.2 shard_map.228
  77.4 2.3 %shard_map.229 = (f32[256,1024]{1,0:T(8,128)S(1)}, f32[256,1024]{1,0:T(8,128)S(1)}, f32[256,1024]{1,0:T(8,128)S(1)}, f32[256,1024]{1,0:T(8,128)S(1)}, f32[16,2048]{1,0:T(8,128)S(1)}) custom-call(s32[3]{0:T(128)S(1)} %copy-done.7, bf16[512,512]{1,0:T(8,128)(2,1)S(1)} %get-tuple-element.98.gated_ref.channels_ref, ...), custom_call_target="tpu_custom_call" | custom-call | flops 2000000000 | bytes 100000000 | tf_op jit(solution)/shard_map/pallas_call | solution.py:60
  79.7 1.4 %collective-permute-done.13.other_ref = f32[8,512]{1,0:T(8,128)S(1)} collective-permute-done((f32[8,512]{1,0:T(8,128)S(1)}, f32[8,512]{1,0:T(8,128)S(1)}, u32[]{:S(2)}, u32[]{:S(2)}) %collective-permute-start.13) | collective-permute-done | bytes 16416 | tf_op jit(solution)/shard_map/ppermute | solution.py:27
  81.1 1.4 %shard_map.233 = (bf16[256,1024]{1,0:T(8,128)(2,1)}, bf16[256,1024]{1,0:T(8,128)(2,1)S(1)}, bf16[256,1024]{1,0:T(8,128)(2,1)}, bf16[256,1024]{1,0:T(8,128)(2,1)S(1)}, f32[16,2048]{1,0:T(8,128)S(1)}) custom-call(s32[1]{0:T(128)} %constant.31.clone.1.unused, f32[8,512]{1,0:T(8,128)S(1)} %get-tuple-element.99.own_ref.other_ref, ...), custom_call_target="tpu_custom_call" | custom-call | bytes 1000 | tf_op jit(solution)/shard_map/pallas_call | solution.py:60
  82.5 0.8 copy-done.8
  83.3 1.3 collective-permute-start.19
  84.6 0.9 collective-permute-start.20
  86.1 2.2 %copy-done.3 = bf16[512,4096]{1,0:T(8,128)(2,1)S(1)} copy-done((bf16[512,4096]{1,0:T(8,128)(2,1)S(1)}, bf16[512,4096]{1,0:T(8,128)(2,1)}, u32[]{:S(2)}) %copy-start.3) | copy-done | bytes 4194328
  88.3 2.4 %shard_map.230 = (bf16[256,1024]{1,0:T(8,128)(2,1)S(1)}, bf16[256,1024]{1,0:T(8,128)(2,1)S(1)}, bf16[256,1024]{1,0:T(8,128)(2,1)S(1)}, bf16[256,1024]{1,0:T(8,128)(2,1)S(1)}, f32[16,2048]{1,0:T(8,128)S(1)}) custom-call(s32[3]{0:T(128)S(1)} %copy-done.7, bf16[512,512]{1,0:T(8,128)(2,1)S(1)} %get-tuple-element.98.gated_ref.channels_ref, ...), custom_call_target="tpu_custom_call" | custom-call | bytes 1000 | tf_op jit(solution)/shard_map/pallas_call | solution.py:60
  90.7 1.0 collective-permute-start.14
  91.6 0.9 collective-permute-start.15
  92.5 6.0 %collective-permute-done.19.upper_got = bf16[256,1024]{1,0:T(8,128)(2,1)} collective-permute-done((bf16[256,1024]{1,0:T(8,128)(2,1)}, bf16[256,1024]{1,0:T(8,128)(2,1)}, u32[]{:S(2)}, u32[]{:S(2)}) %collective-permute-start.19) | collective-permute-done | bytes 524320 | tf_op jit(solution)/shard_map/ppermute | solution.py:27
  98.5 1.3 collective-permute-done.20.lower_got
  101.1 1.4 %shard_map.234 = (f32[256,512]{1,0:T(8,128)S(1)}, bf16[256,512]{1,0:T(8,128)(2,1)S(1)}, f32[256,512]{1,0:T(8,128)S(1)}, bf16[256,512]{1,0:T(8,128)(2,1)S(1)}) custom-call(s32[1]{0:T(128)} %constant.31.clone.1.unused, bf16[256,1024]{1,0:T(8,128)(2,1)S(1)} %get-tuple-element.116.upper_ref, bf16[256,1024]{1,0:T(8,128)(2,1)} %collective-permute-done.19.upper_got, ...), custom_call_target="tpu_custom_call" | custom-call | flops 10000000000 | bytes 100000000 | tf_op jit(solution)/shard_map/pallas_call | solution.py:60
  102.5 1.0 collective-permute-start.21
  103.5 0.9 collective-permute-start.22
  104.4 1.3 collective-permute-done.26
  105.8 1.6 %collective-permute-start.27 = (bf16[16,4096]{1,0:T(8,128)(2,1)S(1)}, bf16[16,4096]{1,0:T(8,128)(2,1)S(1)}, u32[]{:S(2)}, u32[]{:S(2)}) collective-permute-start(bf16[16,4096]{1,0:T(8,128)(2,1)S(1)} %fusion.5), channel_id=1, source_target_pairs={{0,2},{1,3},{2,0},{3,1},{4,6},{5,7},{6,4},{7,5},{8,10},{9,11},{10,... | collective-permute-start | bytes 393224 | tf_op jit(solution)/shard_map/ppermute | solution.py:27
  107.4 2.2 %collective-permute-done.14.upper_got = bf16[256,1024]{1,0:T(8,128)(2,1)S(1)} collective-permute-done((bf16[256,1024]{1,0:T(8,128)(2,1)S(1)}, bf16[256,1024]{1,0:T(8,128)(2,1)S(1)}, u32[]{:S(2)}, u32[]{:S(2)}) %collective-permute-start.14) | collective-permute-done | bytes 524320 | tf_op jit(solution)/shard_map/ppermute | solution.py:27
  109.6 1.3 collective-permute-done.15.lower_got
  111.2 1.0 collective-permute-start.16
  112.2 0.9 collective-permute-start.17
  113.1 1.2 collective-permute-start.28
  114.3 2.0 %collective-permute-done.21.upper_got = bf16[256,512]{1,0:T(8,128)(2,1)S(1)} collective-permute-done((bf16[256,512]{1,0:T(8,128)(2,1)S(1)}, bf16[256,512]{1,0:T(8,128)(2,1)S(1)}, u32[]{:S(2)}, u32[]{:S(2)}) %collective-permute-start.21) | collective-permute-done | bytes 262176 | tf_op jit(solution)/shard_map/ppermute | solution.py:27
  116.4 1.2 collective-permute-start.23
  117.6 2.1 %collective-permute-start.24 = (bf16[512,256]{1,0:T(8,128)(2,1)S(1)}, bf16[512,256]{1,0:T(8,128)(2,1)S(1)}, u32[]{:S(2)}, u32[]{:S(2)}) collective-permute-start(bf16[512,256]{1,0:T(8,128)(2,1)S(1)} %get-tuple-element.125), channel_id=1, source_target_pairs={{1,0},{2,1},{3,2},{0,3},{5,4},{6,5},{7,6},{4,7},{9,8},{10,9},{11,1... | collective-permute-start | bytes 786440 | tf_op jit(solution)/shard_map/ppermute | solution.py:32
  119.7 1.4 %shard_map.237 = f32[8,512,128]{2,1,0:T(8,128)S(1)} custom-call(s32[1]{0:T(128)} %bitcast.16.first, bf16[512,512]{1,0:T(8,128)(2,1)S(1)} %get-tuple-element.126.spread_ref, bf16[512,128]{1,0:T(8,128)(2,1)S(1)} %get-tuple-element.92.keys_ref, s32[512,128]{1,0:T(8,128)S(1)} %get-tuple-element.90.marks_ref, f32[16,1,128]{2,1,0:T(1,128)S(1)} %bitcast.37, ...), custom_call_target="tpu_custom_call" | custom-call | bytes 1000 | tf_op jit(solution)/shard_map/pallas_call | solution.py:60
  121.3 1.0 collective-permute-start.29
  122.4 1.6 %collective-permute-start.18 = (bf16[512,256]{1,0:T(8,128)(2,1)S(1)}, bf16[512,256]{1,0:T(8,128)(2,1)S(1)}, u32[]{:S(2)}, u32[]{:S(2)}) collective-permute-start(bf16[512,256]{1,0:T(8,128)(2,1)S(1)} %get-tuple-element.111), channel_id=1, source_target_pairs={{3,0},{0,1},{1,2},{2,3},{7,4},{4,5},{5,6},{6,7},{11,8},{8,9},{9,10... | collective-permute-start | bytes 786440 | tf_op jit(solution)/shard_map/ppermute | solution.py:32
  124.0 3.3 %collective-permute-done.29 = bf16[16,4096]{1,0:T(8,128)(2,1)S(1)} collective-permute-done((bf16[16,4096]{1,0:T(8,128)(2,1)S(1)}, bf16[16,4096]{1,0:T(8,128)(2,1)S(1)}, u32[]{:S(2)}, u32[]{:S(2)}) %collective-permute-start.29) | collective-permute-done | bytes 131104 | tf_op jit(solution)/shard_map/ppermute | solution.py:27
  127.4 2.8 %shard_map.238 = f32[8,512,128]{2,1,0:T(8,128)} custom-call(s32[1]{0:T(128)} %bitcast.14.first, bf16[512,512]{1,0:T(8,128)(2,1)S(1)} %get-tuple-element.126.spread_ref, bf16[512,128]{1,0:T(8,128)(2,1)S(1)} %get-tuple-element.92.keys_ref, s32[512,128]{1,0:T(8,128)S(1)} %get-tuple-element.90.marks_ref, f32[16,1,128]{2,1,0:T(1,128)S(1)} %bitcast.38, ...), custom_call_target="tpu_custom_call" | custom-call | bytes 1000 | tf_op jit(solution)/shard_map/pallas_call | solution.py:60
  130.2 3.6 %collective-permute-done.23.refs_1_ = bf16[512,256]{1,0:T(8,128)(2,1)S(1)} collective-permute-done((bf16[512,256]{1,0:T(8,128)(2,1)S(1)}, bf16[512,256]{1,0:T(8,128)(2,1)S(1)}, u32[]{:S(2)}, u32[]{:S(2)}) %collective-permute-start.23) | collective-permute-done | bytes 262176 | tf_op jit(solution)/shard_map/ppermute | solution.py:32
  133.9 0.9 shard_map.236
  134.9 1.2 slice-done.1
  136.1 1.9 %fusion.7 = f32[16,1024]{1,0:T(8,128)} fusion(bf16[4096,1024]{1,0:T(8,128)(2,1)S(1)} %bitcast.41, bf16[16,4096]{1,0:T(8,128)(2,1)S(1)} %get-tuple-element.138, f32[4096]{0:T(1024)S(1)} %copy-done.15, f32[16]{0:T(128)S(1)} %add_rsqrt_fusion), kind=kOutput, calls=%fused_computation.20 | convolution fusion | flops 134479872 | bytes 8601664 | tf_op jit(solution)/shard_map/dot_general | solution.py:938
  (108 shorter events, 6.8 us)
Async XLA Ops:
  0.6 38.8 %copy-start = (bf16[16,3,2,2,128]{4,3,2,1,0:T(2,128)(2,1)S(1)}, bf16[16,3,2,2,128]{4,3,2,1,0:T(2,128)(2,1)}, u32[]{:S(2)}) copy-start(bf16[16,3,2,2,128]{4,3,2,1,0:T(2,128)(2,1)} %param.33) | copy-start | bytes 147460
  0.6 11.0 %collective-permute-start = (bf16[512,256]{1,0:T(8,128)(2,1)}, bf16[512,256]{1,0:T(8,128)(2,1)S(1)}, u32[]{:S(2)}, u32[]{:S(2)}) collective-permute-start(bf16[512,256]{1,0:T(8,128)(2,1)} %tokens_ref.1), channel_id=1, source_target_pairs={{1,0},{2,1},{3,2},{0,3},{5,4},{6,5},{7,6},{4,7},{9,8},{10,9},{11,1... | collective-permute-start | bytes 786440 | tf_op jit(solution)/shard_map/ppermute | solution.py:32
  11.7 14.6 %collective-permute-start.7 = (bf16[256,512]{1,0:T(8,128)(2,1)S(1)}, bf16[256,512]{1,0:T(8,128)(2,1)S(1)}, u32[]{:S(2)}, u32[]{:S(2)}) collective-permute-start(bf16[256,512]{1,0:T(8,128)(2,1)S(1)} %get-tuple-element.140.refs_0_), channel_id=1, source_target_pairs={{0,8},{4,12},{8,0},{12,4},{1,9},{5,13},{9,1},{13,5},{2,10},{6,14},... | collective-permute-start | bytes 786440 | tf_op jit(solution)/shard_map/ppermute | solution.py:27
  13.3 14.4 %collective-permute-start.9 = (bf16[256,512]{1,0:T(8,128)(2,1)S(1)}, bf16[256,512]{1,0:T(8,128)(2,1)S(1)}, u32[]{:S(2)}, u32[]{:S(2)}) collective-permute-start(bf16[256,512]{1,0:T(8,128)(2,1)S(1)} %get-tuple-element.139.refs_3_), channel_id=1, source_target_pairs={{0,4},{4,0},{8,12},{12,8},{1,5},{5,1},{9,13},{13,9},{2,6},{6,2},{1... | collective-permute-start | bytes 786440 | tf_op jit(solution)/shard_map/ppermute | solution.py:27
  14.8 21.5 %collective-permute-start.2 = (bf16[512,256]{1,0:T(8,128)(2,1)}, bf16[512,256]{1,0:T(8,128)(2,1)S(1)}, u32[]{:S(2)}, u32[]{:S(2)}) collective-permute-start(bf16[512,256]{1,0:T(8,128)(2,1)} %tokens_ref.1), channel_id=1, source_target_pairs={{3,0},{0,1},{1,2},{2,3},{7,4},{4,5},{5,6},{6,7},{11,8},{8,9},{9,10... | collective-permute-start | bytes 786440 | tf_op jit(solution)/shard_map/ppermute | solution.py:32
  22.2 14.0 %collective-permute-start.1 = (bf16[512,256]{1,0:T(8,128)(2,1)S(1)}, bf16[512,256]{1,0:T(8,128)(2,1)S(1)}, u32[]{:S(2)}, u32[]{:S(2)}) collective-permute-start(bf16[512,256]{1,0:T(8,128)(2,1)S(1)} %collective-permute-done), channel_id=1, source_target_pairs={{1,0},{2,1},{3,2},{0,3},{5,4},{6,5},{7,6},{4,7},{9,8},{10,9},{11,1... | collective-permute-start | bytes 786440 | tf_op jit(solution)/shard_map/ppermute | solution.py:32
  27.2 21.5 %collective-permute-start.8 = (bf16[256,1024]{1,0:T(8,128)(2,1)}, bf16[256,1024]{1,0:T(8,128)(2,1)S(1)}, u32[]{:S(2)}, u32[]{:S(2)}) collective-permute-start(bf16[256,1024]{1,0:T(8,128)(2,1)} %pad_maximum_fusion.2), channel_id=1, source_target_pairs={{0,4},{4,0},{8,12},{12,8},{1,5},{5,1},{9,13},{13,9},{2,6},{6,2},{1... | collective-permute-start | bytes 1572872 | tf_op jit(solution)/shard_map/ppermute | solution.py:27
  28.6 11.1 %copy-start.16 = (bf16[16,3,512]{2,0,1:T(8,128)(2,1)S(1)}, bf16[16,3,512]{2,0,1:T(8,128)(2,1)}, u32[]{:S(2)}) copy-start(bf16[16,3,512]{2,0,1:T(8,128)(2,1)} %param.32) | copy-start | bytes 147460
  28.6 11.2 %copy-start.19 = (f32[4,2,2,128]{3,2,1,0:T(2,128)S(1)}, f32[4,2,2,128]{3,2,1,0:T(2,128)}, u32[]{:S(2)}) copy-start(f32[4,2,2,128]{3,2,1,0:T(2,128)} %param.29) | copy-start | bytes 24580
  28.6 11.2 %copy-start.17 = (f32[4,512]{1,0:T(4,128)S(1)}, f32[4,512]{1,0:T(4,128)}, u32[]{:S(2)}) copy-start(f32[4,512]{1,0:T(4,128)} %param.28) | copy-start | bytes 24580
  28.6 11.2 %copy-start.20 = (f32[2,2,128]{2,1,0:T(2,128)S(1)}, f32[2,2,128]{2,1,0:T(2,128)}, u32[]{:S(2)}) copy-start(f32[2,2,128]{2,1,0:T(2,128)} %param.31) | copy-start | bytes 6148
  28.6 20.1 %collective-permute-start.10 = (bf16[256,1024]{1,0:T(8,128)(2,1)}, bf16[256,1024]{1,0:T(8,128)(2,1)}, u32[]{:S(2)}, u32[]{:S(2)}) collective-permute-start(bf16[256,1024]{1,0:T(8,128)(2,1)} %pad_maximum_fusion.3), channel_id=1, source_target_pairs={{0,8},{4,12},{8,0},{12,4},{1,9},{5,13},{9,1},{13,5},{2,10},{6,14},... | collective-permute-start | bytes 1572872 | tf_op jit(solution)/shard_map/ppermute | solution.py:27
  36.3 12.5 %copy-start.13 = (f32[1,2048]{1,0:T(1,128)S(1)}, f32[1,2048]{1,0:T(1,128)}, u32[]{:S(2)}) copy-start(f32[1,2048]{1,0:T(1,128)} %get-tuple-element.76.refs_7_) | copy-start | bytes 24580
  36.4 8.6 %collective-permute-start.5 = (bf16[256,512]{1,0:T(8,128)(2,1)S(1)}, bf16[256,512]{1,0:T(8,128)(2,1)S(1)}, u32[]{:S(2)}, u32[]{:S(2)}) collective-permute-start(bf16[256,512]{1,0:T(8,128)(2,1)S(1)} %get-tuple-element.141.refs_3_), channel_id=1, source_target_pairs={{0,4},{4,0},{8,12},{12,8},{1,5},{5,1},{9,13},{13,9},{2,6},{6,2},{1... | collective-permute-start | bytes 786440 | tf_op jit(solution)/shard_map/ppermute | solution.py:27
  37.9 9.1 %collective-permute-start.3 = (bf16[256,512]{1,0:T(8,128)(2,1)S(1)}, bf16[256,512]{1,0:T(8,128)(2,1)S(1)}, u32[]{:S(2)}, u32[]{:S(2)}) collective-permute-start(bf16[256,512]{1,0:T(8,128)(2,1)S(1)} %get-tuple-element.142.refs_0_), channel_id=1, source_target_pairs={{0,8},{4,12},{8,0},{12,4},{1,9},{5,13},{9,1},{13,5},{2,10},{6,14},... | collective-permute-start | bytes 786440 | tf_op jit(solution)/shard_map/ppermute | solution.py:27
  45.0 12.4 %collective-permute-start.6 = (bf16[256,1024]{1,0:T(8,128)(2,1)S(1)}, bf16[256,1024]{1,0:T(8,128)(2,1)S(1)}, u32[]{:S(2)}, u32[]{:S(2)}) collective-permute-start(bf16[256,1024]{1,0:T(8,128)(2,1)S(1)} %pad_maximum_fusion.1), channel_id=1, source_target_pairs={{0,8},{4,12},{8,0},{12,4},{1,9},{5,13},{9,1},{13,5},{2,10},{6,14},... | collective-permute-start | bytes 1572872 | tf_op jit(solution)/shard_map/ppermute | solution.py:27
  47.1 10.5 %collective-permute-start.4 = (bf16[256,1024]{1,0:T(8,128)(2,1)S(1)}, bf16[256,1024]{1,0:T(8,128)(2,1)S(1)}, u32[]{:S(2)}, u32[]{:S(2)}) collective-permute-start(bf16[256,1024]{1,0:T(8,128)(2,1)S(1)} %pad_maximum_fusion), channel_id=1, source_target_pairs={{0,4},{4,0},{8,12},{12,8},{1,5},{5,1},{9,13},{13,9},{2,6},{6,2},{1... | collective-permute-start | bytes 1572872 | tf_op jit(solution)/shard_map/ppermute | solution.py:27
  48.7 2.6 %copy-start.11 = (bf16[2048,1408]{1,0:T(8,128)(2,1)S(1)}, bf16[2048,1408]{1,0:T(8,128)(2,1)}, u32[]{:S(2)}) copy-start(bf16[2048,1408]{1,0:T(8,128)(2,1)} %get-tuple-element.77.refs_8_) | copy-start | bytes 17301508
  51.3 6.3 %copy-start.14 = (f32[1,2048]{1,0:T(1,128)S(1)}, f32[1,2048]{1,0:T(1,128)}, u32[]{:S(2)}) copy-start(f32[1,2048]{1,0:T(1,128)} %get-tuple-element.74.refs_7_) | copy-start | bytes 24580
  57.6 2.6 %copy-start.12 = (bf16[2048,1408]{1,0:T(8,128)(2,1)S(1)}, bf16[2048,1408]{1,0:T(8,128)(2,1)}, u32[]{:S(2)}) copy-start(bf16[2048,1408]{1,0:T(8,128)(2,1)} %get-tuple-element.75.refs_8_) | copy-start | bytes 17301508
  60.2 5.5 %copy-start.18 = (f32[512]{0:T(512)S(1)}, f32[512]{0:T(512)}, u32[]{:S(2)}) copy-start(f32[512]{0:T(512)} %param.30) | copy-start | bytes 6148
  60.2 5.5 %copy-start.4 = (f32[16,8,64,128]{3,2,1,0:T(8,128)S(1)}, f32[16,8,64,128]{3,2,1,0:T(8,128)}, u32[]{:S(2)}) copy-start(f32[16,8,64,128]{3,2,1,0:T(8,128)} %param.34) | copy-start | bytes 12582916
  64.2 2.5 %collective-permute-start.11 = (bf16[16,768]{1,0:T(8,128)(2,1)S(1)}, bf16[16,768]{1,0:T(8,128)(2,1)S(1)}, u32[]{:S(2)}, u32[]{:S(2)}) collective-permute-start(bf16[16,768]{1,0:T(8,128)(2,1)S(1)} %slice.31), channel_id=1, source_target_pairs={{0,16},{1,17},{2,18},{3,19},{4,20},{5,21},{6,22},{7,23},{8,24},{9,... | collective-permute-start | bytes 73736 | tf_op jit(solution)/shard_map/ppermute | solution.py:23
  66.7 6.2 %copy-start.21 = (f32[8]{0:T(128)S(1)}, f32[8]{0:T(128)}, u32[]{:S(2)}) copy-start(f32[8]{0:T(128)} %param.37) | copy-start | bytes 100
  70.8 5.4 %copy-start.10 = (f32[512]{0:T(512)S(1)}, f32[512]{0:T(512)}, u32[]{:S(2)}) copy-start(f32[512]{0:T(512)} %param.38) | copy-start | bytes 6148
  70.8 6.6 %copy-start.2 = (bf16[512,4096]{1,0:T(8,128)(2,1)S(1)}, bf16[512,4096]{1,0:T(8,128)(2,1)}, u32[]{:S(2)}) copy-start(bf16[512,4096]{1,0:T(8,128)(2,1)} %refs_7_.7) | copy-start | bytes 12582916
  70.8 6.6 %copy-start.7 = (s32[3]{0:T(128)S(1)}, s32[3]{0:T(128)}, u32[]{:S(2)}) copy-start(s32[3]{0:T(128)} %pad_add_fusion.place.blocks) | copy-start | bytes 40
  70.8 5.4 %collective-permute-start.12 = (f32[512,128]{1,0:T(8,128)S(1)}, f32[512,128]{1,0:T(8,128)S(1)}, u32[]{:S(2)}, u32[]{:S(2)}) collective-permute-start(f32[512,128]{1,0:T(8,128)S(1)} %get-tuple-element.96), channel_id=1, source_target_pairs={{0,16},{1,17},{2,18},{3,19},{4,20},{5,21},{6,22},{7,23},{8,24},{9,... | collective-permute-start | bytes 786440 | tf_op jit(solution)/shard_map/ppermute | solution.py:23
  77.3 3.8 %collective-permute-start.13 = (f32[8,512]{1,0:T(8,128)S(1)}, f32[8,512]{1,0:T(8,128)S(1)}, u32[]{:S(2)}, u32[]{:S(2)}) collective-permute-start(f32[8,512]{1,0:T(8,128)S(1)} %get-tuple-element.99.own_ref.other_ref), channel_id=1, source_target_pairs={{0,1},{1,0},{2,3},{3,2},{4,5},{5,4},{6,7},{7,6},{8,9},{9,8},{10,11... | collective-permute-start | bytes 49160 | tf_op jit(solution)/shard_map/ppermute | solution.py:27
  82.5 0.8 copy-start.8
  83.3 15.2 %collective-permute-start.19 = (bf16[256,1024]{1,0:T(8,128)(2,1)}, bf16[256,1024]{1,0:T(8,128)(2,1)}, u32[]{:S(2)}, u32[]{:S(2)}) collective-permute-start(bf16[256,1024]{1,0:T(8,128)(2,1)} %get-tuple-element.117), channel_id=1, source_target_pairs={{0,4},{4,0},{8,12},{12,8},{1,5},{5,1},{9,13},{13,9},{2,6},{6,2},{1... | collective-permute-start | bytes 1572872 | tf_op jit(solution)/shard_map/ppermute | solution.py:27
  84.6 15.2 %collective-permute-start.20 = (bf16[256,1024]{1,0:T(8,128)(2,1)}, bf16[256,1024]{1,0:T(8,128)(2,1)}, u32[]{:S(2)}, u32[]{:S(2)}) collective-permute-start(bf16[256,1024]{1,0:T(8,128)(2,1)} %get-tuple-element.119), channel_id=1, source_target_pairs={{0,8},{4,12},{8,0},{12,4},{1,9},{5,13},{9,1},{13,5},{2,10},{6,14},... | collective-permute-start | bytes 1572872 | tf_op jit(solution)/shard_map/ppermute | solution.py:27
  86.1 2.2 %copy-start.3 = (bf16[512,4096]{1,0:T(8,128)(2,1)S(1)}, bf16[512,4096]{1,0:T(8,128)(2,1)}, u32[]{:S(2)}) copy-start(bf16[512,4096]{1,0:T(8,128)(2,1)} %refs_7_.7) | copy-start | bytes 12582916
  88.2 12.9 %copy-start.9 = (bf16[256,1024]{1,0:T(8,128)(2,1)S(1)}, bf16[256,1024]{1,0:T(8,128)(2,1)}, u32[]{:S(2)}) copy-start(bf16[256,1024]{1,0:T(8,128)(2,1)} %copy-done.8) | copy-start | bytes 1572868
  90.7 19.0 %collective-permute-start.14 = (bf16[256,1024]{1,0:T(8,128)(2,1)S(1)}, bf16[256,1024]{1,0:T(8,128)(2,1)S(1)}, u32[]{:S(2)}, u32[]{:S(2)}) collective-permute-start(bf16[256,1024]{1,0:T(8,128)(2,1)S(1)} %get-tuple-element.103), channel_id=1, source_target_pairs={{0,4},{4,0},{8,12},{12,8},{1,5},{5,1},{9,13},{13,9},{2,6},{6,2},{1... | collective-permute-start | bytes 1572872 | tf_op jit(solution)/shard_map/ppermute | solution.py:27
  91.6 19.3 %collective-permute-start.15 = (bf16[256,1024]{1,0:T(8,128)(2,1)S(1)}, bf16[256,1024]{1,0:T(8,128)(2,1)S(1)}, u32[]{:S(2)}, u32[]{:S(2)}) collective-permute-start(bf16[256,1024]{1,0:T(8,128)(2,1)S(1)} %get-tuple-element.105), channel_id=1, source_target_pairs={{0,8},{4,12},{8,0},{12,4},{1,9},{5,13},{9,1},{13,5},{2,10},{6,14},... | collective-permute-start | bytes 1572872 | tf_op jit(solution)/shard_map/ppermute | solution.py:27
  100.5 5.3 %collective-permute-start.26 = (bf16[16,4096]{1,0:T(8,128)(2,1)S(1)}, bf16[16,4096]{1,0:T(8,128)(2,1)S(1)}, u32[]{:S(2)}, u32[]{:S(2)}) collective-permute-start(bf16[16,4096]{1,0:T(8,128)(2,1)S(1)} %convert_element_type.38), channel_id=1, source_target_pairs={{0,1},{1,0},{2,3},{3,2},{4,5},{5,4},{6,7},{7,6},{8,9},{9,8},{10,11... | collective-permute-start | bytes 393224 | tf_op jit(solution)/shard_map/ppermute | solution.py:27
  102.5 13.7 %collective-permute-start.21 = (bf16[256,512]{1,0:T(8,128)(2,1)S(1)}, bf16[256,512]{1,0:T(8,128)(2,1)S(1)}, u32[]{:S(2)}, u32[]{:S(2)}) collective-permute-start(bf16[256,512]{1,0:T(8,128)(2,1)S(1)} %get-tuple-element.121), channel_id=1, source_target_pairs={{0,8},{4,12},{8,0},{12,4},{1,9},{5,13},{9,1},{13,5},{2,10},{6,14},... | collective-permute-start | bytes 786440 | tf_op jit(solution)/shard_map/ppermute | solution.py:27
  103.5 12.8 %collective-permute-start.22 = (bf16[256,512]{1,0:T(8,128)(2,1)S(1)}, bf16[256,512]{1,0:T(8,128)(2,1)S(1)}, u32[]{:S(2)}, u32[]{:S(2)}) collective-permute-start(bf16[256,512]{1,0:T(8,128)(2,1)S(1)} %get-tuple-element.123), channel_id=1, source_target_pairs={{0,4},{4,0},{8,12},{12,8},{1,5},{5,1},{9,13},{13,9},{2,6},{6,2},{1... | collective-permute-start | bytes 786440 | tf_op jit(solution)/shard_map/ppermute | solution.py:27
  105.8 7.3 %collective-permute-start.27 = (bf16[16,4096]{1,0:T(8,128)(2,1)S(1)}, bf16[16,4096]{1,0:T(8,128)(2,1)S(1)}, u32[]{:S(2)}, u32[]{:S(2)}) collective-permute-start(bf16[16,4096]{1,0:T(8,128)(2,1)S(1)} %fusion.5), channel_id=1, source_target_pairs={{0,2},{1,3},{2,0},{3,1},{4,6},{5,7},{6,4},{7,5},{8,10},{9,11},{10,... | collective-permute-start | bytes 393224 | tf_op jit(solution)/shard_map/ppermute | solution.py:27
  111.2 10.1 %collective-permute-start.16 = (bf16[256,512]{1,0:T(8,128)(2,1)S(1)}, bf16[256,512]{1,0:T(8,128)(2,1)S(1)}, u32[]{:S(2)}, u32[]{:S(2)}) collective-permute-start(bf16[256,512]{1,0:T(8,128)(2,1)S(1)} %get-tuple-element.107), channel_id=1, source_target_pairs={{0,8},{4,12},{8,0},{12,4},{1,9},{5,13},{9,1},{13,5},{2,10},{6,14},... | collective-permute-start | bytes 786440 | tf_op jit(solution)/shard_map/ppermute | solution.py:27
  112.2 10.1 %collective-permute-start.17 = (bf16[256,512]{1,0:T(8,128)(2,1)S(1)}, bf16[256,512]{1,0:T(8,128)(2,1)S(1)}, u32[]{:S(2)}, u32[]{:S(2)}) collective-permute-start(bf16[256,512]{1,0:T(8,128)(2,1)S(1)} %get-tuple-element.109), channel_id=1, source_target_pairs={{0,4},{4,0},{8,12},{12,8},{1,5},{5,1},{9,13},{13,9},{2,6},{6,2},{1... | collective-permute-start | bytes 786440 | tf_op jit(solution)/shard_map/ppermute | solution.py:27
  113.1 8.0 %collective-permute-start.28 = (bf16[16,4096]{1,0:T(8,128)(2,1)S(1)}, bf16[16,4096]{1,0:T(8,128)(2,1)S(1)}, u32[]{:S(2)}, u32[]{:S(2)}) collective-permute-start(bf16[16,4096]{1,0:T(8,128)(2,1)S(1)} %fusion.11), channel_id=1, source_target_pairs={{0,4},{4,0},{8,12},{12,8},{1,5},{5,1},{9,13},{13,9},{2,6},{6,2},{1... | collective-permute-start | bytes 393224 | tf_op jit(solution)/shard_map/ppermute | solution.py:27
  116.3 3.4 %copy-start.5 = (f32[16,8,64,128]{3,2,1,0:T(8,128)S(1)}, f32[16,8,64,128]{3,2,1,0:T(8,128)}, u32[]{:S(2)}) copy-start(f32[16,8,64,128]{3,2,1,0:T(8,128)} %param.34) | copy-start | bytes 12582916
  116.4 17.4 %collective-permute-start.23 = (bf16[512,256]{1,0:T(8,128)(2,1)S(1)}, bf16[512,256]{1,0:T(8,128)(2,1)S(1)}, u32[]{:S(2)}, u32[]{:S(2)}) collective-permute-start(bf16[512,256]{1,0:T(8,128)(2,1)S(1)} %get-tuple-element.124), channel_id=1, source_target_pairs={{2,0},{3,1},{0,2},{1,3},{6,4},{7,5},{4,6},{5,7},{10,8},{11,9},{8,1... | collective-permute-start | bytes 786440 | tf_op jit(solution)/shard_map/ppermute | solution.py:32
  117.6 16.2 %collective-permute-start.24 = (bf16[512,256]{1,0:T(8,128)(2,1)S(1)}, bf16[512,256]{1,0:T(8,128)(2,1)S(1)}, u32[]{:S(2)}, u32[]{:S(2)}) collective-permute-start(bf16[512,256]{1,0:T(8,128)(2,1)S(1)} %get-tuple-element.125), channel_id=1, source_target_pairs={{1,0},{2,1},{3,2},{0,3},{5,4},{6,5},{7,6},{4,7},{9,8},{10,9},{11,1... | collective-permute-start | bytes 786440 | tf_op jit(solution)/shard_map/ppermute | solution.py:32
  121.2 6.2 %collective-permute-start.25 = (f32[8,512,128]{2,1,0:T(8,128)S(1)}, f32[8,512,128]{2,1,0:T(8,128)S(1)}, u32[]{:S(2)}, u32[]{:S(2)}) collective-permute-start(f32[8,512,128]{2,1,0:T(8,128)S(1)} %shard_map.237), channel_id=1, source_target_pairs={{0,16},{16,0},{1,17},{17,1},{2,18},{18,2},{3,19},{19,3},{4,20},{20... | collective-permute-start | bytes 6291464 | tf_op jit(solution)/shard_map/ppermute | solution.py:27
  121.3 6.0 %collective-permute-start.29 = (bf16[16,4096]{1,0:T(8,128)(2,1)S(1)}, bf16[16,4096]{1,0:T(8,128)(2,1)S(1)}, u32[]{:S(2)}, u32[]{:S(2)}) collective-permute-start(bf16[16,4096]{1,0:T(8,128)(2,1)S(1)} %fusion.6), channel_id=1, source_target_pairs={{0,8},{4,12},{8,0},{12,4},{1,9},{5,13},{9,1},{13,5},{2,10},{6,14},... | collective-permute-start | bytes 393224 | tf_op jit(solution)/shard_map/ppermute | solution.py:27
  122.4 11.4 %collective-permute-start.18 = (bf16[512,256]{1,0:T(8,128)(2,1)S(1)}, bf16[512,256]{1,0:T(8,128)(2,1)S(1)}, u32[]{:S(2)}, u32[]{:S(2)}) collective-permute-start(bf16[512,256]{1,0:T(8,128)(2,1)S(1)} %get-tuple-element.111), channel_id=1, source_target_pairs={{3,0},{0,1},{1,2},{2,3},{7,4},{4,5},{5,6},{6,7},{11,8},{8,9},{9,10... | collective-permute-start | bytes 786440 | tf_op jit(solution)/shard_map/ppermute | solution.py:32
  127.4 6.5 %copy-start.6 = (bf16[512,256]{1,0:T(8,128)(2,1)S(1)}, bf16[512,256]{1,0:T(8,128)(2,1)}, u32[]{:S(2)}) copy-start(bf16[512,256]{1,0:T(8,128)(2,1)} %tokens_ref.1) | copy-start | bytes 786436
  127.4 7.5 %slice-start = ((s8[8388608]{0:T(1024)(128)(4,1)}), s8[4194304]{0:T(1024)(128)(4,1)S(1)}, s32[]{:S(2)}) async-start(s8[8388608]{0:T(1024)(128)(4,1)} %bitcast.40), calls=%async_computation | async-start | bytes 8388608
  130.2 4.5 %collective-permute-start.30 = (f32[16,4096]{1,0:T(8,128)S(1)}, f32[16,4096]{1,0:T(8,128)S(1)}, u32[]{:S(2)}, u32[]{:S(2)}) collective-permute-start(f32[16,4096]{1,0:T(8,128)S(1)} %add_add_fusion), channel_id=1, source_target_pairs={{0,16},{16,0},{1,17},{17,1},{2,18},{18,2},{3,19},{19,3},{4,20},{20... | collective-permute-start | bytes 786440 | tf_op jit(solution)/shard_map/ppermute | solution.py:27
  133.8 2.3 %slice-start.1 = ((s8[8388608]{0:T(1024)(128)(4,1)}), s8[4194304]{0:T(1024)(128)(4,1)S(1)}, s32[]{:S(2)}) async-start(s8[8388608]{0:T(1024)(128)(4,1)} %bitcast.40), calls=%async_computation.1 | async-start | bytes 8388608
  133.9 2.3 %copy-start.15 = (f32[4096]{0:T(1024)S(1)}, f32[4096]{0:T(1024)}, u32[]{:S(2)}) copy-start(f32[4096]{0:T(1024)} %param.40) | copy-start | bytes 49156
  134.9 3.1 %copy-start.1 = (bf16[16,3,2,2,128]{4,3,2,1,0:T(2,128)(2,1)S(1)}, bf16[16,3,2,2,128]{4,3,2,1,0:T(2,128)(2,1)}, u32[]{:S(2)}) copy-start(bf16[16,3,2,2,128]{4,3,2,1,0:T(2,128)(2,1)} %param.33) | copy-start | bytes 147460

commit v6 on v5

--- a/solution.py
+++ b/solution.py
@@ -498,7 +498,7 @@
     for at, (source, out_ref) in enumerate(zip(raw, outs)):
         factor = end_scale if at == 4 else scale[:half] if at < 2 else scale[half:]
         for lane in range(0, source.shape[1], LANES):
-            value = source[:, lane : lane + LANES] * factor
+            value = source[:, lane : lane + LANES].astype(F32) * factor
             out_ref[:, lane : lane + LANES] = value.astype(out_ref.dtype)
 
 
@@ -791,7 +791,7 @@
         ends_out = ((requests, row_size * count * width), F32)
         outs = call(
             functools.partial(out_kernel, width, count, not first),
-            [(side, F32 if first else kind) for kind in kinds] + [ends_out],
+            [(side, kind) for kind in kinds] + [ends_out],
             gated,
             own_squares,
             own_squares if first else other_squares,

time: 139 us -> 139 us (level)
  no operation moved by 1% of the time
where the time goes in v6:
time: 139 us; the launch traced here: 138 us
  Pallas kernels  47.6 us (34%)
  starting transfers between devices  39.9 us (29%)
  waiting for transfers between devices  28.5 us (21%)
  local copies, waits for them, and re-layouts  13.4 us (10%)
  other arithmetic  3.72 us (3%)
  between operations  2.84 us (2%)
  matrix products  2.08 us (1%)
    pallas_call x19, Pallas kernels, call(): pl.pallas_call(kernel, out_shape=shapes, grid_spec=spec, compiler_params=...  44.4 us
    ppermute x23, waiting for transfers between devices, from_partner(): lax.ppermute(x, axis, [(i, i ^ 1 << bit) for i in range(lax.axis_size(axi...  23.5 us
    ppermute x23, starting transfers between devices, from_partner(): lax.ppermute(x, axis, [(i, i ^ 1 << bit) for i in range(lax.axis_size(axi...  21.9 us
    ppermute x6, starting transfers between devices, from_ahead(): lax.ppermute(x, axis, [((i + distance) % size, i) for i in range(size)])  14.4 us
    unnamed x52, local copies, waits for them, and re-layouts  10.6 us
    ppermute x6, waiting for transfers between devices, from_ahead(): lax.ppermute(x, axis, [((i + distance) % size, i) for i in range(size)])  5.07 us
    ppermute x2, starting transfers between devices, from_behind(): return lax.ppermute(block, axis, route)  3.66 us
    pallas_call x1, Pallas kernels, per_device(): pl.pallas_call(functools.partial(scan_kernel, heads, block), out_shape=ja...  3.18 us
  transfers between devices with their start and end apart: 31, of which 14 were waited for; matrix products, arithmetic and copies ran while one was open for 5% of the time, Pallas kernels for 27%

profile of v6, /device:TPU:0, one launch (start us, length us, event | category | flops | bytes accessed | tf_op | source)
XLA Modules:
  0.0 138.1 jit_solution(6483209739400009249)
XLA Ops:
  0.6 5.1 %collective-permute-start = (bf16[512,256]{1,0:T(8,128)(2,1)}, bf16[512,256]{1,0:T(8,128)(2,1)S(1)}, u32[]{:S(2)}, u32[]{:S(2)}) collective-permute-start(bf16[512,256]{1,0:T(8,128)(2,1)} %tokens_ref.1), channel_id=1, source_target_pairs={{1,0},{2,1},{3,2},{0,3},{5,4},{6,5},{7,6},{4,7},{9,8},{10,9},{11,1... | collective-permute-start | bytes 786440 | tf_op jit(solution)/shard_map/ppermute | solution.py:32
  6.4 0.7 pad_add_fusion.1.counts
  7.1 1.4 %shard_map.220 = (s32[512,128]{1,0:T(8,128)S(1)}, s32[8,512]{1,0:T(8,128)S(1)}, bf16[16,512]{1,0:T(8,128)(2,1)S(1)}, f32[16,256]{1,0:T(8,128)S(1)}) custom-call(s32[33]{0:T(128)S(1)} %pad_add_fusion.1.counts), custom_call_target="tpu_custom_call" | custom-call | bytes 1000 | tf_op jit(solution)/shard_map/pallas_call | solution.py:60
  8.5 0.7 pad_bitcast_fusion.1
  9.2 1.0 constant_dynamic-update-slice_fusion.3
  10.2 1.4 %collective-permute-done = bf16[512,256]{1,0:T(8,128)(2,1)S(1)} collective-permute-done((bf16[512,256]{1,0:T(8,128)(2,1)}, bf16[512,256]{1,0:T(8,128)(2,1)S(1)}, u32[]{:S(2)}, u32[]{:S(2)}) %collective-permute-start) | collective-permute-done | bytes 262176 | tf_op jit(solution)/shard_map/ppermute | solution.py:32
  11.7 1.6 %collective-permute-start.7 = (bf16[256,512]{1,0:T(8,128)(2,1)S(1)}, bf16[256,512]{1,0:T(8,128)(2,1)S(1)}, u32[]{:S(2)}, u32[]{:S(2)}) collective-permute-start(bf16[256,512]{1,0:T(8,128)(2,1)S(1)} %get-tuple-element.140.refs_0_), channel_id=1, source_target_pairs={{0,8},{4,12},{8,0},{12,4},{1,9},{5,13},{9,1},{13,5},{2,10},{6,14},... | collective-permute-start | bytes 786440 | tf_op jit(solution)/shard_map/ppermute | solution.py:27
  13.3 1.5 %collective-permute-start.9 = (bf16[256,512]{1,0:T(8,128)(2,1)S(1)}, bf16[256,512]{1,0:T(8,128)(2,1)S(1)}, u32[]{:S(2)}, u32[]{:S(2)}) collective-permute-start(bf16[256,512]{1,0:T(8,128)(2,1)S(1)} %get-tuple-element.139.refs_3_), channel_id=1, source_target_pairs={{0,4},{4,0},{8,12},{12,8},{1,5},{5,1},{9,13},{13,9},{2,6},{6,2},{1... | collective-permute-start | bytes 786440 | tf_op jit(solution)/shard_map/ppermute | solution.py:27
  15.1 7.1 %shard_map.222 = (bf16[2048,1408]{1,0:T(8,128)(2,1)}, f32[1,2048]{1,0:T(1,128)}) custom-call(s32[3]{0:T(128)} %pad_add_fusion.place.blocks, bf16[4096,2,512]{2,1,0:T(2,128)(2,1)} %refs_3_.5, bf16[4096,2,512]{2,1,0:T(2,128)(2,1)} %refs_3_.5, bf16[4096,2,512]{2,1,0:T(2,128)(2,1)} %refs_3_.5, bf16[4096,2,512]{2,1,0:T(2,128)(2,1)} %refs_3_.5, ...), custom_call_target="tpu_custom_call" | custom-call | flops 20000000000 | bytes 100000000 | tf_op jit(solution)/shard_map/pallas_call | solution.py:60
  22.2 4.1 %collective-permute-start.1 = (bf16[512,256]{1,0:T(8,128)(2,1)S(1)}, bf16[512,256]{1,0:T(8,128)(2,1)S(1)}, u32[]{:S(2)}, u32[]{:S(2)}) collective-permute-start(bf16[512,256]{1,0:T(8,128)(2,1)S(1)} %collective-permute-done), channel_id=1, source_target_pairs={{1,0},{2,1},{3,2},{0,3},{5,4},{6,5},{7,6},{4,7},{9,8},{10,9},{11,1... | collective-permute-start | bytes 786440 | tf_op jit(solution)/shard_map/ppermute | solution.py:32
  26.3 0.9 pad_maximum_fusion.2
  27.7 0.9 pad_maximum_fusion.3
  29.2 7.1 %shard_map.221 = (bf16[2048,1408]{1,0:T(8,128)(2,1)}, f32[1,2048]{1,0:T(1,128)}) custom-call(s32[3]{0:T(128)} %pad_add_fusion.place.blocks, bf16[4096,2,512]{2,1,0:T(2,128)(2,1)} %refs_3_.5, bf16[4096,2,512]{2,1,0:T(2,128)(2,1)} %refs_3_.5, bf16[4096,2,512]{2,1,0:T(2,128)(2,1)} %refs_3_.5, bf16[4096,2,512]{2,1,0:T(2,128)(2,1)} %refs_3_.5, ...), custom_call_target="tpu_custom_call" | custom-call | flops 20000000000 | bytes 100000000 | tf_op jit(solution)/shard_map/pallas_call | solution.py:60
  36.4 1.6 %collective-permute-start.5 = (bf16[256,512]{1,0:T(8,128)(2,1)S(1)}, bf16[256,512]{1,0:T(8,128)(2,1)S(1)}, u32[]{:S(2)}, u32[]{:S(2)}) collective-permute-start(bf16[256,512]{1,0:T(8,128)(2,1)S(1)} %get-tuple-element.141.refs_3_), channel_id=1, source_target_pairs={{0,4},{4,0},{8,12},{12,8},{1,5},{5,1},{9,13},{13,9},{2,6},{6,2},{1... | collective-permute-start | bytes 786440 | tf_op jit(solution)/shard_map/ppermute | solution.py:27
  37.9 1.5 %collective-permute-start.3 = (bf16[256,512]{1,0:T(8,128)(2,1)S(1)}, bf16[256,512]{1,0:T(8,128)(2,1)S(1)}, u32[]{:S(2)}, u32[]{:S(2)}) collective-permute-start(bf16[256,512]{1,0:T(8,128)(2,1)S(1)} %get-tuple-element.142.refs_0_), channel_id=1, source_target_pairs={{0,8},{4,12},{8,0},{12,4},{1,9},{5,13},{9,1},{13,5},{2,10},{6,14},... | collective-permute-start | bytes 786440 | tf_op jit(solution)/shard_map/ppermute | solution.py:27
  42.1 1.0 dynamic-slice_bitcast_fusion.init_ref
  43.0 1.9 %collective-permute-done.5.refs_4_ = bf16[256,512]{1,0:T(8,128)(2,1)S(1)} collective-permute-done((bf16[256,512]{1,0:T(8,128)(2,1)S(1)}, bf16[256,512]{1,0:T(8,128)(2,1)S(1)}, u32[]{:S(2)}, u32[]{:S(2)}) %collective-permute-start.5) | collective-permute-done | bytes 262176 | tf_op jit(solution)/shard_map/ppermute | solution.py:27
  45.6 1.5 %collective-permute-done.3.refs_1_ = bf16[256,512]{1,0:T(8,128)(2,1)S(1)} collective-permute-done((bf16[256,512]{1,0:T(8,128)(2,1)S(1)}, bf16[256,512]{1,0:T(8,128)(2,1)S(1)}, u32[]{:S(2)}, u32[]{:S(2)}) %collective-permute-start.3) | collective-permute-done | bytes 262176 | tf_op jit(solution)/shard_map/ppermute | solution.py:27
  47.1 1.6 %collective-permute-start.4 = (bf16[256,1024]{1,0:T(8,128)(2,1)S(1)}, bf16[256,1024]{1,0:T(8,128)(2,1)S(1)}, u32[]{:S(2)}, u32[]{:S(2)}) collective-permute-start(bf16[256,1024]{1,0:T(8,128)(2,1)S(1)} %pad_maximum_fusion), channel_id=1, source_target_pairs={{0,4},{4,0},{8,12},{12,8},{1,5},{5,1},{9,13},{13,9},{2,6},{6,2},{1... | collective-permute-start | bytes 1572872 | tf_op jit(solution)/shard_map/ppermute | solution.py:27
  48.7 2.6 %copy-done.11 = bf16[2048,1408]{1,0:T(8,128)(2,1)S(1)} copy-done((bf16[2048,1408]{1,0:T(8,128)(2,1)S(1)}, bf16[2048,1408]{1,0:T(8,128)(2,1)}, u32[]{:S(2)}) %copy-start.11) | copy-done | bytes 5767192
  51.3 5.0 %shard_map.223 = (f32[16,2048]{1,0:T(8,128)S(1)}, f32[512,1408]{1,0:T(8,128)S(1)}, f32[512,128]{1,0:T(8,128)S(1)}) custom-call(s32[1]{0:T(128)} %constant.31.clone.1.unused, bf16[256,512]{1,0:T(8,128)(2,1)S(1)} %get-tuple-element.140.refs_0_, bf16[256,512]{1,0:T(8,128)(2,1)S(1)} %collective-permute-done.7.refs_1_, ...), custom_call_target="tpu_custom_call" | custom-call | flops 20000000000 | bytes 100000000 | tf_op jit(solution)/shard_map/pallas_call | solution.py:60
  56.4 1.1 collective-permute-done.6.refs_5_
  57.6 2.6 %copy-done.12 = bf16[2048,1408]{1,0:T(8,128)(2,1)S(1)} copy-done((bf16[2048,1408]{1,0:T(8,128)(2,1)S(1)}, bf16[2048,1408]{1,0:T(8,128)(2,1)}, u32[]{:S(2)}) %copy-start.12) | copy-done | bytes 5767192
  60.2 3.9 %shard_map.224 = (f32[16,2048]{1,0:T(8,128)S(1)}, bf16[512,512]{1,0:T(8,128)(2,1)S(1)}, bf16[512,768]{1,0:T(8,128)(2,1)S(1)}, f32[512,128]{1,0:T(8,128)S(1)}) custom-call(s32[1]{0:T(128)} %constant.31.clone.1.unused, bf16[256,512]{1,0:T(8,128)(2,1)S(1)} %get-tuple-element.142.refs_0_, bf16[256,512]{1,0:T(8,128)(2,1)S(1)} %collective-permute-done.3.refs_1_, ...), custom_call_target="tpu_custom_call" | custom-call | flops 20000000000 | bytes 100000000 | tf_op jit(solution)/shard_map/pallas_call | solution.py:60
  64.2 1.5 %collective-permute-start.11 = (bf16[16,768]{1,0:T(8,128)(2,1)S(1)}, bf16[16,768]{1,0:T(8,128)(2,1)S(1)}, u32[]{:S(2)}, u32[]{:S(2)}) collective-permute-start(bf16[16,768]{1,0:T(8,128)(2,1)S(1)} %slice.31), channel_id=1, source_target_pairs={{0,16},{1,17},{2,18},{3,19},{4,20},{5,21},{6,22},{7,23},{8,24},{9,... | collective-permute-start | bytes 73736 | tf_op jit(solution)/shard_map/ppermute | solution.py:23
  65.8 0.9 shard_map.225.table_ref
  66.7 4.1 %shard_map.226 = (bf16[512,512]{1,0:T(8,128)(2,1)S(1)}, bf16[512,128]{1,0:T(8,128)(2,1)S(1)}, bf16[512,128]{1,0:T(8,128)(2,1)S(1)}, f32[512,128]{1,0:T(8,128)S(1...) custom-call(s32[1]{0:T(128)} %constant.31.clone.1.unused, ...), custom_call_target="tpu_custom_call" | custom-call | flops 4000000000 | bytes 100000000 | tf_op jit(solution)/shard_map/pallas_call | solution.py:60
  70.8 2.2 %collective-permute-start.12 = (f32[512,128]{1,0:T(8,128)S(1)}, f32[512,128]{1,0:T(8,128)S(1)}, u32[]{:S(2)}, u32[]{:S(2)}) collective-permute-start(f32[512,128]{1,0:T(8,128)S(1)} %get-tuple-element.96), channel_id=1, source_target_pairs={{0,16},{1,17},{2,18},{3,19},{4,20},{5,21},{6,22},{7,23},{8,24},{9,... | collective-permute-start | bytes 786440 | tf_op jit(solution)/shard_map/ppermute | solution.py:23
  73.0 3.2 %shard_map.227.y_ref = f32[512,512]{1,0:T(8,128)S(1)} custom-call(s32[1]{0:T(128)} %constant.31.clone.1.unused, bf16[512,512]{1,0:T(8,128)(2,1)S(1)} %get-tuple-element.91.x_ref, bf16[512,128]{1,0:T(8,128)(2,1)S(1)} %get-tuple-element.92.keys_ref, bf16[512,128]{1,0:T(8,128)(2,1)S(1)} %get-tuple-element.93.queries_ref, ...), custom_call_target="tpu_custom_call" | custom-call | tf_op jit(solution)/shard_map/pallas_call | solution.py:742
  76.2 1.2 shard_map.228
  77.4 2.3 %shard_map.229 = (bf16[256,1024]{1,0:T(8,128)(2,1)S(1)}, bf16[256,1024]{1,0:T(8,128)(2,1)S(1)}, bf16[256,1024]{1,0:T(8,128)(2,1)S(1)}, bf16[256,1024]{1,0:T(8,128)(2,1)S(1)}, f32[16,2048]{1,0:T(8,128)S(1)}) custom-call(s32[3]{0:T(128)S(1)} %copy-done.7, bf16[512,512]{1,0:T(8,128)(2,1)S(1)} %get-tuple-element.98.gated_ref.channels_ref, ...), custom_call_target="tpu_custom_call" | custom-call | flops 2000000000 | bytes 100000000 | tf_op jit(solution)/shard_map/pallas_call | solution.py:60
  79.7 1.4 %collective-permute-done.13.other_ref = f32[8,512]{1,0:T(8,128)S(1)} collective-permute-done((f32[8,512]{1,0:T(8,128)S(1)}, f32[8,512]{1,0:T(8,128)S(1)}, u32[]{:S(2)}, u32[]{:S(2)}) %collective-permute-start.13) | collective-permute-done | bytes 16416 | tf_op jit(solution)/shard_map/ppermute | solution.py:27
  81.1 1.5 %shard_map.233 = (bf16[256,1024]{1,0:T(8,128)(2,1)}, bf16[256,1024]{1,0:T(8,128)(2,1)S(1)}, bf16[256,1024]{1,0:T(8,128)(2,1)}, bf16[256,1024]{1,0:T(8,128)(2,1)S(1)}, f32[16,2048]{1,0:T(8,128)S(1)}) custom-call(s32[1]{0:T(128)} %constant.31.clone.1.unused, f32[8,512]{1,0:T(8,128)S(1)} %get-tuple-element.99.own_ref.other_ref, ...), custom_call_target="tpu_custom_call" | custom-call | bytes 1000 | tf_op jit(solution)/shard_map/pallas_call | solution.py:60
  82.6 0.8 copy-done.8
  83.4 1.3 collective-permute-start.19
  84.7 0.9 collective-permute-start.20
  86.1 2.2 %copy-done.3 = bf16[512,4096]{1,0:T(8,128)(2,1)S(1)} copy-done((bf16[512,4096]{1,0:T(8,128)(2,1)S(1)}, bf16[512,4096]{1,0:T(8,128)(2,1)}, u32[]{:S(2)}) %copy-start.3) | copy-done | bytes 4194328
  88.3 2.4 %shard_map.230 = (bf16[256,1024]{1,0:T(8,128)(2,1)S(1)}, bf16[256,1024]{1,0:T(8,128)(2,1)S(1)}, bf16[256,1024]{1,0:T(8,128)(2,1)S(1)}, bf16[256,1024]{1,0:T(8,128)(2,1)S(1)}, f32[16,2048]{1,0:T(8,128)S(1)}) custom-call(s32[3]{0:T(128)S(1)} %copy-done.7, bf16[512,512]{1,0:T(8,128)(2,1)S(1)} %get-tuple-element.98.gated_ref.channels_ref, ...), custom_call_target="tpu_custom_call" | custom-call | bytes 1000 | tf_op jit(solution)/shard_map/pallas_call | solution.py:60
  90.8 1.0 collective-permute-start.14
  91.7 0.9 collective-permute-start.15
  92.6 6.0 %collective-permute-done.19.upper_got = bf16[256,1024]{1,0:T(8,128)(2,1)} collective-permute-done((bf16[256,1024]{1,0:T(8,128)(2,1)}, bf16[256,1024]{1,0:T(8,128)(2,1)}, u32[]{:S(2)}, u32[]{:S(2)}) %collective-permute-start.19) | collective-permute-done | bytes 524320 | tf_op jit(solution)/shard_map/ppermute | solution.py:27
  98.6 1.3 collective-permute-done.20.lower_got
  101.2 1.4 %shard_map.234 = (f32[256,512]{1,0:T(8,128)S(1)}, bf16[256,512]{1,0:T(8,128)(2,1)S(1)}, f32[256,512]{1,0:T(8,128)S(1)}, bf16[256,512]{1,0:T(8,128)(2,1)S(1)}) custom-call(s32[1]{0:T(128)} %constant.31.clone.1.unused, bf16[256,1024]{1,0:T(8,128)(2,1)S(1)} %get-tuple-element.116.upper_ref, bf16[256,1024]{1,0:T(8,128)(2,1)} %collective-permute-done.19.upper_got, ...), custom_call_target="tpu_custom_call" | custom-call | flops 10000000000 | bytes 100000000 | tf_op jit(solution)/shard_map/pallas_call | solution.py:60
  102.6 1.0 collective-permute-start.21
  103.6 0.9 collective-permute-start.22
  104.5 1.3 collective-permute-done.26
  105.8 1.6 %collective-permute-start.27 = (bf16[16,4096]{1,0:T(8,128)(2,1)S(1)}, bf16[16,4096]{1,0:T(8,128)(2,1)S(1)}, u32[]{:S(2)}, u32[]{:S(2)}) collective-permute-start(bf16[16,4096]{1,0:T(8,128)(2,1)S(1)} %fusion.5), channel_id=1, source_target_pairs={{0,2},{1,3},{2,0},{3,1},{4,6},{5,7},{6,4},{7,5},{8,10},{9,11},{10,... | collective-permute-start | bytes 393224 | tf_op jit(solution)/shard_map/ppermute | solution.py:27
  107.5 2.2 %collective-permute-done.14.upper_got = bf16[256,1024]{1,0:T(8,128)(2,1)S(1)} collective-permute-done((bf16[256,1024]{1,0:T(8,128)(2,1)S(1)}, bf16[256,1024]{1,0:T(8,128)(2,1)S(1)}, u32[]{:S(2)}, u32[]{:S(2)}) %collective-permute-start.14) | collective-permute-done | bytes 524320 | tf_op jit(solution)/shard_map/ppermute | solution.py:27
  109.7 1.3 collective-permute-done.15.lower_got
  111.3 1.0 collective-permute-start.16
  112.3 0.9 collective-permute-start.17
  113.2 1.2 collective-permute-start.28
  114.4 2.0 %collective-permute-done.21.upper_got = bf16[256,512]{1,0:T(8,128)(2,1)S(1)} collective-permute-done((bf16[256,512]{1,0:T(8,128)(2,1)S(1)}, bf16[256,512]{1,0:T(8,128)(2,1)S(1)}, u32[]{:S(2)}, u32[]{:S(2)}) %collective-permute-start.21) | collective-permute-done | bytes 262176 | tf_op jit(solution)/shard_map/ppermute | solution.py:27
  116.5 1.2 collective-permute-start.23
  117.7 2.1 %collective-permute-start.24 = (bf16[512,256]{1,0:T(8,128)(2,1)S(1)}, bf16[512,256]{1,0:T(8,128)(2,1)S(1)}, u32[]{:S(2)}, u32[]{:S(2)}) collective-permute-start(bf16[512,256]{1,0:T(8,128)(2,1)S(1)} %get-tuple-element.125), channel_id=1, source_target_pairs={{1,0},{2,1},{3,2},{0,3},{5,4},{6,5},{7,6},{4,7},{9,8},{10,9},{11,1... | collective-permute-start | bytes 786440 | tf_op jit(solution)/shard_map/ppermute | solution.py:32
  119.8 1.4 %shard_map.237 = f32[8,512,128]{2,1,0:T(8,128)S(1)} custom-call(s32[1]{0:T(128)} %bitcast.16.first, bf16[512,512]{1,0:T(8,128)(2,1)S(1)} %get-tuple-element.126.spread_ref, bf16[512,128]{1,0:T(8,128)(2,1)S(1)} %get-tuple-element.92.keys_ref, s32[512,128]{1,0:T(8,128)S(1)} %get-tuple-element.90.marks_ref, f32[16,1,128]{2,1,0:T(1,128)S(1)} %bitcast.37, ...), custom_call_target="tpu_custom_call" | custom-call | bytes 1000 | tf_op jit(solution)/shard_map/pallas_call | solution.py:60
  121.4 1.0 collective-permute-start.29
  122.5 1.6 %collective-permute-start.18 = (bf16[512,256]{1,0:T(8,128)(2,1)S(1)}, bf16[512,256]{1,0:T(8,128)(2,1)S(1)}, u32[]{:S(2)}, u32[]{:S(2)}) collective-permute-start(bf16[512,256]{1,0:T(8,128)(2,1)S(1)} %get-tuple-element.111), channel_id=1, source_target_pairs={{3,0},{0,1},{1,2},{2,3},{7,4},{4,5},{5,6},{6,7},{11,8},{8,9},{9,10... | collective-permute-start | bytes 786440 | tf_op jit(solution)/shard_map/ppermute | solution.py:32
  124.1 3.3 %collective-permute-done.29 = bf16[16,4096]{1,0:T(8,128)(2,1)S(1)} collective-permute-done((bf16[16,4096]{1,0:T(8,128)(2,1)S(1)}, bf16[16,4096]{1,0:T(8,128)(2,1)S(1)}, u32[]{:S(2)}, u32[]{:S(2)}) %collective-permute-start.29) | collective-permute-done | bytes 131104 | tf_op jit(solution)/shard_map/ppermute | solution.py:27
  127.5 2.8 %shard_map.238 = f32[8,512,128]{2,1,0:T(8,128)} custom-call(s32[1]{0:T(128)} %bitcast.14.first, bf16[512,512]{1,0:T(8,128)(2,1)S(1)} %get-tuple-element.126.spread_ref, bf16[512,128]{1,0:T(8,128)(2,1)S(1)} %get-tuple-element.92.keys_ref, s32[512,128]{1,0:T(8,128)S(1)} %get-tuple-element.90.marks_ref, f32[16,1,128]{2,1,0:T(1,128)S(1)} %bitcast.38, ...), custom_call_target="tpu_custom_call" | custom-call | bytes 1000 | tf_op jit(solution)/shard_map/pallas_call | solution.py:60
  130.3 3.6 %collective-permute-done.23.refs_1_ = bf16[512,256]{1,0:T(8,128)(2,1)S(1)} collective-permute-done((bf16[512,256]{1,0:T(8,128)(2,1)S(1)}, bf16[512,256]{1,0:T(8,128)(2,1)S(1)}, u32[]{:S(2)}, u32[]{:S(2)}) %collective-permute-start.23) | collective-permute-done | bytes 262176 | tf_op jit(solution)/shard_map/ppermute | solution.py:32
  134.0 0.9 shard_map.236
  135.0 1.2 slice-done.1
  136.2 1.9 %fusion.7 = f32[16,1024]{1,0:T(8,128)} fusion(bf16[4096,1024]{1,0:T(8,128)(2,1)S(1)} %bitcast.41, bf16[16,4096]{1,0:T(8,128)(2,1)S(1)} %get-tuple-element.138, f32[4096]{0:T(1024)S(1)} %copy-done.15, f32[16]{0:T(128)S(1)} %add_rsqrt_fusion), kind=kOutput, calls=%fused_computation.20 | convolution fusion | flops 134479872 | bytes 8601664 | tf_op jit(solution)/shard_map/dot_general | solution.py:938
  (108 shorter events, 6.8 us)
Async XLA Ops:
  0.6 38.8 %copy-start = (bf16[16,3,2,2,128]{4,3,2,1,0:T(2,128)(2,1)S(1)}, bf16[16,3,2,2,128]{4,3,2,1,0:T(2,128)(2,1)}, u32[]{:S(2)}) copy-start(bf16[16,3,2,2,128]{4,3,2,1,0:T(2,128)(2,1)} %param.33) | copy-start | bytes 147460
  0.6 11.0 %collective-permute-start = (bf16[512,256]{1,0:T(8,128)(2,1)}, bf16[512,256]{1,0:T(8,128)(2,1)S(1)}, u32[]{:S(2)}, u32[]{:S(2)}) collective-permute-start(bf16[512,256]{1,0:T(8,128)(2,1)} %tokens_ref.1), channel_id=1, source_target_pairs={{1,0},{2,1},{3,2},{0,3},{5,4},{6,5},{7,6},{4,7},{9,8},{10,9},{11,1... | collective-permute-start | bytes 786440 | tf_op jit(solution)/shard_map/ppermute | solution.py:32
  11.7 14.6 %collective-permute-start.7 = (bf16[256,512]{1,0:T(8,128)(2,1)S(1)}, bf16[256,512]{1,0:T(8,128)(2,1)S(1)}, u32[]{:S(2)}, u32[]{:S(2)}) collective-permute-start(bf16[256,512]{1,0:T(8,128)(2,1)S(1)} %get-tuple-element.140.refs_0_), channel_id=1, source_target_pairs={{0,8},{4,12},{8,0},{12,4},{1,9},{5,13},{9,1},{13,5},{2,10},{6,14},... | collective-permute-start | bytes 786440 | tf_op jit(solution)/shard_map/ppermute | solution.py:27
  13.3 14.4 %collective-permute-start.9 = (bf16[256,512]{1,0:T(8,128)(2,1)S(1)}, bf16[256,512]{1,0:T(8,128)(2,1)S(1)}, u32[]{:S(2)}, u32[]{:S(2)}) collective-permute-start(bf16[256,512]{1,0:T(8,128)(2,1)S(1)} %get-tuple-element.139.refs_3_), channel_id=1, source_target_pairs={{0,4},{4,0},{8,12},{12,8},{1,5},{5,1},{9,13},{13,9},{2,6},{6,2},{1... | collective-permute-start | bytes 786440 | tf_op jit(solution)/shard_map/ppermute | solution.py:27
  14.8 21.5 %collective-permute-start.2 = (bf16[512,256]{1,0:T(8,128)(2,1)}, bf16[512,256]{1,0:T(8,128)(2,1)S(1)}, u32[]{:S(2)}, u32[]{:S(2)}) collective-permute-start(bf16[512,256]{1,0:T(8,128)(2,1)} %tokens_ref.1), channel_id=1, source_target_pairs={{3,0},{0,1},{1,2},{2,3},{7,4},{4,5},{5,6},{6,7},{11,8},{8,9},{9,10... | collective-permute-start | bytes 786440 | tf_op jit(solution)/shard_map/ppermute | solution.py:32
  22.2 14.0 %collective-permute-start.1 = (bf16[512,256]{1,0:T(8,128)(2,1)S(1)}, bf16[512,256]{1,0:T(8,128)(2,1)S(1)}, u32[]{:S(2)}, u32[]{:S(2)}) collective-permute-start(bf16[512,256]{1,0:T(8,128)(2,1)S(1)} %collective-permute-done), channel_id=1, source_target_pairs={{1,0},{2,1},{3,2},{0,3},{5,4},{6,5},{7,6},{4,7},{9,8},{10,9},{11,1... | collective-permute-start | bytes 786440 | tf_op jit(solution)/shard_map/ppermute | solution.py:32
  27.2 21.5 %collective-permute-start.8 = (bf16[256,1024]{1,0:T(8,128)(2,1)}, bf16[256,1024]{1,0:T(8,128)(2,1)S(1)}, u32[]{:S(2)}, u32[]{:S(2)}) collective-permute-start(bf16[256,1024]{1,0:T(8,128)(2,1)} %pad_maximum_fusion.2), channel_id=1, source_target_pairs={{0,4},{4,0},{8,12},{12,8},{1,5},{5,1},{9,13},{13,9},{2,6},{6,2},{1... | collective-permute-start | bytes 1572872 | tf_op jit(solution)/shard_map/ppermute | solution.py:27
  28.6 11.1 %copy-start.16 = (bf16[16,3,512]{2,0,1:T(8,128)(2,1)S(1)}, bf16[16,3,512]{2,0,1:T(8,128)(2,1)}, u32[]{:S(2)}) copy-start(bf16[16,3,512]{2,0,1:T(8,128)(2,1)} %param.32) | copy-start | bytes 147460
  28.6 11.2 %copy-start.19 = (f32[4,2,2,128]{3,2,1,0:T(2,128)S(1)}, f32[4,2,2,128]{3,2,1,0:T(2,128)}, u32[]{:S(2)}) copy-start(f32[4,2,2,128]{3,2,1,0:T(2,128)} %param.29) | copy-start | bytes 24580
  28.6 11.2 %copy-start.17 = (f32[4,512]{1,0:T(4,128)S(1)}, f32[4,512]{1,0:T(4,128)}, u32[]{:S(2)}) copy-start(f32[4,512]{1,0:T(4,128)} %param.28) | copy-start | bytes 24580
  28.6 11.2 %copy-start.20 = (f32[2,2,128]{2,1,0:T(2,128)S(1)}, f32[2,2,128]{2,1,0:T(2,128)}, u32[]{:S(2)}) copy-start(f32[2,2,128]{2,1,0:T(2,128)} %param.31) | copy-start | bytes 6148
  28.6 20.1 %collective-permute-start.10 = (bf16[256,1024]{1,0:T(8,128)(2,1)}, bf16[256,1024]{1,0:T(8,128)(2,1)}, u32[]{:S(2)}, u32[]{:S(2)}) collective-permute-start(bf16[256,1024]{1,0:T(8,128)(2,1)} %pad_maximum_fusion.3), channel_id=1, source_target_pairs={{0,8},{4,12},{8,0},{12,4},{1,9},{5,13},{9,1},{13,5},{2,10},{6,14},... | collective-permute-start | bytes 1572872 | tf_op jit(solution)/shard_map/ppermute | solution.py:27
  36.3 12.5 %copy-start.13 = (f32[1,2048]{1,0:T(1,128)S(1)}, f32[1,2048]{1,0:T(1,128)}, u32[]{:S(2)}) copy-start(f32[1,2048]{1,0:T(1,128)} %get-tuple-element.76.refs_7_) | copy-start | bytes 24580
  36.4 8.6 %collective-permute-start.5 = (bf16[256,512]{1,0:T(8,128)(2,1)S(1)}, bf16[256,512]{1,0:T(8,128)(2,1)S(1)}, u32[]{:S(2)}, u32[]{:S(2)}) collective-permute-start(bf16[256,512]{1,0:T(8,128)(2,1)S(1)} %get-tuple-element.141.refs_3_), channel_id=1, source_target_pairs={{0,4},{4,0},{8,12},{12,8},{1,5},{5,1},{9,13},{13,9},{2,6},{6,2},{1... | collective-permute-start | bytes 786440 | tf_op jit(solution)/shard_map/ppermute | solution.py:27
  37.9 9.1 %collective-permute-start.3 = (bf16[256,512]{1,0:T(8,128)(2,1)S(1)}, bf16[256,512]{1,0:T(8,128)(2,1)S(1)}, u32[]{:S(2)}, u32[]{:S(2)}) collective-permute-start(bf16[256,512]{1,0:T(8,128)(2,1)S(1)} %get-tuple-element.142.refs_0_), channel_id=1, source_target_pairs={{0,8},{4,12},{8,0},{12,4},{1,9},{5,13},{9,1},{13,5},{2,10},{6,14},... | collective-permute-start | bytes 786440 | tf_op jit(solution)/shard_map/ppermute | solution.py:27
  45.0 12.4 %collective-permute-start.6 = (bf16[256,1024]{1,0:T(8,128)(2,1)S(1)}, bf16[256,1024]{1,0:T(8,128)(2,1)S(1)}, u32[]{:S(2)}, u32[]{:S(2)}) collective-permute-start(bf16[256,1024]{1,0:T(8,128)(2,1)S(1)} %pad_maximum_fusion.1), channel_id=1, source_target_pairs={{0,8},{4,12},{8,0},{12,4},{1,9},{5,13},{9,1},{13,5},{2,10},{6,14},... | collective-permute-start | bytes 1572872 | tf_op jit(solution)/shard_map/ppermute | solution.py:27
  47.1 10.5 %collective-permute-start.4 = (bf16[256,1024]{1,0:T(8,128)(2,1)S(1)}, bf16[256,1024]{1,0:T(8,128)(2,1)S(1)}, u32[]{:S(2)}, u32[]{:S(2)}) collective-permute-start(bf16[256,1024]{1,0:T(8,128)(2,1)S(1)} %pad_maximum_fusion), channel_id=1, source_target_pairs={{0,4},{4,0},{8,12},{12,8},{1,5},{5,1},{9,13},{13,9},{2,6},{6,2},{1... | collective-permute-start | bytes 1572872 | tf_op jit(solution)/shard_map/ppermute | solution.py:27
  48.7 2.6 %copy-start.11 = (bf16[2048,1408]{1,0:T(8,128)(2,1)S(1)}, bf16[2048,1408]{1,0:T(8,128)(2,1)}, u32[]{:S(2)}) copy-start(bf16[2048,1408]{1,0:T(8,128)(2,1)} %get-tuple-element.77.refs_8_) | copy-start | bytes 17301508
  51.3 6.3 %copy-start.14 = (f32[1,2048]{1,0:T(1,128)S(1)}, f32[1,2048]{1,0:T(1,128)}, u32[]{:S(2)}) copy-start(f32[1,2048]{1,0:T(1,128)} %get-tuple-element.74.refs_7_) | copy-start | bytes 24580
  57.6 2.6 %copy-start.12 = (bf16[2048,1408]{1,0:T(8,128)(2,1)S(1)}, bf16[2048,1408]{1,0:T(8,128)(2,1)}, u32[]{:S(2)}) copy-start(bf16[2048,1408]{1,0:T(8,128)(2,1)} %get-tuple-element.75.refs_8_) | copy-start | bytes 17301508
  60.2 5.5 %copy-start.18 = (f32[512]{0:T(512)S(1)}, f32[512]{0:T(512)}, u32[]{:S(2)}) copy-start(f32[512]{0:T(512)} %param.30) | copy-start | bytes 6148
  60.2 5.5 %copy-start.4 = (f32[16,8,64,128]{3,2,1,0:T(8,128)S(1)}, f32[16,8,64,128]{3,2,1,0:T(8,128)}, u32[]{:S(2)}) copy-start(f32[16,8,64,128]{3,2,1,0:T(8,128)} %param.34) | copy-start | bytes 12582916
  64.2 2.5 %collective-permute-start.11 = (bf16[16,768]{1,0:T(8,128)(2,1)S(1)}, bf16[16,768]{1,0:T(8,128)(2,1)S(1)}, u32[]{:S(2)}, u32[]{:S(2)}) collective-permute-start(bf16[16,768]{1,0:T(8,128)(2,1)S(1)} %slice.31), channel_id=1, source_target_pairs={{0,16},{1,17},{2,18},{3,19},{4,20},{5,21},{6,22},{7,23},{8,24},{9,... | collective-permute-start | bytes 73736 | tf_op jit(solution)/shard_map/ppermute | solution.py:23
  66.7 6.2 %copy-start.21 = (f32[8]{0:T(128)S(1)}, f32[8]{0:T(128)}, u32[]{:S(2)}) copy-start(f32[8]{0:T(128)} %param.37) | copy-start | bytes 100
  70.8 5.4 %copy-start.10 = (f32[512]{0:T(512)S(1)}, f32[512]{0:T(512)}, u32[]{:S(2)}) copy-start(f32[512]{0:T(512)} %param.38) | copy-start | bytes 6148
  70.8 6.6 %copy-start.2 = (bf16[512,4096]{1,0:T(8,128)(2,1)S(1)}, bf16[512,4096]{1,0:T(8,128)(2,1)}, u32[]{:S(2)}) copy-start(bf16[512,4096]{1,0:T(8,128)(2,1)} %refs_7_.7) | copy-start | bytes 12582916
  70.8 6.6 %copy-start.7 = (s32[3]{0:T(128)S(1)}, s32[3]{0:T(128)}, u32[]{:S(2)}) copy-start(s32[3]{0:T(128)} %pad_add_fusion.place.blocks) | copy-start | bytes 40
  70.8 5.4 %collective-permute-start.12 = (f32[512,128]{1,0:T(8,128)S(1)}, f32[512,128]{1,0:T(8,128)S(1)}, u32[]{:S(2)}, u32[]{:S(2)}) collective-permute-start(f32[512,128]{1,0:T(8,128)S(1)} %get-tuple-element.96), channel_id=1, source_target_pairs={{0,16},{1,17},{2,18},{3,19},{4,20},{5,21},{6,22},{7,23},{8,24},{9,... | collective-permute-start | bytes 786440 | tf_op jit(solution)/shard_map/ppermute | solution.py:23
  77.3 3.8 %collective-permute-start.13 = (f32[8,512]{1,0:T(8,128)S(1)}, f32[8,512]{1,0:T(8,128)S(1)}, u32[]{:S(2)}, u32[]{:S(2)}) collective-permute-start(f32[8,512]{1,0:T(8,128)S(1)} %get-tuple-element.99.own_ref.other_ref), channel_id=1, source_target_pairs={{0,1},{1,0},{2,3},{3,2},{4,5},{5,4},{6,7},{7,6},{8,9},{9,8},{10,11... | collective-permute-start | bytes 49160 | tf_op jit(solution)/shard_map/ppermute | solution.py:27
  82.6 0.8 copy-start.8
  83.4 15.2 %collective-permute-start.19 = (bf16[256,1024]{1,0:T(8,128)(2,1)}, bf16[256,1024]{1,0:T(8,128)(2,1)}, u32[]{:S(2)}, u32[]{:S(2)}) collective-permute-start(bf16[256,1024]{1,0:T(8,128)(2,1)} %get-tuple-element.117), channel_id=1, source_target_pairs={{0,4},{4,0},{8,12},{12,8},{1,5},{5,1},{9,13},{13,9},{2,6},{6,2},{1... | collective-permute-start | bytes 1572872 | tf_op jit(solution)/shard_map/ppermute | solution.py:27
  84.7 15.2 %collective-permute-start.20 = (bf16[256,1024]{1,0:T(8,128)(2,1)}, bf16[256,1024]{1,0:T(8,128)(2,1)}, u32[]{:S(2)}, u32[]{:S(2)}) collective-permute-start(bf16[256,1024]{1,0:T(8,128)(2,1)} %get-tuple-element.119), channel_id=1, source_target_pairs={{0,8},{4,12},{8,0},{12,4},{1,9},{5,13},{9,1},{13,5},{2,10},{6,14},... | collective-permute-start | bytes 1572872 | tf_op jit(solution)/shard_map/ppermute | solution.py:27
  86.1 2.2 %copy-start.3 = (bf16[512,4096]{1,0:T(8,128)(2,1)S(1)}, bf16[512,4096]{1,0:T(8,128)(2,1)}, u32[]{:S(2)}) copy-start(bf16[512,4096]{1,0:T(8,128)(2,1)} %refs_7_.7) | copy-start | bytes 12582916
  88.3 12.9 %copy-start.9 = (bf16[256,1024]{1,0:T(8,128)(2,1)S(1)}, bf16[256,1024]{1,0:T(8,128)(2,1)}, u32[]{:S(2)}) copy-start(bf16[256,1024]{1,0:T(8,128)(2,1)} %copy-done.8) | copy-start | bytes 1572868
  90.8 19.0 %collective-permute-start.14 = (bf16[256,1024]{1,0:T(8,128)(2,1)S(1)}, bf16[256,1024]{1,0:T(8,128)(2,1)S(1)}, u32[]{:S(2)}, u32[]{:S(2)}) collective-permute-start(bf16[256,1024]{1,0:T(8,128)(2,1)S(1)} %get-tuple-element.103), channel_id=1, source_target_pairs={{0,4},{4,0},{8,12},{12,8},{1,5},{5,1},{9,13},{13,9},{2,6},{6,2},{1... | collective-permute-start | bytes 1572872 | tf_op jit(solution)/shard_map/ppermute | solution.py:27
  91.7 19.3 %collective-permute-start.15 = (bf16[256,1024]{1,0:T(8,128)(2,1)S(1)}, bf16[256,1024]{1,0:T(8,128)(2,1)S(1)}, u32[]{:S(2)}, u32[]{:S(2)}) collective-permute-start(bf16[256,1024]{1,0:T(8,128)(2,1)S(1)} %get-tuple-element.105), channel_id=1, source_target_pairs={{0,8},{4,12},{8,0},{12,4},{1,9},{5,13},{9,1},{13,5},{2,10},{6,14},... | collective-permute-start | bytes 1572872 | tf_op jit(solution)/shard_map/ppermute | solution.py:27
  100.5 5.3 %collective-permute-start.26 = (bf16[16,4096]{1,0:T(8,128)(2,1)S(1)}, bf16[16,4096]{1,0:T(8,128)(2,1)S(1)}, u32[]{:S(2)}, u32[]{:S(2)}) collective-permute-start(bf16[16,4096]{1,0:T(8,128)(2,1)S(1)} %convert_element_type.38), channel_id=1, source_target_pairs={{0,1},{1,0},{2,3},{3,2},{4,5},{5,4},{6,7},{7,6},{8,9},{9,8},{10,11... | collective-permute-start | bytes 393224 | tf_op jit(solution)/shard_map/ppermute | solution.py:27
  102.6 13.7 %collective-permute-start.21 = (bf16[256,512]{1,0:T(8,128)(2,1)S(1)}, bf16[256,512]{1,0:T(8,128)(2,1)S(1)}, u32[]{:S(2)}, u32[]{:S(2)}) collective-permute-start(bf16[256,512]{1,0:T(8,128)(2,1)S(1)} %get-tuple-element.121), channel_id=1, source_target_pairs={{0,8},{4,12},{8,0},{12,4},{1,9},{5,13},{9,1},{13,5},{2,10},{6,14},... | collective-permute-start | bytes 786440 | tf_op jit(solution)/shard_map/ppermute | solution.py:27
  103.6 12.8 %collective-permute-start.22 = (bf16[256,512]{1,0:T(8,128)(2,1)S(1)}, bf16[256,512]{1,0:T(8,128)(2,1)S(1)}, u32[]{:S(2)}, u32[]{:S(2)}) collective-permute-start(bf16[256,512]{1,0:T(8,128)(2,1)S(1)} %get-tuple-element.123), channel_id=1, source_target_pairs={{0,4},{4,0},{8,12},{12,8},{1,5},{5,1},{9,13},{13,9},{2,6},{6,2},{1... | collective-permute-start | bytes 786440 | tf_op jit(solution)/shard_map/ppermute | solution.py:27
  105.8 7.3 %collective-permute-start.27 = (bf16[16,4096]{1,0:T(8,128)(2,1)S(1)}, bf16[16,4096]{1,0:T(8,128)(2,1)S(1)}, u32[]{:S(2)}, u32[]{:S(2)}) collective-permute-start(bf16[16,4096]{1,0:T(8,128)(2,1)S(1)} %fusion.5), channel_id=1, source_target_pairs={{0,2},{1,3},{2,0},{3,1},{4,6},{5,7},{6,4},{7,5},{8,10},{9,11},{10,... | collective-permute-start | bytes 393224 | tf_op jit(solution)/shard_map/ppermute | solution.py:27
  111.3 10.1 %collective-permute-start.16 = (bf16[256,512]{1,0:T(8,128)(2,1)S(1)}, bf16[256,512]{1,0:T(8,128)(2,1)S(1)}, u32[]{:S(2)}, u32[]{:S(2)}) collective-permute-start(bf16[256,512]{1,0:T(8,128)(2,1)S(1)} %get-tuple-element.107), channel_id=1, source_target_pairs={{0,8},{4,12},{8,0},{12,4},{1,9},{5,13},{9,1},{13,5},{2,10},{6,14},... | collective-permute-start | bytes 786440 | tf_op jit(solution)/shard_map/ppermute | solution.py:27
  112.3 10.1 %collective-permute-start.17 = (bf16[256,512]{1,0:T(8,128)(2,1)S(1)}, bf16[256,512]{1,0:T(8,128)(2,1)S(1)}, u32[]{:S(2)}, u32[]{:S(2)}) collective-permute-start(bf16[256,512]{1,0:T(8,128)(2,1)S(1)} %get-tuple-element.109), channel_id=1, source_target_pairs={{0,4},{4,0},{8,12},{12,8},{1,5},{5,1},{9,13},{13,9},{2,6},{6,2},{1... | collective-permute-start | bytes 786440 | tf_op jit(solution)/shard_map/ppermute | solution.py:27
  113.2 8.0 %collective-permute-start.28 = (bf16[16,4096]{1,0:T(8,128)(2,1)S(1)}, bf16[16,4096]{1,0:T(8,128)(2,1)S(1)}, u32[]{:S(2)}, u32[]{:S(2)}) collective-permute-start(bf16[16,4096]{1,0:T(8,128)(2,1)S(1)} %fusion.11), channel_id=1, source_target_pairs={{0,4},{4,0},{8,12},{12,8},{1,5},{5,1},{9,13},{13,9},{2,6},{6,2},{1... | collective-permute-start | bytes 393224 | tf_op jit(solution)/shard_map/ppermute | solution.py:27
  116.4 3.4 %copy-start.5 = (f32[16,8,64,128]{3,2,1,0:T(8,128)S(1)}, f32[16,8,64,128]{3,2,1,0:T(8,128)}, u32[]{:S(2)}) copy-start(f32[16,8,64,128]{3,2,1,0:T(8,128)} %param.34) | copy-start | bytes 12582916
  116.5 17.4 %collective-permute-start.23 = (bf16[512,256]{1,0:T(8,128)(2,1)S(1)}, bf16[512,256]{1,0:T(8,128)(2,1)S(1)}, u32[]{:S(2)}, u32[]{:S(2)}) collective-permute-start(bf16[512,256]{1,0:T(8,128)(2,1)S(1)} %get-tuple-element.124), channel_id=1, source_target_pairs={{2,0},{3,1},{0,2},{1,3},{6,4},{7,5},{4,6},{5,7},{10,8},{11,9},{8,1... | collective-permute-start | bytes 786440 | tf_op jit(solution)/shard_map/ppermute | solution.py:32
  117.7 16.2 %collective-permute-start.24 = (bf16[512,256]{1,0:T(8,128)(2,1)S(1)}, bf16[512,256]{1,0:T(8,128)(2,1)S(1)}, u32[]{:S(2)}, u32[]{:S(2)}) collective-permute-start(bf16[512,256]{1,0:T(8,128)(2,1)S(1)} %get-tuple-element.125), channel_id=1, source_target_pairs={{1,0},{2,1},{3,2},{0,3},{5,4},{6,5},{7,6},{4,7},{9,8},{10,9},{11,1... | collective-permute-start | bytes 786440 | tf_op jit(solution)/shard_map/ppermute | solution.py:32
  121.2 6.2 %collective-permute-start.25 = (f32[8,512,128]{2,1,0:T(8,128)S(1)}, f32[8,512,128]{2,1,0:T(8,128)S(1)}, u32[]{:S(2)}, u32[]{:S(2)}) collective-permute-start(f32[8,512,128]{2,1,0:T(8,128)S(1)} %shard_map.237), channel_id=1, source_target_pairs={{0,16},{16,0},{1,17},{17,1},{2,18},{18,2},{3,19},{19,3},{4,20},{20... | collective-permute-start | bytes 6291464 | tf_op jit(solution)/shard_map/ppermute | solution.py:27
  121.4 6.0 %collective-permute-start.29 = (bf16[16,4096]{1,0:T(8,128)(2,1)S(1)}, bf16[16,4096]{1,0:T(8,128)(2,1)S(1)}, u32[]{:S(2)}, u32[]{:S(2)}) collective-permute-start(bf16[16,4096]{1,0:T(8,128)(2,1)S(1)} %fusion.6), channel_id=1, source_target_pairs={{0,8},{4,12},{8,0},{12,4},{1,9},{5,13},{9,1},{13,5},{2,10},{6,14},... | collective-permute-start | bytes 393224 | tf_op jit(solution)/shard_map/ppermute | solution.py:27
  122.5 11.4 %collective-permute-start.18 = (bf16[512,256]{1,0:T(8,128)(2,1)S(1)}, bf16[512,256]{1,0:T(8,128)(2,1)S(1)}, u32[]{:S(2)}, u32[]{:S(2)}) collective-permute-start(bf16[512,256]{1,0:T(8,128)(2,1)S(1)} %get-tuple-element.111), channel_id=1, source_target_pairs={{3,0},{0,1},{1,2},{2,3},{7,4},{4,5},{5,6},{6,7},{11,8},{8,9},{9,10... | collective-permute-start | bytes 786440 | tf_op jit(solution)/shard_map/ppermute | solution.py:32
  127.5 6.5 %copy-start.6 = (bf16[512,256]{1,0:T(8,128)(2,1)S(1)}, bf16[512,256]{1,0:T(8,128)(2,1)}, u32[]{:S(2)}) copy-start(bf16[512,256]{1,0:T(8,128)(2,1)} %tokens_ref.1) | copy-start | bytes 786436
  127.5 7.5 %slice-start = ((s8[8388608]{0:T(1024)(128)(4,1)}), s8[4194304]{0:T(1024)(128)(4,1)S(1)}, s32[]{:S(2)}) async-start(s8[8388608]{0:T(1024)(128)(4,1)} %bitcast.40), calls=%async_computation | async-start | bytes 8388608
  130.3 4.5 %collective-permute-start.30 = (f32[16,4096]{1,0:T(8,128)S(1)}, f32[16,4096]{1,0:T(8,128)S(1)}, u32[]{:S(2)}, u32[]{:S(2)}) collective-permute-start(f32[16,4096]{1,0:T(8,128)S(1)} %add_add_fusion), channel_id=1, source_target_pairs={{0,16},{16,0},{1,17},{17,1},{2,18},{18,2},{3,19},{19,3},{4,20},{20... | collective-permute-start | bytes 786440 | tf_op jit(solution)/shard_map/ppermute | solution.py:27
  133.9 2.3 %slice-start.1 = ((s8[8388608]{0:T(1024)(128)(4,1)}), s8[4194304]{0:T(1024)(128)(4,1)S(1)}, s32[]{:S(2)}) async-start(s8[8388608]{0:T(1024)(128)(4,1)} %bitcast.40), calls=%async_computation.1 | async-start | bytes 8388608
  133.9 2.3 %copy-start.15 = (f32[4096]{0:T(1024)S(1)}, f32[4096]{0:T(1024)}, u32[]{:S(2)}) copy-start(f32[4096]{0:T(1024)} %param.40) | copy-start | bytes 49156
  135.0 3.1 %copy-start.1 = (bf16[16,3,2,2,128]{4,3,2,1,0:T(2,128)(2,1)S(1)}, bf16[16,3,2,2,128]{4,3,2,1,0:T(2,128)(2,1)}, u32[]{:S(2)}) copy-start(bf16[16,3,2,2,128]{4,3,2,1,0:T(2,128)(2,1)} %param.33) | copy-start | bytes 147460
